TPU v7x, 32 devices: a whole 2x2x4 slice. The times are simulated.
32 devices in a mesh: dp: 4 (over y, x), tensor: 4 (over z), context: 2 (over core).
Axes of the slice: x: 2, y: 2, z: 4, core: 2. Of those that a mesh axis runs over, the one named last changes fastest.
Arguments:
- embedded: bfloat16 [8, 1024, 2048], P('dp', ('tensor', 'context')), may hold values from -6 to 6
- initial_state: bfloat16 [8, 1024, 2048], P('dp', ('tensor', 'context')), may hold values from -6 to 6
- cotangent: bfloat16 [8, 1024, 2048], P('dp', ('tensor', 'context')), may hold values from -6 to 6
- doc_ids: int32 [8, 1024], replicated, may hold values from 0 to 3, as said below
- recurrences: int32 [8], replicated, may hold values from 1 to 4, as said below
- adapter_weight: bfloat16 [4096, 2048], P(('dp', 'context')), may hold values from -0.09375 to 0.09375
- norm_gains: bfloat16 [2, 2048], P(None, ('dp', 'context')), may hold values from 0.5 to 1.5
- qkv_weight: bfloat16 [2048, 16, 384], P(('dp', 'context'), 'tensor'), may hold values from -0.125 to 0.125
- output_head_weight: bfloat16 [16, 128, 2048], P('tensor', None, ('dp', 'context')), may hold values from -0.75 to 0.75
- gate_up_weight: bfloat16 [2048, 2, 5632], P(('dp', 'context'), None, 'tensor'), may hold values from -0.125 to 0.125
- down_weight: bfloat16 [5632, 2048], P('tensor', ('dp', 'context')), may hold values from -0.078125 to 0.078125
Outputs:
- final_state: float32 [8, 1024, 2048], P('dp', ('tensor', 'context'))
- embed_grad: float32 [8, 1024, 2048], P('dp', ('tensor', 'context'))
- adapter_grad: float32 [4096, 2048], P(('dp', 'context'))
- gains_grad: float32 [2, 2048], P(None, ('dp', 'context'))
- qkv_grad: float32 [2048, 16, 384], P(('dp', 'context'), 'tensor')
- out_grad: float32 [16, 128, 2048], P('tensor', None, ('dp', 'context'))
- gate_up_grad: float32 [2048, 2, 5632], P(('dp', 'context'), None, 'tensor')
- down_grad: float32 [5632, 2048], P('tensor', ('dp', 'context'))
Inputs may be any that keep to these rules, and one draw needn't show every extreme that they name: `doc_ids`: along a sequence the number never falls and rises by one at a time; at most 4 documents a sequence. In every draw some sequence takes exactly 4 recurrences and some exactly 1.
All inputs are finite; a program needn't handle non-finite values.
Results may differ from a plain program's by a relative error of at most 0.028.
Values may be sent and summed in bfloat16 or wider, within the bound.
A program may use at most 256 MiB of HBM per device.

v0:
```python
from functools import partial
import math

import jax
import jax.numpy as jnp
from jax import lax
from jax.sharding import PartitionSpec as P

BACK = 1


rope_base = 50000.0
norm_eps = 1e-06
masked_score = -1e30


def rope_angles(positions, head_dim):
    freq_index = jnp.arange(head_dim // 2, dtype=jnp.float32)
    inv_freq = 1.0 / rope_base ** (2.0 * freq_index / head_dim)
    angles = positions.astype(jnp.float32)[:, None] * inv_freq[None, :]
    return (jnp.cos(angles), jnp.sin(angles))


def rotate_fwd(values, cos_t, sin_t):
    half_dim = values.shape[-1] // 2
    first_half = values[..., :half_dim]
    second_half = values[..., half_dim:]
    return jnp.concatenate(
        [first_half * cos_t - second_half * sin_t, second_half * cos_t + first_half * sin_t],
        axis=-1,
    )


def rotate_back(grad_vals, cos_t, sin_t):
    half_dim = grad_vals.shape[-1] // 2
    first_half = grad_vals[..., :half_dim]
    second_half = grad_vals[..., half_dim:]
    return jnp.concatenate(
        [first_half * cos_t + second_half * sin_t, second_half * cos_t - first_half * sin_t],
        axis=-1,
    )


def rms_parts(rows):
    factor = lax.rsqrt(jnp.mean(rows * rows, axis=-1, keepdims=True) + norm_eps)
    return (rows * factor, factor)


def score_block(query_blk, key_blk, doc_query, doc_key, query_pos, key_pos, score_scale):
    scores = (
        jnp.einsum("qhd,khd->hqk", query_blk, key_blk, preferred_element_type=jnp.float32)
        * score_scale
    )
    allowed = (key_pos[None, :] <= query_pos[:, None]) & (doc_query[:, None] == doc_key[None, :])
    return jnp.where(allowed[None], scores, masked_score)


def attend_block(packed, query_pos, key_pos, score_scale):
    query_blk, key_blk, value_blk, doc_query, doc_key = packed
    scores = score_block(query_blk, key_blk, doc_query, doc_key, query_pos, key_pos, score_scale)
    row_max = jnp.max(scores, axis=-1, keepdims=True)
    exp_vals = jnp.exp(scores - row_max)
    totals = jnp.sum(exp_vals, axis=-1, keepdims=True)
    prob_vals = exp_vals / totals
    head_vals = jnp.einsum(
        "hqk,khd->qhd",
        prob_vals.astype(jnp.bfloat16),
        value_blk,
        preferred_element_type=jnp.float32,
    )
    return (head_vals.astype(jnp.bfloat16), row_max + jnp.log(totals))


def attend_back(packed, query_pos, key_pos, score_scale):
    query_blk, key_blk, value_blk, grad_blk, lse_blk, doc_query, doc_key = packed
    scores = score_block(query_blk, key_blk, doc_query, doc_key, query_pos, key_pos, score_scale)
    prob_vals = jnp.exp(scores - lse_blk)
    grad_value = jnp.einsum(
        "hqk,qhd->khd", prob_vals.astype(jnp.bfloat16), grad_blk, preferred_element_type=jnp.float32
    )
    grad_prob = jnp.einsum("qhd,khd->hqk", grad_blk, value_blk, preferred_element_type=jnp.float32)
    row_dot = jnp.sum(prob_vals * grad_prob, axis=-1, keepdims=True)
    grad_score = (prob_vals * (grad_prob - row_dot)).astype(jnp.bfloat16)
    grad_query = (
        jnp.einsum("hqk,khd->qhd", grad_score, key_blk, preferred_element_type=jnp.float32)
        * score_scale
    )
    grad_key = (
        jnp.einsum("hqk,qhd->khd", grad_score, query_blk, preferred_element_type=jnp.float32)
        * score_scale
    )
    return (grad_query, grad_key, grad_value)


def tensor_rows(rows):
    return lax.all_gather(rows, "tensor", axis=1, tiled=True)


def tensor_sum(part):
    return lax.psum_scatter(
        part.astype(jnp.bfloat16), "tensor", scatter_dimension=1, tiled=True
    ).astype(jnp.float32)


def shards(
    embedded,
    initial_state,
    cotangent,
    doc_ids,
    recurrences,
    adapter_weight,
    norm_gains,
    qkv_weight,
    output_head_weight,
    gate_up_weight,
    down_weight,
):
    (
        adapter_full,
        gains_full,
        query_key_value_gathered,
        out_full,
        gate_up_full,
        down_weight_gathered,
    ) = (
        lax.all_gather(adapter_weight, ("dp", "context"), axis=0, tiled=True),
        lax.all_gather(norm_gains, ("dp", "context"), axis=1, tiled=True),
        lax.all_gather(qkv_weight, ("dp", "context"), axis=0, tiled=True),
        lax.all_gather(output_head_weight, ("dp", "context"), axis=2, tiled=True),
        lax.all_gather(gate_up_weight, ("dp", "context"), axis=0, tiled=True),
        lax.all_gather(down_weight, ("dp", "context"), axis=1, tiled=True),
    )
    gate_up_use, down_use = (gate_up_full, down_weight_gathered)
    gains_f = gains_full.astype(jnp.float32)
    tensor_parallel_count = lax.axis_size("tensor")
    n_context = lax.axis_size("context")
    ctx_index = lax.axis_index("context")
    dp_index = lax.axis_index("dp")
    seq_count, block_rows, model_width = embedded.shape
    seq_len = doc_ids.shape[1]
    head_dim = query_key_value_gathered.shape[2] // 3
    score_scale = 1.0 / math.sqrt(head_dim)
    key_pos = jnp.arange(seq_len, dtype=jnp.int32)
    query_pos = lax.dynamic_index_in_dim(
        key_pos.reshape(tensor_parallel_count, n_context, block_rows),
        ctx_index,
        axis=1,
        keepdims=False,
    ).reshape(-1)
    cos_all, sin_all = rope_angles(key_pos, head_dim)
    cos_own, sin_own = rope_angles(query_pos, head_dim)
    cos_all = cos_all[:, None, :]
    sin_all = sin_all[:, None, :]
    cos_own = cos_own[:, None, :]
    sin_own = sin_own[:, None, :]
    own_start = dp_index * seq_count
    own_docs = lax.dynamic_slice_in_dim(doc_ids, own_start, seq_count, 0)
    steps_all = recurrences - BACK
    steps_own = lax.dynamic_slice_in_dim(steps_all, own_start, seq_count, 0)
    forward_fn = partial(
        attend_block, query_pos=query_pos, key_pos=key_pos, score_scale=score_scale
    )
    backward_fn = partial(
        attend_back, query_pos=query_pos, key_pos=key_pos, score_scale=score_scale
    )
    full_weights = (query_key_value_gathered, out_full, gate_up_use, down_use)

    def core_step(latent, embed_rows, doc_rows, layer_weights):
        qkv_use, out_use, gate_up_here, down_here = layer_weights
        doc_query = doc_rows[:, query_pos]
        joined = jnp.concatenate([latent.astype(jnp.bfloat16), embed_rows], axis=-1)
        adapted = jnp.einsum(
            "srk,kd->srd", joined, adapter_full, preferred_element_type=jnp.float32
        )
        unit_a, factor_a = rms_parts(adapted)
        normed_a = (unit_a * gains_f[0]).astype(jnp.bfloat16)
        feature_rows = lax.all_gather(normed_a, ("tensor", "context"), axis=1, tiled=True)
        seq_here = feature_rows.shape[0]
        query_src = lax.dynamic_index_in_dim(
            feature_rows.reshape(
                seq_here, tensor_parallel_count, n_context, block_rows, model_width
            ),
            ctx_index,
            axis=2,
            keepdims=False,
        ).reshape(seq_here, -1, model_width)
        query_lin = jnp.einsum(
            "sqd,dhk->sqhk", query_src, qkv_use[:, :, :head_dim], preferred_element_type=jnp.float32
        )
        pair_lin = jnp.einsum(
            "vbx,xyf->vbyf",
            feature_rows,
            qkv_use[:, :, head_dim:],
            preferred_element_type=jnp.float32,
        )
        query_rot = rotate_fwd(query_lin, cos_own, sin_own).astype(jnp.bfloat16)
        key_rot = rotate_fwd(pair_lin[..., :head_dim], cos_all, sin_all).astype(jnp.bfloat16)
        value_rows = pair_lin[..., head_dim:].astype(jnp.bfloat16)
        head_vals, lse_vals = lax.map(
            forward_fn, (query_rot, key_rot, value_rows, doc_query, doc_rows)
        )
        attn_part = jnp.einsum(
            "sqhd,hdm->sqm", head_vals, out_use, preferred_element_type=jnp.float32
        )
        attn_rows = tensor_sum(attn_part)
        mixed_rows = adapted + attn_rows
        unit_b, factor_b = rms_parts(mixed_rows)
        normed_b = (unit_b * gains_f[1]).astype(jnp.bfloat16)
        ffn_input = tensor_rows(normed_b)
        gate_up = jnp.einsum(
            "sqd,dgf->sqgf", ffn_input, gate_up_here, preferred_element_type=jnp.float32
        )
        gate_pre = gate_up[:, :, 0]
        up_pre = gate_up[:, :, 1]
        hidden_activations = (jax.nn.silu(gate_pre) * up_pre).astype(jnp.bfloat16)
        ffn_part = jnp.einsum(
            "sqf,fd->sqd", hidden_activations, down_here, preferred_element_type=jnp.float32
        )
        ffn_total = tensor_sum(ffn_part)
        saved_vals = (
            joined,
            adapted,
            feature_rows,
            query_rot,
            key_rot,
            value_rows,
            head_vals,
            lse_vals,
            mixed_rows,
            ffn_input,
            gate_pre,
            up_pre,
            hidden_activations,
            doc_rows,
            doc_query,
        )
        return (mixed_rows + ffn_total, saved_vals)

    def advance_all(step_index, current_rows):
        advanced = core_step(current_rows, embedded, own_docs, full_weights)[0]
        return jnp.where((step_index < steps_own)[:, None, None], advanced, current_rows)

    detached = lax.fori_loop(0, jnp.max(steps_all), advance_all, initial_state.astype(jnp.float32))
    current = detached
    round_index = 0
    current, saved_vals = core_step(current, embedded, own_docs, full_weights)
    saved_list = [saved_vals]
    grad_latent = cotangent.astype(jnp.float32)
    embed_grad = jnp.zeros(embedded.shape, jnp.float32)
    total_grads = None
    for round_index in reversed(range(BACK)):
        grad_out = grad_latent
        (
            back_joined,
            back_adapted,
            back_feature_rows,
            back_query_rot,
            back_key_rot,
            back_value_rows,
            back_head_vals,
            back_lse_vals,
            back_mixed_rows,
            back_ffn_input,
            back_gate_pre,
            back_up_pre,
            back_hidden_activations,
            back_doc_rows,
            back_doc_query,
        ) = saved_list[round_index]
        grad_low = grad_out.astype(jnp.bfloat16)
        grad_ffn = tensor_rows(grad_low)
        down_grad = jnp.einsum(
            "sqf,sqd->fd", back_hidden_activations, grad_ffn, preferred_element_type=jnp.float32
        )
        grad_hidden = jnp.einsum(
            "sqd,fd->sqf", grad_ffn, down_use, preferred_element_type=jnp.float32
        )
        sigmoid_gate = jax.nn.sigmoid(back_gate_pre)
        grad_gate = (
            grad_hidden * back_up_pre * sigmoid_gate * (1.0 + back_gate_pre * (1.0 - sigmoid_gate))
        )
        grad_up = grad_hidden * jax.nn.silu(back_gate_pre)
        grad_pair = jnp.stack([grad_gate, grad_up], axis=2).astype(jnp.bfloat16)
        gate_up_grad = jnp.einsum(
            "sqd,sqgf->dgf", back_ffn_input, grad_pair, preferred_element_type=jnp.float32
        )
        normb_part = jnp.einsum(
            "sqgf,dgf->sqd", grad_pair, gate_up_use, preferred_element_type=jnp.float32
        )
        grad_normb = tensor_sum(normb_part)
        back_unit_b, back_factor_b = rms_parts(back_mixed_rows)
        weighted_b = grad_normb * gains_f[1]
        gain_b = jnp.sum(grad_normb * back_unit_b, axis=(0, 1))
        grad_mixed = grad_out + back_factor_b * (
            weighted_b - back_unit_b * jnp.mean(weighted_b * back_unit_b, axis=-1, keepdims=True)
        )
        grad_heads = tensor_rows(grad_mixed.astype(jnp.bfloat16))
        out_grad = jnp.einsum(
            "sqhd,sqm->hdm", back_head_vals, grad_heads, preferred_element_type=jnp.float32
        )
        grad_head_vals = jnp.einsum(
            "sqm,hdm->sqhd", grad_heads, out_full, preferred_element_type=jnp.float32
        ).astype(jnp.bfloat16)
        grad_query, grad_key, grad_value = lax.map(
            backward_fn,
            (
                back_query_rot,
                back_key_rot,
                back_value_rows,
                grad_head_vals,
                back_lse_vals,
                back_doc_query,
                back_doc_rows,
            ),
        )
        grad_query = rotate_back(grad_query, cos_own, sin_own)
        grad_key = rotate_back(grad_key, cos_all, sin_all)
        back_seq_here = grad_query.shape[0]
        heads_here = grad_query.shape[2]
        query_full = jnp.zeros(
            (back_seq_here, tensor_parallel_count, n_context, block_rows, heads_here, head_dim),
            jnp.float32,
        )
        query_full = lax.dynamic_update_slice_in_dim(
            query_full,
            grad_query.reshape(
                back_seq_here, tensor_parallel_count, 1, block_rows, heads_here, head_dim
            ),
            ctx_index,
            axis=2,
        )
        projection_gradient = jnp.concatenate(
            [
                query_full.reshape(back_seq_here, seq_len, heads_here, head_dim),
                grad_key,
                grad_value,
            ],
            axis=-1,
        ).astype(jnp.bfloat16)
        qkv_grad = jnp.einsum(
            "cxq,cxtu->qtu",
            back_feature_rows,
            projection_gradient,
            preferred_element_type=jnp.float32,
        )
        norma_part = jnp.einsum(
            "raew,iew->rai",
            projection_gradient,
            query_key_value_gathered,
            preferred_element_type=jnp.float32,
        )
        grad_norma = lax.psum_scatter(
            norma_part.astype(jnp.bfloat16), ("tensor", "context"), scatter_dimension=1, tiled=True
        ).astype(jnp.float32)
        back_unit_a, back_factor_a = rms_parts(back_adapted)
        weighted_a = grad_norma * gains_f[0]
        gain_a = jnp.sum(grad_norma * back_unit_a, axis=(0, 1))
        grad_adapted = grad_mixed + back_factor_a * (
            weighted_a - back_unit_a * jnp.mean(weighted_a * back_unit_a, axis=-1, keepdims=True)
        )
        adapted_low = grad_adapted.astype(jnp.bfloat16)
        adapter_grad = jnp.einsum(
            "srk,srd->kd", back_joined, adapted_low, preferred_element_type=jnp.float32
        )
        back_grad_latent = None
        grad_embed = jnp.einsum(
            "srd,kd->srk",
            adapted_low,
            adapter_full[model_width:],
            preferred_element_type=jnp.float32,
        )
        grad_latent, grad_embed, round_grads = (
            back_grad_latent,
            grad_embed,
            (
                adapter_grad,
                jnp.stack([gain_a, gain_b]),
                qkv_grad,
                out_grad,
                gate_up_grad,
                down_grad,
            ),
        )
        embed_grad = grad_embed
        total_grads = round_grads
    adapter_g, gains_g, qkv_g, out_g, gate_up_g, down_g = total_grads
    adapter_s, gains_s, qkv_s, out_s, gate_up_s, down_weight_shard = (
        lax.psum_scatter(
            adapter_g.astype(jnp.bfloat16), ("dp", "context"), scatter_dimension=0, tiled=True
        ).astype(jnp.float32),
        lax.psum_scatter(
            gains_g.astype(jnp.bfloat16), ("dp", "context"), scatter_dimension=1, tiled=True
        ).astype(jnp.float32),
        lax.psum_scatter(
            qkv_g.astype(jnp.bfloat16), ("dp", "context"), scatter_dimension=0, tiled=True
        ).astype(jnp.float32),
        lax.psum_scatter(
            out_g.astype(jnp.bfloat16), ("dp", "context"), scatter_dimension=2, tiled=True
        ).astype(jnp.float32),
        lax.psum_scatter(
            gate_up_g.astype(jnp.bfloat16), ("dp", "context"), scatter_dimension=0, tiled=True
        ).astype(jnp.float32),
        lax.psum_scatter(
            down_g.astype(jnp.bfloat16), ("dp", "context"), scatter_dimension=1, tiled=True
        ).astype(jnp.float32),
    )
    adapter_s, gains_s = (
        lax.psum(adapter_s.astype(jnp.bfloat16), "tensor").astype(jnp.float32),
        lax.psum(gains_s.astype(jnp.bfloat16), "tensor").astype(jnp.float32),
    )
    return (current, embed_grad, adapter_s, gains_s, qkv_s, out_s, gate_up_s, down_weight_shard)


def solution(mesh):
    placed = (
        P("dp", ("tensor", "context"), None),
        P("dp", ("tensor", "context"), None),
        P("dp", ("tensor", "context"), None),
        P(),
        P(),
        P(("dp", "context"), None),
        P(None, ("dp", "context")),
        P(("dp", "context"), "tensor", None),
        P("tensor", None, ("dp", "context")),
        P(("dp", "context"), None, "tensor"),
        P("tensor", ("dp", "context")),
    )
    return jax.shard_map(
        shards,
        mesh=mesh,
        in_specs=placed,
        out_specs=(
            P("dp", ("tensor", "context"), None),
            P("dp", ("tensor", "context"), None),
            P(("dp", "context"), None),
            P(None, ("dp", "context")),
            P(("dp", "context"), "tensor", None),
            P("tensor", None, ("dp", "context")),
            P(("dp", "context"), None, "tensor"),
            P("tensor", ("dp", "context")),
        ),
        check_vma=False,
    )
```

profile of v0, /device:TPU:1, one launch (start us, length us, event | category | flops | bytes accessed | tf_op | source)
XLA Modules:
  0.0 2933.4 jit_solution(7699187761280370199)
XLA Ops:
  136.1 70.1 %all-gather.18.cloned.1.call-done = bf16[2048,2,1408]{2,0,1:T(8,128)(2,1)} async-done(((bf16[256,2,1408]{2,0,1:T(8,128)(2,1)}), bf16[2048,2,1408]{2,0,1:T(8,128)(2,1)}) %all-gather.18.cloned.1.call-update) | async-done | bytes 11534352 | tf_op jit(solution)/shard_map/all_gather | solution.py:130
  206.1 91.6 %all-gather.12.cloned.1.call-done = bf16[4096,2048]{1,0:T(8,128)(2,1)} async-done(((bf16[512,2048]{1,0:T(8,128)(2,1)}), bf16[4096,2048]{1,0:T(8,128)(2,1)}) %all-gather.12.cloned.1.call-update) | async-done | bytes 16777232 | tf_op jit(solution)/shard_map/all_gather | solution.py:126
  297.8 1267.0 %while.65 = (s32[]{:T(128)}, bf16[2,128,2048]{2,1,0:T(8,128)(2,1)}, s32[]{:T(128)}, s32[2]{0:T(128)}, bf16[2,128,2048]{2,1,0:T(8,128)(2,1)}, /*index=5*/bf16[409...) while((s32[]{:T(128)}, bf16[2,128,2048]{2,1,0:T(8,128)(2,1)}, ...), condition=%wide.region_10.11_spmd.clone.clone.clone, body=%wide.region_1.10_spmd.clone.clone.clone.sunk | while | flops 36028649472 | bytes 304407872 | solution.py:243
  315.7 75.1 %all-gather.30.cloned.1.call-done = bf16[2,1024,2048]{2,1,0:T(8,128)(2,1)} async-done(((bf16[2,128,2048]{2,1,0:T(8,128)(2,1)}), bf16[2,1024,2048]{2,1,0:T(8,128)(2,1)}) %all-gather.30.cloned.1.call-update) | async-done | bytes 8388624 | tf_op jit(solution)/shard_map/while/body/all_gather | solution.py:177
  449.1 75.0 %reduce-scatter.35.cloned.1.call-done = bf16[2,128,2048]{2,1,0:T(8,128)(2,1)} async-done(((bf16[2,512,2048]{2,1,0:T(8,128)(2,1)}), bf16[2,128,2048]{2,1,0:T(8,128)(2,1)}) %reduce-scatter.35.cloned.1.call-update) | async-done | bytes 1048592 | tf_op jit(solution)/shard_map/while/body/reduce_scatter | solution.py:100
  528.3 81.3 %all-gather.32.cloned.1.call-done = bf16[2,512,2048]{2,1,0:T(8,128)(2,1)} async-done(((bf16[2,128,2048]{2,1,0:T(8,128)(2,1)}), bf16[2,512,2048]{2,1,0:T(8,128)(2,1)}) %all-gather.32.cloned.1.call-update) | async-done | bytes 4194320 | tf_op jit(solution)/shard_map/while/body/all_gather | solution.py:96
  638.3 74.9 %reduce-scatter.37.cloned.1.call-done = bf16[2,128,2048]{2,1,0:T(8,128)(2,1)} async-done(((bf16[2,512,2048]{2,1,0:T(8,128)(2,1)}), bf16[2,128,2048]{2,1,0:T(8,128)(2,1)}) %reduce-scatter.37.cloned.1.call-update) | async-done | bytes 1048592 | tf_op jit(solution)/shard_map/while/body/reduce_scatter | solution.py:100
  734.3 76.1 %all-gather.30.cloned.1.call-done = bf16[2,1024,2048]{2,1,0:T(8,128)(2,1)} async-done(((bf16[2,128,2048]{2,1,0:T(8,128)(2,1)}), bf16[2,1024,2048]{2,1,0:T(8,128)(2,1)}) %all-gather.30.cloned.1.call-update) | async-done | bytes 8388624 | tf_op jit(solution)/shard_map/while/body/all_gather | solution.py:177
  868.6 75.0 %reduce-scatter.35.cloned.1.call-done = bf16[2,128,2048]{2,1,0:T(8,128)(2,1)} async-done(((bf16[2,512,2048]{2,1,0:T(8,128)(2,1)}), bf16[2,128,2048]{2,1,0:T(8,128)(2,1)}) %reduce-scatter.35.cloned.1.call-update) | async-done | bytes 1048592 | tf_op jit(solution)/shard_map/while/body/reduce_scatter | solution.py:100
  947.9 81.3 %all-gather.32.cloned.1.call-done = bf16[2,512,2048]{2,1,0:T(8,128)(2,1)} async-done(((bf16[2,128,2048]{2,1,0:T(8,128)(2,1)}), bf16[2,512,2048]{2,1,0:T(8,128)(2,1)}) %all-gather.32.cloned.1.call-update) | async-done | bytes 4194320 | tf_op jit(solution)/shard_map/while/body/all_gather | solution.py:96
  1057.8 74.9 %reduce-scatter.37.cloned.1.call-done = bf16[2,128,2048]{2,1,0:T(8,128)(2,1)} async-done(((bf16[2,512,2048]{2,1,0:T(8,128)(2,1)}), bf16[2,128,2048]{2,1,0:T(8,128)(2,1)}) %reduce-scatter.37.cloned.1.call-update) | async-done | bytes 1048592 | tf_op jit(solution)/shard_map/while/body/reduce_scatter | solution.py:100
  1153.8 76.1 %all-gather.30.cloned.1.call-done = bf16[2,1024,2048]{2,1,0:T(8,128)(2,1)} async-done(((bf16[2,128,2048]{2,1,0:T(8,128)(2,1)}), bf16[2,1024,2048]{2,1,0:T(8,128)(2,1)}) %all-gather.30.cloned.1.call-update) | async-done | bytes 8388624 | tf_op jit(solution)/shard_map/while/body/all_gather | solution.py:177
  1288.2 75.0 %reduce-scatter.35.cloned.1.call-done = bf16[2,128,2048]{2,1,0:T(8,128)(2,1)} async-done(((bf16[2,512,2048]{2,1,0:T(8,128)(2,1)}), bf16[2,128,2048]{2,1,0:T(8,128)(2,1)}) %reduce-scatter.35.cloned.1.call-update) | async-done | bytes 1048592 | tf_op jit(solution)/shard_map/while/body/reduce_scatter | solution.py:100
  1367.4 81.3 %all-gather.32.cloned.1.call-done = bf16[2,512,2048]{2,1,0:T(8,128)(2,1)} async-done(((bf16[2,128,2048]{2,1,0:T(8,128)(2,1)}), bf16[2,512,2048]{2,1,0:T(8,128)(2,1)}) %all-gather.32.cloned.1.call-update) | async-done | bytes 4194320 | tf_op jit(solution)/shard_map/while/body/all_gather | solution.py:96
  1477.4 74.9 %reduce-scatter.37.cloned.1.call-done = bf16[2,128,2048]{2,1,0:T(8,128)(2,1)} async-done(((bf16[2,512,2048]{2,1,0:T(8,128)(2,1)}), bf16[2,128,2048]{2,1,0:T(8,128)(2,1)}) %reduce-scatter.37.cloned.1.call-update) | async-done | bytes 1048592 | tf_op jit(solution)/shard_map/while/body/reduce_scatter | solution.py:100
  1581.6 77.8 %all-gather.22.cloned.1.call-done = bf16[2,1024,2048]{2,1,0:T(8,128)(2,1)} async-done(((bf16[2,128,2048]{2,1,0:T(8,128)(2,1)}), bf16[2,1024,2048]{2,1,0:T(8,128)(2,1)}) %all-gather.22.cloned.1.call-update) | async-done | bytes 8388624 | tf_op jit(solution)/shard_map/all_gather | solution.py:177
  1711.6 75.0 %reduce-scatter.15.cloned.1.call-done = bf16[2,128,2048]{2,1,0:T(8,128)(2,1)} async-done(((bf16[2,512,2048]{2,1,0:T(8,128)(2,1)}), bf16[2,128,2048]{2,1,0:T(8,128)(2,1)}) %reduce-scatter.15.cloned.1.call-update) | async-done | bytes 1048592 | tf_op jit(solution)/shard_map/reduce_scatter | solution.py:100
  1792.5 80.6 %all-gather.24.cloned.1.call-done = bf16[2,512,2048]{2,1,0:T(8,128)(2,1)} async-done(((bf16[2,128,2048]{2,1,0:T(8,128)(2,1)}), bf16[2,512,2048]{2,1,0:T(8,128)(2,1)}) %all-gather.24.cloned.1.call-update) | async-done | bytes 4194320 | tf_op jit(solution)/shard_map/all_gather | solution.py:96
  1987.8 75.4 %reduce-scatter.19.cloned.1.call-done = bf16[2,128,2048]{2,1,0:T(8,128)(2,1)} async-done(((bf16[2,512,2048]{2,1,0:T(8,128)(2,1)}), bf16[2,128,2048]{2,1,0:T(8,128)(2,1)}) %reduce-scatter.19.cloned.1.call-update) | async-done | bytes 1048592 | tf_op jit(solution)/shard_map/reduce_scatter | solution.py:100
  2068.5 81.3 %all-gather.28.cloned.1.call-done = bf16[2,512,2048]{2,1,0:T(8,128)(2,1)} async-done(((bf16[2,128,2048]{2,1,0:T(8,128)(2,1)}), bf16[2,512,2048]{2,1,0:T(8,128)(2,1)}) %all-gather.28.cloned.1.call-update) | async-done | bytes 4194320 | tf_op jit(solution)/shard_map/all_gather | solution.py:96
  2244.7 73.4 %reduce-scatter.21.cloned.1.call-done = bf16[2,128,2048]{2,1,0:T(8,128)(2,1)} async-done(((bf16[2,1024,2048]{2,1,0:T(8,128)(2,1)}), bf16[2,128,2048]{2,1,0:T(8,128)(2,1)}) %reduce-scatter.21.cloned.1.call-update) | async-done | bytes 1048592 | tf_op jit(solution)/shard_map/reduce_scatter | solution.py:352
  2320.6 77.7 %reduce-scatter.17.cloned.1.call-done = bf16[2,128,2048]{2,1,0:T(8,128)(2,1)} async-done(((bf16[2,512,2048]{2,1,0:T(8,128)(2,1)}), bf16[2,128,2048]{2,1,0:T(8,128)(2,1)}) %reduce-scatter.17.cloned.1.call-update) | async-done | bytes 1048592 | tf_op jit(solution)/shard_map/reduce_scatter | solution.py:100
  2597.5 88.0 %reduce-scatter.29.cloned.1.call-done = bf16[256,2,1408]{2,0,1:T(8,128)(2,1)} async-done(((bf16[2048,2,1408]{2,0,1:T(8,128)(2,1)}), bf16[256,2,1408]{2,0,1:T(8,128)(2,1)}) %reduce-scatter.29.cloned.1.call-update) | async-done | bytes 1441808 | tf_op jit(solution)/shard_map/reduce_scatter | solution.py:400
  2844.1 78.2 %all-reduce.2.cloned.1.call-done = bf16[512,2048]{1,0:T(8,128)(2,1)} async-done(((bf16[512,2048]{1,0:T(8,128)(2,1)}), bf16[512,2048]{1,0:T(8,128)(2,1)}) %all-reduce.2.cloned.1.call-update) | async-done | bytes 2097168 | tf_op jit(solution)/shard_map/psum | solution.py:408
  (479 shorter events, 1268.0 us)
Async XLA Ops:
  12.7 193.4 %all-gather.18.cloned.1.call-start = ((), (), s32[]{:S(2)}) async-start(), calls=%async_computation.15 | async-start | bytes 12976128 | tf_op jit(solution)/shard_map/all_gather | solution.py:130
  14.0 283.7 %all-gather.12.cloned.1.call-start = ((), (), s32[]{:S(2)}) async-start(), calls=%async_computation.12 | async-start | bytes 18874368 | tf_op jit(solution)/shard_map/all_gather | solution.py:126
  308.6 215.5 %reduce-scatter.35.cloned.1.call-start = ((), (), s32[]{:S(2)}) async-start(), calls=%async_computation.33 | async-start | bytes 5242880 | tf_op jit(solution)/shard_map/while/body/reduce_scatter | solution.py:100
  449.0 160.6 %all-gather.32.cloned.1.call-start = ((), (), s32[]{:S(2)}) async-start(), calls=%async_computation.34 | async-start | bytes 5242880 | tf_op jit(solution)/shard_map/while/body/all_gather | solution.py:96
  528.2 184.9 %reduce-scatter.37.cloned.1.call-start = ((), (), s32[]{:S(2)}) async-start(), calls=%async_computation.35 | async-start | bytes 5242880 | tf_op jit(solution)/shard_map/while/body/reduce_scatter | solution.py:100
  727.2 216.5 %reduce-scatter.35.cloned.1.call-start = ((), (), s32[]{:S(2)}) async-start(), calls=%async_computation.33 | async-start | bytes 5242880 | tf_op jit(solution)/shard_map/while/body/reduce_scatter | solution.py:100
  868.6 160.6 %all-gather.32.cloned.1.call-start = ((), (), s32[]{:S(2)}) async-start(), calls=%async_computation.34 | async-start | bytes 5242880 | tf_op jit(solution)/shard_map/while/body/all_gather | solution.py:96
  947.8 184.9 %reduce-scatter.37.cloned.1.call-start = ((), (), s32[]{:S(2)}) async-start(), calls=%async_computation.35 | async-start | bytes 5242880 | tf_op jit(solution)/shard_map/while/body/reduce_scatter | solution.py:100
  1146.7 216.5 %reduce-scatter.35.cloned.1.call-start = ((), (), s32[]{:S(2)}) async-start(), calls=%async_computation.33 | async-start | bytes 5242880 | tf_op jit(solution)/shard_map/while/body/reduce_scatter | solution.py:100
  1367.4 184.9 %reduce-scatter.37.cloned.1.call-start = ((), (), s32[]{:S(2)}) async-start(), calls=%async_computation.35 | async-start | bytes 5242880 | tf_op jit(solution)/shard_map/while/body/reduce_scatter | solution.py:100
  1576.3 210.3 %reduce-scatter.15.cloned.1.call-start = ((), (), s32[]{:S(2)}) async-start(), calls=%async_computation.18 | async-start | bytes 5242880 | tf_op jit(solution)/shard_map/reduce_scatter | solution.py:100
  1711.6 161.6 %all-gather.24.cloned.1.call-start = ((), (), s32[]{:S(2)}) async-start(), calls=%async_computation.19 | async-start | bytes 5242880 | tf_op jit(solution)/shard_map/all_gather | solution.py:96
  1791.8 162.4 %all-gather.26.cloned.1.call-start = ((), (), s32[]{:S(2)}) async-start(), calls=%async_computation.21 | async-start | bytes 5242880 | tf_op jit(solution)/shard_map/all_gather | solution.py:96
  1792.5 270.7 %reduce-scatter.19.cloned.1.call-start = ((), (), s32[]{:S(2)}) async-start(), calls=%async_computation.22 | async-start | bytes 5242880 | tf_op jit(solution)/shard_map/reduce_scatter | solution.py:100
  1987.7 162.1 %all-gather.28.cloned.1.call-start = ((), (), s32[]{:S(2)}) async-start(), calls=%async_computation.23 | async-start | bytes 5242880 | tf_op jit(solution)/shard_map/all_gather | solution.py:96
  2068.4 249.7 %reduce-scatter.21.cloned.1.call-start = ((), (), s32[]{:S(2)}) async-start(), calls=%async_computation.24 | async-start | bytes 9437184 | tf_op jit(solution)/shard_map/reduce_scatter | solution.py:352
  2232.0 166.3 %reduce-scatter.17.cloned.1.call-start = ((), (), s32[]{:S(2)}) async-start(), calls=%async_computation.20 | async-start | bytes 5242880 | tf_op jit(solution)/shard_map/reduce_scatter | solution.py:100
  2244.6 287.8 %reduce-scatter.23.cloned.1.call-start = ((), (), s32[]{:S(2)}) async-start(), calls=%async_computation.25 | async-start | bytes 18874368 | tf_op jit(solution)/shard_map/reduce_scatter | solution.py:388
  2415.9 179.3 %reduce-scatter.31.cloned.1.call-start = ((), (), s32[]{:S(2)}) async-start(), calls=%async_computation.30 | async-start | bytes 6488064 | tf_op jit(solution)/shard_map/reduce_scatter | solution.py:403
  2428.7 256.8 %reduce-scatter.29.cloned.1.call-start = ((), (), s32[]{:S(2)}) async-start(), calls=%async_computation.29 | async-start | bytes 12976128 | tf_op jit(solution)/shard_map/reduce_scatter | solution.py:400
  2449.3 281.4 %reduce-scatter.27.cloned.1.call-start = ((), (), s32[]{:S(2)}) async-start(), calls=%async_computation.28 | async-start | bytes 2359296 | tf_op jit(solution)/shard_map/reduce_scatter | solution.py:397
  2456.3 339.7 %reduce-scatter.25.cloned.1.call-start = ((), (), s32[]{:S(2)}) async-start(), calls=%async_computation.27 | async-start | bytes 7077888 | tf_op jit(solution)/shard_map/reduce_scatter | solution.py:394
  2476.5 356.3 %reduce-scatter.33.cloned.1.call-start = ((), (), s32[]{:S(2)}) async-start(), calls=%async_computation.31 | async-start | bytes 589824
  2478.3 444.0 %all-reduce.2.cloned.1.call-start = ((), (), s32[]{:S(2)}) async-start(), calls=%async_computation.26 | async-start | bytes 4194304 | tf_op jit(solution)/shard_map/psum | solution.py:408
  (86 other events, 4136.7 us)
Sparse Core Ops, SparseCore 0:
  207.9 89.8 all-gather.11
  308.7 82.0 all-gather.29
  449.1 74.9 reduce-scatter.34
  528.4 81.2 all-gather.31
  637.8 75.2 reduce-scatter.36
  727.3 83.0 all-gather.29
  868.7 74.9 reduce-scatter.34
  947.9 81.2 all-gather.31
  1057.4 75.2 reduce-scatter.36
  1146.9 83.0 all-gather.29
  1288.3 74.9 reduce-scatter.34
  1367.5 81.2 all-gather.31
  1477.0 75.2 reduce-scatter.36
  1576.4 82.9 all-gather.21
  1711.7 74.9 reduce-scatter.14
  1791.9 81.2 all-gather.23
  1874.8 79.2 all-gather.25
  1987.8 75.2 reduce-scatter.18
  2068.6 81.2 all-gather.27
  2232.1 85.9 reduce-scatter.20
  2321.0 77.2 reduce-scatter.16
  2416.0 116.3 reduce-scatter.22
  2598.7 86.7 reduce-scatter.28
  2835.3 86.9 all-reduce.1
  (8 shorter events, 384.6 us)
where the time goes:
time: 2960 us; the launch traced here: 2930 us
  waiting for transfers between devices  2210 us (75%)
  matrix products  461 us (16%)
  other arithmetic  136 us (5%)
  local copies, waits for them, and re-layouts  77.4 us (3%)
    reduce_scatter x9, waiting for transfers between devices, tensor_sum(): lax.psum_scatter(part.astype(jnp.bfloat16), 'tensor', scatter_dimension=1...  678 us
    all_gather x6, waiting for transfers between devices, tensor_rows(): return lax.all_gather(rows, 'tensor', axis=1, tiled=True)  468 us
    all_gather x4, waiting for transfers between devices, core_step(): lax.all_gather(normed_a, ('tensor', 'context'), axis=1, tiled=True)  305 us
    all_gather x1, waiting for transfers between devices, shards(): lax.all_gather(adapter_weight, ('dp', 'context'), axis=0, tiled=True)  91.6 us
    reduce_scatter x1, waiting for transfers between devices, shards(): lax.psum_scatter(gate_up_g.astype(jnp.bfloat16), ('dp', 'context'), scatt...  88 us
    psum x1, waiting for transfers between devices, shards(): lax.psum(adapter_s.astype(jnp.bfloat16), 'tensor').astype(jnp.float32)  78.2 us
    reduce_scatter x1, waiting for transfers between devices, shards(): lax.psum_scatter(norma_part.astype(jnp.bfloat16), ('tensor', 'context'),...  73.4 us
    dot_general x4, matrix products, core_step(): jnp.einsum('sqd,dgf->sqgf', ffn_input, gate_up_here, preferred_element_ty...  70.7 us
  transfers between devices with their start and end apart: 32, of which 32 were waited for; matrix products, arithmetic and copies ran while one was open for 5% of the time, Pallas kernels for 0%

commit v1 on v0

v1 whole, which is shorter than its diff:
```python
from functools import partial
import math

import jax
import jax.numpy as jnp
from jax import lax
from jax.sharding import PartitionSpec as P

BACK = 1


rope_base = 50000.0
norm_eps = 1e-06
masked_score = -1e30


def rope_angles(positions, head_dim):
    freq_index = jnp.arange(head_dim // 2, dtype=jnp.float32)
    inv_freq = 1.0 / rope_base ** (2.0 * freq_index / head_dim)
    angles = positions.astype(jnp.float32)[:, None] * inv_freq[None, :]
    return (jnp.cos(angles), jnp.sin(angles))


def rotate_fwd(values, cos_t, sin_t):
    half_dim = values.shape[-1] // 2
    first_half = values[..., :half_dim]
    second_half = values[..., half_dim:]
    return jnp.concatenate(
        [first_half * cos_t - second_half * sin_t, second_half * cos_t + first_half * sin_t],
        axis=-1,
    )


def rotate_back(grad_vals, cos_t, sin_t):
    half_dim = grad_vals.shape[-1] // 2
    first_half = grad_vals[..., :half_dim]
    second_half = grad_vals[..., half_dim:]
    return jnp.concatenate(
        [first_half * cos_t + second_half * sin_t, second_half * cos_t - first_half * sin_t],
        axis=-1,
    )


def rms_parts(rows):
    factor = lax.rsqrt(jnp.mean(rows * rows, axis=-1, keepdims=True) + norm_eps)
    return (rows * factor, factor)


def score_block(query_blk, key_blk, doc_query, doc_key, query_pos, key_pos, score_scale):
    scores = (
        jnp.einsum("qhd,khd->hqk", query_blk, key_blk, preferred_element_type=jnp.float32)
        * score_scale
    )
    allowed = (key_pos[None, :] <= query_pos[:, None]) & (doc_query[:, None] == doc_key[None, :])
    return jnp.where(allowed[None], scores, masked_score)


def attend_block(packed, query_pos, key_pos, score_scale):
    query_blk, key_blk, value_blk, doc_query, doc_key = packed
    scores = score_block(query_blk, key_blk, doc_query, doc_key, query_pos, key_pos, score_scale)
    row_max = jnp.max(scores, axis=-1, keepdims=True)
    exp_vals = jnp.exp(scores - row_max)
    totals = jnp.sum(exp_vals, axis=-1, keepdims=True)
    prob_vals = exp_vals / totals
    head_vals = jnp.einsum(
        "hqk,khd->qhd",
        prob_vals.astype(jnp.bfloat16),
        value_blk,
        preferred_element_type=jnp.float32,
    )
    return (head_vals.astype(jnp.bfloat16), row_max + jnp.log(totals))


def attend_back(packed, query_pos, key_pos, score_scale):
    query_blk, key_blk, value_blk, grad_blk, lse_blk, doc_query, doc_key = packed
    scores = score_block(query_blk, key_blk, doc_query, doc_key, query_pos, key_pos, score_scale)
    prob_vals = jnp.exp(scores - lse_blk)
    grad_value = jnp.einsum(
        "hqk,qhd->khd", prob_vals.astype(jnp.bfloat16), grad_blk, preferred_element_type=jnp.float32
    )
    grad_prob = jnp.einsum("qhd,khd->hqk", grad_blk, value_blk, preferred_element_type=jnp.float32)
    row_dot = jnp.sum(prob_vals * grad_prob, axis=-1, keepdims=True)
    grad_score = (prob_vals * (grad_prob - row_dot)).astype(jnp.bfloat16)
    grad_query = (
        jnp.einsum("hqk,khd->qhd", grad_score, key_blk, preferred_element_type=jnp.float32)
        * score_scale
    )
    grad_key = (
        jnp.einsum("hqk,qhd->khd", grad_score, query_blk, preferred_element_type=jnp.float32)
        * score_scale
    )
    return (grad_query, grad_key, grad_value)


def shards(
    embedded,
    initial_state,
    cotangent,
    doc_ids,
    recurrences,
    adapter_weight,
    norm_gains,
    qkv_weight,
    output_head_weight,
    gate_up_weight,
    down_weight,
):
    n_dp = lax.axis_size("dp")
    n_tensor = lax.axis_size("tensor")
    n_context = lax.axis_size("context")
    dp_index = lax.axis_index("dp")
    t_index = lax.axis_index("tensor")
    ctx_index = lax.axis_index("context")
    seq_count, block_rows, model_width = embedded.shape
    seq_len = doc_ids.shape[1]
    half = n_tensor // seq_count
    group = t_index // half
    part = t_index % half
    heads_here = qkv_weight.shape[1]
    head_dim = qkv_weight.shape[2] // 3
    ff_here = down_weight.shape[0]
    score_scale = 1.0 / math.sqrt(head_dim)
    pair_swap = [(i, (i + half) % n_tensor) for i in range(n_tensor)]
    members = half * n_context
    groups = [
        [g * members + i for i in range(members)] for g in range(seq_count)
    ]

    def swap_in(rows):
        own = lax.dynamic_index_in_dim(rows, group, 0, keepdims=False)
        other = lax.dynamic_index_in_dim(rows, 1 - group, 0, keepdims=False)
        got = lax.ppermute(other, "tensor", pair_swap)
        first = jnp.where(group == 0, own, got)
        second = jnp.where(group == 0, got, own)
        return jnp.concatenate([first, second], axis=0)

    def swap_out(rows):
        first, second = rows[:block_rows], rows[block_rows:]
        own = jnp.where(group == 0, first, second)
        other = jnp.where(group == 0, second, first)
        got = lax.ppermute(other, "tensor", pair_swap)
        return jnp.stack(
            [jnp.where(group == 0, own, got), jnp.where(group == 0, got, own)], axis=0
        )

    def role_perm(flip):
        pairs = []
        for t in range(n_tensor):
            for c in range(n_context):
                g = (c + flip) % n_context
                dest = (g * half + t // n_context) * n_context + t % n_context
                pairs.append((t * n_context + c, dest))
        return pairs

    role_perms = [role_perm(0), role_perm(1)]

    def role_weight(block, axis):
        got = [lax.ppermute(block, ("tensor", "context"), perm) for perm in role_perms]
        low = jnp.where(group == 0, got[0], got[1])
        high = jnp.where(group == 0, got[1], got[0])
        both = jnp.concatenate([low, high], axis=axis)
        return lax.all_gather(both, "dp", axis=axis, tiled=True)

    def role_grad(grad, axis):
        piece = lax.psum_scatter(
            grad.astype(jnp.bfloat16), "dp", scatter_dimension=axis, tiled=True
        )
        low, high = jnp.split(piece, 2, axis=axis)
        give = [jnp.where(group == 0, low, high), jnp.where(group == 0, high, low)]
        back = [
            lax.ppermute(g, ("tensor", "context"), [(b, a) for a, b in perm])
            for g, perm in zip(give, role_perms)
        ]
        return back[0].astype(jnp.float32) + back[1].astype(jnp.float32)

    def gather_rows(rows):
        return lax.all_gather(
            rows, ("tensor", "context"), axis=0, tiled=True, axis_index_groups=groups
        )

    def sum_rows(partial_rows):
        return lax.psum_scatter(
            partial_rows.astype(jnp.bfloat16),
            ("tensor", "context"),
            scatter_dimension=0,
            tiled=True,
            axis_index_groups=groups,
        ).astype(jnp.float32)

    embed_rows = swap_in(embedded)
    state_rows = swap_in(initial_state)
    cot_rows = swap_in(cotangent)
    adapter_full = lax.all_gather(adapter_weight, ("dp", "context"), axis=0, tiled=True)
    gains_full = lax.all_gather(norm_gains, ("dp", "context"), axis=1, tiled=True)
    qkv_use = role_weight(qkv_weight, 0)
    out_use = role_weight(output_head_weight, 2)
    gate_up_use = role_weight(gate_up_weight, 0)
    down_use = role_weight(down_weight, 1)
    gains_f = gains_full.astype(jnp.float32)

    order = (
        jnp.arange(seq_len, dtype=jnp.int32)
        .reshape(seq_count, half, n_context, block_rows)
        .transpose(1, 2, 0, 3)
        .reshape(-1)
    )
    cos_t, sin_t = rope_angles(order, head_dim)
    cos_t = cos_t[:, None, :]
    sin_t = sin_t[:, None, :]
    own_seq = dp_index * seq_count + group
    docs = lax.dynamic_index_in_dim(doc_ids, own_seq, 0, keepdims=False)[order]
    steps_own = lax.dynamic_index_in_dim(recurrences, own_seq, 0, keepdims=False) - BACK
    embed_part = jnp.dot(
        embed_rows, adapter_full[model_width:], preferred_element_type=jnp.float32
    )

    def core_step(latent):
        low = latent.astype(jnp.bfloat16)
        adapted = (
            jnp.dot(low, adapter_full[:model_width], preferred_element_type=jnp.float32)
            + embed_part
        )
        unit_a, factor_a = rms_parts(adapted)
        normed_a = (unit_a * gains_f[0]).astype(jnp.bfloat16)
        feature_rows = gather_rows(normed_a)
        proj = jnp.einsum(
            "bx,xyf->byf", feature_rows, qkv_use, preferred_element_type=jnp.float32
        )
        query_rot = rotate_fwd(proj[..., :head_dim], cos_t, sin_t).astype(jnp.bfloat16)
        key_rot = rotate_fwd(proj[..., head_dim : 2 * head_dim], cos_t, sin_t).astype(
            jnp.bfloat16
        )
        value_rows = proj[..., 2 * head_dim :].astype(jnp.bfloat16)
        head_vals, lse_vals = attend_block(
            (query_rot, key_rot, value_rows, docs, docs), order, order, score_scale
        )
        attn_part = jnp.einsum(
            "qhd,hdm->qm", head_vals, out_use, preferred_element_type=jnp.float32
        )
        mixed_rows = adapted + sum_rows(attn_part)
        unit_b, factor_b = rms_parts(mixed_rows)
        normed_b = (unit_b * gains_f[1]).astype(jnp.bfloat16)
        ffn_input = gather_rows(normed_b)
        gate_up = jnp.einsum(
            "qd,dgf->qgf", ffn_input, gate_up_use, preferred_element_type=jnp.float32
        )
        gate_pre = gate_up[:, 0]
        up_pre = gate_up[:, 1]
        hidden = (jax.nn.silu(gate_pre) * up_pre).astype(jnp.bfloat16)
        ffn_part = jnp.dot(hidden, down_use, preferred_element_type=jnp.float32)
        result = mixed_rows + sum_rows(ffn_part)
        saved = (
            low,
            adapted,
            feature_rows,
            query_rot,
            key_rot,
            value_rows,
            head_vals,
            lse_vals,
            mixed_rows,
            ffn_input,
            gate_pre,
            up_pre,
            hidden,
        )
        return result, saved

    def advance(step_index, current):
        return jnp.where(step_index < steps_own, core_step(current)[0], current)

    detached = lax.fori_loop(
        0, jnp.max(recurrences) - BACK, advance, state_rows.astype(jnp.float32)
    )
    current, saved = core_step(detached)
    (
        latent_low,
        adapted,
        feature_rows,
        query_rot,
        key_rot,
        value_rows,
        head_vals,
        lse_vals,
        mixed_rows,
        ffn_input,
        gate_pre,
        up_pre,
        hidden,
    ) = saved
    grad_out = cot_rows.astype(jnp.float32)
    grad_ffn = gather_rows(cot_rows)
    down_g = jnp.einsum("qf,qd->fd", hidden, grad_ffn, preferred_element_type=jnp.float32)
    grad_hidden = jnp.einsum("qd,fd->qf", grad_ffn, down_use, preferred_element_type=jnp.float32)
    sig = jax.nn.sigmoid(gate_pre)
    grad_gate = grad_hidden * up_pre * sig * (1.0 + gate_pre * (1.0 - sig))
    grad_up = grad_hidden * jax.nn.silu(gate_pre)
    grad_pair = jnp.stack([grad_gate, grad_up], axis=1).astype(jnp.bfloat16)
    gate_up_g = jnp.einsum(
        "qd,qgf->dgf", ffn_input, grad_pair, preferred_element_type=jnp.float32
    )
    grad_normb = sum_rows(
        jnp.einsum("qgf,dgf->qd", grad_pair, gate_up_use, preferred_element_type=jnp.float32)
    )
    unit_b, factor_b = rms_parts(mixed_rows)
    weighted_b = grad_normb * gains_f[1]
    gain_b = jnp.sum(grad_normb * unit_b, axis=0)
    grad_mixed = grad_out + factor_b * (
        weighted_b - unit_b * jnp.mean(weighted_b * unit_b, axis=-1, keepdims=True)
    )
    grad_heads = gather_rows(grad_mixed.astype(jnp.bfloat16))
    out_g = jnp.einsum("qhd,qm->hdm", head_vals, grad_heads, preferred_element_type=jnp.float32)
    grad_head_vals = jnp.einsum(
        "qm,hdm->qhd", grad_heads, out_use, preferred_element_type=jnp.float32
    ).astype(jnp.bfloat16)
    grad_query, grad_key, grad_value = attend_back(
        (query_rot, key_rot, value_rows, grad_head_vals, lse_vals, docs, docs),
        order,
        order,
        score_scale,
    )
    grad_proj = jnp.concatenate(
        [
            rotate_back(grad_query, cos_t, sin_t),
            rotate_back(grad_key, cos_t, sin_t),
            grad_value,
        ],
        axis=-1,
    ).astype(jnp.bfloat16)
    qkv_g = jnp.einsum(
        "xq,xtu->qtu", feature_rows, grad_proj, preferred_element_type=jnp.float32
    )
    grad_norma = sum_rows(
        jnp.einsum("aew,iew->ai", grad_proj, qkv_use, preferred_element_type=jnp.float32)
    )
    unit_a, factor_a = rms_parts(adapted)
    weighted_a = grad_norma * gains_f[0]
    gain_a = jnp.sum(grad_norma * unit_a, axis=0)
    grad_adapted = grad_mixed + factor_a * (
        weighted_a - unit_a * jnp.mean(weighted_a * unit_a, axis=-1, keepdims=True)
    )
    adapted_low = grad_adapted.astype(jnp.bfloat16)
    joined = jnp.concatenate([latent_low, embed_rows], axis=-1)
    adapter_g = jnp.einsum("rk,rd->kd", joined, adapted_low, preferred_element_type=jnp.float32)
    embed_out = jnp.einsum(
        "srd,kd->srk",
        swap_out(adapted_low),
        adapter_full[model_width:],
        preferred_element_type=jnp.float32,
    )
    down_s = role_grad(down_g, 1)
    gate_up_s = role_grad(gate_up_g, 0)
    out_s = role_grad(out_g, 2)
    qkv_s = role_grad(qkv_g, 0)
    adapter_s = lax.psum_scatter(
        adapter_g.astype(jnp.bfloat16), ("dp", "context"), scatter_dimension=0, tiled=True
    )
    gains_s = lax.psum_scatter(
        jnp.stack([gain_a, gain_b]).astype(jnp.bfloat16),
        ("dp", "context"),
        scatter_dimension=1,
        tiled=True,
    )
    adapter_s = lax.psum(adapter_s, "tensor").astype(jnp.float32)
    gains_s = lax.psum(gains_s, "tensor").astype(jnp.float32)
    return (swap_out(current), embed_out, adapter_s, gains_s, qkv_s, out_s, gate_up_s, down_s)


def solution(mesh):
    placed = (
        P("dp", ("tensor", "context"), None),
        P("dp", ("tensor", "context"), None),
        P("dp", ("tensor", "context"), None),
        P(),
        P(),
        P(("dp", "context"), None),
        P(None, ("dp", "context")),
        P(("dp", "context"), "tensor", None),
        P("tensor", None, ("dp", "context")),
        P(("dp", "context"), None, "tensor"),
        P("tensor", ("dp", "context")),
    )
    return jax.shard_map(
        shards,
        mesh=mesh,
        in_specs=placed,
        out_specs=(
            P("dp", ("tensor", "context"), None),
            P("dp", ("tensor", "context"), None),
            P(("dp", "context"), None),
            P(None, ("dp", "context")),
            P(("dp", "context"), "tensor", None),
            P("tensor", None, ("dp", "context")),
            P(("dp", "context"), None, "tensor"),
            P("tensor", ("dp", "context")),
        ),
        check_vma=False,
    )
```

time: 2960 us -> 2260 us (0.76)
  waiting for transfers between devices: 2210 us -> 1490 us
  starting transfers between devices: 1.37 us -> 124 us
  local copies, waits for them, and re-layouts: 77.4 us -> 27.2 us
  matrix products: 461 us -> 422 us
    reduce_scatter x14, waiting for transfers between devices: 1010 us -> 604 us  [the longest x10 379 us: sum_rows(): lax.psum_scatter(partial_rows.astype(jnp.bfloat16), ('tensor', 'context')...]
    all_gather x14, waiting for transfers between devices: 950 us -> 568 us  [the longest x10 393 us: gather_rows(): lax.all_gather(rows, ('tensor', 'context'), axis=0, tiled=True, axis_inde...]
    ppermute x0 -> x21, waiting for transfers between devices: none -> 153 us  [the longest x8 64.4 us: role_weight(): lax.ppermute(block, ('tensor', 'context'), perm)]
    ppermute x0 -> x21, starting transfers between devices: none -> 123 us  [the longest x8 53.9 us: role_weight(): lax.ppermute(block, ('tensor', 'context'), perm)]
    all_gather x1, waiting for transfers between devices: 91.6 us -> 0.02 us  [shards(): lax.all_gather(adapter_weight, ('dp', 'context'), axis=0, tiled=True)]
    sub x7 -> x0, other arithmetic: 37.1 us -> none  [the longest x6 36.5 us: attend_block(): exp_vals = jnp.exp(scores - row_max)]
    sub x0 -> x3, matrix products: none -> 34.4 us  [attend_block(): exp_vals = jnp.exp(scores - row_max)]
    reduce_scatter x1, waiting for transfers between devices: 54.1 us -> 87.7 us  [shards(): lax.psum_scatter(adapter_g.astype(jnp.bfloat16), ('dp', 'context'), scatt...]
  transfers between devices with their start and end apart: 32 -> 53, of which waited for: 32 -> 41; matrix products, arithmetic and copies ran while one was open for 5% -> 8% of each run, Pallas kernels for 0% -> 0%
where the time goes in v1:
time: 2260 us; the launch traced here: 2250 us
  waiting for transfers between devices  1490 us (66%)
  matrix products  422 us (19%)
  starting transfers between devices  124 us (5%)
  other arithmetic  117 us (5%)
  blocking collectives  37.1 us (2%)
  local copies, waits for them, and re-layouts  27.2 us (1%)
    all_gather x10, waiting for transfers between devices, gather_rows(): lax.all_gather(rows, ('tensor', 'context'), axis=0, tiled=True, axis_inde...  393 us
    reduce_scatter x10, waiting for transfers between devices, sum_rows(): lax.psum_scatter(partial_rows.astype(jnp.bfloat16), ('tensor', 'context')...  379 us
    reduce_scatter x4, waiting for transfers between devices, role_grad(): lax.psum_scatter(grad.astype(jnp.bfloat16), 'dp', scatter_dimension=axis,...  225 us
    all_gather x4, waiting for transfers between devices, role_weight(): return lax.all_gather(both, 'dp', axis=axis, tiled=True)  175 us
    reduce_scatter x1, waiting for transfers between devices, shards(): lax.psum_scatter(adapter_g.astype(jnp.bfloat16), ('dp', 'context'), scatt...  87.7 us
    dot_general x4, matrix products, core_step(): jnp.einsum('qd,dgf->qgf', ffn_input, gate_up_use, preferred_element_type=...  70.6 us
    ppermute x8, waiting for transfers between devices, role_weight(): lax.ppermute(block, ('tensor', 'context'), perm)  64.4 us
    psum x1, waiting for transfers between devices, shards(): adapter_s = lax.psum(adapter_s, 'tensor').astype(jnp.float32)  55.2 us
  transfers between devices with their start and end apart: 53, of which 41 were waited for; matrix products, arithmetic and copies ran while one was open for 8% of the time, Pallas kernels for 0%

profile of v1, /device:TPU:1, one launch (start us, length us, event | category | flops | bytes accessed | tf_op | source)
XLA Modules:
  0.0 2246.9 jit_solution(11454176838764542370)
XLA Ops:
  221.4 58.5 %all-gather.14.cloned.1.call-done = bf16[2048,4,384]{0,2,1:T(8,128)(2,1)} async-done(((bf16[512,4,384]{0,2,1:T(8,128)(2,1)}), bf16[2048,4,384]{0,2,1:T(8,128)(2,1)}) %all-gather.14.cloned.1.call-update) | async-done | bytes 6291472 | tf_op jit(solution)/shard_map/all_gather | solution.py:162
  279.9 116.1 %all-gather.18.cloned.1.call-done = bf16[2048,2,1408]{2,0,1:T(8,128)(2,1)} async-done(((bf16[512,2,1408]{2,0,1:T(8,128)(2,1)}), bf16[2048,2,1408]{2,0,1:T(8,128)(2,1)}) %all-gather.18.cloned.1.call-update) | async-done | bytes 11534352 | tf_op jit(solution)/shard_map/all_gather | solution.py:162
  396.0 767.9 %while.13 = (s32[]{:T(128)}, bf16[256,2048]{1,0:T(8,128)(2,1)}, s32[]{:T(128)}, s32[]{:T(128)}, bf16[4096,2048]{1,0:T(8,128)(2,1)}, /*index=5*/f32[256,2048]{1,0...) while((s32[]{:T(128)}, bf16[256,2048]{1,0:T(8,128)(2,1)}, ...), condition=%wide.region_8.9_spmd.clone.clone.clone, body=%wide.region_1.8_spmd.clone.clone.clone.sunk | while | flops 30662270976 | bytes 241803952 | solution.py:272
  407.4 41.6 %all-gather.30.cloned.1.call-done = bf16[1024,2048]{1,0:T(8,128)(2,1)} async-done(((bf16[256,2048]{1,0:T(8,128)(2,1)}), bf16[1024,2048]{1,0:T(8,128)(2,1)}) %all-gather.30.cloned.1.call-update) | async-done | bytes 4194320 | tf_op jit(solution)/shard_map/while/body/all_gather | solution.py:177
  486.4 42.7 %reduce-scatter.35.cloned.1.call-done = bf16[256,2048]{1,0:T(8,128)(2,1)} async-done(((bf16[1024,2048]{1,0:T(8,128)(2,1)}), bf16[256,2048]{1,0:T(8,128)(2,1)}) %reduce-scatter.35.cloned.1.call-update) | async-done | bytes 1048592 | tf_op jit(solution)/shard_map/while/body/reduce_scatter | solution.py:182
  532.1 44.3 %all-gather.32.cloned.1.call-done = bf16[1024,2048]{1,0:T(8,128)(2,1)} async-done(((bf16[256,2048]{1,0:T(8,128)(2,1)}), bf16[1024,2048]{1,0:T(8,128)(2,1)}) %all-gather.32.cloned.1.call-update) | async-done | bytes 4194320 | tf_op jit(solution)/shard_map/while/body/all_gather | solution.py:177
  604.5 42.7 %reduce-scatter.37.cloned.1.call-done = bf16[256,2048]{1,0:T(8,128)(2,1)} async-done(((bf16[1024,2048]{1,0:T(8,128)(2,1)}), bf16[256,2048]{1,0:T(8,128)(2,1)}) %reduce-scatter.37.cloned.1.call-update) | async-done | bytes 1048592 | tf_op jit(solution)/shard_map/while/body/reduce_scatter | solution.py:182
  661.4 41.0 %all-gather.30.cloned.1.call-done = bf16[1024,2048]{1,0:T(8,128)(2,1)} async-done(((bf16[256,2048]{1,0:T(8,128)(2,1)}), bf16[1024,2048]{1,0:T(8,128)(2,1)}) %all-gather.30.cloned.1.call-update) | async-done | bytes 4194320 | tf_op jit(solution)/shard_map/while/body/all_gather | solution.py:177
  739.8 42.7 %reduce-scatter.35.cloned.1.call-done = bf16[256,2048]{1,0:T(8,128)(2,1)} async-done(((bf16[1024,2048]{1,0:T(8,128)(2,1)}), bf16[256,2048]{1,0:T(8,128)(2,1)}) %reduce-scatter.35.cloned.1.call-update) | async-done | bytes 1048592 | tf_op jit(solution)/shard_map/while/body/reduce_scatter | solution.py:182
  785.5 44.3 %all-gather.32.cloned.1.call-done = bf16[1024,2048]{1,0:T(8,128)(2,1)} async-done(((bf16[256,2048]{1,0:T(8,128)(2,1)}), bf16[1024,2048]{1,0:T(8,128)(2,1)}) %all-gather.32.cloned.1.call-update) | async-done | bytes 4194320 | tf_op jit(solution)/shard_map/while/body/all_gather | solution.py:177
  857.9 42.7 %reduce-scatter.37.cloned.1.call-done = bf16[256,2048]{1,0:T(8,128)(2,1)} async-done(((bf16[1024,2048]{1,0:T(8,128)(2,1)}), bf16[256,2048]{1,0:T(8,128)(2,1)}) %reduce-scatter.37.cloned.1.call-update) | async-done | bytes 1048592 | tf_op jit(solution)/shard_map/while/body/reduce_scatter | solution.py:182
  914.8 41.0 %all-gather.30.cloned.1.call-done = bf16[1024,2048]{1,0:T(8,128)(2,1)} async-done(((bf16[256,2048]{1,0:T(8,128)(2,1)}), bf16[1024,2048]{1,0:T(8,128)(2,1)}) %all-gather.30.cloned.1.call-update) | async-done | bytes 4194320 | tf_op jit(solution)/shard_map/while/body/all_gather | solution.py:177
  993.2 42.7 %reduce-scatter.35.cloned.1.call-done = bf16[256,2048]{1,0:T(8,128)(2,1)} async-done(((bf16[1024,2048]{1,0:T(8,128)(2,1)}), bf16[256,2048]{1,0:T(8,128)(2,1)}) %reduce-scatter.35.cloned.1.call-update) | async-done | bytes 1048592 | tf_op jit(solution)/shard_map/while/body/reduce_scatter | solution.py:182
  1039.0 44.2 %all-gather.32.cloned.1.call-done = bf16[1024,2048]{1,0:T(8,128)(2,1)} async-done(((bf16[256,2048]{1,0:T(8,128)(2,1)}), bf16[1024,2048]{1,0:T(8,128)(2,1)}) %all-gather.32.cloned.1.call-update) | async-done | bytes 4194320 | tf_op jit(solution)/shard_map/while/body/all_gather | solution.py:177
  1111.3 42.7 %reduce-scatter.37.cloned.1.call-done = bf16[256,2048]{1,0:T(8,128)(2,1)} async-done(((bf16[1024,2048]{1,0:T(8,128)(2,1)}), bf16[256,2048]{1,0:T(8,128)(2,1)}) %reduce-scatter.37.cloned.1.call-update) | async-done | bytes 1048592 | tf_op jit(solution)/shard_map/while/body/reduce_scatter | solution.py:182
  1175.0 41.3 %all-gather.22.cloned.1.call-done = bf16[1024,2048]{1,0:T(8,128)(2,1)} async-done(((bf16[256,2048]{1,0:T(8,128)(2,1)}), bf16[1024,2048]{1,0:T(8,128)(2,1)}) %all-gather.22.cloned.1.call-update) | async-done | bytes 4194320 | tf_op jit(solution)/shard_map/all_gather | solution.py:177
  1259.1 42.7 %reduce-scatter.15.cloned.1.call-done = bf16[256,2048]{1,0:T(8,128)(2,1)} async-done(((bf16[1024,2048]{1,0:T(8,128)(2,1)}), bf16[256,2048]{1,0:T(8,128)(2,1)}) %reduce-scatter.15.cloned.1.call-update) | async-done | bytes 1048592 | tf_op jit(solution)/shard_map/reduce_scatter | solution.py:182
  1439.9 42.7 %reduce-scatter.19.cloned.1.call-done = bf16[256,2048]{1,0:T(8,128)(2,1)} async-done(((bf16[1024,2048]{1,0:T(8,128)(2,1)}), bf16[256,2048]{1,0:T(8,128)(2,1)}) %reduce-scatter.19.cloned.1.call-update) | async-done | bytes 1048592 | tf_op jit(solution)/shard_map/reduce_scatter | solution.py:182
  1486.9 44.1 %all-gather.28.cloned.1.call-done = bf16[1024,2048]{1,0:T(8,128)(2,1)} async-done(((bf16[256,2048]{1,0:T(8,128)(2,1)}), bf16[1024,2048]{1,0:T(8,128)(2,1)}) %all-gather.28.cloned.1.call-update) | async-done | bytes 4194320 | tf_op jit(solution)/shard_map/all_gather | solution.py:177
  1705.4 37.7 %reduce-scatter.31.cloned.1.call-done = bf16[1408,512]{1,0:T(8,128)(2,1)} async-done(((bf16[1408,2048]{1,0:T(8,128)(2,1)}), bf16[1408,512]{1,0:T(8,128)(2,1)}) %reduce-scatter.31.cloned.1.call-update) | async-done | bytes 1441808 | tf_op jit(solution)/shard_map/reduce_scatter | solution.py:165
  1803.4 93.9 %reduce-scatter.29.cloned.1.call-done = bf16[512,2,1408]{2,0,1:T(8,128)(2,1)} async-done(((bf16[2048,2,1408]{2,0,1:T(8,128)(2,1)}), bf16[512,2,1408]{2,0,1:T(8,128)(2,1)}) %reduce-scatter.29.cloned.1.call-update) | async-done | bytes 2883600 | tf_op jit(solution)/shard_map/reduce_scatter | solution.py:165
  1966.5 87.7 %reduce-scatter.23.cloned.1.call-done = bf16[512,2048]{1,0:T(8,128)(2,1)} async-done(((bf16[4096,2048]{1,0:T(8,128)(2,1)}), bf16[512,2048]{1,0:T(8,128)(2,1)}) %reduce-scatter.23.cloned.1.call-update) | async-done | bytes 2097168 | tf_op jit(solution)/shard_map/reduce_scatter | solution.py:355
  2064.1 63.4 %reduce-scatter.25.cloned.1.call-done = bf16[512,4,384]{0,2,1:T(8,128)(2,1)} async-done(((bf16[2048,4,384]{0,2,1:T(8,128)(2,1)}), bf16[512,4,384]{0,2,1:T(8,128)(2,1)}) %reduce-scatter.25.cloned.1.call-update) | async-done | bytes 1572880 | tf_op jit(solution)/shard_map/reduce_scatter | solution.py:165
  2180.8 55.2 %all-reduce.2.cloned.1.call-done = bf16[512,2048]{1,0:T(8,128)(2,1)} async-done(((bf16[512,2048]{1,0:T(8,128)(2,1)}), bf16[512,2048]{1,0:T(8,128)(2,1)}) %all-reduce.2.cloned.1.call-update) | async-done | bytes 2097168 | tf_op jit(solution)/shard_map/psum | solution.py:364
  (370 shorter events, 1027.3 us)
Async XLA Ops:
  7.2 206.5 %all-gather.12.cloned.1.call-start = ((), (), s32[]{:S(2)}) async-start(), calls=%async_computation.12 | async-start | bytes 18874368 | tf_op jit(solution)/shard_map/all_gather | solution.py:193
  7.9 213.5 %all-gather.16.cloned.1.call-start = ((), (), s32[]{:S(2)}) async-start(), calls=%async_computation.14 | async-start | bytes 2621440 | tf_op jit(solution)/shard_map/all_gather | solution.py:162
  19.7 201.7 %all-gather.20.cloned.1.call-start = ((), (), s32[]{:S(2)}) async-start(), calls=%async_computation.16 | async-start | bytes 7208960 | tf_op jit(solution)/shard_map/all_gather | solution.py:162
  43.3 236.7 %all-gather.14.cloned.1.call-start = ((), (), s32[]{:S(2)}) async-start(), calls=%async_computation.13 | async-start | bytes 7864320 | tf_op jit(solution)/shard_map/all_gather | solution.py:162
  80.4 315.6 %all-gather.18.cloned.1.call-start = ((), (), s32[]{:S(2)}) async-start(), calls=%async_computation.15 | async-start | bytes 14417920 | tf_op jit(solution)/shard_map/all_gather | solution.py:162
  404.4 124.7 %reduce-scatter.35.cloned.1.call-start = ((), (), s32[]{:S(2)}) async-start(), calls=%async_computation.33 | async-start | bytes 5242880 | tf_op jit(solution)/shard_map/while/body/reduce_scatter | solution.py:182
  532.1 115.1 %reduce-scatter.37.cloned.1.call-start = ((), (), s32[]{:S(2)}) async-start(), calls=%async_computation.35 | async-start | bytes 5242880 | tf_op jit(solution)/shard_map/while/body/reduce_scatter | solution.py:182
  658.4 124.1 %reduce-scatter.35.cloned.1.call-start = ((), (), s32[]{:S(2)}) async-start(), calls=%async_computation.33 | async-start | bytes 5242880 | tf_op jit(solution)/shard_map/while/body/reduce_scatter | solution.py:182
  785.5 115.1 %reduce-scatter.37.cloned.1.call-start = ((), (), s32[]{:S(2)}) async-start(), calls=%async_computation.35 | async-start | bytes 5242880 | tf_op jit(solution)/shard_map/while/body/reduce_scatter | solution.py:182
  911.8 124.1 %reduce-scatter.35.cloned.1.call-start = ((), (), s32[]{:S(2)}) async-start(), calls=%async_computation.33 | async-start | bytes 5242880 | tf_op jit(solution)/shard_map/while/body/reduce_scatter | solution.py:182
  1172.0 129.7 %reduce-scatter.15.cloned.1.call-start = ((), (), s32[]{:S(2)}) async-start(), calls=%async_computation.18 | async-start | bytes 5242880 | tf_op jit(solution)/shard_map/reduce_scatter | solution.py:182
  1335.1 147.5 %reduce-scatter.19.cloned.1.call-start = ((), (), s32[]{:S(2)}) async-start(), calls=%async_computation.22 | async-start | bytes 5242880 | tf_op jit(solution)/shard_map/reduce_scatter | solution.py:182
  1486.6 147.0 %reduce-scatter.21.cloned.1.call-start = ((), (), s32[]{:S(2)}) async-start(), calls=%async_computation.24 | async-start | bytes 5242880 | tf_op jit(solution)/shard_map/reduce_scatter | solution.py:182
  1597.7 145.4 %reduce-scatter.31.cloned.1.call-start = ((), (), s32[]{:S(2)}) async-start(), calls=%async_computation.30 | async-start | bytes 7208960 | tf_op jit(solution)/shard_map/reduce_scatter | solution.py:165
  1608.4 173.4 %reduce-scatter.27.cloned.1.call-start = ((), (), s32[]{:S(2)}) async-start(), calls=%async_computation.28 | async-start | bytes 2621440 | tf_op jit(solution)/shard_map/reduce_scatter | solution.py:165
  1614.7 282.6 %reduce-scatter.29.cloned.1.call-start = ((), (), s32[]{:S(2)}) async-start(), calls=%async_computation.29 | async-start | bytes 14417920 | tf_op jit(solution)/shard_map/reduce_scatter | solution.py:165
  1633.5 300.9 %reduce-scatter.33.cloned.1.call-start = ((), (), s32[]{:S(2)}) async-start(), calls=%async_computation.31 | async-start | bytes 589824
  1637.3 416.9 %reduce-scatter.23.cloned.1.call-start = ((), (), s32[]{:S(2)}) async-start(), calls=%async_computation.25 | async-start | bytes 18874368 | tf_op jit(solution)/shard_map/reduce_scatter | solution.py:355
  1692.4 435.1 %reduce-scatter.25.cloned.1.call-start = ((), (), s32[]{:S(2)}) async-start(), calls=%async_computation.27 | async-start | bytes 7864320 | tf_op jit(solution)/shard_map/reduce_scatter | solution.py:165
  1705.4 530.7 %all-reduce.2.cloned.1.call-start = ((), (), s32[]{:S(2)}) async-start(), calls=%async_computation.26 | async-start | bytes 4194304 | tf_op jit(solution)/shard_map/psum | solution.py:364
  1795.9 168.4 %collective-permute-start.12 = (bf16[128,2048]{1,0:T(8,128)(2,1)}, bf16[128,2048]{1,0:T(8,128)(2,1)}, u32[]{:S(2)}, u32[]{:S(2)}) collective-permute-start(bf16[128,2048]{1,0:T(8,128)(2,1)} %broadcast_select_fusion.12), channel_id=1, source_target_pairs={{0,4},{2,6},{4,0},{6,2},{1,5},{3,7},{5,1},{7,3},{8,12},{10,14},{12... | collective-permute-start | bytes 1572872 | tf_op jit(solution)/shard_map/ppermute | solution.py:141
  1901.0 235.4 %collective-permute-start.17 = (bf16[256,2,1408]{2,0,1:T(8,128)(2,1)}, bf16[256,2,1408]{2,0,1:T(8,128)(2,1)}, u32[]{:S(2)}, u32[]{:S(2)}) collective-permute-start(bf16[256,2,1408]{2,0,1:T(8,128)(2,1)} %get-tuple-element.304), channel_id=1, source_target_pairs={{0,0},{4,1},{1,2},{5,3},{2,4},{6,5},{3,6},{7,7},{8,8},{12,9},{9,10... | collective-permute-start | bytes 4325384 | tf_op jit(solution)/shard_map/ppermute | solution.py:171
  1904.6 231.7 %collective-permute-start.18 = (bf16[256,2,1408]{2,0,1:T(8,128)(2,1)}, bf16[256,2,1408]{2,0,1:T(8,128)(2,1)}, u32[]{:S(2)}, u32[]{:S(2)}) collective-permute-start(bf16[256,2,1408]{2,0,1:T(8,128)(2,1)} %get-tuple-element.305), channel_id=1, source_target_pairs={{4,0},{0,1},{5,2},{1,3},{6,4},{2,5},{7,6},{3,7},{12,8},{8,9},{13,1... | collective-permute-start | bytes 4325384 | tf_op jit(solution)/shard_map/ppermute | solution.py:171
  1907.9 153.8 %collective-permute-start.10 = (f32[128,2048]{1,0:T(8,128)}, f32[128,2048]{1,0:T(8,128)}, u32[]{:S(2)}, u32[]{:S(2)}) collective-permute-start(f32[128,2048]{1,0:T(8,128)} %slice_select_fusion), channel_id=1, source_target_pairs={{0,4},{2,6},{4,0},{6,2},{1,5},{3,7},{5,1},{7,3},{8,12},{10,14},{12... | collective-permute-start | bytes 3145736 | tf_op jit(solution)/shard_map/ppermute | solution.py:141
  (83 other events, 2501.5 us)
Sparse Core Ops, SparseCore 0:
  9.9 92.3 all-gather.11
  141.9 65.6 all-gather.19
  209.9 69.9 all-gather.13
  282.2 113.7 all-gather.17
  404.5 44.4 all-gather.29
  532.2 44.1 all-gather.31
  604.6 42.5 reduce-scatter.36
  658.5 43.8 all-gather.29
  785.6 44.1 all-gather.31
  858.0 42.5 reduce-scatter.36
  911.9 43.8 all-gather.29
  1039.1 44.1 all-gather.31
  1111.4 42.5 reduce-scatter.36
  1172.1 44.1 all-gather.21
  1304.9 55.2 all-gather.23
  1362.4 42.9 all-gather.25
  1486.7 44.1 all-gather.27
  1586.9 42.5 reduce-scatter.20
  1631.9 42.7 reduce-scatter.16
  1677.5 65.5 reduce-scatter.30
  1785.2 112.1 reduce-scatter.28
  1937.8 116.4 reduce-scatter.22
  2057.2 70.2 reduce-scatter.24
  2129.9 106.1 all-reduce.1
  (8 shorter events, 315.9 us)

commit v2 on v1

--- a/solution.py
+++ b/solution.py
@@ -1,9 +1,12 @@
 from functools import partial
 import math
+from typing import NamedTuple
 
 import jax
 import jax.numpy as jnp
 from jax import lax
+from jax.experimental import pallas as pl
+from jax.experimental.pallas import tpu as pltpu
 from jax.sharding import PartitionSpec as P
 
 BACK = 1
@@ -90,6 +93,568 @@
         * score_scale
     )
     return (grad_query, grad_key, grad_value)
+
+
+MESH = pl.DeviceIdType.MESH
+LOG2E = 1.4426950408889634
+VMEM_BYTES = 62 << 20
+
+
+class Sizes(NamedTuple):
+    n_tensor: int
+    n_context: int
+    seqs: int
+    half: int
+    block: int
+    tile: int
+    rows: int
+    seq_len: int
+    width: int
+    heads: int
+    head_dim: int
+    ff: int
+
+
+def full_spec():
+    return pl.BlockSpec(memory_space=pltpu.VMEM)
+
+
+def any_spec():
+    return pl.BlockSpec(memory_space=pl.ANY)
+
+
+def nt_dot(a, b):
+    return lax.dot_general(a, b, (((1,), (1,)), ((), ())), preferred_element_type=jnp.float32)
+
+
+def tn_dot(a, b):
+    return lax.dot_general(a, b, (((0,), (0,)), ((), ())), preferred_element_type=jnp.float32)
+
+
+def nn_dot(a, b):
+    return jnp.dot(a, b, preferred_element_type=jnp.float32)
+
+
+class Place:
+    def __init__(self, sz):
+        t = lax.axis_index("tensor")
+        self.sz = sz
+        self.dp = lax.axis_index("dp")
+        self.ctx = lax.axis_index("context")
+        self.group = t // sz.half
+        self.part = lax.rem(t, sz.half)
+
+    def device(self, part, ctx):
+        return (self.dp, self.group * self.sz.half + part, ctx)
+
+    def ahead(self, q):
+        return lax.rem(self.part + q, self.sz.half)
+
+    def behind(self, q):
+        return lax.rem(self.part + (self.sz.half - q), self.sz.half)
+
+    def sibling(self):
+        return self.device(self.part, 1 - self.ctx)
+
+    def block(self, part, ctx, j):
+        sz = self.sz
+        first = ((part + j * sz.half) * sz.n_context + ctx) * sz.block
+        return pl.ds(pl.multiple_of(first, sz.block), sz.block)
+
+    def tile(self, q, j):
+        sz = self.sz
+        first = (self.ahead(q) + j * sz.half) * sz.tile
+        return pl.ds(pl.multiple_of(first, sz.tile), sz.tile)
+
+    def enter(self):
+        barrier = pltpu.get_barrier_semaphore()
+        pl.semaphore_signal(
+            barrier, inc=1, device_id=self.sibling(), device_id_type=MESH
+        )
+        for q in range(1, self.sz.half):
+            pl.semaphore_signal(
+                barrier,
+                inc=1,
+                device_id=self.device(self.ahead(q), self.ctx),
+                device_id_type=MESH,
+            )
+        pl.semaphore_wait(barrier, self.sz.half)
+
+
+class Gather:
+    @staticmethod
+    def scratch(sz):
+        kinds = 2 * sz.half - 1
+        return [
+            pltpu.SemaphoreType.DMA((kinds, sz.seqs)),
+            pltpu.SemaphoreType.DMA((kinds, sz.seqs)),
+        ]
+
+    def __init__(self, place, ref, send, recv):
+        self.place, self.ref, self.send, self.recv = place, ref, send, recv
+
+    def copy(self, kind, j, rows):
+        place, half = self.place, self.place.sz.half
+        if 0 < kind < half:
+            target = place.device(place.ahead(kind), place.ctx)
+        else:
+            target = place.sibling()
+        return pltpu.make_async_remote_copy(
+            src_ref=self.ref.at[rows],
+            dst_ref=self.ref.at[rows],
+            send_sem=self.send.at[kind, j],
+            recv_sem=self.recv.at[kind, j],
+            device_id=target,
+            device_id_type=MESH,
+        )
+
+    def own(self, j):
+        return self.place.block(self.place.part, self.place.ctx, j)
+
+    def start(self, j):
+        for q in range(1, self.place.sz.half):
+            self.copy(q, j, self.own(j)).start()
+        self.copy(0, j, self.own(j)).start()
+
+    def wait_near(self, j):
+        place = self.place
+        self.copy(0, j, place.block(place.part, 1 - place.ctx, j)).wait_recv()
+
+    def forward(self, q, j):
+        place = self.place
+        rows = place.block(place.behind(q), place.ctx, j)
+        self.copy(q, j, rows).wait_recv()
+        self.copy(place.sz.half - 1 + q, j, rows).start()
+
+    def wait_far(self, q, j):
+        place = self.place
+        rows = place.block(place.behind(q), 1 - place.ctx, j)
+        self.copy(place.sz.half - 1 + q, j, rows).wait_recv()
+
+    def finish(self):
+        place, half = self.place, self.place.sz.half
+        for j in range(place.sz.seqs):
+            for kind in range(half):
+                self.copy(kind, j, self.own(j)).wait_send()
+            for q in range(1, half):
+                rows = place.block(place.behind(q), place.ctx, j)
+                self.copy(half - 1 + q, j, rows).wait_send()
+
+
+class Scatter:
+    @staticmethod
+    def scratch(sz):
+        kinds = 2 * sz.half - 1
+        near = (sz.half, sz.seqs, sz.block, sz.width)
+        far = (max(sz.half - 1, 1), sz.seqs, sz.block, sz.width)
+        return [
+            pltpu.VMEM((sz.tile, sz.width), jnp.float32),
+            pltpu.VMEM(near, jnp.float32),
+            pltpu.VMEM(near, jnp.bfloat16),
+            pltpu.VMEM(near, jnp.bfloat16),
+            pltpu.VMEM(far, jnp.bfloat16),
+            pltpu.VMEM(far, jnp.bfloat16),
+            pltpu.SemaphoreType.DMA((kinds, sz.seqs)),
+            pltpu.SemaphoreType.DMA((kinds, sz.seqs)),
+        ]
+
+    def __init__(self, place, part, mine, near_out, near_in, far_out, far_in, send, recv):
+        self.place, self.part, self.mine = place, part, mine
+        self.near_out, self.near_in = near_out, near_in
+        self.far_out, self.far_in = far_out, far_in
+        self.send, self.recv = send, recv
+
+    def near(self, q, j):
+        return pltpu.make_async_remote_copy(
+            src_ref=self.near_out.at[q, j],
+            dst_ref=self.near_in.at[q, j],
+            send_sem=self.send.at[q, j],
+            recv_sem=self.recv.at[q, j],
+            device_id=self.place.sibling(),
+            device_id_type=MESH,
+        )
+
+    def far(self, q, j):
+        place = self.place
+        return pltpu.make_async_remote_copy(
+            src_ref=self.far_out.at[q - 1, j],
+            dst_ref=self.far_in.at[q - 1, j],
+            send_sem=self.send.at[place.sz.half - 1 + q, j],
+            recv_sem=self.recv.at[place.sz.half - 1 + q, j],
+            device_id=place.device(place.ahead(q), place.ctx),
+            device_id_type=MESH,
+        )
+
+    def give(self, q, j):
+        sz, ctx = self.place.sz, self.place.ctx
+        mine = pl.ds(pl.multiple_of(ctx * sz.block, sz.block), sz.block)
+        other = pl.ds(pl.multiple_of((1 - ctx) * sz.block, sz.block), sz.block)
+        self.near_out[q, j] = self.part[other, :].astype(jnp.bfloat16)
+        self.near(q, j).start()
+        self.mine[q, j] = self.part[mine, :]
+
+    def onward(self, q, j):
+        self.near(q, j).wait_recv()
+        self.far_out[q - 1, j] = (
+            self.mine[q, j] + self.near_in[q, j].astype(jnp.float32)
+        ).astype(jnp.bfloat16)
+        self.far(q, j).start()
+
+    def total(self, j):
+        self.near(0, j).wait_recv()
+        total = self.mine[0, j] + self.near_in[0, j].astype(jnp.float32)
+        for q in range(1, self.place.sz.half):
+            self.far(q, j).wait_recv()
+            total = total + self.far_in[q - 1, j].astype(jnp.float32)
+        return total
+
+    def finish(self):
+        half = self.place.sz.half
+        for j in range(self.place.sz.seqs):
+            for q in range(half):
+                self.near(q, j).wait_send()
+            for q in range(1, half):
+                self.far(q, j).wait_send()
+
+
+def column_loads(blocks_ref, vmem_ref, sem):
+    count, _, columns = blocks_ref.shape
+    return [
+        pltpu.make_async_copy(
+            blocks_ref.at[b], vmem_ref.at[:, pl.ds(b * columns, columns)], sem.at[b]
+        )
+        for b in range(count)
+    ]
+
+
+def split_loads(src_ref, vmem_ref, sem, count):
+    columns = src_ref.shape[1] // count
+    return [
+        pltpu.make_async_copy(
+            src_ref.at[:, pl.ds(n * columns, columns)],
+            vmem_ref.at[:, pl.ds(n * columns, columns)],
+            sem.at[n],
+        )
+        for n in range(count)
+    ]
+
+
+def rms_factor(rows):
+    return lax.rsqrt(jnp.mean(rows * rows, axis=-1, keepdims=True) + norm_eps)
+
+
+def turn(x, cos_t, sin_t):
+    return x * cos_t + pltpu.roll(x, x.shape[-1] // 2, 1) * sin_t
+
+
+def attn_kernel(sz, keep, *refs):
+    (latent, embed, gains, cos_t, sin_t, begin, adapter_hbm, qkv_hbm, out_hbm) = refs[:9]
+    refs = refs[9:]
+    mixed = refs[0]
+    refs = refs[1:]
+    if keep:
+        adapted_out, rows_out, q_out, k_out, v_out, head_out, lse_out = refs[:7]
+        refs = refs[7:]
+    (wa, wqkv, wout, adapted, rows_s, q_s, k_s, v_s, head_s, lse_s) = refs[:10]
+    load_a, load_qkv, load_out, keep_sem = refs[10:14]
+    gather_refs = refs[14:16]
+    scatter_refs = refs[16:]
+
+    place = Place(sz)
+    a_loads = split_loads(adapter_hbm, wa, load_a, load_a.shape[0])
+    qkv_load = pltpu.make_async_copy(qkv_hbm, wqkv, load_qkv)
+    out_loads = column_loads(out_hbm, wout, load_out)
+    for copy in a_loads:
+        copy.start()
+    qkv_load.start()
+    for copy in out_loads:
+        copy.start()
+    place.enter()
+    gather = Gather(place, rows_s, *gather_refs)
+    scatter = Scatter(place, *scatter_refs)
+
+    low = latent[...].astype(jnp.bfloat16)
+    columns = sz.width // len(a_loads)
+    square = None
+    for n, copy in enumerate(a_loads):
+        copy.wait()
+        cols = pl.ds(n * columns, columns)
+        chunk = nn_dot(low, wa[:, cols]) + embed[:, cols]
+        adapted[:, cols] = chunk
+        here = jnp.sum(chunk * chunk, axis=-1, keepdims=True)
+        square = here if square is None else square + here
+    factor = lax.rsqrt(square / sz.width + norm_eps)
+    for j in range(sz.seqs):
+        span = slice(j * sz.block, (j + 1) * sz.block)
+        normed = (adapted[span, :] * factor[span]) * gains[0:1, :]
+        rows_s[gather.own(j), :] = normed.astype(jnp.bfloat16)
+        gather.start(j)
+
+    qkv_load.wait()
+    pair = min(2, sz.heads)
+    d = sz.head_dim
+
+    def project(q, j):
+        rows = place.tile(q, j)
+        x = rows_s[rows, :]
+        cos_here, sin_here = cos_t[rows, :], sin_t[rows, :]
+        for h0 in range(0, sz.heads, pair):
+            proj = nn_dot(x, wqkv[:, 3 * d * h0 : 3 * d * (h0 + pair)])
+            for h in range(pair):
+                at = 3 * d * h
+                q_s[h0 + h, rows, :] = turn(proj[:, at : at + d], cos_here, sin_here).astype(
+                    jnp.bfloat16
+                )
+                k_s[h0 + h, rows, :] = turn(
+                    proj[:, at + d : at + 2 * d], cos_here, sin_here
+                ).astype(jnp.bfloat16)
+                v_s[h0 + h, rows, :] = proj[:, at + 2 * d : at + 3 * d].astype(jnp.bfloat16)
+
+    def attend(q, j):
+        rows = place.tile(q, j)
+        first = (place.ahead(q) + j * sz.half) * sz.tile
+        length = (j + 1) * sz.half * sz.tile
+        start = begin[:, pl.ds(pl.multiple_of(first, sz.tile), sz.tile)]
+        key_at = lax.broadcasted_iota(jnp.int32, (length, sz.tile), 0)
+        query_at = first + lax.broadcasted_iota(jnp.int32, (1, sz.tile), 1)
+        allowed = (key_at >= start) & (key_at <= query_at)
+
+        def head(h, carry):
+            scores = nt_dot(k_s[h, 0:length, :], q_s[h, rows, :])
+            scores = jnp.where(allowed, scores * (LOG2E / math.sqrt(d)), masked_score)
+            top = jnp.max(scores, axis=0, keepdims=True)
+            weight = jnp.exp2(scores - top)
+            total = jnp.sum(weight, axis=0, keepdims=True)
+            mixed_t = tn_dot(v_s[h, 0:length, :], weight.astype(jnp.bfloat16))
+            result = jnp.transpose(mixed_t / total)
+            head_s[rows, pl.ds(pl.multiple_of(h * d, d), d)] = result.astype(jnp.bfloat16)
+            if keep:
+                lse_s[h, :, rows] = top + jnp.log2(total)
+            return carry
+
+        lax.fori_loop(0, sz.heads, head, 0)
+
+    def give(q, j):
+        rows = place.tile(q, j)
+        scatter.part[...] = nn_dot(head_s[rows, :], wout[...])
+        scatter.give(q, j)
+
+    copies = []
+
+    def save(src, dst):
+        copy = pltpu.make_async_copy(src, dst, keep_sem.at[len(copies)])
+        copy.start()
+        copies.append(copy)
+
+    if keep:
+        save(adapted, adapted_out)
+    far = range(1, sz.half)
+    for j in range(sz.seqs):
+        gather.wait_near(j)
+        project(0, j)
+    for copy in out_loads:
+        copy.wait()
+    for j in range(sz.seqs):
+        for q in far:
+            gather.forward(q, j)
+        for q in far:
+            gather.wait_far(sz.half - q, j)
+            project(q, j)
+        for q in far:
+            attend(q, j)
+            give(q, j)
+        attend(0, j)
+        for q in far:
+            scatter.onward(q, j)
+        give(0, j)
+    if keep:
+        for src, dst in ((rows_s, rows_out), (q_s, q_out), (k_s, k_out), (v_s, v_out)):
+            save(src, dst)
+        save(head_s, head_out)
+        save(lse_s, lse_out)
+    gather.finish()
+    for j in range(sz.seqs):
+        span = slice(j * sz.block, (j + 1) * sz.block)
+        mixed[span, :] = adapted[span, :] + scatter.total(j)
+    scatter.finish()
+    for copy in copies:
+        copy.wait()
+
+
+def run_attn(sz, keep, latent, embed_part, gains, cos_t, sin_t, begin, adapter, qkv, out):
+    f32, bf16 = jnp.float32, jnp.bfloat16
+    heads_shape = (sz.heads, sz.seq_len, sz.head_dim)
+    shape = jax.ShapeDtypeStruct
+    outs = [shape((sz.rows, sz.width), f32)]
+    if keep:
+        outs += [
+            shape((sz.rows, sz.width), f32),
+            shape((sz.seq_len, sz.width), bf16),
+            shape(heads_shape, bf16),
+            shape(heads_shape, bf16),
+            shape(heads_shape, bf16),
+            shape((sz.seq_len, sz.heads * sz.head_dim), bf16),
+            shape((sz.heads, 1, sz.seq_len), f32),
+        ]
+    scratch = [
+        pltpu.VMEM(adapter.shape, bf16),
+        pltpu.VMEM(qkv.shape, bf16),
+        pltpu.VMEM((sz.heads * sz.head_dim, sz.width), bf16),
+        pltpu.VMEM((sz.rows, sz.width), f32),
+        pltpu.VMEM((sz.seq_len, sz.width), bf16),
+        pltpu.VMEM(heads_shape, bf16),
+        pltpu.VMEM(heads_shape, bf16),
+        pltpu.VMEM(heads_shape, bf16),
+        pltpu.VMEM((sz.seq_len, sz.heads * sz.head_dim), bf16),
+        pltpu.VMEM((sz.heads, 1, sz.seq_len), f32),
+        pltpu.SemaphoreType.DMA((4,)),
+        pltpu.SemaphoreType.DMA,
+        pltpu.SemaphoreType.DMA((out.shape[0],)),
+        pltpu.SemaphoreType.DMA((8,)),
+    ]
+    scratch += Gather.scratch(sz) + Scatter.scratch(sz)
+    flops = 2 * sz.rows * sz.width * sz.width + 2 * sz.seq_len * sz.width * qkv.shape[1]
+    return pl.pallas_call(
+        partial(attn_kernel, sz, keep),
+        out_shape=outs,
+        in_specs=[full_spec()] * 6 + [any_spec()] * 3,
+        out_specs=[full_spec()] + [any_spec()] * (len(outs) - 1),
+        scratch_shapes=scratch,
+        compiler_params=pltpu.CompilerParams(
+            collective_id=2 if keep else 1, has_side_effects=True, vmem_limit_bytes=VMEM_BYTES
+        ),
+        cost_estimate=pl.CostEstimate(
+            flops=flops, bytes_accessed=20 << 20, transcendentals=0
+        ),
+        name="attn_keep" if keep else "attn_round",
+    )(latent, embed_part, gains, cos_t, sin_t, begin, adapter, qkv, out)
+
+
+def ffn_kernel(sz, keep, *refs):
+    (mixed, latent, active, gains, gate_hbm, up_hbm, down_hbm, result) = refs[:8]
+    refs = refs[8:]
+    if keep:
+        rows_out, gate_out, up_out, hidden_out = refs[:4]
+        refs = refs[4:]
+    wg, wu, wd, rows_s = refs[:4]
+    refs = refs[4:]
+    if keep:
+        gate_s, up_s, hidden_s = refs[:3]
+        refs = refs[3:]
+    load_gu, load_down, keep_sem = refs[:3]
+    gather_refs = refs[3:5]
+    scatter_refs = refs[5:]
+
+    place = Place(sz)
+    gate_load = pltpu.make_async_copy(gate_hbm, wg, load_gu.at[0])
+    up_load = pltpu.make_async_copy(up_hbm, wu, load_gu.at[1])
+    down_loads = column_loads(down_hbm, wd, load_down)
+    gate_load.start()
+    up_load.start()
+    for copy in down_loads:
+        copy.start()
+    place.enter()
+    gather = Gather(place, rows_s, *gather_refs)
+    scatter = Scatter(place, *scatter_refs)
+    for j in range(sz.seqs):
+        span = slice(j * sz.block, (j + 1) * sz.block)
+        rows = mixed[span, :]
+        normed = (rows * rms_factor(rows)) * gains[1:2, :]
+        rows_s[gather.own(j), :] = normed.astype(jnp.bfloat16)
+        gather.start(j)
+    gate_load.wait()
+    up_load.wait()
+    for copy in down_loads:
+        copy.wait()
+
+    copies = []
+
+    def save(src, dst):
+        copy = pltpu.make_async_copy(src, dst, keep_sem.at[len(copies)])
+        copy.start()
+        copies.append(copy)
+
+    def work(q, j):
+        rows = place.tile(q, j)
+        x = rows_s[rows, :]
+        gate = nn_dot(x, wg[...])
+        up = nn_dot(x, wu[...])
+        hidden = (gate / (1.0 + jnp.exp(-gate)) * up).astype(jnp.bfloat16)
+        if keep:
+            gate_s[rows, :] = gate.astype(jnp.bfloat16)
+            up_s[rows, :] = up.astype(jnp.bfloat16)
+            hidden_s[rows, :] = hidden
+        scatter.part[...] = nn_dot(hidden, wd[...])
+        scatter.give(q, j)
+
+    far = range(1, sz.half)
+    for j in range(sz.seqs):
+        gather.wait_near(j)
+        work(0, j)
+    for j in range(sz.seqs):
+        for q in far:
+            gather.forward(q, j)
+        for q in far:
+            gather.wait_far(sz.half - q, j)
+            work(q, j)
+        for q in far:
+            scatter.onward(q, j)
+    if keep:
+        save(rows_s, rows_out)
+        save(gate_s, gate_out)
+        save(up_s, up_out)
+        save(hidden_s, hidden_out)
+    gather.finish()
+    for j in range(sz.seqs):
+        span = slice(j * sz.block, (j + 1) * sz.block)
+        total = mixed[span, :] + scatter.total(j)
+        if not keep:
+            total = jnp.where(active[...] > 0, total, latent[span, :])
+        result[span, :] = total
+    scatter.finish()
+    for copy in copies:
+        copy.wait()
+
+
+def run_ffn(sz, keep, mixed, latent, active, gains, gate, up, down):
+    f32, bf16 = jnp.float32, jnp.bfloat16
+    shape = jax.ShapeDtypeStruct
+    outs = [shape((sz.rows, sz.width), f32)]
+    if keep:
+        outs += [
+            shape((sz.seq_len, sz.width), bf16),
+            shape((sz.seq_len, sz.ff), bf16),
+            shape((sz.seq_len, sz.ff), bf16),
+            shape((sz.seq_len, sz.ff), bf16),
+        ]
+    scratch = [
+        pltpu.VMEM(gate.shape, bf16),
+        pltpu.VMEM(up.shape, bf16),
+        pltpu.VMEM((sz.ff, sz.width), bf16),
+        pltpu.VMEM((sz.seq_len, sz.width), bf16),
+    ]
+    if keep:
+        scratch += [pltpu.VMEM((sz.seq_len, sz.ff), bf16)] * 3
+    scratch += [
+        pltpu.SemaphoreType.DMA((2,)),
+        pltpu.SemaphoreType.DMA((down.shape[0],)),
+        pltpu.SemaphoreType.DMA((4,)),
+    ]
+    scratch += Gather.scratch(sz) + Scatter.scratch(sz)
+    return pl.pallas_call(
+        partial(ffn_kernel, sz, keep),
+        out_shape=outs,
+        in_specs=[full_spec()] * 4 + [any_spec()] * 3,
+        out_specs=[full_spec()] + [any_spec()] * (len(outs) - 1),
+        scratch_shapes=scratch,
+        compiler_params=pltpu.CompilerParams(
+            collective_id=4 if keep else 3, has_side_effects=True, vmem_limit_bytes=VMEM_BYTES
+        ),
+        cost_estimate=pl.CostEstimate(
+            flops=6 * sz.seq_len * sz.width * sz.ff, bytes_accessed=20 << 20, transcendentals=0
+        ),
+        name="ffn_keep" if keep else "ffn_round",
+    )(mixed, latent, active, gains, gate, up, down)
 
 
 def shards(
@@ -158,8 +723,15 @@
         got = [lax.ppermute(block, ("tensor", "context"), perm) for perm in role_perms]
         low = jnp.where(group == 0, got[0], got[1])
         high = jnp.where(group == 0, got[1], got[0])
-        both = jnp.concatenate([low, high], axis=axis)
-        return lax.all_gather(both, "dp", axis=axis, tiled=True)
+        if axis == 0:
+            both = jnp.concatenate([low, high], axis=0)
+        else:
+            both = jnp.stack([low, high], axis=0)
+        return lax.all_gather(both, "dp", axis=0, tiled=True)
+
+    def side_by_side(blocks):
+        count, depth, columns = blocks.shape
+        return blocks.transpose(1, 0, 2).reshape(depth, count * columns)
 
     def role_grad(grad, axis):
         piece = lax.psum_scatter(
@@ -174,13 +746,18 @@
         return back[0].astype(jnp.float32) + back[1].astype(jnp.float32)
 
     def gather_rows(rows):
-        return lax.all_gather(
+        full = lax.all_gather(
             rows, ("tensor", "context"), axis=0, tiled=True, axis_index_groups=groups
         )
+        split = full.reshape(half, n_context, seq_count, block_rows, model_width)
+        return split.transpose(2, 0, 1, 3, 4).reshape(seq_len, model_width)
 
     def sum_rows(partial_rows):
+        split = partial_rows.astype(jnp.bfloat16).reshape(
+            seq_count, half, n_context, block_rows, model_width
+        )
         return lax.psum_scatter(
-            partial_rows.astype(jnp.bfloat16),
+            split.transpose(1, 2, 0, 3, 4).reshape(seq_len, model_width),
             ("tensor", "context"),
             scatter_dimension=0,
             tiled=True,
@@ -192,102 +769,80 @@
     cot_rows = swap_in(cotangent)
     adapter_full = lax.all_gather(adapter_weight, ("dp", "context"), axis=0, tiled=True)
     gains_full = lax.all_gather(norm_gains, ("dp", "context"), axis=1, tiled=True)
-    qkv_use = role_weight(qkv_weight, 0)
-    out_use = role_weight(output_head_weight, 2)
-    gate_up_use = role_weight(gate_up_weight, 0)
-    down_use = role_weight(down_weight, 1)
+    qkv_use = role_weight(qkv_weight.reshape(qkv_weight.shape[0], -1), 0)
+    out_blocks = role_weight(output_head_weight.reshape(heads_here * head_dim, -1), 1)
+    gate_use = role_weight(gate_up_weight[:, 0], 0)
+    up_use = role_weight(gate_up_weight[:, 1], 0)
+    down_blocks = role_weight(down_weight, 1)
+    out_use = side_by_side(out_blocks)
+    down_use = side_by_side(down_blocks)
+    if out_blocks.shape[2] % 128:
+        out_blocks = out_use[None]
+        down_blocks = down_use[None]
     gains_f = gains_full.astype(jnp.float32)
 
-    order = (
-        jnp.arange(seq_len, dtype=jnp.int32)
-        .reshape(seq_count, half, n_context, block_rows)
-        .transpose(1, 2, 0, 3)
-        .reshape(-1)
-    )
+    order = jnp.arange(seq_len, dtype=jnp.int32)
     cos_t, sin_t = rope_angles(order, head_dim)
+    cos_full = jnp.concatenate([cos_t, cos_t], axis=1)
+    sin_full = jnp.concatenate([-sin_t, sin_t], axis=1)
     cos_t = cos_t[:, None, :]
     sin_t = sin_t[:, None, :]
     own_seq = dp_index * seq_count + group
-    docs = lax.dynamic_index_in_dim(doc_ids, own_seq, 0, keepdims=False)[order]
+    docs = lax.dynamic_index_in_dim(doc_ids, own_seq, 0, keepdims=False)
+    begin = jnp.sum((docs[None, :] < docs[:, None]).astype(jnp.int32), axis=1)[None, :]
     steps_own = lax.dynamic_index_in_dim(recurrences, own_seq, 0, keepdims=False) - BACK
     embed_part = jnp.dot(
         embed_rows, adapter_full[model_width:], preferred_element_type=jnp.float32
     )
 
-    def core_step(latent):
-        low = latent.astype(jnp.bfloat16)
-        adapted = (
-            jnp.dot(low, adapter_full[:model_width], preferred_element_type=jnp.float32)
-            + embed_part
-        )
-        unit_a, factor_a = rms_parts(adapted)
-        normed_a = (unit_a * gains_f[0]).astype(jnp.bfloat16)
-        feature_rows = gather_rows(normed_a)
-        proj = jnp.einsum(
-            "bx,xyf->byf", feature_rows, qkv_use, preferred_element_type=jnp.float32
-        )
-        query_rot = rotate_fwd(proj[..., :head_dim], cos_t, sin_t).astype(jnp.bfloat16)
-        key_rot = rotate_fwd(proj[..., head_dim : 2 * head_dim], cos_t, sin_t).astype(
-            jnp.bfloat16
-        )
-        value_rows = proj[..., 2 * head_dim :].astype(jnp.bfloat16)
-        head_vals, lse_vals = attend_block(
-            (query_rot, key_rot, value_rows, docs, docs), order, order, score_scale
-        )
-        attn_part = jnp.einsum(
-            "qhd,hdm->qm", head_vals, out_use, preferred_element_type=jnp.float32
-        )
-        mixed_rows = adapted + sum_rows(attn_part)
-        unit_b, factor_b = rms_parts(mixed_rows)
-        normed_b = (unit_b * gains_f[1]).astype(jnp.bfloat16)
-        ffn_input = gather_rows(normed_b)
-        gate_up = jnp.einsum(
-            "qd,dgf->qgf", ffn_input, gate_up_use, preferred_element_type=jnp.float32
-        )
-        gate_pre = gate_up[:, 0]
-        up_pre = gate_up[:, 1]
-        hidden = (jax.nn.silu(gate_pre) * up_pre).astype(jnp.bfloat16)
-        ffn_part = jnp.dot(hidden, down_use, preferred_element_type=jnp.float32)
-        result = mixed_rows + sum_rows(ffn_part)
-        saved = (
-            low,
-            adapted,
-            feature_rows,
-            query_rot,
-            key_rot,
-            value_rows,
-            head_vals,
-            lse_vals,
-            mixed_rows,
-            ffn_input,
-            gate_pre,
-            up_pre,
-            hidden,
-        )
-        return result, saved
+    sz = Sizes(
+        n_tensor,
+        n_context,
+        seq_count,
+        half,
+        block_rows,
+        n_context * block_rows,
+        seq_count * block_rows,
+        seq_len,
+        model_width,
+        heads_here,
+        head_dim,
+        ff_here,
+    )
+    adapter_top = adapter_full[:model_width]
 
     def advance(step_index, current):
-        return jnp.where(step_index < steps_own, core_step(current)[0], current)
+        (mixed,) = run_attn(
+            sz, False, current, embed_part, gains_f, cos_full, sin_full, begin,
+            adapter_top, qkv_use, out_blocks,
+        )
+        active = jnp.broadcast_to((step_index < steps_own).astype(jnp.float32), (1, model_width))
+        (result,) = run_ffn(
+            sz, False, mixed, current, active, gains_f, gate_use, up_use, down_blocks
+        )
+        return result
 
     detached = lax.fori_loop(
         0, jnp.max(recurrences) - BACK, advance, state_rows.astype(jnp.float32)
     )
-    current, saved = core_step(detached)
-    (
-        latent_low,
-        adapted,
-        feature_rows,
-        query_rot,
-        key_rot,
-        value_rows,
-        head_vals,
-        lse_vals,
-        mixed_rows,
-        ffn_input,
-        gate_pre,
-        up_pre,
-        hidden,
-    ) = saved
+    (mixed_rows, adapted, feature_rows, query_hm, key_hm, value_hm, head_flat, lse) = run_attn(
+        sz, True, detached, embed_part, gains_f, cos_full, sin_full, begin,
+        adapter_top, qkv_use, out_blocks,
+    )
+    (current, ffn_input, gate_pre, up_pre, hidden) = run_ffn(
+        sz, True, mixed_rows, detached, gains_f[:1], gains_f, gate_use, up_use, down_blocks
+    )
+    latent_low = detached.astype(jnp.bfloat16)
+    query_rot = query_hm.transpose(1, 0, 2)
+    key_rot = key_hm.transpose(1, 0, 2)
+    value_rows = value_hm.transpose(1, 0, 2)
+    head_vals = head_flat.reshape(seq_len, heads_here, head_dim)
+    lse_vals = lse.transpose(0, 2, 1) * math.log(2.0)
+    gate_pre = gate_pre.astype(jnp.float32)
+    up_pre = up_pre.astype(jnp.float32)
+    gate_up_use = jnp.stack([gate_use, up_use], axis=1)
+    out_use = out_use.reshape(heads_here, head_dim, model_width)
+    qkv_use = qkv_use.reshape(model_width, heads_here, 3 * head_dim)
     grad_out = cot_rows.astype(jnp.float32)
     grad_ffn = gather_rows(cot_rows)
     down_g = jnp.einsum("qf,qd->fd", hidden, grad_ffn, preferred_element_type=jnp.float32)

time: 2260 us -> 1810 us (0.80)
  waiting for transfers between devices: 1490 us -> 887 us
  Pallas kernels: 0 us -> 447 us
  matrix products: 422 us -> 147 us
  other arithmetic: 117 us -> 67.6 us
  local copies, waits for them, and re-layouts: 27.2 us -> 75.5 us
    pallas_call x0 -> x8, Pallas kernels: none -> 447 us  [the longest x4 236 us: run_attn(): pl.pallas_call(partial(attn_kernel, sz, keep), out_shape=outs, in_specs=[...]
    all_gather x10 -> x2, waiting for transfers between devices: 393 us -> 32 us  [gather_rows(): lax.all_gather(rows, ('tensor', 'context'), axis=0, tiled=True, axis_inde...]
    reduce_scatter x10 -> x2, waiting for transfers between devices: 379 us -> 44.4 us  [sum_rows(): lax.psum_scatter(split.transpose(1, 2, 0, 3, 4).reshape(seq_len, model_wi...]
    dot_general x21 -> x0, matrix products: 233 us -> none  [the longest x4 70.6 us: core_step(): jnp.einsum('qd,dgf->qgf', ffn_input, gate_up_use, preferred_element_type=...]
    all_gather x4 -> x5, waiting for transfers between devices: 175 us -> 230 us  [role_weight(): return lax.all_gather(both, 'dp', axis=0, tiled=True)]
    sub x3 -> x0, matrix products: 34.4 us -> none  [attend_block(): exp_vals = jnp.exp(scores - row_max)]
    ppermute x8 -> x10, waiting for transfers between devices: 64.4 us -> 77.3 us  [role_weight(): lax.ppermute(block, ('tensor', 'context'), perm)]
    ppermute x8 -> x10, starting transfers between devices: 53.9 us -> 53.4 us  [role_weight(): lax.ppermute(block, ('tensor', 'context'), perm)]
  transfers between devices with their start and end apart: 53 -> 40, of which waited for: 41 -> 31; matrix products, arithmetic and copies ran while one was open for 8% -> 9% of each run, Pallas kernels for 0% -> 0%
where the time goes in v2:
time: 1810 us; the launch traced here: 1800 us
  waiting for transfers between devices  887 us (49%)
  Pallas kernels  447 us (25%)
  matrix products  147 us (8%)
  starting transfers between devices  111 us (6%)
  local copies, waits for them, and re-layouts  75.5 us (4%)
  other arithmetic  67.6 us (4%)
  loops' own time  26.3 us (1%)
  blocking collectives  18.8 us (1%)
    pallas_call x4, Pallas kernels, run_attn(): pl.pallas_call(partial(attn_kernel, sz, keep), out_shape=outs, in_specs=[...  236 us
    all_gather x5, waiting for transfers between devices, role_weight(): return lax.all_gather(both, 'dp', axis=0, tiled=True)  230 us
    reduce_scatter x4, waiting for transfers between devices, role_grad(): lax.psum_scatter(grad.astype(jnp.bfloat16), 'dp', scatter_dimension=axis,...  224 us
    pallas_call x4, Pallas kernels, run_ffn(): pl.pallas_call(partial(ffn_kernel, sz, keep), out_shape=outs, in_specs=[f...  211 us
    reduce_scatter x1, waiting for transfers between devices, shards(): lax.psum_scatter(adapter_g.astype(jnp.bfloat16), ('dp', 'context'), scatt...  108 us
    ppermute x10, waiting for transfers between devices, role_weight(): lax.ppermute(block, ('tensor', 'context'), perm)  77.3 us
    psum x1, waiting for transfers between devices, shards(): adapter_s = lax.psum(adapter_s, 'tensor').astype(jnp.float32)  54.2 us
    ppermute x10, starting transfers between devices, role_weight(): lax.ppermute(block, ('tensor', 'context'), perm)  53.4 us
  transfers between devices with their start and end apart: 40, of which 31 were waited for; matrix products, arithmetic and copies ran while one was open for 9% of the time, Pallas kernels for 0%

profile of v2, /device:TPU:1, one launch (start us, length us, event | category | flops | bytes accessed | tf_op | source)
XLA Modules:
  0.0 1796.4 jit_solution(12434737528577311731)
XLA Ops:
  11.5 22.9 %collective-permute-done.13 = bf16[128,2048]{1,0:T(8,128)(2,1)S(1)} collective-permute-done((bf16[128,2048]{1,0:T(8,128)(2,1)S(1)}, bf16[128,2048]{1,0:T(8,128)(2,1)S(1)}, u32[]{:S(2)}, u32[]{:S(2)}) %collective-permute-start.13) | collective-permute-done | bytes 524320 | tf_op jit(solution)/shard_map/ppermute | solution.py:697
  129.3 31.4 %collective-permute-start.2 = (bf16[256,1536]{1,0:T(8,128)(2,1)S(1)}, bf16[256,1536]{1,0:T(8,128)(2,1)S(1)}, u32[]{:S(2)}, u32[]{:S(2)}) collective-permute-start(bf16[256,1536]{1,0:T(8,128)(2,1)S(1)} %bitcast.154), channel_id=1, source_target_pairs={{0,0},{1,4},{2,1},{3,5},{4,2},{5,6},{6,3},{7,7},{8,8},{9,12},{10,9... | collective-permute-start | bytes 2359304 | tf_op jit(solution)/shard_map/ppermute | solution.py:723
  297.3 68.1 %all-gather.17.cloned.1.call-done.refs_5_ = bf16[2048,1408]{1,0:T(8,128)(2,1)} async-done(((bf16[512,1408]{1,0:T(8,128)(2,1)}), bf16[2048,1408]{1,0:T(8,128)(2,1)}) %all-gather.17.cloned.1.call-update) | async-done | bytes 5767184 | tf_op jit(solution)/shard_map/all_gather | solution.py:730
  365.4 68.1 %all-gather.15.cloned.1.call-done.refs_4_ = bf16[2048,1408]{1,0:T(8,128)(2,1)} async-done(((bf16[512,1408]{1,0:T(8,128)(2,1)}), bf16[2048,1408]{1,0:T(8,128)(2,1)}) %all-gather.15.cloned.1.call-update) | async-done | bytes 5767184 | tf_op jit(solution)/shard_map/all_gather | solution.py:730
  433.5 72.6 %all-gather.11.cloned.1.call-done.refs_7_ = bf16[2048,1536]{1,0:T(8,128)(2,1)} async-done(((bf16[512,1536]{1,0:T(8,128)(2,1)}), bf16[2048,1536]{1,0:T(8,128)(2,1)}) %all-gather.11.cloned.1.call-update) | async-done | bytes 6291472 | tf_op jit(solution)/shard_map/all_gather | solution.py:730
  506.1 371.6 %while.10 = (s32[]{:T(128)}, f32[256,2048]{1,0:T(8,128)}, s32[]{:T(128)}, f32[256,2048]{1,0:T(8,128)}, f32[2,2048]{1,0:T(2,128)S(1)}, /*index=5*/f32[1024,128]{1...) while((s32[]{:T(128)}, f32[256,2048]{1,0:T(8,128)}, ...), condition=%wide.region_3.4_spmd, body=%wide.region_2.3_spmd.sunk | while | flops 26306674688 | bytes 46145708 | solution.py:825
  530.9 57.5 %attn_round.1.refs_0_ = f32[256,2048]{1,0:T(8,128)} custom-call(f32[256,2048]{1,0:T(8,128)} %copy.159.refs_0_.refs_1_, f32[256,2048]{1,0:T(8,128)} %get-tuple-element.349.refs_1_, f32[2,2048]{1,0:T(2,128)S(1)} %get-tuple-element.350.refs_2_.refs_3_, f32[1024,128]{1,0:T(8,128)S(1)} %get-tuple-element.351.refs_3_, f32[1024,128]{1,0:T(8,128)S(1)} %get-tuple-element.352.refs_4_, ...), custom_call_target="tpu_custom_call" | custom-call | flops 8589934592 | bytes 20971520 | tf_op jit(solution)/shard_map/while/body/attn_round/pallas_call | solution.py:517
  588.5 53.0 %ffn_round.1 = f32[256,2048]{1,0:T(8,128)} custom-call(f32[256,2048]{1,0:T(8,128)} %attn_round.1.refs_0_, f32[256,2048]{1,0:T(8,128)} %copy.159.refs_0_.refs_1_, f32[1,2048]{1,0:T(1,128)} %broadcast_in_dim.19.refs_2_, f32[2,2048]{1,0:T(2,128)S(1)} %get-tuple-element.350.refs_2_.refs_3_, bf16[2048,1408]{1,0:T(8,128)(2,1)} %get-tuple-element.358.refs_4_, ...), custom_call_target="tpu_custom_call" | custom-call | flops 17716740096 | bytes 20971520 | tf_op jit(solution)/shard_map/while/body/ffn_round/pallas_call | solution.py:644
  645.2 59.3 %attn_round.1.refs_0_ = f32[256,2048]{1,0:T(8,128)} custom-call(f32[256,2048]{1,0:T(8,128)} %copy.159.refs_0_.refs_1_, f32[256,2048]{1,0:T(8,128)} %get-tuple-element.349.refs_1_, f32[2,2048]{1,0:T(2,128)S(1)} %get-tuple-element.350.refs_2_.refs_3_, f32[1024,128]{1,0:T(8,128)S(1)} %get-tuple-element.351.refs_3_, f32[1024,128]{1,0:T(8,128)S(1)} %get-tuple-element.352.refs_4_, ...), custom_call_target="tpu_custom_call" | custom-call | flops 8589934592 | bytes 20971520 | tf_op jit(solution)/shard_map/while/body/attn_round/pallas_call | solution.py:517
  704.5 52.0 %ffn_round.1 = f32[256,2048]{1,0:T(8,128)} custom-call(f32[256,2048]{1,0:T(8,128)} %attn_round.1.refs_0_, f32[256,2048]{1,0:T(8,128)} %copy.159.refs_0_.refs_1_, f32[1,2048]{1,0:T(1,128)} %broadcast_in_dim.19.refs_2_, f32[2,2048]{1,0:T(2,128)S(1)} %get-tuple-element.350.refs_2_.refs_3_, bf16[2048,1408]{1,0:T(8,128)(2,1)} %get-tuple-element.358.refs_4_, ...), custom_call_target="tpu_custom_call" | custom-call | flops 17716740096 | bytes 20971520 | tf_op jit(solution)/shard_map/while/body/ffn_round/pallas_call | solution.py:644
  760.3 59.3 %attn_round.1.refs_0_ = f32[256,2048]{1,0:T(8,128)} custom-call(f32[256,2048]{1,0:T(8,128)} %copy.159.refs_0_.refs_1_, f32[256,2048]{1,0:T(8,128)} %get-tuple-element.349.refs_1_, f32[2,2048]{1,0:T(2,128)S(1)} %get-tuple-element.350.refs_2_.refs_3_, f32[1024,128]{1,0:T(8,128)S(1)} %get-tuple-element.351.refs_3_, f32[1024,128]{1,0:T(8,128)S(1)} %get-tuple-element.352.refs_4_, ...), custom_call_target="tpu_custom_call" | custom-call | flops 8589934592 | bytes 20971520 | tf_op jit(solution)/shard_map/while/body/attn_round/pallas_call | solution.py:517
  819.5 53.0 %ffn_round.1 = f32[256,2048]{1,0:T(8,128)} custom-call(f32[256,2048]{1,0:T(8,128)} %attn_round.1.refs_0_, f32[256,2048]{1,0:T(8,128)} %copy.159.refs_0_.refs_1_, f32[1,2048]{1,0:T(1,128)} %broadcast_in_dim.19.refs_2_, f32[2,2048]{1,0:T(2,128)S(1)} %get-tuple-element.350.refs_2_.refs_3_, bf16[2048,1408]{1,0:T(8,128)(2,1)} %get-tuple-element.358.refs_4_, ...), custom_call_target="tpu_custom_call" | custom-call | flops 17716740096 | bytes 20971520 | tf_op jit(solution)/shard_map/while/body/ffn_round/pallas_call | solution.py:644
  877.7 59.8 %attn_keep.1 = (f32[256,2048]{1,0:T(8,128)}, f32[256,2048]{1,0:T(8,128)}, bf16[1024,2048]{1,0:T(8,128)(2,1)}, bf16[4,1024,128]{2,1,0:T(8,128)(2,1)}, bf16[4,1024...) custom-call(f32[256,2048]{1,0:T(8,128)} %get-tuple-element.99.refs_0_.ref, ...), custom_call_target="tpu_custom_call" | custom-call | flops 8589934592 | bytes 20971520 | tf_op jit(solution)/shard_map/attn_keep/pallas_call | solution.py:517
  937.5 53.0 %ffn_keep.1 = (f32[256,2048]{1,0:T(8,128)}, bf16[1024,2048]{1,0:T(8,128)(2,1)}, bf16[1024,1408]{1,0:T(8,128)(2,1)}, bf16[1024,1408]{1,0:T(8,128)(2,1)}, bf16[1024,1408]{1,0:T(8,128)(2,1)}) custom-call(f32[256,2048]{1,0:T(8,128)} %get-tuple-element.100.refs_0_, f32[256,2048]{1,0:T(8,128)} %get-tuple-element.99.refs_0_.refs_1_, ...), custom_call_target="tpu_custom_call" | custom-call | flops 17716740096 | bytes 20971520 | tf_op jit(solution)/shard_map/ffn_keep/pallas_call | solution.py:644
  1025.1 43.0 %reduce-scatter.11.cloned.1.call-done = bf16[256,2048]{1,0:T(8,128)(2,1)} async-done(((bf16[1024,2048]{1,0:T(8,128)(2,1)}), bf16[256,2048]{1,0:T(8,128)(2,1)}) %reduce-scatter.11.cloned.1.call-update) | async-done | bytes 1048592 | tf_op jit(solution)/shard_map/reduce_scatter | solution.py:759
  1084.3 32.0 %all-gather.23.cloned.1.call-done = bf16[1024,2048]{1,0:T(8,128)(2,1)} async-done(((bf16[256,2048]{1,0:T(8,128)(2,1)}), bf16[1024,2048]{1,0:T(8,128)(2,1)}) %all-gather.23.cloned.1.call-update) | async-done | bytes 4194320 | tf_op jit(solution)/shard_map/all_gather | solution.py:749
  1256.7 34.6 %reduce-scatter.23.cloned.1.call-done = bf16[1408,512]{1,0:T(8,128)(2,1)} async-done(((bf16[1408,2048]{1,0:T(8,128)(2,1)}), bf16[1408,512]{1,0:T(8,128)(2,1)}) %reduce-scatter.23.cloned.1.call-update) | async-done | bytes 1441808 | tf_op jit(solution)/shard_map/reduce_scatter | solution.py:737
  1306.3 23.7 %reduce-scatter.19.cloned.1.call-done = bf16[4,128,512]{2,1,0:T(8,128)(2,1)} async-done(((bf16[4,128,2048]{2,1,0:T(8,128)(2,1)}), bf16[4,128,512]{2,1,0:T(8,128)(2,1)}) %reduce-scatter.19.cloned.1.call-update) | async-done | bytes 524304 | tf_op jit(solution)/shard_map/reduce_scatter | solution.py:737
  1350.9 94.7 %reduce-scatter.21.cloned.1.call-done = bf16[512,2,1408]{2,0,1:T(8,128)(2,1)} async-done(((bf16[2048,2,1408]{2,0,1:T(8,128)(2,1)}), bf16[512,2,1408]{2,0,1:T(8,128)(2,1)}) %reduce-scatter.21.cloned.1.call-update) | async-done | bytes 2883600 | tf_op jit(solution)/shard_map/reduce_scatter | solution.py:737
  1454.6 29.1 %reduce-scatter.25.cloned.1.call-done = bf16[256,2]{1,0:T(8,128)(2,1)} async-done(((bf16[2048,2]{1,0:T(8,128)(2,1)}), bf16[256,2]{1,0:T(8,128)(2,1)}) %reduce-scatter.25.cloned.1.call-update) | async-done | bytes 1040
  1495.4 108.2 %reduce-scatter.15.cloned.1.call-done = bf16[512,2048]{1,0:T(8,128)(2,1)} async-done(((bf16[4096,2048]{1,0:T(8,128)(2,1)}), bf16[512,2048]{1,0:T(8,128)(2,1)}) %reduce-scatter.15.cloned.1.call-update) | async-done | bytes 2097168 | tf_op jit(solution)/shard_map/reduce_scatter | solution.py:910
  1605.5 71.1 %reduce-scatter.17.cloned.1.call-done = bf16[512,4,384]{2,0,1:T(8,128)(2,1)} async-done(((bf16[2048,4,384]{2,0,1:T(8,128)(2,1)}), bf16[512,4,384]{2,0,1:T(8,128)(2,1)}) %reduce-scatter.17.cloned.1.call-update) | async-done | bytes 1572880 | tf_op jit(solution)/shard_map/reduce_scatter | solution.py:737
  1697.5 31.3 %collective-permute-done.15 = bf16[256,4,384]{2,0,1:T(8,128)(2,1)S(1)} collective-permute-done((bf16[256,4,384]{2,0,1:T(8,128)(2,1)S(1)}, bf16[256,4,384]{2,0,1:T(8,128)(2,1)S(1)}, u32[]{:S(2)}, u32[]{:S(2)}) %collective-permute-start.15) | collective-permute-done | bytes 786464 | tf_op jit(solution)/shard_map/ppermute | solution.py:743
  1731.1 54.2 %all-reduce.2.cloned.1.call-done = bf16[512,2048]{1,0:T(8,128)(2,1)} async-done(((bf16[512,2048]{1,0:T(8,128)(2,1)}), bf16[512,2048]{1,0:T(8,128)(2,1)}) %all-reduce.2.cloned.1.call-update) | async-done | bytes 2097168 | tf_op jit(solution)/shard_map/psum | solution.py:919
  (265 shorter events, 521.7 us)
Async XLA Ops:
  7.2 238.4 %all-gather.21.cloned.1.call-start = ((), (), s32[]{:S(2)}) async-start(), calls=%async_computation.14 | async-start | bytes 5242880 | tf_op jit(solution)/shard_map/all_gather | solution.py:749
  37.7 213.3 %all-gather.19.cloned.1.call-start = ((), (), s32[]{:S(2)}) async-start(), calls=%async_computation.13 | async-start | bytes 7208960 | tf_op jit(solution)/shard_map/all_gather | solution.py:730
  68.9 191.8 %all-gather.9.cloned.1.call-start = ((), (), s32[]{:S(2)}) async-start(), calls=%async_computation.8 | async-start | bytes 18874368 | tf_op jit(solution)/shard_map/all_gather | solution.py:770
  69.6 227.7 %all-gather.13.cloned.1.call-start = ((), (), s32[]{:S(2)}) async-start(), calls=%async_computation.10 | async-start | bytes 2621440 | tf_op jit(solution)/shard_map/all_gather | solution.py:730
  89.9 275.5 %all-gather.17.cloned.1.call-start = ((), (), s32[]{:S(2)}) async-start(), calls=%async_computation.12 | async-start | bytes 7208960 | tf_op jit(solution)/shard_map/all_gather | solution.py:730
  127.8 305.7 %all-gather.15.cloned.1.call-start = ((), (), s32[]{:S(2)}) async-start(), calls=%async_computation.11 | async-start | bytes 7208960 | tf_op jit(solution)/shard_map/all_gather | solution.py:730
  129.1 377.0 %all-gather.11.cloned.1.call-start = ((), (), s32[]{:S(2)}) async-start(), calls=%async_computation.9 | async-start | bytes 7864320 | tf_op jit(solution)/shard_map/all_gather | solution.py:730
  129.3 47.5 %collective-permute-start.2 = (bf16[256,1536]{1,0:T(8,128)(2,1)S(1)}, bf16[256,1536]{1,0:T(8,128)(2,1)S(1)}, u32[]{:S(2)}, u32[]{:S(2)}) collective-permute-start(bf16[256,1536]{1,0:T(8,128)(2,1)S(1)} %bitcast.154), channel_id=1, source_target_pairs={{0,0},{1,4},{2,1},{3,5},{4,2},{5,6},{6,3},{7,7},{8,8},{9,12},{10,9... | collective-permute-start | bytes 2359304 | tf_op jit(solution)/shard_map/ppermute | solution.py:723
  178.2 889.9 %reduce-scatter.11.cloned.1.call-start = ((), (), s32[]{:S(2)}) async-start(), calls=%async_computation.15 | async-start | bytes 5242880 | tf_op jit(solution)/shard_map/reduce_scatter | solution.py:759
  179.7 55.0 %collective-permute-start = (bf16[128,2048]{1,0:T(8,128)(2,1)}, bf16[128,2048]{1,0:T(8,128)(2,1)}, u32[]{:S(2)}, u32[]{:S(2)}) collective-permute-start(bf16[128,2048]{1,0:T(8,128)(2,1)} %dynamic-slice_bitcast_fusion.2), channel_id=1, source_target_pairs={{0,4},{2,6},{4,0},{6,2},{1,5},{3,7},{5,1},{7,3},{8,12},{10,14},{12... | collective-permute-start | bytes 1572872 | tf_op jit(solution)/shard_map/ppermute | solution.py:697
  1023.3 92.9 %all-gather.23.cloned.1.call-start = ((), (), s32[]{:S(2)}) async-start(), calls=%async_computation.16 | async-start | bytes 5242880 | tf_op jit(solution)/shard_map/all_gather | solution.py:749
  1072.0 150.9 %reduce-scatter.13.cloned.1.call-start = ((), (), s32[]{:S(2)}) async-start(), calls=%async_computation.17 | async-start | bytes 5242880 | tf_op jit(solution)/shard_map/reduce_scatter | solution.py:759
  1180.1 111.3 %reduce-scatter.23.cloned.1.call-start = ((), (), s32[]{:S(2)}) async-start(), calls=%async_computation.23 | async-start | bytes 7208960 | tf_op jit(solution)/shard_map/reduce_scatter | solution.py:737
  1190.9 139.1 %reduce-scatter.19.cloned.1.call-start = ((), (), s32[]{:S(2)}) async-start(), calls=%async_computation.21 | async-start | bytes 2621440 | tf_op jit(solution)/shard_map/reduce_scatter | solution.py:737
  1199.7 245.9 %reduce-scatter.21.cloned.1.call-start = ((), (), s32[]{:S(2)}) async-start(), calls=%async_computation.22 | async-start | bytes 14417920 | tf_op jit(solution)/shard_map/reduce_scatter | solution.py:737
  1218.0 265.7 %reduce-scatter.25.cloned.1.call-start = ((), (), s32[]{:S(2)}) async-start(), calls=%async_computation.24 | async-start | bytes 589824
  1226.6 376.9 %reduce-scatter.15.cloned.1.call-start = ((), (), s32[]{:S(2)}) async-start(), calls=%async_computation.18 | async-start | bytes 18874368 | tf_op jit(solution)/shard_map/reduce_scatter | solution.py:910
  1240.4 436.2 %reduce-scatter.17.cloned.1.call-start = ((), (), s32[]{:S(2)}) async-start(), calls=%async_computation.20 | async-start | bytes 7864320 | tf_op jit(solution)/shard_map/reduce_scatter | solution.py:737
  1252.0 533.3 %all-reduce.2.cloned.1.call-start = ((), (), s32[]{:S(2)}) async-start(), calls=%async_computation.19 | async-start | bytes 4194304 | tf_op jit(solution)/shard_map/psum | solution.py:919
  1254.6 48.8 %collective-permute-start.12 = (f32[128,2048]{1,0:T(8,128)}, f32[128,2048]{1,0:T(8,128)}, u32[]{:S(2)}, u32[]{:S(2)}) collective-permute-start(f32[128,2048]{1,0:T(8,128)} %slice_select_fusion), channel_id=1, source_target_pairs={{0,4},{2,6},{4,0},{6,2},{1,5},{3,7},{5,1},{7,3},{8,12},{10,14},{12... | collective-permute-start | bytes 3145736 | tf_op jit(solution)/shard_map/ppermute | solution.py:706
  1343.4 260.2 %collective-permute-start.14 = (bf16[128,2048]{1,0:T(8,128)(2,1)S(1)}, bf16[128,2048]{1,0:T(8,128)(2,1)}, u32[]{:S(2)}, u32[]{:S(2)}) collective-permute-start(bf16[128,2048]{1,0:T(8,128)(2,1)S(1)} %broadcast_select_fusion.12), channel_id=1, source_target_pairs={{0,4},{2,6},{4,0},{6,2},{1,5},{3,7},{5,1},{7,3},{8,12},{10,14},{12... | collective-permute-start | bytes 1572872 | tf_op jit(solution)/shard_map/ppermute | solution.py:706
  1448.7 242.8 %collective-permute-start.19 = (bf16[256,2,1408]{2,0,1:T(8,128)(2,1)}, bf16[256,2,1408]{2,0,1:T(8,128)(2,1)}, u32[]{:S(2)}, u32[]{:S(2)}) collective-permute-start(bf16[256,2,1408]{2,0,1:T(8,128)(2,1)} %get-tuple-element.183), channel_id=1, source_target_pairs={{0,0},{4,1},{1,2},{5,3},{2,4},{6,5},{3,6},{7,7},{8,8},{12,9},{9,10... | collective-permute-start | bytes 4325384 | tf_op jit(solution)/shard_map/ppermute | solution.py:743
  1452.4 239.2 %collective-permute-start.20 = (bf16[256,2,1408]{2,0,1:T(8,128)(2,1)S(1)}, bf16[256,2,1408]{2,0,1:T(8,128)(2,1)}, u32[]{:S(2)}, u32[]{:S(2)}) collective-permute-start(bf16[256,2,1408]{2,0,1:T(8,128)(2,1)S(1)} %get-tuple-element.184), channel_id=1, source_target_pairs={{4,0},{0,1},{5,2},{1,3},{6,4},{2,5},{7,6},{3,7},{12,8},{8,9},{13,1... | collective-permute-start | bytes 4325384 | tf_op jit(solution)/shard_map/ppermute | solution.py:743
  1678.2 50.6 %collective-permute-start.15 = (bf16[256,4,384]{2,0,1:T(8,128)(2,1)S(1)}, bf16[256,4,384]{2,0,1:T(8,128)(2,1)S(1)}, u32[]{:S(2)}, u32[]{:S(2)}) collective-permute-start(bf16[256,4,384]{2,0,1:T(8,128)(2,1)S(1)} %get-tuple-element.185), channel_id=1, source_target_pairs={{0,0},{4,1},{1,2},{5,3},{2,4},{6,5},{3,6},{7,7},{8,8},{12,9},{9,10... | collective-permute-start | bytes 2359304 | tf_op jit(solution)/shard_map/ppermute | solution.py:743
  (54 other events, 1182.5 us)
Sparse Core Ops, SparseCore 0:
  37.8 57.7 all-gather.20
  98.0 70.3 all-gather.18
  170.3 90.2 all-gather.8
  262.4 34.8 all-gather.12
  299.6 65.7 all-gather.16
  367.7 65.7 all-gather.14
  435.9 70.1 all-gather.10
  1023.4 44.6 reduce-scatter.10
  1072.1 44.1 all-gather.22
  1180.2 42.5 reduce-scatter.12
  1225.8 65.5 reduce-scatter.22
  1294.8 35.1 reduce-scatter.18
  1333.4 112.1 reduce-scatter.20
  1449.4 34.2 reduce-scatter.24
  1487.1 116.3 reduce-scatter.14
  1606.4 70.2 reduce-scatter.16
  1678.9 106.3 all-reduce.1

commit v3 on v2

--- a/solution.py
+++ b/solution.py
@@ -327,14 +327,18 @@
     ]
 
 
-def split_loads(src_ref, vmem_ref, sem, count):
-    columns = src_ref.shape[1] // count
+def adapter_loads(blocks_ref, vmem_ref, sem):
+    count, tops = sem.shape
+    depth, columns = vmem_ref.shape[0] // tops, vmem_ref.shape[1] // count
     return [
-        pltpu.make_async_copy(
-            src_ref.at[:, pl.ds(n * columns, columns)],
-            vmem_ref.at[:, pl.ds(n * columns, columns)],
-            sem.at[n],
-        )
+        [
+            pltpu.make_async_copy(
+                blocks_ref.at[b, pl.ds(0, depth), pl.ds(n * columns, columns)],
+                vmem_ref.at[pl.ds(b * depth, depth), pl.ds(n * columns, columns)],
+                sem.at[n, b],
+            )
+            for b in range(tops)
+        ]
         for n in range(count)
     ]
 
@@ -361,11 +365,12 @@
     scatter_refs = refs[16:]
 
     place = Place(sz)
-    a_loads = split_loads(adapter_hbm, wa, load_a, load_a.shape[0])
+    a_loads = adapter_loads(adapter_hbm, wa, load_a)
     qkv_load = pltpu.make_async_copy(qkv_hbm, wqkv, load_qkv)
     out_loads = column_loads(out_hbm, wout, load_out)
-    for copy in a_loads:
-        copy.start()
+    for group in a_loads:
+        for copy in group:
+            copy.start()
     qkv_load.start()
     for copy in out_loads:
         copy.start()
@@ -376,8 +381,9 @@
     low = latent[...].astype(jnp.bfloat16)
     columns = sz.width // len(a_loads)
     square = None
-    for n, copy in enumerate(a_loads):
-        copy.wait()
+    for n, group in enumerate(a_loads):
+        for copy in group:
+            copy.wait()
         cols = pl.ds(n * columns, columns)
         chunk = nn_dot(low, wa[:, cols]) + embed[:, cols]
         adapted[:, cols] = chunk
@@ -497,7 +503,7 @@
             shape((sz.heads, 1, sz.seq_len), f32),
         ]
     scratch = [
-        pltpu.VMEM(adapter.shape, bf16),
+        pltpu.VMEM((sz.width, sz.width), bf16),
         pltpu.VMEM(qkv.shape, bf16),
         pltpu.VMEM((sz.heads * sz.head_dim, sz.width), bf16),
         pltpu.VMEM((sz.rows, sz.width), f32),
@@ -507,7 +513,7 @@
         pltpu.VMEM(heads_shape, bf16),
         pltpu.VMEM((sz.seq_len, sz.heads * sz.head_dim), bf16),
         pltpu.VMEM((sz.heads, 1, sz.seq_len), f32),
-        pltpu.SemaphoreType.DMA((4,)),
+        pltpu.SemaphoreType.DMA((4, adapter.shape[0] // 2)),
         pltpu.SemaphoreType.DMA,
         pltpu.SemaphoreType.DMA((out.shape[0],)),
         pltpu.SemaphoreType.DMA((8,)),
@@ -657,6 +663,268 @@
     )(mixed, latent, active, gains, gate, up, down)
 
 
+class Ring:
+    def __init__(self, place, n_dp):
+        self.place, self.count = place, n_dp
+        self.at = self.swap(place.dp)
+
+    def swap(self, i):
+        if self.count != 4:
+            return i
+        x, y = lax.rem(i, 2), i // 2
+        return 2 * y + x + y - 2 * x * y
+
+    def index(self, offset):
+        return self.swap(lax.rem(self.at + offset + 2 * self.count, self.count))
+
+    def device(self, offset):
+        return (self.index(offset), lax.axis_index("tensor"), self.place.ctx)
+
+
+def weights_kernel(sz, n_dp, *refs):
+    count = 5
+    adapter_in, blocks_in = refs[0], refs[1 : 1 + count]
+    adapter_out, blocks_out = refs[1 + count], refs[2 + count : 2 + 2 * count]
+    (move_send, move_recv, ring_send, ring_recv, a_send, a_recv, x_send, x_recv, own_sem) = refs[
+        2 + 2 * count :
+    ]
+    place = Place(sz)
+    ring = Ring(place, n_dp)
+    t = lax.axis_index("tensor")
+    ctx, part, half, n_c = place.ctx, place.part, sz.half, sz.n_context
+    role = part * n_c + ctx
+    at_home = role == t
+    steps = n_dp - 1
+    sub = adapter_in.shape[0] // half
+    ahead = 1 - 2 * ctx
+
+    def holder(g):
+        return (place.dp, g * half + t // n_c, lax.rem(t, n_c))
+
+    barrier = pltpu.get_barrier_semaphore()
+
+    def greet(device):
+        pl.semaphore_signal(barrier, inc=1, device_id=device, device_id_type=MESH)
+
+    greet(ring.device(1))
+    greet(ring.device(n_dp - 1))
+    greet(place.sibling())
+    for q in range(1, half):
+        greet(place.device(place.ahead(q), ctx))
+    for c in range(n_c):
+        pl.when(jnp.logical_not(at_home & (ctx == c)))(
+            lambda c=c: greet((place.dp, role, c))
+        )
+    waits = 2 + half + sz.seqs - jnp.where(at_home, 1, 0)
+    pl.semaphore_wait(barrier, waits)
+
+    def move(w, g):
+        slot = place.dp * n_c + ctx
+        return pltpu.make_async_remote_copy(
+            src_ref=blocks_in[w],
+            dst_ref=blocks_out[w].at[slot],
+            send_sem=move_send.at[w, g],
+            recv_sem=move_recv.at[w, ctx],
+            device_id=holder(g),
+            device_id_type=MESH,
+        )
+
+    def stay(w):
+        return pltpu.make_async_copy(
+            blocks_in[w], blocks_out[w].at[place.dp * n_c + ctx], own_sem.at[w]
+        )
+
+    def moved(w, c):
+        slot = place.dp * n_c + c
+        arrival = pltpu.make_async_remote_copy(
+            src_ref=blocks_in[w],
+            dst_ref=blocks_out[w].at[slot],
+            send_sem=move_send.at[w, 0],
+            recv_sem=move_recv.at[w, c],
+            device_id=place.sibling(),
+            device_id_type=MESH,
+        )
+        here = at_home & (ctx == c)
+        pl.when(here)(lambda: stay(w).wait())
+        pl.when(jnp.logical_not(here))(lambda: arrival.wait_recv())
+
+    def adapter_rows(offset, c, p):
+        return adapter_out.at[
+            ring.index(offset) * n_c + c, pl.ds(pl.multiple_of(p * sub, sub), sub)
+        ]
+
+    own_rows = adapter_in.at[pl.ds(pl.multiple_of(part * sub, sub), sub)]
+
+    def around(s):
+        rows = adapter_rows(-ahead * s, ctx, part)
+        return pltpu.make_async_remote_copy(
+            src_ref=own_rows if s == 0 else rows,
+            dst_ref=rows,
+            send_sem=a_send.at[s],
+            recv_sem=a_recv.at[s],
+            device_id=ring.device(ahead),
+            device_id_type=MESH,
+        )
+
+    def across(kind, s):
+        offset = -ahead * s
+        if kind < half:
+            dst = adapter_rows(offset, ctx, part)
+            src = own_rows if s == 0 else dst
+        else:
+            src = dst = adapter_rows(offset, ctx, place.behind(kind - half + 1))
+        target = place.device(place.ahead(kind), ctx) if 0 < kind < half else place.sibling()
+        return pltpu.make_async_remote_copy(
+            src_ref=src,
+            dst_ref=dst,
+            send_sem=x_send.at[kind, s],
+            recv_sem=x_recv.at[kind, s],
+            device_id=target,
+            device_id_type=MESH,
+        )
+
+    def crossed(kind, s):
+        if kind == 0:
+            rows = adapter_rows(ahead * s, 1 - ctx, part)
+        elif kind < half:
+            rows = adapter_rows(-ahead * s, ctx, place.behind(kind))
+        else:
+            rows = adapter_rows(ahead * s, 1 - ctx, place.behind(kind - half + 1))
+        return pltpu.make_async_remote_copy(
+            src_ref=rows,
+            dst_ref=rows,
+            send_sem=x_send.at[kind, s],
+            recv_sem=x_recv.at[kind, s],
+            device_id=place.sibling(),
+            device_id_type=MESH,
+        )
+
+    def hop(w, way, s):
+        offset = -s if way == 0 else s
+        rows = blocks_out[w].at[ring.index(offset) * n_c + way]
+        return pltpu.make_async_remote_copy(
+            src_ref=rows,
+            dst_ref=rows,
+            send_sem=ring_send.at[w, way, s],
+            recv_sem=ring_recv.at[w, way, s],
+            device_id=ring.device(1 if way == 0 else n_dp - 1),
+            device_id_type=MESH,
+        )
+
+    def hopped(w, way, s):
+        offset = -(s + 1) if way == 0 else s + 1
+        rows = blocks_out[w].at[ring.index(offset) * n_c + way]
+        return pltpu.make_async_remote_copy(
+            src_ref=rows,
+            dst_ref=rows,
+            send_sem=ring_send.at[w, way, s],
+            recv_sem=ring_recv.at[w, way, s],
+            device_id=ring.device(1),
+            device_id_type=MESH,
+        )
+
+    around(0).start()
+    own = pltpu.make_async_copy(own_rows, adapter_rows(0, ctx, part), own_sem.at[count])
+    own.start()
+    for w in range(count):
+        for g in range(sz.seqs):
+            here = at_home & (place.group == g)
+            pl.when(jnp.logical_not(here))(lambda w=w, g=g: move(w, g).start())
+        pl.when(at_home)(lambda w=w: stay(w).start())
+    for kind in range(half):
+        across(kind, 0).start()
+
+    def adapter_step(s):
+        if s < steps:
+            arrival = pltpu.make_async_remote_copy(
+                src_ref=own_rows,
+                dst_ref=adapter_rows(-ahead * (s + 1), ctx, part),
+                send_sem=a_send.at[s],
+                recv_sem=a_recv.at[s],
+                device_id=ring.device(1),
+                device_id_type=MESH,
+            )
+            arrival.wait_recv()
+            if s + 1 < steps:
+                around(s + 1).start()
+            for kind in range(half):
+                across(kind, s + 1).start()
+
+    def adapter_pass(s):
+        for q in range(1, half):
+            crossed(q, s).wait_recv()
+            across(half - 1 + q, s).start()
+
+    todo = []
+    for k in range(count + steps):
+        for s in range(min(k, steps - 1), -1, -1):
+            w = k - s
+            if w < count:
+                todo.append((w, s))
+    done = 0
+    for w, s in todo:
+        for way in range(n_c):
+            if s == 0:
+                moved(w, way)
+            else:
+                hopped(w, way, s - 1).wait_recv()
+            hop(w, way, s).start()
+        if done < steps:
+            adapter_step(done)
+        done += 1
+    for s in range(done, steps):
+        adapter_step(s)
+    for s in range(n_dp):
+        adapter_pass(s)
+    for w in range(count):
+        for way in range(n_c):
+            hopped(w, way, steps - 1).wait_recv()
+    for s in range(n_dp):
+        crossed(0, s).wait_recv()
+        for q in range(1, half):
+            crossed(half - 1 + q, s).wait_recv()
+    own.wait()
+    for w in range(count):
+        for g in range(sz.seqs):
+            here = at_home & (place.group == g)
+            pl.when(jnp.logical_not(here))(lambda w=w, g=g: move(w, g).wait_send())
+        for way in range(n_c):
+            for s in range(steps):
+                hop(w, way, s).wait_send()
+    for s in range(steps):
+        around(s).wait_send()
+    for s in range(n_dp):
+        for kind in range(2 * half - 1):
+            across(kind, s).wait_send()
+
+
+def run_weights(sz, n_dp, adapter, blocks):
+    bf16 = jnp.bfloat16
+    slots = n_dp * sz.n_context
+    outs = [jax.ShapeDtypeStruct((slots,) + a.shape, bf16) for a in [adapter] + blocks]
+    count, steps, dma = len(blocks), n_dp - 1, pltpu.SemaphoreType.DMA
+    kinds = 2 * sz.half - 1
+    return pl.pallas_call(
+        partial(weights_kernel, sz, n_dp),
+        out_shape=outs,
+        in_specs=[any_spec()] * (1 + count),
+        out_specs=[any_spec()] * (1 + count),
+        scratch_shapes=[
+            dma((count, sz.seqs)),
+            dma((count, sz.n_context)),
+            dma((count, sz.n_context, steps)),
+            dma((count, sz.n_context, steps)),
+            dma((steps,)),
+            dma((steps,)),
+            dma((kinds, n_dp)),
+            dma((kinds, n_dp)),
+            dma((count + 1,)),
+        ],
+        compiler_params=pltpu.CompilerParams(collective_id=5, has_side_effects=True),
+        name="weights",
+    )(adapter, *blocks)
+
+
 def shards(
     embedded,
     initial_state,
@@ -719,16 +987,6 @@
 
     role_perms = [role_perm(0), role_perm(1)]
 
-    def role_weight(block, axis):
-        got = [lax.ppermute(block, ("tensor", "context"), perm) for perm in role_perms]
-        low = jnp.where(group == 0, got[0], got[1])
-        high = jnp.where(group == 0, got[1], got[0])
-        if axis == 0:
-            both = jnp.concatenate([low, high], axis=0)
-        else:
-            both = jnp.stack([low, high], axis=0)
-        return lax.all_gather(both, "dp", axis=0, tiled=True)
-
     def side_by_side(blocks):
         count, depth, columns = blocks.shape
         return blocks.transpose(1, 0, 2).reshape(depth, count * columns)
@@ -767,34 +1025,6 @@
     embed_rows = swap_in(embedded)
     state_rows = swap_in(initial_state)
     cot_rows = swap_in(cotangent)
-    adapter_full = lax.all_gather(adapter_weight, ("dp", "context"), axis=0, tiled=True)
-    gains_full = lax.all_gather(norm_gains, ("dp", "context"), axis=1, tiled=True)
-    qkv_use = role_weight(qkv_weight.reshape(qkv_weight.shape[0], -1), 0)
-    out_blocks = role_weight(output_head_weight.reshape(heads_here * head_dim, -1), 1)
-    gate_use = role_weight(gate_up_weight[:, 0], 0)
-    up_use = role_weight(gate_up_weight[:, 1], 0)
-    down_blocks = role_weight(down_weight, 1)
-    out_use = side_by_side(out_blocks)
-    down_use = side_by_side(down_blocks)
-    if out_blocks.shape[2] % 128:
-        out_blocks = out_use[None]
-        down_blocks = down_use[None]
-    gains_f = gains_full.astype(jnp.float32)
-
-    order = jnp.arange(seq_len, dtype=jnp.int32)
-    cos_t, sin_t = rope_angles(order, head_dim)
-    cos_full = jnp.concatenate([cos_t, cos_t], axis=1)
-    sin_full = jnp.concatenate([-sin_t, sin_t], axis=1)
-    cos_t = cos_t[:, None, :]
-    sin_t = sin_t[:, None, :]
-    own_seq = dp_index * seq_count + group
-    docs = lax.dynamic_index_in_dim(doc_ids, own_seq, 0, keepdims=False)
-    begin = jnp.sum((docs[None, :] < docs[:, None]).astype(jnp.int32), axis=1)[None, :]
-    steps_own = lax.dynamic_index_in_dim(recurrences, own_seq, 0, keepdims=False) - BACK
-    embed_part = jnp.dot(
-        embed_rows, adapter_full[model_width:], preferred_element_type=jnp.float32
-    )
-
     sz = Sizes(
         n_tensor,
         n_context,
@@ -809,12 +1039,68 @@
         head_dim,
         ff_here,
     )
-    adapter_top = adapter_full[:model_width]
+    adapter_block = adapter_weight.shape[0]
+    gain_columns = norm_gains.shape[1]
+    unit = 16 * half
+    padded = -(-(adapter_block + 2) // unit) * unit
+    adapter_rows = jnp.concatenate(
+        [
+            adapter_weight,
+            jnp.pad(
+                norm_gains,
+                ((0, padded - adapter_block - 2), (0, model_width - gain_columns)),
+            ),
+        ],
+        axis=0,
+    )
+    adapter_all, qkv_use, out_blocks, gate_use, up_use, down_blocks = run_weights(
+        sz,
+        n_dp,
+        adapter_rows,
+        [
+            qkv_weight.reshape(qkv_weight.shape[0], -1),
+            output_head_weight.reshape(heads_here * head_dim, -1),
+            gate_up_weight[:, 0],
+            gate_up_weight[:, 1],
+            down_weight,
+        ],
+    )
+    qkv_use = qkv_use.reshape(model_width, -1)
+    gate_use = gate_use.reshape(model_width, -1)
+    up_use = up_use.reshape(model_width, -1)
+    gains_full = (
+        adapter_all[:, adapter_block : adapter_block + 2, :gain_columns]
+        .transpose(1, 0, 2)
+        .reshape(2, model_width)
+    )
+    adapter_low = adapter_all[adapter_all.shape[0] // 2 :, :adapter_block].reshape(
+        model_width, model_width
+    )
+    out_use = side_by_side(out_blocks)
+    down_use = side_by_side(down_blocks)
+    if out_blocks.shape[2] % 128:
+        out_blocks = out_use[None]
+        down_blocks = down_use[None]
+    gains_f = gains_full.astype(jnp.float32)
+
+    order = jnp.arange(seq_len, dtype=jnp.int32)
+    cos_t, sin_t = rope_angles(order, head_dim)
+    cos_full = jnp.concatenate([cos_t, cos_t], axis=1)
+    sin_full = jnp.concatenate([-sin_t, sin_t], axis=1)
+    cos_t = cos_t[:, None, :]
+    sin_t = sin_t[:, None, :]
+    own_seq = dp_index * seq_count + group
+    docs = lax.dynamic_index_in_dim(doc_ids, own_seq, 0, keepdims=False)
+    begin = jnp.sum((docs[None, :] < docs[:, None]).astype(jnp.int32), axis=1)[None, :]
+    steps_own = lax.dynamic_index_in_dim(recurrences, own_seq, 0, keepdims=False) - BACK
+    embed_part = jnp.dot(
+        embed_rows, adapter_low, preferred_element_type=jnp.float32
+    )
 
     def advance(step_index, current):
         (mixed,) = run_attn(
             sz, False, current, embed_part, gains_f, cos_full, sin_full, begin,
-            adapter_top, qkv_use, out_blocks,
+            adapter_all, qkv_use, out_blocks,
         )
         active = jnp.broadcast_to((step_index < steps_own).astype(jnp.float32), (1, model_width))
         (result,) = run_ffn(
@@ -827,7 +1113,7 @@
     )
     (mixed_rows, adapted, feature_rows, query_hm, key_hm, value_hm, head_flat, lse) = run_attn(
         sz, True, detached, embed_part, gains_f, cos_full, sin_full, begin,
-        adapter_top, qkv_use, out_blocks,
+        adapter_all, qkv_use, out_blocks,
     )
     (current, ffn_input, gate_pre, up_pre, hidden) = run_ffn(
         sz, True, mixed_rows, detached, gains_f[:1], gains_f, gate_use, up_use, down_blocks
@@ -900,7 +1186,7 @@
     embed_out = jnp.einsum(
         "srd,kd->srk",
         swap_out(adapted_low),
-        adapter_full[model_width:],
+        adapter_low,
         preferred_element_type=jnp.float32,
     )
     down_s = role_grad(down_g, 1)

time: 1810 us -> 1660 us (0.917)
  waiting for transfers between devices: 887 us -> 521 us
  Pallas kernels: 447 us -> 748 us
  starting transfers between devices: 111 us -> 38.3 us
    pallas_call x0 -> x1, Pallas kernels: none -> 277 us  [run_weights(): pl.pallas_call(partial(weights_kernel, sz, n_dp), out_shape=outs, in_spec...]
    all_gather x6 -> x0, waiting for transfers between devices: 231 us -> none  [the longest x5 230 us: role_weight(): return lax.all_gather(both, 'dp', axis=0, tiled=True)]
    ppermute x10 -> x0, waiting for transfers between devices: 77.3 us -> none  [role_weight(): lax.ppermute(block, ('tensor', 'context'), perm)]
    ppermute x10 -> x0, starting transfers between devices: 53.4 us -> none  [role_weight(): lax.ppermute(block, ('tensor', 'context'), perm)]
    ppermute x3, waiting for transfers between devices: 48.4 us -> 0.01 us  [swap_in(): got = lax.ppermute(other, 'tensor', pair_swap)]
    pallas_call x4, Pallas kernels: 236 us -> 260 us  [run_attn(): pl.pallas_call(partial(attn_kernel, sz, keep), out_shape=outs, in_specs=[...]
  transfers between devices with their start and end apart: 40 -> 24, of which waited for: 31 -> 14; matrix products, arithmetic and copies ran while one was open for 9% -> 11% of each run, Pallas kernels for 0% -> 45%
where the time goes in v3:
time: 1660 us; the launch traced here: 1650 us
  Pallas kernels  748 us (45%)
  waiting for transfers between devices  521 us (31%)
  matrix products  143 us (9%)
  local copies, waits for them, and re-layouts  87.3 us (5%)
  other arithmetic  63.9 us (4%)
  starting transfers between devices  38.3 us (2%)
  loops' own time  26.4 us (2%)
    pallas_call x1, Pallas kernels, run_weights(): pl.pallas_call(partial(weights_kernel, sz, n_dp), out_shape=outs, in_spec...  277 us
    pallas_call x4, Pallas kernels, run_attn(): pl.pallas_call(partial(attn_kernel, sz, keep), out_shape=outs, in_specs=[...  260 us
    reduce_scatter x4, waiting for transfers between devices, role_grad(): lax.psum_scatter(grad.astype(jnp.bfloat16), 'dp', scatter_dimension=axis,...  224 us
    pallas_call x4, Pallas kernels, run_ffn(): pl.pallas_call(partial(ffn_kernel, sz, keep), out_shape=outs, in_specs=[f...  211 us
    reduce_scatter x1, waiting for transfers between devices, shards(): lax.psum_scatter(adapter_g.astype(jnp.bfloat16), ('dp', 'context'), scatt...  109 us
    psum x1, waiting for transfers between devices, shards(): adapter_s = lax.psum(adapter_s, 'tensor').astype(jnp.float32)  54.6 us
    reduce_scatter x2, waiting for transfers between devices, sum_rows(): lax.psum_scatter(split.transpose(1, 2, 0, 3, 4).reshape(seq_len, model_wi...  43.8 us
    ppermute x8, waiting for transfers between devices, role_grad(): lax.ppermute(g, ('tensor', 'context'), [(b, a) for a, b in perm])  33.8 us
  transfers between devices with their start and end apart: 24, of which 14 were waited for; matrix products, arithmetic and copies ran while one was open for 11% of the time, Pallas kernels for 45%

profile of v3, /device:TPU:1, one launch (start us, length us, event | category | flops | bytes accessed | tf_op | source)
XLA Modules:
  0.0 1653.6 jit_solution(13397599977732900881)
XLA Ops:
  23.8 276.6 %weights.1 = (bf16[8,544,2048]{2,1,0:T(8,128)(2,1)}, bf16[8,256,1536]{2,1,0:T(8,128)(2,1)}, bf16[8,512,256]{2,1,0:T(8,128)(2,1)}, bf16[8,256,1408]{2,1,0:T(8,128...) custom-call(bf16[544,2048]{1,0:T(8,128)(2,1)} %fusion.30.refs_0_, bf16[256,1536]{1,0:T(8,128)(2,1)} %bitcast.150, ...), custom_call_target="tpu_custom_call" | custom-call | tf_op jit(solution)/shard_map/weights/pallas_call | solution.py:907
  339.0 396.3 %while.10 = (s32[]{:T(128)}, f32[256,2048]{1,0:T(8,128)}, s32[]{:T(128)}, f32[256,2048]{1,0:T(8,128)}, f32[2,2048]{1,0:T(2,128)S(1)}, /*index=5*/f32[1024,128]{1...) while((s32[]{:T(128)}, f32[256,2048]{1,0:T(8,128)}, ...), condition=%wide.region_3.4_spmd, body=%wide.region_2.3_spmd.sunk | while | flops 26306674688 | bytes 46145700 | solution.py:1111
  363.5 82.5 %attn_round.1.refs_0_ = f32[256,2048]{1,0:T(8,128)} custom-call(f32[256,2048]{1,0:T(8,128)} %copy.154.refs_0_.refs_1_, f32[256,2048]{1,0:T(8,128)} %get-tuple-element.353.refs_1_, f32[2,2048]{1,0:T(2,128)S(1)} %get-tuple-element.354.refs_2_.refs_3_, f32[1024,128]{1,0:T(8,128)S(1)} %get-tuple-element.355.refs_3_, f32[1024,128]{1,0:T(8,128)S(1)} %get-tuple-element.356.refs_4_, ...), custom_call_target="tpu_custom_call" | custom-call | flops 8589934592 | bytes 20971520 | tf_op jit(solution)/shard_map/while/body/attn_round/pallas_call | solution.py:523
  446.7 52.9 %ffn_round.1 = f32[256,2048]{1,0:T(8,128)} custom-call(f32[256,2048]{1,0:T(8,128)} %attn_round.1.refs_0_, f32[256,2048]{1,0:T(8,128)} %copy.154.refs_0_.refs_1_, f32[1,2048]{1,0:T(1,128)} %broadcast_in_dim.19.refs_2_, f32[2,2048]{1,0:T(2,128)S(1)} %get-tuple-element.354.refs_2_.refs_3_, bf16[2048,1408]{1,0:T(8,128)(2,1)} %get-tuple-element.362.refs_4_, ...), custom_call_target="tpu_custom_call" | custom-call | flops 17716740096 | bytes 20971520 | tf_op jit(solution)/shard_map/while/body/ffn_round/pallas_call | solution.py:650
  502.7 59.0 %attn_round.1.refs_0_ = f32[256,2048]{1,0:T(8,128)} custom-call(f32[256,2048]{1,0:T(8,128)} %copy.154.refs_0_.refs_1_, f32[256,2048]{1,0:T(8,128)} %get-tuple-element.353.refs_1_, f32[2,2048]{1,0:T(2,128)S(1)} %get-tuple-element.354.refs_2_.refs_3_, f32[1024,128]{1,0:T(8,128)S(1)} %get-tuple-element.355.refs_3_, f32[1024,128]{1,0:T(8,128)S(1)} %get-tuple-element.356.refs_4_, ...), custom_call_target="tpu_custom_call" | custom-call | flops 8589934592 | bytes 20971520 | tf_op jit(solution)/shard_map/while/body/attn_round/pallas_call | solution.py:523
  562.4 52.1 %ffn_round.1 = f32[256,2048]{1,0:T(8,128)} custom-call(f32[256,2048]{1,0:T(8,128)} %attn_round.1.refs_0_, f32[256,2048]{1,0:T(8,128)} %copy.154.refs_0_.refs_1_, f32[1,2048]{1,0:T(1,128)} %broadcast_in_dim.19.refs_2_, f32[2,2048]{1,0:T(2,128)S(1)} %get-tuple-element.354.refs_2_.refs_3_, bf16[2048,1408]{1,0:T(8,128)(2,1)} %get-tuple-element.362.refs_4_, ...), custom_call_target="tpu_custom_call" | custom-call | flops 17716740096 | bytes 20971520 | tf_op jit(solution)/shard_map/while/body/ffn_round/pallas_call | solution.py:650
  617.6 59.0 %attn_round.1.refs_0_ = f32[256,2048]{1,0:T(8,128)} custom-call(f32[256,2048]{1,0:T(8,128)} %copy.154.refs_0_.refs_1_, f32[256,2048]{1,0:T(8,128)} %get-tuple-element.353.refs_1_, f32[2,2048]{1,0:T(2,128)S(1)} %get-tuple-element.354.refs_2_.refs_3_, f32[1024,128]{1,0:T(8,128)S(1)} %get-tuple-element.355.refs_3_, f32[1024,128]{1,0:T(8,128)S(1)} %get-tuple-element.356.refs_4_, ...), custom_call_target="tpu_custom_call" | custom-call | flops 8589934592 | bytes 20971520 | tf_op jit(solution)/shard_map/while/body/attn_round/pallas_call | solution.py:523
  677.2 52.9 %ffn_round.1 = f32[256,2048]{1,0:T(8,128)} custom-call(f32[256,2048]{1,0:T(8,128)} %attn_round.1.refs_0_, f32[256,2048]{1,0:T(8,128)} %copy.154.refs_0_.refs_1_, f32[1,2048]{1,0:T(1,128)} %broadcast_in_dim.19.refs_2_, f32[2,2048]{1,0:T(2,128)S(1)} %get-tuple-element.354.refs_2_.refs_3_, bf16[2048,1408]{1,0:T(8,128)(2,1)} %get-tuple-element.362.refs_4_, ...), custom_call_target="tpu_custom_call" | custom-call | flops 17716740096 | bytes 20971520 | tf_op jit(solution)/shard_map/while/body/ffn_round/pallas_call | solution.py:650
  735.3 59.6 %attn_keep.1 = (f32[256,2048]{1,0:T(8,128)}, f32[256,2048]{1,0:T(8,128)}, bf16[1024,2048]{1,0:T(8,128)(2,1)}, bf16[4,1024,128]{2,1,0:T(8,128)(2,1)}, bf16[4,1024...) custom-call(f32[256,2048]{1,0:T(8,128)} %get-tuple-element.111.refs_0_.re, ...), custom_call_target="tpu_custom_call" | custom-call | flops 8589934592 | bytes 20971520 | tf_op jit(solution)/shard_map/attn_keep/pallas_call | solution.py:523
  794.9 53.1 %ffn_keep.1 = (f32[256,2048]{1,0:T(8,128)}, bf16[1024,2048]{1,0:T(8,128)(2,1)}, bf16[1024,1408]{1,0:T(8,128)(2,1)}, bf16[1024,1408]{1,0:T(8,128)(2,1)}, bf16[1024,1408]{1,0:T(8,128)(2,1)}) custom-call(f32[256,2048]{1,0:T(8,128)} %get-tuple-element.112.refs_0_, f32[256,2048]{1,0:T(8,128)} %get-tuple-element.111.refs_0_.refs_1_, f32[1,2048]{1,0:T(1,128)} %bitcast.163, ...), custom_call_target="tpu_custom_call" | custom-call | flops 17716740096 | bytes 20971520 | tf_op jit(solution)/shard_map/ffn_keep/pallas_call | solution.py:650
  852.0 12.5 fusion.25
  864.6 16.0 bitcast_convert_fusion.1
  885.0 43.4 %reduce-scatter.11.cloned.1.call-done = bf16[256,2048]{1,0:T(8,128)(2,1)} async-done(((bf16[1024,2048]{1,0:T(8,128)(2,1)}), bf16[256,2048]{1,0:T(8,128)(2,1)}) %reduce-scatter.11.cloned.1.call-update) | async-done | bytes 1048592 | tf_op jit(solution)/shard_map/reduce_scatter | solution.py:1017
  954.0 22.5 %all-gather.5.cloned.1.call-done = bf16[1024,2048]{1,0:T(8,128)(2,1)} async-done(((bf16[256,2048]{1,0:T(8,128)(2,1)}), bf16[1024,2048]{1,0:T(8,128)(2,1)}) %all-gather.5.cloned.1.call-update) | async-done | bytes 4194320 | tf_op jit(solution)/shard_map/all_gather | solution.py:1007
  1001.8 12.1 multiply_convert_fusion
  1058.2 18.4 %convolution_convert_fusion.1 = bf16[2048,2,1408]{2,0,1:T(8,128)(2,1)} fusion(bf16[1024,2048]{1,0:T(8,128)(2,1)} %get-tuple-element.123, bf16[1024,1,1408]{2,0,1:T(8,128)(2,1)} %get-tuple-element.194, bf16[1024,1,1408]{2,0,1:T(8,128)(2,1)} %copy-done.39), kind=kOutput, calls=%fused_computation.8 | convolution fusion | flops 11828461568 | bytes 21495808 | tf_op jit(solution)/shard_map/qd,qgf->dgf/dot_general | solution.py:1140
  1114.5 34.5 %reduce-scatter.23.cloned.1.call-done = bf16[1408,512]{1,0:T(8,128)(2,1)} async-done(((bf16[1408,2048]{1,0:T(8,128)(2,1)}), bf16[1408,512]{1,0:T(8,128)(2,1)}) %reduce-scatter.23.cloned.1.call-update) | async-done | bytes 1441808 | tf_op jit(solution)/shard_map/reduce_scatter | solution.py:995
  1164.0 23.6 %reduce-scatter.19.cloned.1.call-done = bf16[4,128,512]{2,1,0:T(8,128)(2,1)} async-done(((bf16[4,128,2048]{2,1,0:T(8,128)(2,1)}), bf16[4,128,512]{2,1,0:T(8,128)(2,1)}) %reduce-scatter.19.cloned.1.call-update) | async-done | bytes 524304 | tf_op jit(solution)/shard_map/reduce_scatter | solution.py:995
  1208.5 94.7 %reduce-scatter.21.cloned.1.call-done = bf16[512,2,1408]{2,0,1:T(8,128)(2,1)} async-done(((bf16[2048,2,1408]{2,0,1:T(8,128)(2,1)}), bf16[512,2,1408]{2,0,1:T(8,128)(2,1)}) %reduce-scatter.21.cloned.1.call-update) | async-done | bytes 2883600 | tf_op jit(solution)/shard_map/reduce_scatter | solution.py:995
  1310.9 30.2 %reduce-scatter.25.cloned.1.call-done = bf16[256,2]{1,0:T(8,128)(2,1)} async-done(((bf16[2048,2]{1,0:T(8,128)(2,1)}), bf16[256,2]{1,0:T(8,128)(2,1)}) %reduce-scatter.25.cloned.1.call-update) | async-done | bytes 1040
  1352.2 108.6 %reduce-scatter.15.cloned.1.call-done = bf16[512,2048]{1,0:T(8,128)(2,1)} async-done(((bf16[4096,2048]{1,0:T(8,128)(2,1)}), bf16[512,2048]{1,0:T(8,128)(2,1)}) %reduce-scatter.15.cloned.1.call-update) | async-done | bytes 2097168 | tf_op jit(solution)/shard_map/reduce_scatter | solution.py:1196
  1462.7 71.1 %reduce-scatter.17.cloned.1.call-done = bf16[512,4,384]{2,0,1:T(8,128)(2,1)} async-done(((bf16[2048,4,384]{2,0,1:T(8,128)(2,1)}), bf16[512,4,384]{2,0,1:T(8,128)(2,1)}) %reduce-scatter.17.cloned.1.call-update) | async-done | bytes 1572880 | tf_op jit(solution)/shard_map/reduce_scatter | solution.py:995
  1554.7 30.7 %collective-permute-done.5 = bf16[256,4,384]{2,0,1:T(8,128)(2,1)S(1)} collective-permute-done((bf16[256,4,384]{2,0,1:T(8,128)(2,1)S(1)}, bf16[256,4,384]{2,0,1:T(8,128)(2,1)S(1)}, u32[]{:S(2)}, u32[]{:S(2)}) %collective-permute-start.5) | collective-permute-done | bytes 786464 | tf_op jit(solution)/shard_map/ppermute | solution.py:1001
  1587.9 54.6 %all-reduce.3.cloned.1.call-done = bf16[512,2048]{1,0:T(8,128)(2,1)} async-done(((bf16[512,2048]{1,0:T(8,128)(2,1)}), bf16[512,2048]{1,0:T(8,128)(2,1)}) %all-reduce.3.cloned.1.call-update) | async-done | bytes 2097168 | tf_op jit(solution)/shard_map/psum | solution.py:1205
  (233 shorter events, 290.2 us)
Async XLA Ops:
  7.2 840.8 %all-gather.3.cloned.1.call-start = ((), (), s32[]{:S(2)}) async-start(), calls=%async_computation.8 | async-start | bytes 5242880 | tf_op jit(solution)/shard_map/all_gather | solution.py:1007
  8.5 322.0 %collective-permute-start.1 = (bf16[128,2048]{1,0:T(8,128)(2,1)S(1)}, bf16[128,2048]{1,0:T(8,128)(2,1)}, u32[]{:S(2)}, u32[]{:S(2)}) collective-permute-start(bf16[128,2048]{1,0:T(8,128)(2,1)S(1)} %dynamic-slice_bitcast_fusion.1), channel_id=1, source_target_pairs={{0,4},{2,6},{4,0},{6,2},{1,5},{3,7},{5,1},{7,3},{8,12},{10,14},{12... | collective-permute-start | bytes 1572872 | tf_op jit(solution)/shard_map/ppermute | solution.py:965
  13.5 313.9 %collective-permute-start = (bf16[128,2048]{1,0:T(8,128)(2,1)}, bf16[128,2048]{1,0:T(8,128)(2,1)}, u32[]{:S(2)}, u32[]{:S(2)}) collective-permute-start(bf16[128,2048]{1,0:T(8,128)(2,1)} %dynamic-slice_bitcast_fusion.2), channel_id=1, source_target_pairs={{0,4},{2,6},{4,0},{6,2},{1,5},{3,7},{5,1},{7,3},{8,12},{10,14},{12... | collective-permute-start | bytes 1572872 | tf_op jit(solution)/shard_map/ppermute | solution.py:965
  15.4 308.8 %collective-permute-start.3 = (bf16[128,2048]{1,0:T(8,128)(2,1)}, bf16[128,2048]{1,0:T(8,128)(2,1)}, u32[]{:S(2)}, u32[]{:S(2)}) collective-permute-start(bf16[128,2048]{1,0:T(8,128)(2,1)} %dynamic-slice_bitcast_fusion), channel_id=1, source_target_pairs={{0,4},{2,6},{4,0},{6,2},{1,5},{3,7},{5,1},{7,3},{8,12},{10,14},{12... | collective-permute-start | bytes 1572872 | tf_op jit(solution)/shard_map/ppermute | solution.py:965
  327.4 601.0 %reduce-scatter.11.cloned.1.call-start = ((), (), s32[]{:S(2)}) async-start(), calls=%async_computation.9 | async-start | bytes 5242880 | tf_op jit(solution)/shard_map/reduce_scatter | solution.py:1017
  883.3 93.3 %all-gather.5.cloned.1.call-start = ((), (), s32[]{:S(2)}) async-start(), calls=%async_computation.10 | async-start | bytes 5242880 | tf_op jit(solution)/shard_map/all_gather | solution.py:1007
  932.2 148.3 %reduce-scatter.13.cloned.1.call-start = ((), (), s32[]{:S(2)}) async-start(), calls=%async_computation.11 | async-start | bytes 5242880 | tf_op jit(solution)/shard_map/reduce_scatter | solution.py:1017
  1037.8 111.1 %reduce-scatter.23.cloned.1.call-start = ((), (), s32[]{:S(2)}) async-start(), calls=%async_computation.17 | async-start | bytes 7208960 | tf_op jit(solution)/shard_map/reduce_scatter | solution.py:995
  1050.5 137.1 %reduce-scatter.19.cloned.1.call-start = ((), (), s32[]{:S(2)}) async-start(), calls=%async_computation.15 | async-start | bytes 2621440 | tf_op jit(solution)/shard_map/reduce_scatter | solution.py:995
  1058.2 245.0 %reduce-scatter.21.cloned.1.call-start = ((), (), s32[]{:S(2)}) async-start(), calls=%async_computation.16 | async-start | bytes 14417920 | tf_op jit(solution)/shard_map/reduce_scatter | solution.py:995
  1076.6 264.5 %reduce-scatter.25.cloned.1.call-start = ((), (), s32[]{:S(2)}) async-start(), calls=%async_computation.18 | async-start | bytes 589824
  1084.4 376.4 %reduce-scatter.15.cloned.1.call-start = ((), (), s32[]{:S(2)}) async-start(), calls=%async_computation.12 | async-start | bytes 18874368 | tf_op jit(solution)/shard_map/reduce_scatter | solution.py:1196
  1098.1 435.7 %reduce-scatter.17.cloned.1.call-start = ((), (), s32[]{:S(2)}) async-start(), calls=%async_computation.14 | async-start | bytes 7864320 | tf_op jit(solution)/shard_map/reduce_scatter | solution.py:995
  1109.7 532.8 %all-reduce.3.cloned.1.call-start = ((), (), s32[]{:S(2)}) async-start(), calls=%async_computation.13 | async-start | bytes 4194304 | tf_op jit(solution)/shard_map/psum | solution.py:1205
  1112.3 48.7 %collective-permute-start.2 = (f32[128,2048]{1,0:T(8,128)}, f32[128,2048]{1,0:T(8,128)}, u32[]{:S(2)}, u32[]{:S(2)}) collective-permute-start(f32[128,2048]{1,0:T(8,128)} %slice_select_fusion), channel_id=1, source_target_pairs={{0,4},{2,6},{4,0},{6,2},{1,5},{3,7},{5,1},{7,3},{8,12},{10,14},{12... | collective-permute-start | bytes 3145736 | tf_op jit(solution)/shard_map/ppermute | solution.py:974
  1151.4 43.0 %collective-permute-start.11 = (bf16[1408,256]{1,0:T(8,128)(2,1)}, bf16[1408,256]{1,0:T(8,128)(2,1)}, u32[]{:S(2)}, u32[]{:S(2)}) collective-permute-start(bf16[1408,256]{1,0:T(8,128)(2,1)} %get-tuple-element.209), channel_id=1, source_target_pairs={{0,0},{4,1},{1,2},{5,3},{2,4},{6,5},{3,6},{7,7},{8,8},{12,9},{9,10... | collective-permute-start | bytes 2162696 | tf_op jit(solution)/shard_map/ppermute | solution.py:1001
  1155.1 39.4 %collective-permute-start.12 = (bf16[1408,256]{1,0:T(8,128)(2,1)}, bf16[1408,256]{1,0:T(8,128)(2,1)}, u32[]{:S(2)}, u32[]{:S(2)}) collective-permute-start(bf16[1408,256]{1,0:T(8,128)(2,1)} %get-tuple-element.210), channel_id=1, source_target_pairs={{4,0},{0,1},{5,2},{1,3},{6,4},{2,5},{7,6},{3,7},{12,8},{8,9},{13,1... | collective-permute-start | bytes 2162696 | tf_op jit(solution)/shard_map/ppermute | solution.py:1001
  1188.6 11.4 collective-permute-start.7
  1192.3 7.7 collective-permute-start.8
  1200.9 259.9 %collective-permute-start.4 = (bf16[128,2048]{1,0:T(8,128)(2,1)S(1)}, bf16[128,2048]{1,0:T(8,128)(2,1)}, u32[]{:S(2)}, u32[]{:S(2)}) collective-permute-start(bf16[128,2048]{1,0:T(8,128)(2,1)S(1)} %broadcast_select_fusion.6), channel_id=1, source_target_pairs={{0,4},{2,6},{4,0},{6,2},{1,5},{3,7},{5,1},{7,3},{8,12},{10,14},{12... | collective-permute-start | bytes 1572872 | tf_op jit(solution)/shard_map/ppermute | solution.py:974
  1306.3 242.6 %collective-permute-start.10 = (bf16[256,2,1408]{2,0,1:T(8,128)(2,1)}, bf16[256,2,1408]{2,0,1:T(8,128)(2,1)}, u32[]{:S(2)}, u32[]{:S(2)}) collective-permute-start(bf16[256,2,1408]{2,0,1:T(8,128)(2,1)} %get-tuple-element.198), channel_id=1, source_target_pairs={{4,0},{0,1},{5,2},{1,3},{6,4},{2,5},{7,6},{3,7},{12,8},{8,9},{13,1... | collective-permute-start | bytes 4325384 | tf_op jit(solution)/shard_map/ppermute | solution.py:1001
  1307.5 241.4 %collective-permute-start.9 = (bf16[256,2,1408]{2,0,1:T(8,128)(2,1)S(1)}, bf16[256,2,1408]{2,0,1:T(8,128)(2,1)}, u32[]{:S(2)}, u32[]{:S(2)}) collective-permute-start(bf16[256,2,1408]{2,0,1:T(8,128)(2,1)S(1)} %get-tuple-element.197), channel_id=1, source_target_pairs={{0,0},{4,1},{1,2},{5,3},{2,4},{6,5},{3,6},{7,7},{8,8},{12,9},{9,10... | collective-permute-start | bytes 4325384 | tf_op jit(solution)/shard_map/ppermute | solution.py:1001
  1535.4 50.1 %collective-permute-start.5 = (bf16[256,4,384]{2,0,1:T(8,128)(2,1)S(1)}, bf16[256,4,384]{2,0,1:T(8,128)(2,1)S(1)}, u32[]{:S(2)}, u32[]{:S(2)}) collective-permute-start(bf16[256,4,384]{2,0,1:T(8,128)(2,1)S(1)} %get-tuple-element.199), channel_id=1, source_target_pairs={{0,0},{4,1},{1,2},{5,3},{2,4},{6,5},{3,6},{7,7},{8,8},{12,9},{9,10... | collective-permute-start | bytes 2359304 | tf_op jit(solution)/shard_map/ppermute | solution.py:1001
  1539.1 46.5 %collective-permute-start.6 = (bf16[256,4,384]{2,0,1:T(8,128)(2,1)S(1)}, bf16[256,4,384]{2,0,1:T(8,128)(2,1)S(1)}, u32[]{:S(2)}, u32[]{:S(2)}) collective-permute-start(bf16[256,4,384]{2,0,1:T(8,128)(2,1)S(1)} %get-tuple-element.200), channel_id=1, source_target_pairs={{4,0},{0,1},{5,2},{1,3},{6,4},{2,5},{7,6},{3,7},{12,8},{8,9},{13,1... | collective-permute-start | bytes 2359304 | tf_op jit(solution)/shard_map/ppermute | solution.py:1001
  (44 other events, 788.4 us)
Sparse Core Ops, SparseCore 0:
  327.5 68.7 all-gather.2
  883.4 44.9 reduce-scatter.10
  932.3 44.1 all-gather.4
  1037.9 42.5 reduce-scatter.12
  1083.4 65.5 reduce-scatter.22
  1152.3 35.1 reduce-scatter.18
  1191.0 112.1 reduce-scatter.20
  1307.1 33.9 reduce-scatter.24
  1344.7 116.0 reduce-scatter.14
  1463.6 70.2 reduce-scatter.16
  1536.3 106.1 all-reduce.2

commit v4 on v3

--- a/solution.py
+++ b/solution.py
@@ -22,77 +22,6 @@
     inv_freq = 1.0 / rope_base ** (2.0 * freq_index / head_dim)
     angles = positions.astype(jnp.float32)[:, None] * inv_freq[None, :]
     return (jnp.cos(angles), jnp.sin(angles))
-
-
-def rotate_fwd(values, cos_t, sin_t):
-    half_dim = values.shape[-1] // 2
-    first_half = values[..., :half_dim]
-    second_half = values[..., half_dim:]
-    return jnp.concatenate(
-        [first_half * cos_t - second_half * sin_t, second_half * cos_t + first_half * sin_t],
-        axis=-1,
-    )
-
-
-def rotate_back(grad_vals, cos_t, sin_t):
-    half_dim = grad_vals.shape[-1] // 2
-    first_half = grad_vals[..., :half_dim]
-    second_half = grad_vals[..., half_dim:]
-    return jnp.concatenate(
-        [first_half * cos_t + second_half * sin_t, second_half * cos_t - first_half * sin_t],
-        axis=-1,
-    )
-
-
-def rms_parts(rows):
-    factor = lax.rsqrt(jnp.mean(rows * rows, axis=-1, keepdims=True) + norm_eps)
-    return (rows * factor, factor)
-
-
-def score_block(query_blk, key_blk, doc_query, doc_key, query_pos, key_pos, score_scale):
-    scores = (
-        jnp.einsum("qhd,khd->hqk", query_blk, key_blk, preferred_element_type=jnp.float32)
-        * score_scale
-    )
-    allowed = (key_pos[None, :] <= query_pos[:, None]) & (doc_query[:, None] == doc_key[None, :])
-    return jnp.where(allowed[None], scores, masked_score)
-
-
-def attend_block(packed, query_pos, key_pos, score_scale):
-    query_blk, key_blk, value_blk, doc_query, doc_key = packed
-    scores = score_block(query_blk, key_blk, doc_query, doc_key, query_pos, key_pos, score_scale)
-    row_max = jnp.max(scores, axis=-1, keepdims=True)
-    exp_vals = jnp.exp(scores - row_max)
-    totals = jnp.sum(exp_vals, axis=-1, keepdims=True)
-    prob_vals = exp_vals / totals
-    head_vals = jnp.einsum(
-        "hqk,khd->qhd",
-        prob_vals.astype(jnp.bfloat16),
-        value_blk,
-        preferred_element_type=jnp.float32,
-    )
-    return (head_vals.astype(jnp.bfloat16), row_max + jnp.log(totals))
-
-
-def attend_back(packed, query_pos, key_pos, score_scale):
-    query_blk, key_blk, value_blk, grad_blk, lse_blk, doc_query, doc_key = packed
-    scores = score_block(query_blk, key_blk, doc_query, doc_key, query_pos, key_pos, score_scale)
-    prob_vals = jnp.exp(scores - lse_blk)
-    grad_value = jnp.einsum(
-        "hqk,qhd->khd", prob_vals.astype(jnp.bfloat16), grad_blk, preferred_element_type=jnp.float32
-    )
-    grad_prob = jnp.einsum("qhd,khd->hqk", grad_blk, value_blk, preferred_element_type=jnp.float32)
-    row_dot = jnp.sum(prob_vals * grad_prob, axis=-1, keepdims=True)
-    grad_score = (prob_vals * (grad_prob - row_dot)).astype(jnp.bfloat16)
-    grad_query = (
-        jnp.einsum("hqk,khd->qhd", grad_score, key_blk, preferred_element_type=jnp.float32)
-        * score_scale
-    )
-    grad_key = (
-        jnp.einsum("hqk,qhd->khd", grad_score, query_blk, preferred_element_type=jnp.float32)
-        * score_scale
-    )
-    return (grad_query, grad_key, grad_value)
 
 
 MESH = pl.DeviceIdType.MESH
@@ -925,6 +854,440 @@
     )(adapter, *blocks)
 
 
+def norm_back(grad, rows, factor, gain):
+    unit = rows * factor
+    weighted = grad * gain
+    inner = jnp.mean(weighted * unit, axis=-1, keepdims=True)
+    return factor * (weighted - unit * inner), jnp.sum(grad * unit, axis=0, keepdims=True)
+
+
+def ffn_back_kernel(sz, *refs):
+    (cot, mixed, gains, rows_hbm, gate_hbm, up_hbm, wg_hbm, wu_hbm, down_hbm) = refs[:9]
+    (grad_mixed, gain_grad, dgate_out, dup_out) = refs[9:13]
+    (rows_s, gate_s, up_s, wg, wu, wd, load, load_down, keep_sem) = refs[13:22]
+    scatter_refs = refs[22:]
+    place = Place(sz)
+    pairs = ((rows_hbm, rows_s), (gate_hbm, gate_s), (up_hbm, up_s), (wg_hbm, wg), (wu_hbm, wu))
+    loads = [
+        pltpu.make_async_copy(src, dst, load.at[i]) for i, (src, dst) in enumerate(pairs)
+    ]
+    down_loads = column_loads(down_hbm, wd, load_down)
+    loads[0].start()
+    for copy in down_loads + loads[1:]:
+        copy.start()
+    place.enter()
+    scatter = Scatter(place, *scatter_refs)
+    for copy in [loads[0]] + down_loads + loads[1:]:
+        copy.wait()
+
+    def work(q, j):
+        rows = place.tile(q, j)
+        dh = nt_dot(rows_s[rows, :], wd[...])
+        gate = gate_s[rows, :].astype(jnp.float32)
+        up = up_s[rows, :].astype(jnp.float32)
+        sig = 1.0 / (1.0 + jnp.exp(-gate))
+        dgate = (dh * up * sig * (1.0 + gate * (1.0 - sig))).astype(jnp.bfloat16)
+        dup = (dh * gate * sig).astype(jnp.bfloat16)
+        gate_s[rows, :] = dgate
+        up_s[rows, :] = dup
+        scatter.part[...] = nt_dot(dgate, wg[...]) + nt_dot(dup, wu[...])
+        scatter.give(q, j)
+
+    far = range(1, sz.half)
+    for j in range(sz.seqs):
+        for q in far:
+            work(q, j)
+        if j:
+            for q in far:
+                scatter.onward(q, j - 1)
+    work(0, 0)
+    for q in far:
+        scatter.onward(q, sz.seqs - 1)
+    for j in range(1, sz.seqs):
+        work(0, j)
+    copies = [
+        pltpu.make_async_copy(gate_s, dgate_out, keep_sem.at[0]),
+        pltpu.make_async_copy(up_s, dup_out, keep_sem.at[1]),
+    ]
+    for copy in copies:
+        copy.start()
+    gain_total = None
+    for j in range(sz.seqs):
+        span = slice(j * sz.block, (j + 1) * sz.block)
+        rows = mixed[span, :]
+        grad, gain_here = norm_back(scatter.total(j), rows, rms_factor(rows), gains[1:2, :])
+        grad_mixed[span, :] = cot[span, :].astype(jnp.float32) + grad
+        gain_total = gain_here if gain_total is None else gain_total + gain_here
+    gain_grad[...] = gain_total
+    scatter.finish()
+    for copy in copies:
+        copy.wait()
+
+
+def run_ffn_back(sz, cot, mixed, gains, rows, gate, up, wg, wu, down):
+    f32, bf16, shape = jnp.float32, jnp.bfloat16, jax.ShapeDtypeStruct
+    dma = pltpu.SemaphoreType.DMA
+    return pl.pallas_call(
+        partial(ffn_back_kernel, sz),
+        out_shape=[
+            shape((sz.rows, sz.width), f32),
+            shape((1, sz.width), f32),
+            shape((sz.seq_len, sz.ff), bf16),
+            shape((sz.seq_len, sz.ff), bf16),
+        ],
+        in_specs=[full_spec()] * 3 + [any_spec()] * 6,
+        out_specs=[full_spec()] * 2 + [any_spec()] * 2,
+        scratch_shapes=[
+            pltpu.VMEM((sz.seq_len, sz.width), bf16),
+            pltpu.VMEM((sz.seq_len, sz.ff), bf16),
+            pltpu.VMEM((sz.seq_len, sz.ff), bf16),
+            pltpu.VMEM(wg.shape, bf16),
+            pltpu.VMEM(wu.shape, bf16),
+            pltpu.VMEM((sz.ff, sz.width), bf16),
+            dma((5,)),
+            dma((down.shape[0],)),
+            dma((2,)),
+        ]
+        + Scatter.scratch(sz),
+        compiler_params=pltpu.CompilerParams(
+            collective_id=6, has_side_effects=True, vmem_limit_bytes=VMEM_BYTES
+        ),
+        cost_estimate=pl.CostEstimate(
+            flops=6 * sz.seq_len * sz.width * sz.ff, bytes_accessed=40 << 20, transcendentals=0
+        ),
+        name="ffn_back",
+    )(cot, mixed, gains, rows, gate, up, wg, wu, down)
+
+
+def attn_back_kernel(sz, *refs):
+    (grad_mixed, adapted, gains, cos_t, sin_t, begin) = refs[:6]
+    (q_hbm, k_hbm, v_hbm, lse_hbm, out_hbm, qkv_hbm) = refs[6:12]
+    (grad_low, gain_grad, rows_out, proj_out) = refs[12:16]
+    (rows_s, q_s, k_s, v_s, lse_s, do_s, dk_s, dv_s, proj_s, wout, wqkv) = refs[16:27]
+    (load, load_out, keep_sem) = refs[27:30]
+    gather_refs = refs[30:32]
+    scatter_refs = refs[32:]
+    place = Place(sz)
+    pairs = ((q_hbm, q_s), (k_hbm, k_s), (v_hbm, v_s), (lse_hbm, lse_s), (qkv_hbm, wqkv))
+    loads = [
+        pltpu.make_async_copy(src, dst, load.at[i]) for i, (src, dst) in enumerate(pairs)
+    ]
+    out_loads = column_loads(out_hbm, wout, load_out)
+    for copy in out_loads + loads:
+        copy.start()
+    place.enter()
+    gather = Gather(place, rows_s, *gather_refs)
+    scatter = Scatter(place, *scatter_refs)
+    for j in range(sz.seqs):
+        span = slice(j * sz.block, (j + 1) * sz.block)
+        rows_s[gather.own(j), :] = grad_mixed[span, :].astype(jnp.bfloat16)
+        gather.start(j)
+    for copy in out_loads:
+        copy.wait()
+    d = sz.head_dim
+
+    def heads_grad(q, j):
+        rows = place.tile(q, j)
+        dhead = nt_dot(rows_s[rows, :], wout[...]).astype(jnp.bfloat16)
+        for h in range(sz.heads):
+            do_s[h, rows, :] = dhead[:, h * d : (h + 1) * d]
+
+    far = range(1, sz.half)
+    for j in range(sz.seqs):
+        gather.wait_near(j)
+        heads_grad(0, j)
+    for copy in loads:
+        copy.wait()
+    for j in range(sz.seqs):
+        for q in far:
+            gather.forward(q, j)
+        for q in far:
+            gather.wait_far(sz.half - q, j)
+            heads_grad(q, j)
+    copies = [pltpu.make_async_copy(rows_s, rows_out, keep_sem.at[0])]
+    copies[0].start()
+
+    tiles = sz.n_tensor
+    scale = 1.0 / math.sqrt(d)
+
+    def head(h, carry):
+        for i in reversed(range(tiles)):
+            rows = slice(i * sz.tile, (i + 1) * sz.tile)
+            length = (i + 1) * sz.tile
+            keys, values = k_s[h, 0:length, :], v_s[h, 0:length, :]
+            query, grad = q_s[h, rows, :], do_s[h, rows, :]
+            start = begin[:, rows]
+            key_at = lax.broadcasted_iota(jnp.int32, (length, sz.tile), 0)
+            query_at = i * sz.tile + lax.broadcasted_iota(jnp.int32, (1, sz.tile), 1)
+            allowed = (key_at >= start) & (key_at <= query_at)
+            scores = nt_dot(keys, query)
+            scores = jnp.where(allowed, scores * (LOG2E * scale), masked_score)
+            probs = jnp.exp2(scores - lse_s[h, :, rows])
+            dprobs = nt_dot(values, grad)
+            inner = jnp.sum(probs * dprobs, axis=0, keepdims=True)
+            dscores = (probs * (dprobs - inner)).astype(jnp.bfloat16)
+            dv = nn_dot(probs.astype(jnp.bfloat16), grad)
+            dk = nn_dot(dscores, query)
+            if i == tiles - 1:
+                dv_s[...] = dv
+                dk_s[...] = dk
+            else:
+                dv_s[0:length, :] += dv
+                dk_s[0:length, :] += dk
+            dq = jnp.transpose(tn_dot(keys, dscores)) * scale
+            cos_here, sin_here = cos_t[rows, :], sin_t[rows, :]
+            proj_s[rows, pl.ds(pl.multiple_of(h * 3 * d, d), d)] = turn(
+                dq, cos_here, -sin_here
+            ).astype(jnp.bfloat16)
+        dk = turn(dk_s[...] * scale, cos_t[...], -sin_t[...])
+        proj_s[:, pl.ds(pl.multiple_of(h * 3 * d + d, d), d)] = dk.astype(jnp.bfloat16)
+        proj_s[:, pl.ds(pl.multiple_of(h * 3 * d + 2 * d, d), d)] = dv_s[...].astype(jnp.bfloat16)
+        return carry
+
+    lax.fori_loop(0, sz.heads, head, 0)
+    copies.append(pltpu.make_async_copy(proj_s, proj_out, keep_sem.at[1]))
+    copies[1].start()
+
+    def give(q, j):
+        scatter.part[...] = nt_dot(proj_s[place.tile(q, j), :], wqkv[...])
+        scatter.give(q, j)
+
+    for j in range(sz.seqs):
+        for q in far:
+            give(q, j)
+        if j:
+            for q in far:
+                scatter.onward(q, j - 1)
+    give(0, 0)
+    for q in far:
+        scatter.onward(q, sz.seqs - 1)
+    for j in range(1, sz.seqs):
+        give(0, j)
+    gather.finish()
+    gain_total = None
+    for j in range(sz.seqs):
+        span = slice(j * sz.block, (j + 1) * sz.block)
+        rows = adapted[span, :]
+        grad, gain_here = norm_back(scatter.total(j), rows, rms_factor(rows), gains[0:1, :])
+        grad_low[span, :] = (grad_mixed[span, :] + grad).astype(jnp.bfloat16)
+        gain_total = gain_here if gain_total is None else gain_total + gain_here
+    gain_grad[...] = gain_total
+    scatter.finish()
+    for copy in copies:
+        copy.wait()
+
+
+def run_attn_back(sz, grad_mixed, adapted, gains, cos_t, sin_t, begin, q, k, v, lse, out, qkv):
+    f32, bf16, shape = jnp.float32, jnp.bfloat16, jax.ShapeDtypeStruct
+    dma = pltpu.SemaphoreType.DMA
+    heads_shape = (sz.heads, sz.seq_len, sz.head_dim)
+    return pl.pallas_call(
+        partial(attn_back_kernel, sz),
+        out_shape=[
+            shape((sz.rows, sz.width), bf16),
+            shape((1, sz.width), f32),
+            shape((sz.seq_len, sz.width), bf16),
+            shape((sz.seq_len, qkv.shape[1]), bf16),
+        ],
+        in_specs=[full_spec()] * 6 + [any_spec()] * 6,
+        out_specs=[full_spec()] * 2 + [any_spec()] * 2,
+        scratch_shapes=[
+            pltpu.VMEM((sz.seq_len, sz.width), bf16),
+            pltpu.VMEM(heads_shape, bf16),
+            pltpu.VMEM(heads_shape, bf16),
+            pltpu.VMEM(heads_shape, bf16),
+            pltpu.VMEM((sz.heads, 1, sz.seq_len), f32),
+            pltpu.VMEM(heads_shape, bf16),
+            pltpu.VMEM((sz.seq_len, sz.head_dim), f32),
+            pltpu.VMEM((sz.seq_len, sz.head_dim), f32),
+            pltpu.VMEM((sz.seq_len, qkv.shape[1]), bf16),
+            pltpu.VMEM((sz.heads * sz.head_dim, sz.width), bf16),
+            pltpu.VMEM(qkv.shape, bf16),
+            dma((5,)),
+            dma((out.shape[0],)),
+            dma((2,)),
+        ]
+        + Gather.scratch(sz)
+        + Scatter.scratch(sz),
+        compiler_params=pltpu.CompilerParams(
+            collective_id=7, has_side_effects=True, vmem_limit_bytes=VMEM_BYTES
+        ),
+        cost_estimate=pl.CostEstimate(
+            flops=4 * sz.seq_len * sz.width * qkv.shape[1], bytes_accessed=30 << 20, transcendentals=0
+        ),
+        name="attn_back",
+    )(grad_mixed, adapted, gains, cos_t, sin_t, begin, q, k, v, lse, out, qkv)
+
+
+def grads_kernel(sz, n_dp, count, *refs):
+    xs, ys, outs = refs[:count], refs[count : 2 * count], refs[2 * count : 3 * count]
+    refs = refs[3 * count :]
+    y_s, first, held, landed = (refs[i * count : (i + 1) * count] for i in range(4))
+    (x_s, load_y, load_x, ring_send, ring_recv, move_send, move_recv, own_sem) = refs[4 * count :]
+    place = Place(sz)
+    ring = Ring(place, n_dp)
+    t = lax.axis_index("tensor")
+    ctx, part, half, n_c = place.ctx, place.part, sz.half, sz.n_context
+    role = part * n_c + ctx
+    at_home = role == t
+    depth = x_s.shape[3]
+
+    y_loads = [pltpu.make_async_copy(ys[w], y_s[w], load_y.at[w]) for w in range(count)]
+    for copy in y_loads:
+        copy.start()
+
+    tasks = []
+    for k in range(count + n_dp):
+        for s in range(min(k, n_dp - 1), -1, -1):
+            if k - s < count:
+                tasks.append((k - s, s))
+
+    def slot(way, s):
+        return ring.index(-(s + 1) if way == 0 else s + 1) * n_c + way
+
+    def x_load(k, way):
+        w, s = tasks[k]
+        if xs[w].shape[0] == 1:
+            at = pl.multiple_of(slot(way, s) * depth, depth)
+            src = xs[w].at[0, :, pl.ds(at, depth)]
+        else:
+            src = xs[w].at[slot(way, s)]
+        return pltpu.make_async_copy(src, x_s.at[k % 2, way], load_x.at[k % 2, way])
+
+    for way in range(n_c):
+        x_load(0, way).start()
+
+    barrier = pltpu.get_barrier_semaphore()
+
+    def greet(device):
+        pl.semaphore_signal(barrier, inc=1, device_id=device, device_id_type=MESH)
+
+    def holder(g):
+        return (place.dp, g * half + t // n_c, lax.rem(t, n_c))
+
+    greet(ring.device(1))
+    greet(ring.device(n_dp - 1))
+    for g in range(sz.seqs):
+        pl.when(jnp.logical_not(at_home & (place.group == g)))(lambda g=g: greet(holder(g)))
+    pl.semaphore_wait(barrier, 2 + n_c - jnp.where(at_home, 1, 0))
+
+    def source(w, way, s):
+        return first[w].at[way] if s == 0 else held[w].at[way, s - 1]
+
+    def hop(w, way, s):
+        return pltpu.make_async_remote_copy(
+            src_ref=source(w, way, s),
+            dst_ref=held[w].at[way, s],
+            send_sem=ring_send.at[w, way, s],
+            recv_sem=ring_recv.at[w, way, s],
+            device_id=ring.device(1 if way == 0 else n_dp - 1),
+            device_id_type=MESH,
+        )
+
+    def deliver(w, way):
+        return pltpu.make_async_remote_copy(
+            src_ref=source(w, way, n_dp - 1),
+            dst_ref=landed[w].at[place.group],
+            send_sem=move_send.at[w, way],
+            recv_sem=move_recv.at[w, place.group],
+            device_id=(place.dp, role, way),
+            device_id_type=MESH,
+        )
+
+    def stay(w, way):
+        return pltpu.make_async_copy(
+            source(w, way, n_dp - 1), landed[w].at[place.group], own_sem.at[w]
+        )
+
+    def arrived(w, g):
+        arrival = pltpu.make_async_remote_copy(
+            src_ref=landed[w].at[g],
+            dst_ref=landed[w].at[g],
+            send_sem=move_send.at[w, 0],
+            recv_sem=move_recv.at[w, g],
+            device_id=(place.dp, t, 1 - ctx),
+            device_id_type=MESH,
+        )
+        here = at_home & (place.group == g)
+        pl.when(here)(lambda: stay(w, 0).wait())
+        pl.when(jnp.logical_not(here))(lambda: arrival.wait_recv())
+
+    waited = set()
+    for k, (w, s) in enumerate(tasks):
+        if k + 1 < len(tasks):
+            for way in range(n_c):
+                x_load(k + 1, way).start()
+        if w not in waited:
+            y_loads[w].wait()
+            waited.add(w)
+        for way in range(n_c):
+            x_load(k, way).wait()
+            value = tn_dot(x_s[k % 2, way], y_s[w][...])
+            if s:
+                hop(w, way, s - 1).wait_recv()
+                value = value + held[w][way, s - 1].astype(jnp.float32)
+            ref = source(w, way, s)
+            ref[...] = value.astype(jnp.bfloat16)
+            if s < n_dp - 1:
+                hop(w, way, s).start()
+            else:
+                here = at_home & (ctx == way)
+                pl.when(here)(lambda w=w, way=way: stay(w, way).start())
+                pl.when(jnp.logical_not(here))(lambda w=w, way=way: deliver(w, way).start())
+    for w in range(count):
+        for g in range(sz.seqs):
+            arrived(w, g)
+        total = landed[w][0].astype(jnp.float32)
+        for g in range(1, sz.seqs):
+            total = total + landed[w][g].astype(jnp.float32)
+        outs[w][...] = total
+    for w in range(count):
+        for way in range(n_c):
+            for s in range(n_dp - 1):
+                hop(w, way, s).wait_send()
+            here = at_home & (ctx == way)
+            pl.when(jnp.logical_not(here))(lambda w=w, way=way: deliver(w, way).wait_send())
+
+
+def run_grads(sz, n_dp, xs, ys):
+    bf16, count, dma = jnp.bfloat16, len(xs), pltpu.SemaphoreType.DMA
+    slots = n_dp * sz.n_context
+    depth = sz.width // slots
+    if depth % 128:
+        xs = [x.reshape(sz.seq_len, slots, depth).transpose(1, 0, 2) for x in xs]
+    else:
+        xs = [x[None] for x in xs]
+    wide = [y.shape[1] for y in ys]
+    ways, steps = sz.n_context, n_dp - 1
+    return pl.pallas_call(
+        partial(grads_kernel, sz, n_dp, count),
+        out_shape=[jax.ShapeDtypeStruct((depth, n), jnp.float32) for n in wide],
+        in_specs=[any_spec()] * (2 * count),
+        out_specs=[full_spec()] * count,
+        scratch_shapes=[pltpu.VMEM((sz.seq_len, n), bf16) for n in wide]
+        + [pltpu.VMEM((ways, depth, n), bf16) for n in wide]
+        + [pltpu.VMEM((ways, steps, depth, n), bf16) for n in wide]
+        + [pltpu.VMEM((sz.seqs, depth, n), bf16) for n in wide]
+        + [
+            pltpu.VMEM((2, ways, sz.seq_len, depth), bf16),
+            dma((count,)),
+            dma((2, ways)),
+            dma((count, ways, steps)),
+            dma((count, ways, steps)),
+            dma((count, ways)),
+            dma((count, sz.seqs)),
+            dma((count,)),
+        ],
+        compiler_params=pltpu.CompilerParams(
+            collective_id=8, has_side_effects=True, vmem_limit_bytes=VMEM_BYTES
+        ),
+        cost_estimate=pl.CostEstimate(
+            flops=2 * sz.seq_len * sz.width * sum(wide), bytes_accessed=60 << 20, transcendentals=0
+        ),
+        name="grads",
+    )(*xs, *ys)
+
+
 def shards(
     embedded,
     initial_state,
@@ -952,7 +1315,6 @@
     heads_here = qkv_weight.shape[1]
     head_dim = qkv_weight.shape[2] // 3
     ff_here = down_weight.shape[0]
-    score_scale = 1.0 / math.sqrt(head_dim)
     pair_swap = [(i, (i + half) % n_tensor) for i in range(n_tensor)]
     members = half * n_context
     groups = [
@@ -976,17 +1338,6 @@
             [jnp.where(group == 0, own, got), jnp.where(group == 0, got, own)], axis=0
         )
 
-    def role_perm(flip):
-        pairs = []
-        for t in range(n_tensor):
-            for c in range(n_context):
-                g = (c + flip) % n_context
-                dest = (g * half + t // n_context) * n_context + t % n_context
-                pairs.append((t * n_context + c, dest))
-        return pairs
-
-    role_perms = [role_perm(0), role_perm(1)]
-
     def side_by_side(blocks):
         count, depth, columns = blocks.shape
         return blocks.transpose(1, 0, 2).reshape(depth, count * columns)
@@ -1009,18 +1360,6 @@
         )
         split = full.reshape(half, n_context, seq_count, block_rows, model_width)
         return split.transpose(2, 0, 1, 3, 4).reshape(seq_len, model_width)
-
-    def sum_rows(partial_rows):
-        split = partial_rows.astype(jnp.bfloat16).reshape(
-            seq_count, half, n_context, block_rows, model_width
-        )
-        return lax.psum_scatter(
-            split.transpose(1, 2, 0, 3, 4).reshape(seq_len, model_width),
-            ("tensor", "context"),
-            scatter_dimension=0,
-            tiled=True,
-            axis_index_groups=groups,
-        ).astype(jnp.float32)
 
     embed_rows = swap_in(embedded)
     state_rows = swap_in(initial_state)
@@ -1076,19 +1415,15 @@
     adapter_low = adapter_all[adapter_all.shape[0] // 2 :, :adapter_block].reshape(
         model_width, model_width
     )
-    out_use = side_by_side(out_blocks)
-    down_use = side_by_side(down_blocks)
     if out_blocks.shape[2] % 128:
-        out_blocks = out_use[None]
-        down_blocks = down_use[None]
+        out_blocks = side_by_side(out_blocks)[None]
+        down_blocks = side_by_side(down_blocks)[None]
     gains_f = gains_full.astype(jnp.float32)
 
     order = jnp.arange(seq_len, dtype=jnp.int32)
     cos_t, sin_t = rope_angles(order, head_dim)
     cos_full = jnp.concatenate([cos_t, cos_t], axis=1)
     sin_full = jnp.concatenate([-sin_t, sin_t], axis=1)
-    cos_t = cos_t[:, None, :]
-    sin_t = sin_t[:, None, :]
     own_seq = dp_index * seq_count + group
     docs = lax.dynamic_index_in_dim(doc_ids, own_seq, 0, keepdims=False)
     begin = jnp.sum((docs[None, :] < docs[:, None]).astype(jnp.int32), axis=1)[None, :]
@@ -1119,68 +1454,24 @@
         sz, True, mixed_rows, detached, gains_f[:1], gains_f, gate_use, up_use, down_blocks
     )
     latent_low = detached.astype(jnp.bfloat16)
-    query_rot = query_hm.transpose(1, 0, 2)
-    key_rot = key_hm.transpose(1, 0, 2)
-    value_rows = value_hm.transpose(1, 0, 2)
-    head_vals = head_flat.reshape(seq_len, heads_here, head_dim)
-    lse_vals = lse.transpose(0, 2, 1) * math.log(2.0)
-    gate_pre = gate_pre.astype(jnp.float32)
-    up_pre = up_pre.astype(jnp.float32)
-    gate_up_use = jnp.stack([gate_use, up_use], axis=1)
-    out_use = out_use.reshape(heads_here, head_dim, model_width)
-    qkv_use = qkv_use.reshape(model_width, heads_here, 3 * head_dim)
-    grad_out = cot_rows.astype(jnp.float32)
     grad_ffn = gather_rows(cot_rows)
-    down_g = jnp.einsum("qf,qd->fd", hidden, grad_ffn, preferred_element_type=jnp.float32)
-    grad_hidden = jnp.einsum("qd,fd->qf", grad_ffn, down_use, preferred_element_type=jnp.float32)
-    sig = jax.nn.sigmoid(gate_pre)
-    grad_gate = grad_hidden * up_pre * sig * (1.0 + gate_pre * (1.0 - sig))
-    grad_up = grad_hidden * jax.nn.silu(gate_pre)
-    grad_pair = jnp.stack([grad_gate, grad_up], axis=1).astype(jnp.bfloat16)
-    gate_up_g = jnp.einsum(
-        "qd,qgf->dgf", ffn_input, grad_pair, preferred_element_type=jnp.float32
-    )
-    grad_normb = sum_rows(
-        jnp.einsum("qgf,dgf->qd", grad_pair, gate_up_use, preferred_element_type=jnp.float32)
-    )
-    unit_b, factor_b = rms_parts(mixed_rows)
-    weighted_b = grad_normb * gains_f[1]
-    gain_b = jnp.sum(grad_normb * unit_b, axis=0)
-    grad_mixed = grad_out + factor_b * (
-        weighted_b - unit_b * jnp.mean(weighted_b * unit_b, axis=-1, keepdims=True)
-    )
-    grad_heads = gather_rows(grad_mixed.astype(jnp.bfloat16))
-    out_g = jnp.einsum("qhd,qm->hdm", head_vals, grad_heads, preferred_element_type=jnp.float32)
-    grad_head_vals = jnp.einsum(
-        "qm,hdm->qhd", grad_heads, out_use, preferred_element_type=jnp.float32
-    ).astype(jnp.bfloat16)
-    grad_query, grad_key, grad_value = attend_back(
-        (query_rot, key_rot, value_rows, grad_head_vals, lse_vals, docs, docs),
-        order,
-        order,
-        score_scale,
-    )
-    grad_proj = jnp.concatenate(
-        [
-            rotate_back(grad_query, cos_t, sin_t),
-            rotate_back(grad_key, cos_t, sin_t),
-            grad_value,
-        ],
-        axis=-1,
-    ).astype(jnp.bfloat16)
-    qkv_g = jnp.einsum(
-        "xq,xtu->qtu", feature_rows, grad_proj, preferred_element_type=jnp.float32
-    )
-    grad_norma = sum_rows(
-        jnp.einsum("aew,iew->ai", grad_proj, qkv_use, preferred_element_type=jnp.float32)
-    )
-    unit_a, factor_a = rms_parts(adapted)
-    weighted_a = grad_norma * gains_f[0]
-    gain_a = jnp.sum(grad_norma * unit_a, axis=0)
-    grad_adapted = grad_mixed + factor_a * (
-        weighted_a - unit_a * jnp.mean(weighted_a * unit_a, axis=-1, keepdims=True)
-    )
-    adapted_low = grad_adapted.astype(jnp.bfloat16)
+    grad_mixed, gain_b, grad_gate, grad_up = run_ffn_back(
+        sz, cot_rows, mixed_rows, gains_f, grad_ffn, gate_pre, up_pre, gate_use, up_use, down_blocks
+    )
+    adapted_low, gain_a, grad_rows, grad_proj = run_attn_back(
+        sz, grad_mixed, adapted, gains_f, cos_full, sin_full, begin,
+        query_hm, key_hm, value_hm, lse, out_blocks, qkv_use,
+    )
+    down_t, gate_s, up_s, qkv_s, out_t = run_grads(
+        sz,
+        n_dp,
+        [grad_ffn, ffn_input, ffn_input, feature_rows, grad_rows],
+        [hidden, grad_gate, grad_up, grad_proj, head_flat],
+    )
+    down_s = down_t.T
+    out_s = out_t.T.reshape(heads_here, head_dim, -1)
+    qkv_s = qkv_s.reshape(-1, heads_here, 3 * head_dim)
+    gate_up_s = jnp.stack([gate_s, up_s], axis=1)
     joined = jnp.concatenate([latent_low, embed_rows], axis=-1)
     adapter_g = jnp.einsum("rk,rd->kd", joined, adapted_low, preferred_element_type=jnp.float32)
     embed_out = jnp.einsum(
@@ -1189,15 +1480,11 @@
         adapter_low,
         preferred_element_type=jnp.float32,
     )
-    down_s = role_grad(down_g, 1)
-    gate_up_s = role_grad(gate_up_g, 0)
-    out_s = role_grad(out_g, 2)
-    qkv_s = role_grad(qkv_g, 0)
     adapter_s = lax.psum_scatter(
         adapter_g.astype(jnp.bfloat16), ("dp", "context"), scatter_dimension=0, tiled=True
     )
     gains_s = lax.psum_scatter(
-        jnp.stack([gain_a, gain_b]).astype(jnp.bfloat16),
+        jnp.concatenate([gain_a, gain_b]).astype(jnp.bfloat16),
         ("dp", "context"),
         scatter_dimension=1,
         tiled=True,

time: 1660 us -> 1400 us (0.84)
  waiting for transfers between devices: 521 us -> 109 us
  Pallas kernels: 748 us -> 1130 us
  matrix products: 143 us -> 26.8 us
  other arithmetic: 63.9 us -> 24.2 us
  local copies, waits for them, and re-layouts: 87.3 us -> 49 us
  starting transfers between devices: 38.3 us -> 8.43 us
    pallas_call x0 -> x3, Pallas kernels: none -> 380 us  [the longest x1 259 us: run_grads(): pl.pallas_call(partial(grads_kernel, sz, n_dp, count), out_shape=[jax.Sha...]
    reduce_scatter x6 -> x0, waiting for transfers between devices: 268 us -> none  [the longest x4 224 us: role_grad(): lax.psum_scatter(grad.astype(jnp.bfloat16), 'dp', scatter_dimension=axis,...]
    dot_general x13 -> x0, matrix products: 118 us -> none  [the longest x1 18.4 us: shards(): jnp.einsum('qd,qgf->dgf', ffn_input, grad_pair, preferred_element_type=jn...]
    psum x1, waiting for transfers between devices: 54.6 us -> 0.01 us  [shards(): adapter_s = lax.psum(adapter_s, 'tensor').astype(jnp.float32)]
    reduce_scatter x1, waiting for transfers between devices: 109 us -> 63.3 us  [shards(): lax.psum_scatter(adapter_g.astype(jnp.bfloat16), ('dp', 'context'), scatt...]
    ppermute x2, waiting for transfers between devices: 3.75 us -> 45.5 us  [swap_out(): got = lax.ppermute(other, 'tensor', pair_swap)]
    ppermute x8 -> x0, waiting for transfers between devices: 33.8 us -> none  [role_grad(): lax.ppermute(g, ('tensor', 'context'), [(b, a) for a, b in perm])]
    unnamed x12 -> x5, waiting for transfers between devices: 30.4 us -> 0.07 us
  transfers between devices with their start and end apart: 24 -> 9, of which waited for: 14 -> 2; matrix products, arithmetic and copies ran while one was open for 11% -> 5% of each run, Pallas kernels for 45% -> 72%
where the time goes in v4:
time: 1400 us
  Pallas kernels  1130 us (81%)
  waiting for transfers between devices  109 us (8%)
  local copies, waits for them, and re-layouts  49 us (4%)
  matrix products  26.8 us (2%)
  loops' own time  26.5 us (2%)
  other arithmetic  24.2 us (2%)
  between operations  15.7 us (1%)
    pallas_call x1, Pallas kernels, run_weights(): pl.pallas_call(partial(weights_kernel, sz, n_dp), out_shape=outs, in_spec...  277 us
    pallas_call x4, Pallas kernels, run_attn(): pl.pallas_call(partial(attn_kernel, sz, keep), out_shape=outs, in_specs=[...  262 us
    pallas_call x1, Pallas kernels, run_grads(): pl.pallas_call(partial(grads_kernel, sz, n_dp, count), out_shape=[jax.Sha...  259 us
    pallas_call x4, Pallas kernels, run_ffn(): pl.pallas_call(partial(ffn_kernel, sz, keep), out_shape=outs, in_specs=[f...  211 us
    pallas_call x1, Pallas kernels, run_attn_back(): pl.pallas_call(partial(attn_back_kernel, sz), out_shape=[shape((sz.rows,...  74.2 us
    reduce_scatter x1, waiting for transfers between devices, shards(): lax.psum_scatter(adapter_g.astype(jnp.bfloat16), ('dp', 'context'), scatt...  63.3 us
    pallas_call x1, Pallas kernels, run_ffn_back(): pl.pallas_call(partial(ffn_back_kernel, sz), out_shape=[shape((sz.rows, s...  46.9 us
    ppermute x2, waiting for transfers between devices, swap_out(): got = lax.ppermute(other, 'tensor', pair_swap)  45.5 us
  transfers between devices with their start and end apart: 9, of which 2 were waited for; matrix products, arithmetic and copies ran while one was open for 5% of the time, Pallas kernels for 72%

profile of v4, /device:TPU:1, one launch (start us, length us, event | category | flops | bytes accessed | tf_op | source)
XLA Modules:
  0.0 1395.2 jit_solution(1308861091292299961)
XLA Ops:
  23.4 276.6 %weights.1 = (bf16[8,544,2048]{2,1,0:T(8,128)(2,1)}, bf16[8,256,1536]{2,1,0:T(8,128)(2,1)}, bf16[8,512,256]{2,1,0:T(8,128)(2,1)}, bf16[8,256,1408]{2,1,0:T(8,128...) custom-call(bf16[544,2048]{1,0:T(8,128)(2,1)} %fusion.1.refs_0_, bf16[256,1536]{1,0:T(8,128)(2,1)} %bitcast.69, ...), custom_call_target="tpu_custom_call" | custom-call | tf_op jit(solution)/shard_map/weights/pallas_call | solution.py:836
  300.8 8.3 slice.32
  321.7 7.4 fusion.7.refs_1_
  329.1 397.8 %while.10 = (s32[]{:T(128)}, f32[256,2048]{1,0:T(8,128)}, s32[]{:T(128)}, f32[256,2048]{1,0:T(8,128)}, f32[2,2048]{1,0:T(2,128)S(1)}, /*index=5*/f32[1024,128]{1...) while((s32[]{:T(128)}, f32[256,2048]{1,0:T(8,128)}, ...), condition=%wide.region_3.4_spmd, body=%wide.region_2.3_spmd.sunk | while | flops 26306674688 | bytes 46145708 | solution.py:1446
  350.3 3.4 copy.55.refs_0_.refs_1_
  354.2 83.9 %attn_round.1.refs_0_ = f32[256,2048]{1,0:T(8,128)} custom-call(f32[256,2048]{1,0:T(8,128)} %copy.55.refs_0_.refs_1_, f32[256,2048]{1,0:T(8,128)} %get-tuple-element.353.refs_1_, f32[2,2048]{1,0:T(2,128)S(1)} %get-tuple-element.354.refs_2_.refs_3_, f32[1024,128]{1,0:T(8,128)S(1)} %get-tuple-element.355.refs_3_, f32[1024,128]{1,0:T(8,128)S(1)} %get-tuple-element.356.refs_4_, ...), custom_call_target="tpu_custom_call" | custom-call | flops 8589934592 | bytes 20971520 | tf_op jit(solution)/shard_map/while/body/attn_round/pallas_call | solution.py:452
  438.2 52.9 %ffn_round.1 = f32[256,2048]{1,0:T(8,128)} custom-call(f32[256,2048]{1,0:T(8,128)} %attn_round.1.refs_0_, f32[256,2048]{1,0:T(8,128)} %copy.55.refs_0_.refs_1_, f32[1,2048]{1,0:T(1,128)} %broadcast_in_dim.25.refs_2_, f32[2,2048]{1,0:T(2,128)S(1)} %get-tuple-element.354.refs_2_.refs_3_, bf16[2048,1408]{1,0:T(8,128)(2,1)} %get-tuple-element.362.refs_4_, ...), custom_call_target="tpu_custom_call" | custom-call | flops 17716740096 | bytes 20971520 | tf_op jit(solution)/shard_map/while/body/ffn_round/pallas_call | solution.py:579
  494.9 59.0 %attn_round.1.refs_0_ = f32[256,2048]{1,0:T(8,128)} custom-call(f32[256,2048]{1,0:T(8,128)} %copy.55.refs_0_.refs_1_, f32[256,2048]{1,0:T(8,128)} %get-tuple-element.353.refs_1_, f32[2,2048]{1,0:T(2,128)S(1)} %get-tuple-element.354.refs_2_.refs_3_, f32[1024,128]{1,0:T(8,128)S(1)} %get-tuple-element.355.refs_3_, f32[1024,128]{1,0:T(8,128)S(1)} %get-tuple-element.356.refs_4_, ...), custom_call_target="tpu_custom_call" | custom-call | flops 8589934592 | bytes 20971520 | tf_op jit(solution)/shard_map/while/body/attn_round/pallas_call | solution.py:452
  553.9 52.1 %ffn_round.1 = f32[256,2048]{1,0:T(8,128)} custom-call(f32[256,2048]{1,0:T(8,128)} %attn_round.1.refs_0_, f32[256,2048]{1,0:T(8,128)} %copy.55.refs_0_.refs_1_, f32[1,2048]{1,0:T(1,128)} %broadcast_in_dim.25.refs_2_, f32[2,2048]{1,0:T(2,128)S(1)} %get-tuple-element.354.refs_2_.refs_3_, bf16[2048,1408]{1,0:T(8,128)(2,1)} %get-tuple-element.362.refs_4_, ...), custom_call_target="tpu_custom_call" | custom-call | flops 17716740096 | bytes 20971520 | tf_op jit(solution)/shard_map/while/body/ffn_round/pallas_call | solution.py:579
  609.7 59.0 %attn_round.1.refs_0_ = f32[256,2048]{1,0:T(8,128)} custom-call(f32[256,2048]{1,0:T(8,128)} %copy.55.refs_0_.refs_1_, f32[256,2048]{1,0:T(8,128)} %get-tuple-element.353.refs_1_, f32[2,2048]{1,0:T(2,128)S(1)} %get-tuple-element.354.refs_2_.refs_3_, f32[1024,128]{1,0:T(8,128)S(1)} %get-tuple-element.355.refs_3_, f32[1024,128]{1,0:T(8,128)S(1)} %get-tuple-element.356.refs_4_, ...), custom_call_target="tpu_custom_call" | custom-call | flops 8589934592 | bytes 20971520 | tf_op jit(solution)/shard_map/while/body/attn_round/pallas_call | solution.py:452
  668.8 52.9 %ffn_round.1 = f32[256,2048]{1,0:T(8,128)} custom-call(f32[256,2048]{1,0:T(8,128)} %attn_round.1.refs_0_, f32[256,2048]{1,0:T(8,128)} %copy.55.refs_0_.refs_1_, f32[1,2048]{1,0:T(1,128)} %broadcast_in_dim.25.refs_2_, f32[2,2048]{1,0:T(2,128)S(1)} %get-tuple-element.354.refs_2_.refs_3_, bf16[2048,1408]{1,0:T(8,128)(2,1)} %get-tuple-element.362.refs_4_, ...), custom_call_target="tpu_custom_call" | custom-call | flops 17716740096 | bytes 20971520 | tf_op jit(solution)/shard_map/while/body/ffn_round/pallas_call | solution.py:579
  729.7 59.7 %attn_keep.1 = (f32[256,2048]{1,0:T(8,128)}, f32[256,2048]{1,0:T(8,128)}, bf16[1024,2048]{1,0:T(8,128)(2,1)}, bf16[4,1024,128]{2,1,0:T(8,128)(2,1)}, bf16[4,1024...) custom-call(f32[256,2048]{1,0:T(8,128)} %get-tuple-element.124.refs_0_.re, ...), custom_call_target="tpu_custom_call" | custom-call | flops 8589934592 | bytes 20971520 | tf_op jit(solution)/shard_map/attn_keep/pallas_call | solution.py:452
  789.3 52.6 %ffn_keep.1 = (f32[256,2048]{1,0:T(8,128)}, bf16[1024,2048]{1,0:T(8,128)(2,1)}, bf16[1024,1408]{1,0:T(8,128)(2,1)}, bf16[1024,1408]{1,0:T(8,128)(2,1)}, bf16[1024,1408]{1,0:T(8,128)(2,1)}) custom-call(f32[256,2048]{1,0:T(8,128)} %get-tuple-element.125.refs_0_.refs_1_, f32[256,2048]{1,0:T(8,128)} %get-tuple-element.124.refs_0_.refs_1_, f32[1,2048]{1,0:T(1,128)} %bitcast.82, ...), custom_call_target="tpu_custom_call" | custom-call | flops 17716740096 | bytes 20971520 | tf_op jit(solution)/shard_map/ffn_keep/pallas_call | solution.py:579
  842.0 4.8 copy.33
  846.8 46.9 %ffn_back.1 = (f32[256,2048]{1,0:T(8,128)}, f32[1,2048]{1,0:T(1,128)}, bf16[1024,1408]{1,0:T(8,128)(2,1)}, bf16[1024,1408]{1,0:T(8,128)(2,1)}) custom-call(bf16[256,2048]{1,0:T(8,128)(2,1)} %pad_maximum_fusion.2.refs_0_, f32[256,2048]{1,0:T(8,128)} %get-tuple-element.125.refs_0_.refs_1_, f32[2,2048]{1,0:T(2,128)S(1)} %get-tuple-element.389, ...), custom_call_target="tpu_custom_call" | custom-call | flops 17716740096 | bytes 41943040 | tf_op jit(solution)/shard_map/ffn_back/pallas_call | solution.py:930
  893.7 74.2 %attn_back.1 = (bf16[256,2048]{1,0:T(8,128)(2,1)}, f32[1,2048]{1,0:T(1,128)}, bf16[1024,2048]{1,0:T(8,128)(2,1)}, bf16[1024,1536]{1,0:T(8,128)(2,1)}) custom-call(f32[256,2048]{1,0:T(8,128)} %get-tuple-element.129.refs_0_, f32[256,2048]{1,0:T(8,128)} %get-tuple-element.130.refs_1_, f32[2,2048]{1,0:T(2,128)S(1)} %get-tuple-element.389, ...), custom_call_target="tpu_custom_call" | custom-call | flops 12884901888 | bytes 31457280 | tf_op jit(solution)/shard_map/attn_back/pallas_call | solution.py:1084
  967.9 12.3 convolution_convert_fusion
  984.7 45.5 %collective-permute-done.2 = f32[128,2048]{1,0:T(8,128)S(1)} collective-permute-done((f32[128,2048]{1,0:T(8,128)S(1)}, f32[128,2048]{1,0:T(8,128)S(1)}, u32[]{:S(2)}, u32[]{:S(2)}) %collective-permute-start.2) | collective-permute-done | bytes 1048608 | tf_op jit(solution)/shard_map/ppermute | solution.py:1336
  1033.3 63.3 %reduce-scatter.5.cloned.1.call-done = bf16[512,2048]{1,0:T(8,128)(2,1)} async-done(((bf16[4096,2048]{1,0:T(8,128)(2,1)}), bf16[512,2048]{1,0:T(8,128)(2,1)}) %reduce-scatter.5.cloned.1.call-update) | async-done | bytes 2097168 | tf_op jit(solution)/shard_map/reduce_scatter | solution.py:1483
  1096.6 259.1 %grads.1 = (f32[256,1408]{1,0:T(8,128)}, f32[256,1408]{1,0:T(8,128)}, f32[256,1408]{1,0:T(8,128)}, f32[256,1536]{1,0:T(8,128)}, f32[256,512]{1,0:T(8,128)}) custom-call(bf16[1,1024,2048]{2,1,0:T(8,128)(2,1)} %bitcast.67, bf16[1,1024,2048]{2,1,0:T(8,128)(2,1)} %bitcast.86, bf16[1,1024,2048]{2,1,0:T(8,128)(2,1)} %bitcast.87, bf16[1,1024,2048]{2,1,0:T(8,128)(2,1)} %bitcast.85, ...), custom_call_target="tpu_custom_call" | custom-call | flops 26306674688 | bytes 62914560 | tf_op jit(solution)/shard_map/grads/pallas_call | solution.py:1262
  1364.1 3.8 copy.35
  1368.8 6.6 psum.15
  1377.2 7.1 fusion.11
  1384.3 4.1 convert_element_type.52
  (101 shorter events, 57.4 us)
Async XLA Ops:
  7.2 303.8 %copy-start = (s32[8,1024]{1,0:T(8,128)S(1)}, s32[8,1024]{1,0:T(8,128)}, u32[]{:S(2)}) copy-start(s32[8,1024]{1,0:T(8,128)} %param.16) | copy-start | bytes 98308
  7.2 7.2 copy-start.12
  7.2 10.3 copy-start.14
  7.2 834.8 %all-gather.2.cloned.1.call-start = ((), (), s32[]{:S(2)}) async-start(), calls=%async_computation.2 | async-start | bytes 5242880 | tf_op jit(solution)/shard_map/all_gather | solution.py:1358
  9.3 9.2 copy-start.4
  9.3 305.8 %collective-permute-start.3 = (bf16[128,2048]{1,0:T(8,128)(2,1)}, bf16[128,2048]{1,0:T(8,128)(2,1)}, u32[]{:S(2)}, u32[]{:S(2)}) collective-permute-start(bf16[128,2048]{1,0:T(8,128)(2,1)} %dynamic-slice_bitcast_fusion), channel_id=1, source_target_pairs={{0,4},{2,6},{4,0},{6,2},{1,5},{3,7},{5,1},{7,3},{8,12},{10,14},{12... | collective-permute-start | bytes 1572872 | tf_op jit(solution)/shard_map/ppermute | solution.py:1327
  14.3 303.1 %collective-permute-start = (bf16[128,2048]{1,0:T(8,128)(2,1)}, bf16[128,2048]{1,0:T(8,128)(2,1)}, u32[]{:S(2)}, u32[]{:S(2)}) collective-permute-start(bf16[128,2048]{1,0:T(8,128)(2,1)} %dynamic-slice_bitcast_fusion.2), channel_id=1, source_target_pairs={{0,4},{2,6},{4,0},{6,2},{1,5},{3,7},{5,1},{7,3},{8,12},{10,14},{12... | collective-permute-start | bytes 1572872 | tf_op jit(solution)/shard_map/ppermute | solution.py:1327
  15.2 305.3 %collective-permute-start.1 = (bf16[128,2048]{1,0:T(8,128)(2,1)}, bf16[128,2048]{1,0:T(8,128)(2,1)}, u32[]{:S(2)}, u32[]{:S(2)}) collective-permute-start(bf16[128,2048]{1,0:T(8,128)(2,1)} %dynamic-slice_bitcast_fusion.1), channel_id=1, source_target_pairs={{0,4},{2,6},{4,0},{6,2},{1,5},{3,7},{5,1},{7,3},{8,12},{10,14},{12... | collective-permute-start | bytes 1572872 | tf_op jit(solution)/shard_map/ppermute | solution.py:1327
  18.5 2.1 copy-start.5
  18.5 2.1 copy-start.17
  300.8 8.3 copy-start.18
  312.3 2.8 copy-start.10
  317.3 779.3 %reduce-scatter.5.cloned.1.call-start = ((), (), s32[]{:S(2)}) async-start(), calls=%async_computation.3 | async-start | bytes 18874368 | tf_op jit(solution)/shard_map/reduce_scatter | solution.py:1483
  319.0 1.6 copy-start.13
  321.7 7.5 copy-start.6
  321.7 7.5 copy-start.8
  893.7 74.3 %copy-start.7 = (bf16[128,2048]{1,0:T(8,128)(2,1)S(1)}, bf16[128,2048]{1,0:T(8,128)(2,1)}, u32[]{:S(2)}) copy-start(bf16[128,2048]{1,0:T(8,128)(2,1)} %copy-done.6) | copy-start | bytes 1572868
  980.3 387.6 %reduce-scatter.7.cloned.1.call-start = ((), (), s32[]{:S(2)}) async-start(), calls=%async_computation.5 | async-start | bytes 589824
  982.0 48.2 %collective-permute-start.2 = (f32[128,2048]{1,0:T(8,128)S(1)}, f32[128,2048]{1,0:T(8,128)S(1)}, u32[]{:S(2)}, u32[]{:S(2)}) collective-permute-start(f32[128,2048]{1,0:T(8,128)S(1)} %slice_select_fusion), channel_id=1, source_target_pairs={{0,4},{2,6},{4,0},{6,2},{1,5},{3,7},{5,1},{7,3},{8,12},{10,14},{12... | collective-permute-start | bytes 3145736 | tf_op jit(solution)/shard_map/ppermute | solution.py:1336
  1030.5 2.7 copy-start.2
  1033.1 351.2 %all-reduce.3.cloned.1.call-start = ((), (), s32[]{:S(2)}) async-start(), calls=%async_computation.4 | async-start | bytes 4194304 | tf_op jit(solution)/shard_map/psum | solution.py:1492
  1033.2 342.8 %collective-permute-start.4 = (bf16[128,2048]{1,0:T(8,128)(2,1)S(1)}, bf16[128,2048]{1,0:T(8,128)(2,1)}, u32[]{:S(2)}, u32[]{:S(2)}) collective-permute-start(bf16[128,2048]{1,0:T(8,128)(2,1)S(1)} %broadcast_select_fusion), channel_id=1, source_target_pairs={{0,4},{2,6},{4,0},{6,2},{1,5},{3,7},{5,1},{7,3},{8,12},{10,14},{12... | collective-permute-start | bytes 1572872 | tf_op jit(solution)/shard_map/ppermute | solution.py:1336
  1355.7 4.9 copy-start.9
  1377.2 11.2 copy-start.1
  (4 other events, 6.2 us)
Sparse Core Ops, SparseCore 0:
  317.5 70.0 all-gather.1
  980.4 116.1 reduce-scatter.4
  1100.3 35.8 reduce-scatter.6
  1138.5 106.7 all-reduce.2

commit v5 on v4

--- a/solution.py
+++ b/solution.py
@@ -4,12 +4,14 @@
 
 import jax
 import jax.numpy as jnp
+import numpy as np
 from jax import lax
 from jax.experimental import pallas as pl
 from jax.experimental.pallas import tpu as pltpu
 from jax.sharding import PartitionSpec as P
 
 BACK = 1
+MAXR = 4
 
 
 rope_base = 50000.0
@@ -17,11 +19,15 @@
 masked_score = -1e30
 
 
-def rope_angles(positions, head_dim):
-    freq_index = jnp.arange(head_dim // 2, dtype=jnp.float32)
-    inv_freq = 1.0 / rope_base ** (2.0 * freq_index / head_dim)
-    angles = positions.astype(jnp.float32)[:, None] * inv_freq[None, :]
-    return (jnp.cos(angles), jnp.sin(angles))
+def rope_tables(seq_len, head_dim):
+    freq_index = np.arange(head_dim // 2, dtype=np.float32)
+    inv_freq = 1.0 / np.float32(rope_base) ** (np.float32(2.0) * freq_index / head_dim)
+    angles = np.arange(seq_len, dtype=np.float32)[:, None] * inv_freq.astype(np.float32)[None, :]
+    cos_t, sin_t = np.cos(angles), np.sin(angles)
+    return (
+        jnp.asarray(np.concatenate([cos_t, cos_t], axis=1), jnp.float32),
+        jnp.asarray(np.concatenate([-sin_t, sin_t], axis=1), jnp.float32),
+    )
 
 
 MESH = pl.DeviceIdType.MESH
@@ -95,8 +101,10 @@
         first = (self.ahead(q) + j * sz.half) * sz.tile
         return pl.ds(pl.multiple_of(first, sz.tile), sz.tile)
 
-    def enter(self):
+    def enter(self, others=(), more=0):
         barrier = pltpu.get_barrier_semaphore()
+        for device in others:
+            pl.semaphore_signal(barrier, inc=1, device_id=device, device_id_type=MESH)
         pl.semaphore_signal(
             barrier, inc=1, device_id=self.sibling(), device_id_type=MESH
         )
@@ -107,7 +115,7 @@
                 device_id=self.device(self.ahead(q), self.ctx),
                 device_id_type=MESH,
             )
-        pl.semaphore_wait(barrier, self.sz.half)
+        pl.semaphore_wait(barrier, self.sz.half + len(others) + more)
 
 
 class Gather:
@@ -178,7 +186,7 @@
         far = (max(sz.half - 1, 1), sz.seqs, sz.block, sz.width)
         return [
             pltpu.VMEM((sz.tile, sz.width), jnp.float32),
-            pltpu.VMEM(near, jnp.float32),
+            pltpu.VMEM(near, jnp.bfloat16),
             pltpu.VMEM(near, jnp.bfloat16),
             pltpu.VMEM(near, jnp.bfloat16),
             pltpu.VMEM(far, jnp.bfloat16),
@@ -220,18 +228,18 @@
         other = pl.ds(pl.multiple_of((1 - ctx) * sz.block, sz.block), sz.block)
         self.near_out[q, j] = self.part[other, :].astype(jnp.bfloat16)
         self.near(q, j).start()
-        self.mine[q, j] = self.part[mine, :]
+        self.mine[q, j] = self.part[mine, :].astype(jnp.bfloat16)
 
     def onward(self, q, j):
         self.near(q, j).wait_recv()
         self.far_out[q - 1, j] = (
-            self.mine[q, j] + self.near_in[q, j].astype(jnp.float32)
+            self.mine[q, j].astype(jnp.float32) + self.near_in[q, j].astype(jnp.float32)
         ).astype(jnp.bfloat16)
         self.far(q, j).start()
 
     def total(self, j):
         self.near(0, j).wait_recv()
-        total = self.mine[0, j] + self.near_in[0, j].astype(jnp.float32)
+        total = self.mine[0, j].astype(jnp.float32) + self.near_in[0, j].astype(jnp.float32)
         for q in range(1, self.place.sz.half):
             self.far(q, j).wait_recv()
             total = total + self.far_in[q - 1, j].astype(jnp.float32)
@@ -280,18 +288,22 @@
     return x * cos_t + pltpu.roll(x, x.shape[-1] // 2, 1) * sin_t
 
 
-def attn_kernel(sz, keep, *refs):
+def attn_kernel(sz, n_dp, keep, *refs):
     (latent, embed, gains, cos_t, sin_t, begin, adapter_hbm, qkv_hbm, out_hbm) = refs[:9]
     refs = refs[9:]
+    if keep:
+        embed_hbm, refs = refs[0], refs[1:]
     mixed = refs[0]
     refs = refs[1:]
     if keep:
-        adapted_out, rows_out, q_out, k_out, v_out, head_out, lse_out = refs[:7]
-        refs = refs[7:]
+        adapted_out, rows_out, q_out, k_out, v_out, head_out, lse_out, joined_out = refs[:8]
+        refs = refs[8:]
     (wa, wqkv, wout, adapted, rows_s, q_s, k_s, v_s, head_s, lse_s) = refs[:10]
     load_a, load_qkv, load_out, keep_sem = refs[10:14]
     gather_refs = refs[14:16]
-    scatter_refs = refs[16:]
+    scatter_refs = refs[16:24]
+    if keep:
+        joined_s, load_embed, x_send, x_recv = refs[24:]
 
     place = Place(sz)
     a_loads = adapter_loads(adapter_hbm, wa, load_a)
@@ -303,7 +315,47 @@
     qkv_load.start()
     for copy in out_loads:
         copy.start()
-    place.enter()
+    others = []
+    if keep:
+        ring = Ring(place, n_dp)
+        t = lax.axis_index("tensor")
+        embed_load = pltpu.make_async_copy(
+            embed_hbm, joined_s.at[:, pl.ds(sz.width, sz.width)], load_embed
+        )
+        embed_load.start()
+        plane = [(o, c) for o in range(n_dp) for c in range(2) if (o, c) != (0, 0)]
+
+        def member(o, c):
+            return (ring.index(o), t, place.ctx if c == 0 else 1 - place.ctx)
+
+        def columns_to(o, c):
+            to = member(o, c)
+            depth = joined_out.shape[2]
+            first = pl.multiple_of((to[0] * sz.n_context + to[2]) * depth, depth)
+            return pltpu.make_async_remote_copy(
+                src_ref=joined_s.at[:, pl.ds(first, depth)],
+                dst_ref=joined_out.at[place.dp * sz.n_context + place.ctx],
+                send_sem=x_send.at[o, c],
+                recv_sem=x_recv.at[o, c],
+                device_id=to,
+                device_id_type=MESH,
+            )
+
+        def columns_from(o, c):
+            ref = joined_out.at[
+                ring.index(-o) * sz.n_context + (place.ctx if c == 0 else 1 - place.ctx)
+            ]
+            return pltpu.make_async_remote_copy(
+                src_ref=ref,
+                dst_ref=ref,
+                send_sem=x_send.at[o, c],
+                recv_sem=x_recv.at[o, c],
+                device_id=place.sibling(),
+                device_id_type=MESH,
+            )
+
+        others = [member(o, c) for o, c in plane if o]
+    place.enter(others)
     gather = Gather(place, rows_s, *gather_refs)
     scatter = Scatter(place, *scatter_refs)
 
@@ -383,6 +435,15 @@
 
     if keep:
         save(adapted, adapted_out)
+        joined_s[:, : sz.width] = low
+        embed_load.wait()
+        for o, c in plane:
+            columns_to(o, c).start()
+        mine = place.dp * sz.n_context + place.ctx
+        depth = joined_out.shape[2]
+        save(
+            joined_s.at[:, pl.ds(pl.multiple_of(mine * depth, depth), depth)], joined_out.at[mine]
+        )
     far = range(1, sz.half)
     for j in range(sz.seqs):
         gather.wait_near(j)
@@ -412,11 +473,17 @@
         span = slice(j * sz.block, (j + 1) * sz.block)
         mixed[span, :] = adapted[span, :] + scatter.total(j)
     scatter.finish()
+    if keep:
+        for o, c in plane:
+            columns_from(o, c).wait_recv()
+            columns_to(o, c).wait_send()
     for copy in copies:
         copy.wait()
 
 
-def run_attn(sz, keep, latent, embed_part, gains, cos_t, sin_t, begin, adapter, qkv, out):
+def run_attn(
+    sz, n_dp, keep, latent, embed_part, gains, cos_t, sin_t, begin, adapter, qkv, out, *embed
+):
     f32, bf16 = jnp.float32, jnp.bfloat16
     heads_shape = (sz.heads, sz.seq_len, sz.head_dim)
     shape = jax.ShapeDtypeStruct
@@ -430,6 +497,7 @@
             shape(heads_shape, bf16),
             shape((sz.seq_len, sz.heads * sz.head_dim), bf16),
             shape((sz.heads, 1, sz.seq_len), f32),
+            shape((adapter.shape[0], sz.rows, 2 * sz.width // adapter.shape[0]), bf16),
         ]
     scratch = [
         pltpu.VMEM((sz.width, sz.width), bf16),
@@ -448,11 +516,18 @@
         pltpu.SemaphoreType.DMA((8,)),
     ]
     scratch += Gather.scratch(sz) + Scatter.scratch(sz)
+    if keep:
+        scratch += [
+            pltpu.VMEM((sz.rows, 2 * sz.width), bf16),
+            pltpu.SemaphoreType.DMA,
+            pltpu.SemaphoreType.DMA((n_dp, 2)),
+            pltpu.SemaphoreType.DMA((n_dp, 2)),
+        ]
     flops = 2 * sz.rows * sz.width * sz.width + 2 * sz.seq_len * sz.width * qkv.shape[1]
     return pl.pallas_call(
-        partial(attn_kernel, sz, keep),
+        partial(attn_kernel, sz, n_dp, keep),
         out_shape=outs,
-        in_specs=[full_spec()] * 6 + [any_spec()] * 3,
+        in_specs=[full_spec()] * 6 + [any_spec()] * (3 + len(embed)),
         out_specs=[full_spec()] + [any_spec()] * (len(outs) - 1),
         scratch_shapes=scratch,
         compiler_params=pltpu.CompilerParams(
@@ -462,7 +537,7 @@
             flops=flops, bytes_accessed=20 << 20, transcendentals=0
         ),
         name="attn_keep" if keep else "attn_round",
-    )(latent, embed_part, gains, cos_t, sin_t, begin, adapter, qkv, out)
+    )(latent, embed_part, gains, cos_t, sin_t, begin, adapter, qkv, out, *embed)
 
 
 def ffn_kernel(sz, keep, *refs):
@@ -592,6 +667,10 @@
     )(mixed, latent, active, gains, gate, up, down)
 
 
+def other_group(place):
+    return (place.dp, (1 - place.group) * place.sz.half + place.part, place.ctx)
+
+
 class Ring:
     def __init__(self, place, n_dp):
         self.place, self.count = place, n_dp
@@ -613,10 +692,13 @@
 def weights_kernel(sz, n_dp, *refs):
     count = 5
     adapter_in, blocks_in = refs[0], refs[1 : 1 + count]
-    adapter_out, blocks_out = refs[1 + count], refs[2 + count : 2 + 2 * count]
-    (move_send, move_recv, ring_send, ring_recv, a_send, a_recv, x_send, x_recv, own_sem) = refs[
-        2 + 2 * count :
-    ]
+    rows_in, refs = refs[1 + count : 4 + count], refs[4 + count :]
+    adapter_out, blocks_out = refs[0], refs[1 : 1 + count]
+    embed_out, cot_out, cot_all, embed_part, state_out = refs[1 + count : 6 + count]
+    refs = refs[6 + count :]
+    (move_send, move_recv, ring_send, ring_recv, a_send, a_recv, x_send, x_recv, own_sem) = refs[:9]
+    embed_s, state_s, weight_s, swap_send, swap_recv, keep_sem, weight_sem = refs[9:16]
+    gather_refs = refs[16:]
     place = Place(sz)
     ring = Ring(place, n_dp)
     t = lax.axis_index("tensor")
@@ -644,8 +726,50 @@
         pl.when(jnp.logical_not(at_home & (ctx == c)))(
             lambda c=c: greet((place.dp, role, c))
         )
-    waits = 2 + half + sz.seqs - jnp.where(at_home, 1, 0)
+    other = other_group(place)
+    greet(other)
+    waits = 3 + half + sz.seqs - jnp.where(at_home, 1, 0)
     pl.semaphore_wait(barrier, waits)
+
+    own_at = pl.ds(pl.multiple_of(place.group * sz.block, sz.block), sz.block)
+    other_at = pl.ds(pl.multiple_of((1 - place.group) * sz.block, sz.block), sz.block)
+    rows_to = (embed_s, state_s, cot_out)
+
+    def swap(i):
+        return pltpu.make_async_remote_copy(
+            src_ref=rows_in[i].at[1 - place.group],
+            dst_ref=rows_to[i].at[own_at],
+            send_sem=swap_send.at[i],
+            recv_sem=swap_recv.at[i],
+            device_id=other,
+            device_id_type=MESH,
+        )
+
+    def swapped(i):
+        ref = rows_to[i].at[other_at]
+        return pltpu.make_async_remote_copy(
+            src_ref=ref,
+            dst_ref=ref,
+            send_sem=swap_send.at[i],
+            recv_sem=swap_recv.at[i],
+            device_id=other,
+            device_id_type=MESH,
+        )
+
+    def keep(i):
+        return pltpu.make_async_copy(
+            rows_in[i].at[place.group], rows_to[i].at[own_at], keep_sem.at[i]
+        )
+
+    for i in range(3):
+        swap(i).start()
+        keep(i).start()
+    gather = Gather(place, cot_all, *gather_refs)
+
+    def own_rows_of(j):
+        return pltpu.make_async_copy(
+            cot_out.at[pl.ds(j * sz.block, sz.block)], cot_all.at[gather.own(j)], keep_sem.at[3 + j]
+        )
 
     def move(w, g):
         slot = place.dp * n_c + ctx
@@ -784,6 +908,7 @@
             crossed(q, s).wait_recv()
             across(half - 1 + q, s).start()
 
+    embed_save = pltpu.make_async_copy(embed_s, embed_out, keep_sem.at[3 + sz.seqs])
     todo = []
     for k in range(count + steps):
         for s in range(min(k, steps - 1), -1, -1):
@@ -800,19 +925,58 @@
             hop(w, way, s).start()
         if done < steps:
             adapter_step(done)
+        if done == 5:
+            for i in range(3):
+                keep(i).wait()
+                swapped(i).wait_recv()
+            for j in range(sz.seqs):
+                own_rows_of(j).start()
+            embed_save.start()
+            for j in range(sz.seqs):
+                own_rows_of(j).wait()
+                gather.start(j)
+            state_out[...] = state_s[...].astype(jnp.float32)
         done += 1
     for s in range(done, steps):
         adapter_step(s)
     for s in range(n_dp):
         adapter_pass(s)
-    for w in range(count):
-        for way in range(n_c):
-            hopped(w, way, steps - 1).wait_recv()
+    for j in range(sz.seqs):
+        gather.wait_near(j)
+        for q in range(1, half):
+            gather.forward(q, j)
     for s in range(n_dp):
         crossed(0, s).wait_recv()
         for q in range(1, half):
             crossed(half - 1 + q, s).wait_recv()
     own.wait()
+    slots, depth = adapter_out.shape[0], weight_s.shape[1]
+    loads = [
+        pltpu.make_async_copy(
+            adapter_out.at[slots // 2 + b, pl.ds(0, depth)], weight_s.at[b % 2], weight_sem.at[b % 2]
+        )
+        for b in range(slots // 2)
+    ]
+    loads[0].start()
+    for b, copy in enumerate(loads):
+        if b + 1 < len(loads):
+            loads[b + 1].start()
+        copy.wait()
+        part_here = nn_dot(embed_s[:, b * depth : (b + 1) * depth], weight_s[b % 2])
+        if b:
+            embed_part[...] += part_here
+        else:
+            embed_part[...] = part_here
+    for w in range(count):
+        for way in range(n_c):
+            hopped(w, way, steps - 1).wait_recv()
+    for j in range(sz.seqs):
+        for q in range(1, half):
+            gather.wait_far(q, j)
+    gather.finish()
+    embed_save.wait()
+    for i in range(3):
+        swap(i).wait_send()
     for w in range(count):
         for g in range(sz.seqs):
             here = at_home & (place.group == g)
@@ -827,17 +991,24 @@
             across(kind, s).wait_send()
 
 
-def run_weights(sz, n_dp, adapter, blocks):
-    bf16 = jnp.bfloat16
+def run_weights(sz, n_dp, adapter, adapter_block, blocks, rows):
+    bf16, f32 = jnp.bfloat16, jnp.float32
     slots = n_dp * sz.n_context
     outs = [jax.ShapeDtypeStruct((slots,) + a.shape, bf16) for a in [adapter] + blocks]
+    outs += [
+        jax.ShapeDtypeStruct((sz.rows, sz.width), bf16),
+        jax.ShapeDtypeStruct((sz.rows, sz.width), bf16),
+        jax.ShapeDtypeStruct((sz.seq_len, sz.width), bf16),
+        jax.ShapeDtypeStruct((sz.rows, sz.width), f32),
+        jax.ShapeDtypeStruct((sz.rows, sz.width), f32),
+    ]
     count, steps, dma = len(blocks), n_dp - 1, pltpu.SemaphoreType.DMA
     kinds = 2 * sz.half - 1
     return pl.pallas_call(
         partial(weights_kernel, sz, n_dp),
         out_shape=outs,
-        in_specs=[any_spec()] * (1 + count),
-        out_specs=[any_spec()] * (1 + count),
+        in_specs=[any_spec()] * (4 + count),
+        out_specs=[any_spec()] * (4 + count) + [full_spec()] * 2,
         scratch_shapes=[
             dma((count, sz.seqs)),
             dma((count, sz.n_context)),
@@ -848,10 +1019,20 @@
             dma((kinds, n_dp)),
             dma((kinds, n_dp)),
             dma((count + 1,)),
-        ],
-        compiler_params=pltpu.CompilerParams(collective_id=5, has_side_effects=True),
+            pltpu.VMEM((sz.rows, sz.width), bf16),
+            pltpu.VMEM((sz.rows, sz.width), bf16),
+            pltpu.VMEM((2, adapter_block, sz.width), bf16),
+            dma((3,)),
+            dma((3,)),
+            dma((4 + sz.seqs,)),
+            dma((2,)),
+        ]
+        + Gather.scratch(sz),
+        compiler_params=pltpu.CompilerParams(
+            collective_id=5, has_side_effects=True, vmem_limit_bytes=VMEM_BYTES
+        ),
         name="weights",
-    )(adapter, *blocks)
+    )(adapter, *blocks, *rows)
 
 
 def norm_back(grad, rows, factor, gain):
@@ -861,12 +1042,208 @@
     return factor * (weighted - unit * inner), jnp.sum(grad * unit, axis=0, keepdims=True)
 
 
-def ffn_back_kernel(sz, *refs):
-    (cot, mixed, gains, rows_hbm, gate_hbm, up_hbm, wg_hbm, wu_hbm, down_hbm) = refs[:9]
-    (grad_mixed, gain_grad, dgate_out, dup_out) = refs[9:13]
-    (rows_s, gate_s, up_s, wg, wu, wd, load, load_down, keep_sem) = refs[13:22]
-    scatter_refs = refs[22:]
+class GradRing:
+    @staticmethod
+    def scratch(sz, n_dp, wide):
+        slots, ways, steps, dma = n_dp * sz.n_context, sz.n_context, n_dp - 1, pltpu.SemaphoreType.DMA
+        depth, bf16, count = sz.width // slots, jnp.bfloat16, len(wide)
+        return (
+            [pltpu.VMEM((sz.seq_len, n), bf16) for n in wide]
+            + [pltpu.VMEM((ways, depth, n), bf16) for n in wide]
+            + [pltpu.VMEM((ways, steps, depth, n), bf16) for n in wide]
+            + [
+                pltpu.VMEM((2, ways, sz.seq_len, depth), bf16),
+                dma((count,)),
+                dma((2, ways)),
+                dma((count, ways, steps)),
+                dma((count, ways, steps)),
+            ]
+        )
+
+    def __init__(self, sz, place, ring, xs, ys, refs):
+        count = len(xs)
+        self.sz, self.place, self.ring, self.xs, self.count = sz, place, ring, xs, count
+        self.ys, self.first, self.held = (refs[i * count : (i + 1) * count] for i in range(3))
+        self.x_s, self.load_y, self.load_x, self.send, self.recv = refs[3 * count :]
+        self.y_loads = [
+            pltpu.make_async_copy(ys[w], self.ys[w], self.load_y.at[w]) for w in range(count)
+        ]
+        self.tasks = [
+            (k - s, s)
+            for k in range(count + ring.count)
+            for s in range(min(k, ring.count - 1), -1, -1)
+            if k - s < count
+        ]
+        self.done, self.seen = 0, set()
+
+    def start(self):
+        for copy in self.y_loads:
+            copy.start()
+        for way in range(self.sz.n_context):
+            self.x_load(0, way).start()
+
+    def slot(self, way, s):
+        return self.ring.index(-(s + 1) if way == 0 else s + 1) * self.sz.n_context + way
+
+    def x_load(self, k, way):
+        w, s = self.tasks[k]
+        depth = self.x_s.shape[3]
+        if self.xs[w].shape[0] == 1:
+            at = pl.multiple_of(self.slot(way, s) * depth, depth)
+            src = self.xs[w].at[0, :, pl.ds(at, depth)]
+        else:
+            src = self.xs[w].at[self.slot(way, s)]
+        return pltpu.make_async_copy(src, self.x_s.at[k % 2, way], self.load_x.at[k % 2, way])
+
+    def source(self, w, way, s):
+        return self.first[w].at[way] if s == 0 else self.held[w].at[way, s - 1]
+
+    def hop(self, w, way, s):
+        return pltpu.make_async_remote_copy(
+            src_ref=self.source(w, way, s),
+            dst_ref=self.held[w].at[way, s],
+            send_sem=self.send.at[w, way, s],
+            recv_sem=self.recv.at[w, way, s],
+            device_id=self.ring.device(1 if way == 0 else self.ring.count - 1),
+            device_id_type=MESH,
+        )
+
+    def result(self, w, way):
+        return self.source(w, way, self.ring.count - 1)
+
+    def step(self):
+        k = self.done
+        self.done += 1
+        w, s = self.tasks[k]
+        ways = range(self.sz.n_context)
+        if k + 1 < len(self.tasks):
+            for way in ways:
+                self.x_load(k + 1, way).start()
+        if w not in self.seen:
+            self.y_loads[w].wait()
+            self.seen.add(w)
+        for way in ways:
+            self.x_load(k, way).wait()
+            value = tn_dot(self.x_s[k % 2, way], self.ys[w][...])
+            if s:
+                self.hop(w, way, s - 1).wait_recv()
+                value = value + self.held[w][way, s - 1].astype(jnp.float32)
+            ref = self.source(w, way, s)
+            ref[...] = value.astype(jnp.bfloat16)
+            if s < self.ring.count - 1:
+                self.hop(w, way, s).start()
+        return w, s == self.ring.count - 1
+
+    def left(self):
+        return len(self.tasks) - self.done
+
+    def finish(self):
+        for w in range(self.count):
+            for way in range(self.sz.n_context):
+                for s in range(self.ring.count - 1):
+                    self.hop(w, way, s).wait_send()
+
+
+class Deliver:
+    @staticmethod
+    def scratch(sz, n_dp, wide):
+        depth, count, dma = sz.width // (n_dp * sz.n_context), len(wide), pltpu.SemaphoreType.DMA
+        return [pltpu.VMEM((sz.seqs, depth, n), jnp.bfloat16) for n in wide] + [
+            dma((count, sz.n_context)),
+            dma((count, sz.seqs)),
+            dma((count,)),
+        ]
+
+    def __init__(self, sz, place, refs):
+        self.sz, self.place = sz, place
+        self.landed = refs[:-3]
+        self.send, self.recv, self.own = refs[-3:]
+        self.count = len(self.landed)
+        self.t = lax.axis_index("tensor")
+        self.role = place.part * sz.n_context + place.ctx
+        self.at_home = self.role == self.t
+        self.sources = [None] * self.count
+
+    def greet(self):
+        sz, place = self.sz, self.place
+        barrier = pltpu.get_barrier_semaphore()
+        for g in range(sz.seqs):
+            holder = (place.dp, g * sz.half + self.t // sz.n_context, lax.rem(self.t, sz.n_context))
+            pl.when(jnp.logical_not(self.at_home & (place.group == g)))(
+                lambda holder=holder: pl.semaphore_signal(
+                    barrier, inc=1, device_id=holder, device_id_type=MESH
+                )
+            )
+        return sz.n_context - jnp.where(self.at_home, 1, 0)
+
+    def remote(self, w, way):
+        return pltpu.make_async_remote_copy(
+            src_ref=self.sources[w][way],
+            dst_ref=self.landed[w].at[self.place.group],
+            send_sem=self.send.at[w, way],
+            recv_sem=self.recv.at[w, self.place.group],
+            device_id=(self.place.dp, self.role, way),
+            device_id_type=MESH,
+        )
+
+    def local(self, w, way):
+        return pltpu.make_async_copy(
+            self.sources[w][way], self.landed[w].at[self.place.group], self.own.at[w]
+        )
+
+    def start(self, w, sources):
+        self.sources[w] = sources
+        for way in range(self.sz.n_context):
+            here = self.at_home & (self.place.ctx == way)
+            pl.when(here)(lambda way=way: self.local(w, way).start())
+            pl.when(jnp.logical_not(here))(lambda way=way: self.remote(w, way).start())
+
+    def total(self, w):
+        place = self.place
+        for g in range(self.sz.seqs):
+            ref = self.landed[w].at[g]
+            arrival = pltpu.make_async_remote_copy(
+                src_ref=ref,
+                dst_ref=ref,
+                send_sem=self.send.at[w, 0],
+                recv_sem=self.recv.at[w, g],
+                device_id=(place.dp, self.t, 1 - place.ctx),
+                device_id_type=MESH,
+            )
+            here = self.at_home & (place.group == g)
+            pl.when(here)(lambda: self.local(w, 0).wait())
+            pl.when(jnp.logical_not(here))(lambda arrival=arrival: arrival.wait_recv())
+        total = self.landed[w][0].astype(jnp.float32)
+        for g in range(1, self.sz.seqs):
+            total = total + self.landed[w][g].astype(jnp.float32)
+        return total
+
+    def finish(self):
+        for w in range(self.count):
+            for way in range(self.sz.n_context):
+                here = self.at_home & (self.place.ctx == way)
+                pl.when(jnp.logical_not(here))(lambda w=w, way=way: self.remote(w, way).wait_send())
+
+
+def slot_columns(sz, n_dp, x):
+    slots = n_dp * sz.n_context
+    depth = sz.width // slots
+    if depth % 128:
+        return x.reshape(sz.seq_len, slots, depth).transpose(1, 0, 2)
+    return x[None]
+
+
+def ffn_back_kernel(sz, n_dp, *refs):
+    (cot, mixed, gains, state) = refs[:4]
+    (rows_hbm, gate_hbm, up_hbm, wg_hbm, wu_hbm, down_hbm, x_hbm, hidden_hbm) = refs[4:12]
+    (grad_mixed, gain_grad, state_out, dgate_out, dup_out, down_sum) = refs[12:18]
+    (rows_s, gate_s, up_s, wg, wu, wd, load, load_down, keep_sem) = refs[18:27]
+    (swap_out, swap_in, swap_sem) = refs[27:30]
+    scatter_refs, ring_refs = refs[30:38], refs[38:]
     place = Place(sz)
+    ring = Ring(place, n_dp)
+    grads = GradRing(sz, place, ring, [x_hbm], [hidden_hbm], ring_refs)
+    grads.start()
     pairs = ((rows_hbm, rows_s), (gate_hbm, gate_s), (up_hbm, up_s), (wg_hbm, wg), (wu_hbm, wu))
     loads = [
         pltpu.make_async_copy(src, dst, load.at[i]) for i, (src, dst) in enumerate(pairs)
@@ -875,10 +1252,24 @@
     loads[0].start()
     for copy in down_loads + loads[1:]:
         copy.start()
-    place.enter()
+    other = (place.dp, (1 - place.group) * sz.half + place.part, place.ctx)
+    place.enter([ring.device(1), ring.device(n_dp - 1), other])
     scatter = Scatter(place, *scatter_refs)
+    grads.step()
     for copy in [loads[0]] + down_loads + loads[1:]:
         copy.wait()
+    give_rows = pl.ds(pl.multiple_of((1 - place.group) * sz.block, sz.block), sz.block)
+    keep_rows = pl.ds(pl.multiple_of(place.group * sz.block, sz.block), sz.block)
+    swap = pltpu.make_async_remote_copy(
+        src_ref=swap_out,
+        dst_ref=swap_in,
+        send_sem=swap_sem.at[0],
+        recv_sem=swap_sem.at[1],
+        device_id=other,
+        device_id_type=MESH,
+    )
+    swap_out[...] = state[give_rows, :].astype(jnp.bfloat16)
+    state_out[place.group] = state[keep_rows, :]
 
     def work(q, j):
         rows = place.tile(q, j)
@@ -903,6 +1294,8 @@
     work(0, 0)
     for q in far:
         scatter.onward(q, sz.seqs - 1)
+    swap.start()
+    grads.step()
     for j in range(1, sz.seqs):
         work(0, j)
     copies = [
@@ -919,24 +1312,38 @@
         grad_mixed[span, :] = cot[span, :].astype(jnp.float32) + grad
         gain_total = gain_here if gain_total is None else gain_total + gain_here
     gain_grad[...] = gain_total
+    while grads.left() > 1:
+        grads.step()
+    swap.wait()
+    state_out[1 - place.group] = swap_in[...].astype(jnp.float32)
+    grads.step()
+    for way in range(sz.n_context):
+        copies.append(
+            pltpu.make_async_copy(grads.result(0, way), down_sum.at[way], keep_sem.at[2 + way])
+        )
+        copies[-1].start()
     scatter.finish()
+    grads.finish()
     for copy in copies:
         copy.wait()
 
 
-def run_ffn_back(sz, cot, mixed, gains, rows, gate, up, wg, wu, down):
+def run_ffn_back(sz, n_dp, cot, mixed, gains, state, rows, gate, up, wg, wu, down, hidden):
     f32, bf16, shape = jnp.float32, jnp.bfloat16, jax.ShapeDtypeStruct
     dma = pltpu.SemaphoreType.DMA
+    depth = sz.width // (n_dp * sz.n_context)
     return pl.pallas_call(
-        partial(ffn_back_kernel, sz),
+        partial(ffn_back_kernel, sz, n_dp),
         out_shape=[
             shape((sz.rows, sz.width), f32),
             shape((1, sz.width), f32),
+            shape((sz.seqs, sz.block, sz.width), f32),
             shape((sz.seq_len, sz.ff), bf16),
             shape((sz.seq_len, sz.ff), bf16),
+            shape((sz.n_context, depth, sz.ff), bf16),
         ],
-        in_specs=[full_spec()] * 3 + [any_spec()] * 6,
-        out_specs=[full_spec()] * 2 + [any_spec()] * 2,
+        in_specs=[full_spec()] * 4 + [any_spec()] * 8,
+        out_specs=[full_spec()] * 3 + [any_spec()] * 3,
         scratch_shapes=[
             pltpu.VMEM((sz.seq_len, sz.width), bf16),
             pltpu.VMEM((sz.seq_len, sz.ff), bf16),
@@ -946,28 +1353,36 @@
             pltpu.VMEM((sz.ff, sz.width), bf16),
             dma((5,)),
             dma((down.shape[0],)),
+            dma((2 + sz.n_context,)),
+            pltpu.VMEM((sz.block, sz.width), bf16),
+            pltpu.VMEM((sz.block, sz.width), bf16),
             dma((2,)),
         ]
-        + Scatter.scratch(sz),
+        + Scatter.scratch(sz)
+        + GradRing.scratch(sz, n_dp, [sz.ff]),
         compiler_params=pltpu.CompilerParams(
             collective_id=6, has_side_effects=True, vmem_limit_bytes=VMEM_BYTES
         ),
         cost_estimate=pl.CostEstimate(
-            flops=6 * sz.seq_len * sz.width * sz.ff, bytes_accessed=40 << 20, transcendentals=0
+            flops=8 * sz.seq_len * sz.width * sz.ff, bytes_accessed=40 << 20, transcendentals=0
         ),
         name="ffn_back",
-    )(cot, mixed, gains, rows, gate, up, wg, wu, down)
-
-
-def attn_back_kernel(sz, *refs):
-    (grad_mixed, adapted, gains, cos_t, sin_t, begin) = refs[:6]
-    (q_hbm, k_hbm, v_hbm, lse_hbm, out_hbm, qkv_hbm) = refs[6:12]
-    (grad_low, gain_grad, rows_out, proj_out) = refs[12:16]
-    (rows_s, q_s, k_s, v_s, lse_s, do_s, dk_s, dv_s, proj_s, wout, wqkv) = refs[16:27]
-    (load, load_out, keep_sem) = refs[27:30]
-    gather_refs = refs[30:32]
-    scatter_refs = refs[32:]
+    )(cot, mixed, gains, state, rows, gate, up, wg, wu, down, slot_columns(sz, n_dp, rows), hidden)
+
+
+def attn_back_kernel(sz, n_dp, *refs):
+    (grad_mixed, adapted, gains, cos_t, sin_t, begin, gain_b) = refs[:7]
+    (q_hbm, k_hbm, v_hbm, lse_hbm, out_hbm, qkv_hbm, x_hbm, dgate_hbm, down_sum) = refs[7:16]
+    (grad_low, down_grad, rows_out, proj_out, gate_sum) = refs[16:21]
+    (rows_s, q_s, k_s, v_s, lse_s, do_s, dk_s, dv_s, proj_s, wout, wqkv) = refs[21:32]
+    (load, load_out, keep_sem) = refs[32:35]
+    gather_refs, scatter_refs = refs[35:37], refs[37:45]
+    ring_refs, deliver_refs = refs[45:53], refs[53:]
     place = Place(sz)
+    ring = Ring(place, n_dp)
+    grads = GradRing(sz, place, ring, [x_hbm], [dgate_hbm], ring_refs)
+    deliver = Deliver(sz, place, deliver_refs)
+    grads.start()
     pairs = ((q_hbm, q_s), (k_hbm, k_s), (v_hbm, v_s), (lse_hbm, lse_s), (qkv_hbm, wqkv))
     loads = [
         pltpu.make_async_copy(src, dst, load.at[i]) for i, (src, dst) in enumerate(pairs)
@@ -975,13 +1390,16 @@
     out_loads = column_loads(out_hbm, wout, load_out)
     for copy in out_loads + loads:
         copy.start()
-    place.enter()
+    targets = deliver.greet()
+    place.enter([ring.device(1), ring.device(n_dp - 1)], targets)
     gather = Gather(place, rows_s, *gather_refs)
     scatter = Scatter(place, *scatter_refs)
     for j in range(sz.seqs):
         span = slice(j * sz.block, (j + 1) * sz.block)
         rows_s[gather.own(j), :] = grad_mixed[span, :].astype(jnp.bfloat16)
         gather.start(j)
+    grads.step()
+    deliver.start(0, [down_sum.at[way] for way in range(sz.n_context)])
     for copy in out_loads:
         copy.wait()
     d = sz.head_dim
@@ -1006,6 +1424,7 @@
             heads_grad(q, j)
     copies = [pltpu.make_async_copy(rows_s, rows_out, keep_sem.at[0])]
     copies[0].start()
+    grads.step()
 
     tiles = sz.n_tensor
     scale = 1.0 / math.sqrt(d)
@@ -1044,7 +1463,9 @@
         proj_s[:, pl.ds(pl.multiple_of(h * 3 * d + 2 * d, d), d)] = dv_s[...].astype(jnp.bfloat16)
         return carry
 
-    lax.fori_loop(0, sz.heads, head, 0)
+    lax.fori_loop(0, sz.heads // 2, head, 0)
+    grads.step()
+    lax.fori_loop(sz.heads // 2, sz.heads, head, 0)
     copies.append(pltpu.make_async_copy(proj_s, proj_out, keep_sem.at[1]))
     copies[1].start()
 
@@ -1064,6 +1485,14 @@
     for j in range(1, sz.seqs):
         give(0, j)
     gather.finish()
+    down_grad[...] = deliver.total(0)
+    while grads.left():
+        grads.step()
+    for way in range(sz.n_context):
+        copies.append(
+            pltpu.make_async_copy(grads.result(0, way), gate_sum.at[way], keep_sem.at[2 + way])
+        )
+        copies[-1].start()
     gain_total = None
     for j in range(sz.seqs):
         span = slice(j * sz.block, (j + 1) * sz.block)
@@ -1071,26 +1500,35 @@
         grad, gain_here = norm_back(scatter.total(j), rows, rms_factor(rows), gains[0:1, :])
         grad_low[span, :] = (grad_mixed[span, :] + grad).astype(jnp.bfloat16)
         gain_total = gain_here if gain_total is None else gain_total + gain_here
-    gain_grad[...] = gain_total
+    extra = grad_low.shape[0] - sz.rows
+    at_row = lax.broadcasted_iota(jnp.int32, (extra, sz.width), 0)
+    shares = jnp.where(at_row == 0, gain_total, jnp.where(at_row == 1, gain_b[...], 0.0))
+    grad_low[sz.rows :, :] = shares.astype(jnp.bfloat16)
     scatter.finish()
+    grads.finish()
+    deliver.finish()
     for copy in copies:
         copy.wait()
 
 
-def run_attn_back(sz, grad_mixed, adapted, gains, cos_t, sin_t, begin, q, k, v, lse, out, qkv):
+def run_attn_back(
+    sz, n_dp, grad_mixed, adapted, gains, cos_t, sin_t, begin, gain_b, q, k, v, lse, out, qkv,
+    x, dgate, down_sum,
+):
     f32, bf16, shape = jnp.float32, jnp.bfloat16, jax.ShapeDtypeStruct
     dma = pltpu.SemaphoreType.DMA
     heads_shape = (sz.heads, sz.seq_len, sz.head_dim)
     return pl.pallas_call(
-        partial(attn_back_kernel, sz),
+        partial(attn_back_kernel, sz, n_dp),
         out_shape=[
-            shape((sz.rows, sz.width), bf16),
-            shape((1, sz.width), f32),
+            shape((sz.rows + 16, sz.width), bf16),
+            shape(down_sum.shape[1:], f32),
             shape((sz.seq_len, sz.width), bf16),
             shape((sz.seq_len, qkv.shape[1]), bf16),
+            shape(down_sum.shape, bf16),
         ],
-        in_specs=[full_spec()] * 6 + [any_spec()] * 6,
-        out_specs=[full_spec()] * 2 + [any_spec()] * 2,
+        in_specs=[full_spec()] * 7 + [any_spec()] * 9,
+        out_specs=[full_spec()] * 2 + [any_spec()] * 3,
         scratch_shapes=[
             pltpu.VMEM((sz.seq_len, sz.width), bf16),
             pltpu.VMEM(heads_shape, bf16),
@@ -1105,10 +1543,12 @@
             pltpu.VMEM(qkv.shape, bf16),
             dma((5,)),
             dma((out.shape[0],)),
-            dma((2,)),
+            dma((2 + sz.n_context,)),
         ]
         + Gather.scratch(sz)
-        + Scatter.scratch(sz),
+        + Scatter.scratch(sz)
+        + GradRing.scratch(sz, n_dp, [sz.ff])
+        + Deliver.scratch(sz, n_dp, [sz.ff]),
         compiler_params=pltpu.CompilerParams(
             collective_id=7, has_side_effects=True, vmem_limit_bytes=VMEM_BYTES
         ),
@@ -1116,167 +1556,351 @@
             flops=4 * sz.seq_len * sz.width * qkv.shape[1], bytes_accessed=30 << 20, transcendentals=0
         ),
         name="attn_back",
-    )(grad_mixed, adapted, gains, cos_t, sin_t, begin, q, k, v, lse, out, qkv)
+    )(
+        grad_mixed, adapted, gains, cos_t, sin_t, begin, gain_b, q, k, v, lse, out, qkv,
+        slot_columns(sz, n_dp, x), dgate, down_sum,
+    )
+
+
+class PlaneRows:
+    @staticmethod
+    def scratch(n_dp):
+        dma = pltpu.SemaphoreType.DMA
+        return [dma((n_dp - 1,)), dma((n_dp - 1,)), dma((n_dp,)), dma((n_dp,))]
+
+    def __init__(self, place, ring, own, landed, refs):
+        self.place, self.ring, self.own, self.landed = place, ring, own, landed
+        self.send, self.recv, self.near_send, self.near_recv = refs
+        self.ahead = 1 - 2 * place.ctx
+
+    def slot(self, offset, ctx):
+        return self.landed.at[self.ring.index(offset) * self.place.sz.n_context + ctx]
+
+    def source(self, s):
+        return self.own if s == 0 else self.slot(-self.ahead * s, self.place.ctx)
+
+    def hop(self, s):
+        return pltpu.make_async_remote_copy(
+            src_ref=self.source(s),
+            dst_ref=self.slot(-self.ahead * s, self.place.ctx),
+            send_sem=self.send.at[s],
+            recv_sem=self.recv.at[s],
+            device_id=self.ring.device(self.ahead),
+            device_id_type=MESH,
+        )
+
+    def near(self, s):
+        return pltpu.make_async_remote_copy(
+            src_ref=self.source(s),
+            dst_ref=self.slot(-self.ahead * s, self.place.ctx),
+            send_sem=self.near_send.at[s],
+            recv_sem=self.near_recv.at[s],
+            device_id=self.place.sibling(),
+            device_id_type=MESH,
+        )
+
+    def start(self):
+        self.hop(0).start()
+        self.near(0).start()
+
+    def step(self, s):
+        ref = self.slot(-self.ahead * (s + 1), self.place.ctx)
+        pltpu.make_async_remote_copy(
+            src_ref=ref,
+            dst_ref=ref,
+            send_sem=self.send.at[s],
+            recv_sem=self.recv.at[s],
+            device_id=self.place.sibling(),
+            device_id_type=MESH,
+        ).wait_recv()
+        if s + 1 < self.ring.count - 1:
+            self.hop(s + 1).start()
+        self.near(s + 1).start()
+
+    def wait_near(self, s):
+        ref = self.slot(self.ahead * s, 1 - self.place.ctx)
+        pltpu.make_async_remote_copy(
+            src_ref=ref,
+            dst_ref=ref,
+            send_sem=self.near_send.at[s],
+            recv_sem=self.near_recv.at[s],
+            device_id=self.place.sibling(),
+            device_id_type=MESH,
+        ).wait_recv()
+
+    def finish(self):
+        for s in range(self.ring.count):
+            if s < self.ring.count - 1:
+                self.hop(s).wait_send()
+            self.near(s).wait_send()
+
+
+class LineSum:
+    @staticmethod
+    def scratch(sz, parts, chunk):
+        dma, bf16 = pltpu.SemaphoreType.DMA, jnp.bfloat16
+        far = pltpu.VMEM((max(sz.half - 1, 1), parts, chunk, sz.width), bf16)
+        one = pltpu.VMEM((parts, chunk, sz.width), bf16)
+        kinds = 2 * sz.half - 1
+        return [far, far, one, one, one, far, dma((kinds, parts)), dma((kinds, parts))]
+
+    def __init__(self, place, total, parts, refs):
+        self.place, self.total, self.parts = place, total, parts
+        (self.out, self.got, self.sum, self.cross, self.done, self.back, self.send, self.recv) = refs
+        self.chunk = self.sum.shape[1]
+
+    def rows(self, part, k):
+        first = (part * self.parts + k) * self.chunk
+        return pl.ds(pl.multiple_of(first, self.chunk), self.chunk)
+
+    def copy(self, src, dst, kind, k, device):
+        return pltpu.make_async_remote_copy(
+            src_ref=src,
+            dst_ref=dst,
+            send_sem=self.send.at[kind, k],
+            recv_sem=self.recv.at[kind, k],
+            device_id=device,
+            device_id_type=MESH,
+        )
+
+    def spread(self, q, k):
+        place = self.place
+        device = place.device(place.ahead(q), place.ctx)
+        return self.copy(self.out.at[q - 1, k], self.got.at[q - 1, k], q, k, device)
+
+    def swap(self, k):
+        return self.copy(self.sum.at[k], self.cross.at[k], 0, k, other_group(self.place))
+
+    def collect(self, q, k):
+        place = self.place
+        device = place.device(place.ahead(q), place.ctx)
+        return self.copy(
+            self.done.at[k], self.back.at[q - 1, k], place.sz.half - 1 + q, k, device
+        )
+
+    def start(self, k):
+        for q in range(1, self.place.sz.half):
+            rows = self.rows(self.place.ahead(q), k)
+            self.out[q - 1, k] = self.total[rows, :].astype(jnp.bfloat16)
+            self.spread(q, k).start()
+
+    def cross_over(self, k):
+        value = self.total[self.rows(self.place.part, k), :]
+        for q in range(1, self.place.sz.half):
+            self.spread(q, k).wait_recv()
+            value = value + self.got[q - 1, k].astype(jnp.float32)
+        self.sum[k] = value.astype(jnp.bfloat16)
+        self.swap(k).start()
+
+    def share(self, k):
+        self.swap(k).wait_recv()
+        value = self.sum[k].astype(jnp.float32) + self.cross[k].astype(jnp.float32)
+        self.done[k] = value.astype(jnp.bfloat16)
+        for q in range(1, self.place.sz.half):
+            self.collect(q, k).start()
+        self.total[self.rows(self.place.part, k), :] = self.done[k].astype(jnp.float32)
+
+    def complete(self, k):
+        for q in range(1, self.place.sz.half):
+            self.collect(q, k).wait_recv()
+            rows = self.rows(self.place.behind(q), k)
+            self.total[rows, :] = self.back[q - 1, k].astype(jnp.float32)
+
+    def finish(self):
+        for k in range(self.parts):
+            self.swap(k).wait_send()
+            for q in range(1, self.place.sz.half):
+                self.spread(q, k).wait_send()
+                self.collect(q, k).wait_send()
+
+
+SUM_PARTS = 2
 
 
 def grads_kernel(sz, n_dp, count, *refs):
-    xs, ys, outs = refs[:count], refs[count : 2 * count], refs[2 * count : 3 * count]
-    refs = refs[3 * count :]
-    y_s, first, held, landed = (refs[i * count : (i + 1) * count] for i in range(4))
-    (x_s, load_y, load_x, ring_send, ring_recv, move_send, move_recv, own_sem) = refs[4 * count :]
+    n_in = 4 + 2 * count
+    gate_sum, low, joined, adapter = refs[:4]
+    xs, ys = refs[4 : 4 + count], refs[4 + count : n_in]
+    outs = refs[n_in : n_in + 1 + count]
+    embed_grad, adapter_out, gains_out, landed = refs[n_in + 1 + count : n_in + 5 + count]
+    refs = refs[n_in + 5 + count :]
+
+    def take(n):
+        nonlocal refs
+        head, refs = refs[:n], refs[n:]
+        return head
+
+    ring_refs, deliver_refs = take(3 * count + 5), take(count + 4)
+    plane_refs, sum_refs = take(4), take(8)
+    adapter_grad, d_s, j_s, weight_s, rows_s, swap_in = refs[:6]
+    d_sem, j_sem, weight_sem, swap_sem, out_sem = refs[6:]
     place = Place(sz)
     ring = Ring(place, n_dp)
-    t = lax.axis_index("tensor")
-    ctx, part, half, n_c = place.ctx, place.part, sz.half, sz.n_context
-    role = part * n_c + ctx
-    at_home = role == t
-    depth = x_s.shape[3]
-
-    y_loads = [pltpu.make_async_copy(ys[w], y_s[w], load_y.at[w]) for w in range(count)]
-    for copy in y_loads:
+    grads = GradRing(sz, place, ring, xs, ys, ring_refs)
+    deliver = Deliver(sz, place, deliver_refs)
+    plane = PlaneRows(place, ring, low, landed, plane_refs)
+    line = LineSum(place, adapter_grad, SUM_PARTS, sum_refs)
+    other = other_group(place)
+    grads.start()
+    weight_load = [
+        pltpu.make_async_copy(
+            adapter.at[adapter.shape[0] // 2 + b, pl.ds(0, weight_s.shape[0])], weight_s, weight_sem
+        )
+        for b in range(adapter.shape[0] // 2)
+    ]
+    weight_load[0].start()
+    place.enter([ring.device(1), ring.device(n_dp - 1), other], deliver.greet())
+    plane.start()
+    give_rows = pl.ds(pl.multiple_of((1 - place.group) * sz.block, sz.block), sz.block)
+    keep_rows = pl.ds(pl.multiple_of(place.group * sz.block, sz.block), sz.block)
+    swap = pltpu.make_async_remote_copy(
+        src_ref=low.at[give_rows],
+        dst_ref=swap_in,
+        send_sem=swap_sem.at[0],
+        recv_sem=swap_sem.at[1],
+        device_id=other,
+        device_id_type=MESH,
+    )
+    swap.start()
+    deliver.start(0, [gate_sum.at[way] for way in range(sz.n_context)])
+
+    def ring_step():
+        if grads.left():
+            w, complete = grads.step()
+            if complete:
+                deliver.start(1 + w, [grads.result(w, way) for way in range(sz.n_context)])
+
+    depth = joined.shape[2]
+
+    def batch(ctx):
+        copies = []
+        for d in range(n_dp):
+            at = d * sz.n_context + ctx
+            rows = pl.ds(d * sz.rows, sz.rows)
+            copies.append(
+                pltpu.make_async_copy(landed.at[at, pl.ds(0, sz.rows)], d_s.at[rows], d_sem.at[d, 0])
+            )
+            copies.append(pltpu.make_async_copy(joined.at[at], j_s.at[rows], j_sem.at[d]))
+            copies.append(
+                pltpu.make_async_copy(
+                    landed.at[at, pl.ds(sz.rows, 16)],
+                    d_s.at[pl.ds(n_dp * sz.rows + 16 * d, 16)],
+                    d_sem.at[d, 1],
+                )
+            )
+        return copies
+
+    def product(ctx, first):
+        copies = batch(ctx)
+        for copy in copies:
+            copy.start()
+        for copy in copies:
+            copy.wait()
+        chunk = sz.width // 4
+        for n in range(4):
+            cols = slice(n * chunk, (n + 1) * chunk)
+            value = tn_dot(j_s[...], d_s[: n_dp * sz.rows, cols])
+            tail = d_s[n_dp * sz.rows : n_dp * sz.rows + 16, cols].astype(jnp.float32)
+            for d in range(1, n_dp):
+                at = n_dp * sz.rows + 16 * d
+                tail = tail + d_s[at : at + 16, cols].astype(jnp.float32)
+            if first:
+                adapter_grad[:depth, cols] = value
+                adapter_grad[depth : depth + 16, cols] = tail
+            else:
+                adapter_grad[:depth, cols] += value
+                adapter_grad[depth : depth + 16, cols] += tail
+
+    own = pltpu.make_async_copy(low, landed.at[place.dp * sz.n_context + place.ctx], d_sem.at[0, 0])
+    own.start()
+    rest = adapter_grad.shape[0] - depth - 16
+    if rest:
+        adapter_grad[depth + 16 :, :] = jnp.zeros((rest, sz.width), jnp.float32)
+    for s in range(n_dp - 1):
+        ring_step()
+        plane.step(s)
+    own.wait()
+    product(place.ctx, True)
+    for s in range(n_dp):
+        plane.wait_near(s)
+    product(1 - place.ctx, False)
+    for k in range(SUM_PARTS):
+        line.start(k)
+    ring_step()
+    swap.wait()
+    rows_s[place.group] = low[keep_rows, :]
+    rows_s[1 - place.group] = swap_in[...]
+    rows = rows_s[...].reshape(sz.rows, sz.width)
+    ring_step()
+    for k in range(SUM_PARTS):
+        line.cross_over(k)
+    ring_step()
+    for b, copy in enumerate(weight_load):
+        copy.wait()
+        part = nt_dot(rows, weight_s[...]).reshape(sz.seqs, sz.block, weight_s.shape[0])
+        embed_grad[:, :, b * weight_s.shape[0] : (b + 1) * weight_s.shape[0]] = part
+        if b + 1 < len(weight_load):
+            weight_load[b + 1].start()
+    ring_step()
+    for k in range(SUM_PARTS):
+        line.share(k)
+        ring_step()
+    while grads.left():
+        ring_step()
+    for k in range(SUM_PARTS):
+        line.complete(k)
+    saves = [
+        pltpu.make_async_copy(adapter_grad.at[pl.ds(0, depth)], adapter_out, out_sem.at[0]),
+        pltpu.make_async_copy(adapter_grad.at[pl.ds(depth, 16)], gains_out, out_sem.at[1]),
+    ]
+    for copy in saves:
         copy.start()
-
-    tasks = []
-    for k in range(count + n_dp):
-        for s in range(min(k, n_dp - 1), -1, -1):
-            if k - s < count:
-                tasks.append((k - s, s))
-
-    def slot(way, s):
-        return ring.index(-(s + 1) if way == 0 else s + 1) * n_c + way
-
-    def x_load(k, way):
-        w, s = tasks[k]
-        if xs[w].shape[0] == 1:
-            at = pl.multiple_of(slot(way, s) * depth, depth)
-            src = xs[w].at[0, :, pl.ds(at, depth)]
-        else:
-            src = xs[w].at[slot(way, s)]
-        return pltpu.make_async_copy(src, x_s.at[k % 2, way], load_x.at[k % 2, way])
-
-    for way in range(n_c):
-        x_load(0, way).start()
-
-    barrier = pltpu.get_barrier_semaphore()
-
-    def greet(device):
-        pl.semaphore_signal(barrier, inc=1, device_id=device, device_id_type=MESH)
-
-    def holder(g):
-        return (place.dp, g * half + t // n_c, lax.rem(t, n_c))
-
-    greet(ring.device(1))
-    greet(ring.device(n_dp - 1))
-    for g in range(sz.seqs):
-        pl.when(jnp.logical_not(at_home & (place.group == g)))(lambda g=g: greet(holder(g)))
-    pl.semaphore_wait(barrier, 2 + n_c - jnp.where(at_home, 1, 0))
-
-    def source(w, way, s):
-        return first[w].at[way] if s == 0 else held[w].at[way, s - 1]
-
-    def hop(w, way, s):
-        return pltpu.make_async_remote_copy(
-            src_ref=source(w, way, s),
-            dst_ref=held[w].at[way, s],
-            send_sem=ring_send.at[w, way, s],
-            recv_sem=ring_recv.at[w, way, s],
-            device_id=ring.device(1 if way == 0 else n_dp - 1),
-            device_id_type=MESH,
-        )
-
-    def deliver(w, way):
-        return pltpu.make_async_remote_copy(
-            src_ref=source(w, way, n_dp - 1),
-            dst_ref=landed[w].at[place.group],
-            send_sem=move_send.at[w, way],
-            recv_sem=move_recv.at[w, place.group],
-            device_id=(place.dp, role, way),
-            device_id_type=MESH,
-        )
-
-    def stay(w, way):
-        return pltpu.make_async_copy(
-            source(w, way, n_dp - 1), landed[w].at[place.group], own_sem.at[w]
-        )
-
-    def arrived(w, g):
-        arrival = pltpu.make_async_remote_copy(
-            src_ref=landed[w].at[g],
-            dst_ref=landed[w].at[g],
-            send_sem=move_send.at[w, 0],
-            recv_sem=move_recv.at[w, g],
-            device_id=(place.dp, t, 1 - ctx),
-            device_id_type=MESH,
-        )
-        here = at_home & (place.group == g)
-        pl.when(here)(lambda: stay(w, 0).wait())
-        pl.when(jnp.logical_not(here))(lambda: arrival.wait_recv())
-
-    waited = set()
-    for k, (w, s) in enumerate(tasks):
-        if k + 1 < len(tasks):
-            for way in range(n_c):
-                x_load(k + 1, way).start()
-        if w not in waited:
-            y_loads[w].wait()
-            waited.add(w)
-        for way in range(n_c):
-            x_load(k, way).wait()
-            value = tn_dot(x_s[k % 2, way], y_s[w][...])
-            if s:
-                hop(w, way, s - 1).wait_recv()
-                value = value + held[w][way, s - 1].astype(jnp.float32)
-            ref = source(w, way, s)
-            ref[...] = value.astype(jnp.bfloat16)
-            if s < n_dp - 1:
-                hop(w, way, s).start()
-            else:
-                here = at_home & (ctx == way)
-                pl.when(here)(lambda w=w, way=way: stay(w, way).start())
-                pl.when(jnp.logical_not(here))(lambda w=w, way=way: deliver(w, way).start())
-    for w in range(count):
-        for g in range(sz.seqs):
-            arrived(w, g)
-        total = landed[w][0].astype(jnp.float32)
-        for g in range(1, sz.seqs):
-            total = total + landed[w][g].astype(jnp.float32)
-        outs[w][...] = total
-    for w in range(count):
-        for way in range(n_c):
-            for s in range(n_dp - 1):
-                hop(w, way, s).wait_send()
-            here = at_home & (ctx == way)
-            pl.when(jnp.logical_not(here))(lambda w=w, way=way: deliver(w, way).wait_send())
-
-
-def run_grads(sz, n_dp, xs, ys):
-    bf16, count, dma = jnp.bfloat16, len(xs), pltpu.SemaphoreType.DMA
-    slots = n_dp * sz.n_context
-    depth = sz.width // slots
-    if depth % 128:
-        xs = [x.reshape(sz.seq_len, slots, depth).transpose(1, 0, 2) for x in xs]
-    else:
-        xs = [x[None] for x in xs]
+    for w in range(1 + count):
+        outs[w][...] = deliver.total(w)
+    for copy in saves:
+        copy.wait()
+    grads.finish()
+    deliver.finish()
+    plane.finish()
+    line.finish()
+
+
+def run_grads(sz, n_dp, gate_sum, low, joined, adapter, xs, ys):
+    count, bf16, f32, dma = len(xs), jnp.bfloat16, jnp.float32, pltpu.SemaphoreType.DMA
+    shape = jax.ShapeDtypeStruct
+    depth = sz.width // (n_dp * sz.n_context)
     wide = [y.shape[1] for y in ys]
-    ways, steps = sz.n_context, n_dp - 1
+    all_wide = [gate_sum.shape[2]] + wide
+    slots, columns = joined.shape[0], joined.shape[2]
+    unit = 16 * sz.half * SUM_PARTS
+    total_rows = -(-(columns + 16) // unit) * unit
     return pl.pallas_call(
         partial(grads_kernel, sz, n_dp, count),
-        out_shape=[jax.ShapeDtypeStruct((depth, n), jnp.float32) for n in wide],
-        in_specs=[any_spec()] * (2 * count),
-        out_specs=[full_spec()] * count,
-        scratch_shapes=[pltpu.VMEM((sz.seq_len, n), bf16) for n in wide]
-        + [pltpu.VMEM((ways, depth, n), bf16) for n in wide]
-        + [pltpu.VMEM((ways, steps, depth, n), bf16) for n in wide]
-        + [pltpu.VMEM((sz.seqs, depth, n), bf16) for n in wide]
+        out_shape=[shape((depth, n), f32) for n in all_wide]
         + [
-            pltpu.VMEM((2, ways, sz.seq_len, depth), bf16),
-            dma((count,)),
-            dma((2, ways)),
-            dma((count, ways, steps)),
-            dma((count, ways, steps)),
-            dma((count, ways)),
-            dma((count, sz.seqs)),
-            dma((count,)),
+            shape((sz.seqs, sz.block, sz.width), f32),
+            shape((columns, sz.width), f32),
+            shape((16, sz.width), f32),
+            shape((slots,) + low.shape, bf16),
+        ],
+        in_specs=[any_spec(), full_spec()] + [any_spec()] * (2 + 2 * count),
+        out_specs=[full_spec()] * (2 + count) + [any_spec()] * 3,
+        scratch_shapes=GradRing.scratch(sz, n_dp, wide)
+        + Deliver.scratch(sz, n_dp, all_wide)
+        + PlaneRows.scratch(n_dp)
+        + LineSum.scratch(sz, SUM_PARTS, total_rows // (sz.half * SUM_PARTS))
+        + [
+            pltpu.VMEM((total_rows, sz.width), f32),
+            pltpu.VMEM((n_dp * (sz.rows + 16), sz.width), bf16),
+            pltpu.VMEM((n_dp * sz.rows, columns), bf16),
+            pltpu.VMEM((columns, sz.width), bf16),
+            pltpu.VMEM((sz.seqs, sz.block, sz.width), bf16),
+            pltpu.VMEM((sz.block, sz.width), bf16),
+            dma((n_dp, 2)),
+            dma((n_dp,)),
+            dma,
+            dma((2,)),
+            dma((2,)),
         ],
         compiler_params=pltpu.CompilerParams(
             collective_id=8, has_side_effects=True, vmem_limit_bytes=VMEM_BYTES
@@ -1285,7 +1909,7 @@
             flops=2 * sz.seq_len * sz.width * sum(wide), bytes_accessed=60 << 20, transcendentals=0
         ),
         name="grads",
-    )(*xs, *ys)
+    )(gate_sum, low, joined, adapter, *[slot_columns(sz, n_dp, x) for x in xs], *ys)
 
 
 def shards(
@@ -1315,29 +1939,6 @@
     heads_here = qkv_weight.shape[1]
     head_dim = qkv_weight.shape[2] // 3
     ff_here = down_weight.shape[0]
-    pair_swap = [(i, (i + half) % n_tensor) for i in range(n_tensor)]
-    members = half * n_context
-    groups = [
-        [g * members + i for i in range(members)] for g in range(seq_count)
-    ]
-
-    def swap_in(rows):
-        own = lax.dynamic_index_in_dim(rows, group, 0, keepdims=False)
-        other = lax.dynamic_index_in_dim(rows, 1 - group, 0, keepdims=False)
-        got = lax.ppermute(other, "tensor", pair_swap)
-        first = jnp.where(group == 0, own, got)
-        second = jnp.where(group == 0, got, own)
-        return jnp.concatenate([first, second], axis=0)
-
-    def swap_out(rows):
-        first, second = rows[:block_rows], rows[block_rows:]
-        own = jnp.where(group == 0, first, second)
-        other = jnp.where(group == 0, second, first)
-        got = lax.ppermute(other, "tensor", pair_swap)
-        return jnp.stack(
-            [jnp.where(group == 0, own, got), jnp.where(group == 0, got, own)], axis=0
-        )
-
     def side_by_side(blocks):
         count, depth, columns = blocks.shape
         return blocks.transpose(1, 0, 2).reshape(depth, count * columns)
@@ -1361,9 +1962,6 @@
         split = full.reshape(half, n_context, seq_count, block_rows, model_width)
         return split.transpose(2, 0, 1, 3, 4).reshape(seq_len, model_width)
 
-    embed_rows = swap_in(embedded)
-    state_rows = swap_in(initial_state)
-    cot_rows = swap_in(cotangent)
     sz = Sizes(
         n_tensor,
         n_context,
@@ -1392,10 +1990,23 @@
         ],
         axis=0,
     )
-    adapter_all, qkv_use, out_blocks, gate_use, up_use, down_blocks = run_weights(
+    (
+        adapter_all,
+        qkv_use,
+        out_blocks,
+        gate_use,
+        up_use,
+        down_blocks,
+        embed_rows,
+        cot_rows,
+        grad_ffn,
+        embed_part,
+        current,
+    ) = run_weights(
         sz,
         n_dp,
         adapter_rows,
+        adapter_block,
         [
             qkv_weight.reshape(qkv_weight.shape[0], -1),
             output_head_weight.reshape(heads_here * head_dim, -1),
@@ -1403,6 +2014,7 @@
             gate_up_weight[:, 1],
             down_weight,
         ],
+        [embedded, initial_state, cotangent],
     )
     qkv_use = qkv_use.reshape(model_width, -1)
     gate_use = gate_use.reshape(model_width, -1)
@@ -1412,86 +2024,58 @@
         .transpose(1, 0, 2)
         .reshape(2, model_width)
     )
-    adapter_low = adapter_all[adapter_all.shape[0] // 2 :, :adapter_block].reshape(
-        model_width, model_width
-    )
     if out_blocks.shape[2] % 128:
         out_blocks = side_by_side(out_blocks)[None]
         down_blocks = side_by_side(down_blocks)[None]
     gains_f = gains_full.astype(jnp.float32)
 
-    order = jnp.arange(seq_len, dtype=jnp.int32)
-    cos_t, sin_t = rope_angles(order, head_dim)
-    cos_full = jnp.concatenate([cos_t, cos_t], axis=1)
-    sin_full = jnp.concatenate([-sin_t, sin_t], axis=1)
+    cos_full, sin_full = rope_tables(seq_len, head_dim)
     own_seq = dp_index * seq_count + group
     docs = lax.dynamic_index_in_dim(doc_ids, own_seq, 0, keepdims=False)
     begin = jnp.sum((docs[None, :] < docs[:, None]).astype(jnp.int32), axis=1)[None, :]
     steps_own = lax.dynamic_index_in_dim(recurrences, own_seq, 0, keepdims=False) - BACK
-    embed_part = jnp.dot(
-        embed_rows, adapter_low, preferred_element_type=jnp.float32
-    )
-
-    def advance(step_index, current):
+    for step_index in range(MAXR - BACK):
         (mixed,) = run_attn(
-            sz, False, current, embed_part, gains_f, cos_full, sin_full, begin,
+            sz, n_dp, False, current, embed_part, gains_f, cos_full, sin_full, begin,
             adapter_all, qkv_use, out_blocks,
         )
         active = jnp.broadcast_to((step_index < steps_own).astype(jnp.float32), (1, model_width))
-        (result,) = run_ffn(
+        (current,) = run_ffn(
             sz, False, mixed, current, active, gains_f, gate_use, up_use, down_blocks
         )
-        return result
-
-    detached = lax.fori_loop(
-        0, jnp.max(recurrences) - BACK, advance, state_rows.astype(jnp.float32)
-    )
-    (mixed_rows, adapted, feature_rows, query_hm, key_hm, value_hm, head_flat, lse) = run_attn(
-        sz, True, detached, embed_part, gains_f, cos_full, sin_full, begin,
-        adapter_all, qkv_use, out_blocks,
+    detached = current
+    (mixed_rows, adapted, feature_rows, query_hm, key_hm, value_hm, head_flat, lse, joined) = run_attn(
+        sz, n_dp, True, detached, embed_part, gains_f, cos_full, sin_full, begin,
+        adapter_all, qkv_use, out_blocks, embed_rows,
     )
     (current, ffn_input, gate_pre, up_pre, hidden) = run_ffn(
         sz, True, mixed_rows, detached, gains_f[:1], gains_f, gate_use, up_use, down_blocks
     )
-    latent_low = detached.astype(jnp.bfloat16)
-    grad_ffn = gather_rows(cot_rows)
-    grad_mixed, gain_b, grad_gate, grad_up = run_ffn_back(
-        sz, cot_rows, mixed_rows, gains_f, grad_ffn, gate_pre, up_pre, gate_use, up_use, down_blocks
+    grad_mixed, gain_b, state_out, grad_gate, grad_up, down_sum = run_ffn_back(
+        sz, n_dp, cot_rows, mixed_rows, gains_f, current, grad_ffn, gate_pre, up_pre,
+        gate_use, up_use, down_blocks, hidden,
     )
-    adapted_low, gain_a, grad_rows, grad_proj = run_attn_back(
-        sz, grad_mixed, adapted, gains_f, cos_full, sin_full, begin,
-        query_hm, key_hm, value_hm, lse, out_blocks, qkv_use,
+    grad_low, down_t, grad_rows, grad_proj, gate_sum = run_attn_back(
+        sz, n_dp, grad_mixed, adapted, gains_f, cos_full, sin_full, begin, gain_b,
+        query_hm, key_hm, value_hm, lse, out_blocks, qkv_use, ffn_input, grad_gate, down_sum,
     )
-    down_t, gate_s, up_s, qkv_s, out_t = run_grads(
+    gate_s, up_s, qkv_s, out_t, embed_out, adapter_s, gains_rows, _ = run_grads(
         sz,
         n_dp,
-        [grad_ffn, ffn_input, ffn_input, feature_rows, grad_rows],
-        [hidden, grad_gate, grad_up, grad_proj, head_flat],
+        gate_sum,
+        grad_low,
+        joined,
+        adapter_all,
+        [ffn_input, feature_rows, grad_rows],
+        [grad_up, grad_proj, head_flat],
     )
+    place_at = (dp_index * n_context + ctx_index) * gain_columns
+    gains_s = lax.dynamic_slice_in_dim(gains_rows[:2], place_at, gain_columns, 1)
     down_s = down_t.T
     out_s = out_t.T.reshape(heads_here, head_dim, -1)
     qkv_s = qkv_s.reshape(-1, heads_here, 3 * head_dim)
     gate_up_s = jnp.stack([gate_s, up_s], axis=1)
-    joined = jnp.concatenate([latent_low, embed_rows], axis=-1)
-    adapter_g = jnp.einsum("rk,rd->kd", joined, adapted_low, preferred_element_type=jnp.float32)
-    embed_out = jnp.einsum(
-        "srd,kd->srk",
-        swap_out(adapted_low),
-        adapter_low,
-        preferred_element_type=jnp.float32,
-    )
-    adapter_s = lax.psum_scatter(
-        adapter_g.astype(jnp.bfloat16), ("dp", "context"), scatter_dimension=0, tiled=True
-    )
-    gains_s = lax.psum_scatter(
-        jnp.concatenate([gain_a, gain_b]).astype(jnp.bfloat16),
-        ("dp", "context"),
-        scatter_dimension=1,
-        tiled=True,
-    )
-    adapter_s = lax.psum(adapter_s, "tensor").astype(jnp.float32)
-    gains_s = lax.psum(gains_s, "tensor").astype(jnp.float32)
-    return (swap_out(current), embed_out, adapter_s, gains_s, qkv_s, out_s, gate_up_s, down_s)
+    return (state_out, embed_out, adapter_s, gains_s, qkv_s, out_s, gate_up_s, down_s)
 
 
 def solution(mesh):

time: 1400 us -> 1280 us (0.914)
  waiting for transfers between devices: 109 us -> 0 us
  Pallas kernels: 1130 us -> 1230 us
  matrix products: 26.8 us -> 0 us
  loops' own time: 26.5 us -> 0 us
  local copies, waits for them, and re-layouts: 49 us -> 27 us
  other arithmetic: 24.2 us -> 7.55 us
    reduce_scatter x1 -> x0, waiting for transfers between devices: 63.3 us -> none  [shards(): lax.psum_scatter(adapter_g.astype(jnp.bfloat16), ('dp', 'context'), scatt...]
    pallas_call x7, Pallas kernels: 642 us -> 697 us  [the longest x4 279 us: run_attn(): pl.pallas_call(partial(attn_kernel, sz, n_dp, keep), out_shape=outs, in_s...]
    ppermute x5 -> x0, waiting for transfers between devices: 45.5 us -> none  [the longest x2 45.5 us: swap_out(): got = lax.ppermute(other, 'tensor', pair_swap)]
    pallas_call x1, Pallas kernels: 277 us -> 314 us  [run_weights(): pl.pallas_call(partial(weights_kernel, sz, n_dp), out_shape=outs, in_spec...]
    dot_general x3 -> x0, matrix products: 26.8 us -> none  [the longest x1 12.3 us: shards(): jnp.einsum('rk,rd->kd', joined, adapted_low, preferred_element_type=jnp.f...]
    another operation x1 -> x0, loops' own time: 26.5 us -> none  [shards(): lax.fori_loop(0, jnp.max(recurrences) - BACK, advance, state_rows.astype(...]
  transfers between devices with their start and end apart: 9 -> 0, of which waited for: 2 -> 0; matrix products, arithmetic and copies ran while one was open for 5% -> 0% of each run, Pallas kernels for 72% -> 0%
where the time goes in v5:
time: 1280 us; the launch traced here: 1270 us
  Pallas kernels  1230 us (96%)
  local copies, waits for them, and re-layouts  27 us (2%)
    pallas_call x1, Pallas kernels, run_weights(): pl.pallas_call(partial(weights_kernel, sz, n_dp), out_shape=outs, in_spec...  314 us
    pallas_call x4, Pallas kernels, run_attn(): pl.pallas_call(partial(attn_kernel, sz, n_dp, keep), out_shape=outs, in_s...  279 us
    pallas_call x1, Pallas kernels, run_grads(): pl.pallas_call(partial(grads_kernel, sz, n_dp, count), out_shape=[shape((...  236 us
    pallas_call x4, Pallas kernels, run_ffn(): pl.pallas_call(partial(ffn_kernel, sz, keep), out_shape=outs, in_specs=[f...  221 us
    pallas_call x1, Pallas kernels, run_attn_back(): pl.pallas_call(partial(attn_back_kernel, sz, n_dp), out_shape=[shape((sz....  103 us
    pallas_call x1, Pallas kernels, run_ffn_back(): pl.pallas_call(partial(ffn_back_kernel, sz, n_dp), out_shape=[shape((sz.r...  79.2 us

profile of v5, /device:TPU:1, one launch (start us, length us, event | category | flops | bytes accessed | tf_op | source)
XLA Modules:
  0.0 1269.1 jit_solution(15346824656170703652)
XLA Ops:
  5.6 2.1 copy.34
  7.8 3.4 fusion.1.refs_0_
  11.2 2.0 fusion.3
  14.5 314.2 %weights.1 = (bf16[8,544,2048]{2,1,0:T(8,128)(2,1)}, bf16[8,256,1536]{2,1,0:T(8,128)(2,1)}, bf16[8,512,256]{2,1,0:T(8,128)(2,1)}, bf16[8,256,1408]{2,1,0:T(8,128...) custom-call(bf16[544,2048]{1,0:T(8,128)(2,1)} %fusion.1.refs_0_, ...), custom_call_target="tpu_custom_call" | custom-call | tf_op jit(solution)/shard_map/weights/pallas_call | solution.py:1007
  328.7 1.4 fusion.2
  330.7 100.3 %attn_round.3.refs_0_ = f32[256,2048]{1,0:T(8,128)} custom-call(f32[256,2048]{1,0:T(8,128)} %get-tuple-element.52.refs_0_.refs_1_, f32[256,2048]{1,0:T(8,128)} %get-tuple-element.53.refs_1_, f32[2,2048]{1,0:T(2,128)} %bitcast.41, f32[1024,128]{1,0:T(8,128)} %constant.56.clone.refs_3_, f32[1024,128]{1,0:T(8,128)} %constant.57.clone.refs_4_, ...), custom_call_target="tpu_custom_call" | custom-call | flops 8589934592 | bytes 20971520 | tf_op jit(solution)/shard_map/attn_round/pallas_call | solution.py:527
  430.9 63.3 %ffn_round.3.refs_0_.refs_1_ = f32[256,2048]{1,0:T(8,128)} custom-call(f32[256,2048]{1,0:T(8,128)} %attn_round.3.refs_0_, f32[256,2048]{1,0:T(8,128)} %get-tuple-element.52.refs_0_.refs_1_, f32[1,2048]{1,0:T(1,128)} %broadcast_in_dim.28.refs_2_, f32[2,2048]{1,0:T(2,128)} %bitcast.42, bf16[2048,1408]{1,0:T(8,128)(2,1)} %bitcast.59, ...), custom_call_target="tpu_custom_call" | custom-call | flops 17716740096 | bytes 20971520 | tf_op jit(solution)/shard_map/ffn_round/pallas_call | solution.py:654
  494.3 58.1 %attn_round.4.refs_0_ = f32[256,2048]{1,0:T(8,128)} custom-call(f32[256,2048]{1,0:T(8,128)} %ffn_round.3.refs_0_.refs_1_, f32[256,2048]{1,0:T(8,128)} %get-tuple-element.53.refs_1_, f32[2,2048]{1,0:T(2,128)} %bitcast.43, f32[1024,128]{1,0:T(8,128)} %constant.56.clone.refs_3_, f32[1024,128]{1,0:T(8,128)} %constant.57.clone.refs_4_, s32[1,1024]{1,0:T(1,128)} %bitcast.53, ...), custom_call_target="tpu_custom_call" | custom-call | flops 8589934592 | bytes 20971520 | tf_op jit(solution)/shard_map/attn_round/pallas_call | solution.py:527
  552.3 52.3 %ffn_round.4.refs_0_.refs_1_ = f32[256,2048]{1,0:T(8,128)} custom-call(f32[256,2048]{1,0:T(8,128)} %attn_round.4.refs_0_, f32[256,2048]{1,0:T(8,128)} %ffn_round.3.refs_0_.refs_1_, f32[1,2048]{1,0:T(1,128)} %broadcast_in_dim.29.refs_2_, f32[2,2048]{1,0:T(2,128)} %bitcast.44, bf16[2048,1408]{1,0:T(8,128)(2,1)} %bitcast.60, bf16[2048,1408]{1,0:T(8,128)(2,1)} %bitcast.65, ...), custom_call_target="tpu_custom_call" | custom-call | flops 17716740096 | bytes 20971520 | tf_op jit(solution)/shard_map/ffn_round/pallas_call | solution.py:654
  604.7 59.8 %attn_round.5.refs_0_ = f32[256,2048]{1,0:T(8,128)} custom-call(f32[256,2048]{1,0:T(8,128)} %ffn_round.4.refs_0_.refs_1_, f32[256,2048]{1,0:T(8,128)} %get-tuple-element.53.refs_1_, f32[2,2048]{1,0:T(2,128)} %bitcast.45, f32[1024,128]{1,0:T(8,128)} %constant.56.clone.refs_3_, f32[1024,128]{1,0:T(8,128)} %constant.57.clone.refs_4_, s32[1,1024]{1,0:T(1,128)} %bitcast.54, ...), custom_call_target="tpu_custom_call" | custom-call | flops 8589934592 | bytes 20971520 | tf_op jit(solution)/shard_map/attn_round/pallas_call | solution.py:527
  664.5 53.1 %ffn_round.5.refs_0_.refs_1_ = f32[256,2048]{1,0:T(8,128)} custom-call(f32[256,2048]{1,0:T(8,128)} %attn_round.5.refs_0_, f32[256,2048]{1,0:T(8,128)} %ffn_round.4.refs_0_.refs_1_, f32[1,2048]{1,0:T(1,128)} %broadcast_in_dim.30.refs_2_, f32[2,2048]{1,0:T(2,128)} %bitcast.46, bf16[2048,1408]{1,0:T(8,128)(2,1)} %bitcast.61, bf16[2048,1408]{1,0:T(8,128)(2,1)} %bitcast.66, ...), custom_call_target="tpu_custom_call" | custom-call | flops 17716740096 | bytes 20971520 | tf_op jit(solution)/shard_map/ffn_round/pallas_call | solution.py:654
  717.6 60.8 %attn_keep.1 = (f32[256,2048]{1,0:T(8,128)}, f32[256,2048]{1,0:T(8,128)}, bf16[1024,2048]{1,0:T(8,128)(2,1)}, bf16[4,1024,128]{2,1,0:T(8,128)(2,1)}, bf16[4,1024...) custom-call(f32[256,2048]{1,0:T(8,128)} %ffn_round.5.refs_0_.refs_1_, ...), custom_call_target="tpu_custom_call" | custom-call | flops 8589934592 | bytes 20971520 | tf_op jit(solution)/shard_map/attn_keep/pallas_call | solution.py:527
  778.4 52.6 %ffn_keep.1 = (f32[256,2048]{1,0:T(8,128)}, bf16[1024,2048]{1,0:T(8,128)(2,1)}, bf16[1024,1408]{1,0:T(8,128)(2,1)}, bf16[1024,1408]{1,0:T(8,128)(2,1)}, bf16[1024,1408]{1,0:T(8,128)(2,1)}) custom-call(f32[256,2048]{1,0:T(8,128)} %get-tuple-element.61.refs_0_.refs_1_, f32[256,2048]{1,0:T(8,128)} %ffn_round.5.refs_0_.refs_1_, f32[1,2048]{1,0:T(1,128)} %bitcast.58, ...), custom_call_target="tpu_custom_call" | custom-call | flops 17716740096 | bytes 20971520 | tf_op jit(solution)/shard_map/ffn_keep/pallas_call | solution.py:654
  831.0 79.2 %ffn_back.1 = (f32[256,2048]{1,0:T(8,128)}, f32[1,2048]{1,0:T(1,128)}, f32[2,128,2048]{2,1,0:T(8,128)}, bf16[1024,1408]{1,0:T(8,128)(2,1)}, bf16[1024,1408]{1,0:T(8,128)(2,1)}, /*index=5*/bf16[2,256,1408]{2,1,0:T(8,128)(2,1)}) custom-call(bf16[256,2048]{1,0:T(8,128)(2,1)} %get-tuple-element.51.refs_0_, f32[256,2048]{1,0:T(8,128)} %get-tuple-element.61.refs_0_.refs_1_, ...), custom_call_target="tpu_custom_call" | custom-call | flops 23622320128 | bytes 41943040 | tf_op jit(solution)/shard_map/ffn_back/pallas_call | solution.py:1335
  910.2 103.4 %attn_back.1 = (bf16[272,2048]{1,0:T(8,128)(2,1)}, f32[256,1408]{1,0:T(8,128)}, bf16[1024,2048]{1,0:T(8,128)(2,1)}, bf16[1024,1536]{1,0:T(8,128)(2,1)}, bf16[2,256,1408]{2,1,0:T(8,128)(2,1)}) custom-call(f32[256,2048]{1,0:T(8,128)} %get-tuple-element.68.refs_0_, f32[256,2048]{1,0:T(8,128)} %get-tuple-element.69.refs_1_, f32[2,2048]{1,0:T(2,128)} %bitcast.50, ...), custom_call_target="tpu_custom_call" | custom-call | flops 12884901888 | bytes 31457280 | tf_op jit(solution)/shard_map/attn_back/pallas_call | solution.py:1521
  1013.6 235.6 %grads.1 = (f32[256,1408]{1,0:T(8,128)}, f32[256,1408]{1,0:T(8,128)}, f32[256,1536]{1,0:T(8,128)}, f32[256,512]{1,0:T(8,128)}, f32[2,128,2048]{2,1,0:T(8,128)}, ...) custom-call(bf16[2,256,1408]{2,1,0:T(8,128)(2,1)} %get-tuple-element.78.refs_0_, ...), custom_call_target="tpu_custom_call" | custom-call | flops 14495514624 | bytes 62914560 | tf_op jit(solution)/shard_map/grads/pallas_call | solution.py:1877
  1250.8 2.0 copy.31
  1252.8 1.5 copy.30
  1254.4 1.6 reshape.61
  1256.0 1.5 pad_maximum_fusion
  1257.6 3.8 copy.29
  1261.4 1.3 copy.40
  1265.1 1.6 copy-done.3
  1266.7 2.0 copy.42
  (28 shorter events, 10.1 us)
Async XLA Ops:
  0.6 1.9 copy-start
  7.8 3.4 copy-start.2
  1013.6 239.2 %copy-start.7 = (f32[256,1408]{1,0:T(8,128)S(1)}, f32[256,1408]{1,0:T(8,128)}, u32[]{:S(2)}) copy-start(f32[256,1408]{1,0:T(8,128)} %get-tuple-element.93) | copy-start | bytes 4325380
  1249.2 5.1 copy-start.6
  1254.4 1.7 copy-start.8
  1257.6 3.8 copy-start.4
  1261.4 2.3 copy-start.5
  1263.7 2.9 copy-start.3
  1266.7 2.0 copy-start.1

commit v6 on v5

--- a/solution.py
+++ b/solution.py
@@ -168,14 +168,18 @@
         rows = place.block(place.behind(q), 1 - place.ctx, j)
         self.copy(place.sz.half - 1 + q, j, rows).wait_recv()
 
-    def finish(self):
+    def passed_on(self, j):
         place, half = self.place, self.place.sz.half
-        for j in range(place.sz.seqs):
-            for kind in range(half):
+        for q in range(1, half):
+            rows = place.block(place.behind(q), place.ctx, j)
+            self.copy(half - 1 + q, j, rows).wait_send()
+
+    def finish(self, forwards=True):
+        for j in range(self.place.sz.seqs):
+            for kind in range(self.place.sz.half):
                 self.copy(kind, j, self.own(j)).wait_send()
-            for q in range(1, half):
-                rows = place.block(place.behind(q), place.ctx, j)
-                self.copy(half - 1 + q, j, rows).wait_send()
+            if forwards:
+                self.passed_on(j)
 
 
 class Scatter:
@@ -667,6 +671,204 @@
     )(mixed, latent, active, gains, gate, up, down)
 
 
+def round_kernel(sz, *refs):
+    (latent, active, gains, cos_t, sin_t, begin) = refs[:6]
+    (embed_hbm, adapter_hbm, qkv_hbm, out_hbm, gate_hbm, up_hbm, down_hbm, result) = refs[6:14]
+    (wa, wqkv, wout, wg, wu, mixed, rows_s, q_s, k_s, v_s, head_s) = refs[14:25]
+    load_embed, load_a, load_qkv, load_out, load_gu, load_down = refs[25:31]
+    gather_refs, again_refs, scatter_refs = refs[31:33], refs[33:35], refs[35:43]
+
+    place = Place(sz)
+    embed_load = pltpu.make_async_copy(embed_hbm, mixed, load_embed)
+    a_loads = adapter_loads(adapter_hbm, wa, load_a)
+    qkv_load = pltpu.make_async_copy(qkv_hbm, wqkv, load_qkv)
+    out_loads = column_loads(out_hbm, wout, load_out)
+    gate_load = pltpu.make_async_copy(gate_hbm, wg, load_gu.at[0])
+    up_load = pltpu.make_async_copy(up_hbm, wu, load_gu.at[1])
+    wd = wa.at[pl.ds(0, sz.ff)]
+    down_loads = column_loads(down_hbm, wd, load_down)
+    embed_load.start()
+    for group in a_loads:
+        for copy in group:
+            copy.start()
+    qkv_load.start()
+    for copy in out_loads:
+        copy.start()
+    place.enter()
+    gather = Gather(place, rows_s, *gather_refs)
+    again = Gather(place, rows_s, *again_refs)
+    scatter = Scatter(place, *scatter_refs)
+
+    low = latent[...].astype(jnp.bfloat16)
+    columns = sz.width // len(a_loads)
+    square = None
+    embed_load.wait()
+    for n, group in enumerate(a_loads):
+        for copy in group:
+            copy.wait()
+        cols = pl.ds(n * columns, columns)
+        chunk = nn_dot(low, wa[:, cols]) + mixed[:, cols]
+        mixed[:, cols] = chunk
+        here = jnp.sum(chunk * chunk, axis=-1, keepdims=True)
+        square = here if square is None else square + here
+    factor = lax.rsqrt(square / sz.width + norm_eps)
+    for j in range(sz.seqs):
+        span = slice(j * sz.block, (j + 1) * sz.block)
+        normed = (mixed[span, :] * factor[span]) * gains[0:1, :]
+        rows_s[gather.own(j), :] = normed.astype(jnp.bfloat16)
+        gather.start(j)
+    gate_load.start()
+    up_load.start()
+    for copy in down_loads:
+        copy.start()
+    qkv_load.wait()
+    pair = min(2, sz.heads)
+    d = sz.head_dim
+
+    def project(q, j):
+        rows = place.tile(q, j)
+        x = rows_s[rows, :]
+        cos_here, sin_here = cos_t[rows, :], sin_t[rows, :]
+        for h0 in range(0, sz.heads, pair):
+            proj = nn_dot(x, wqkv[:, 3 * d * h0 : 3 * d * (h0 + pair)])
+            for h in range(pair):
+                at = 3 * d * h
+                q_s[h0 + h, rows, :] = turn(proj[:, at : at + d], cos_here, sin_here).astype(
+                    jnp.bfloat16
+                )
+                k_s[h0 + h, rows, :] = turn(
+                    proj[:, at + d : at + 2 * d], cos_here, sin_here
+                ).astype(jnp.bfloat16)
+                v_s[h0 + h, rows, :] = proj[:, at + 2 * d : at + 3 * d].astype(jnp.bfloat16)
+
+    def attend(q, j):
+        rows = place.tile(q, j)
+        first = (place.ahead(q) + j * sz.half) * sz.tile
+        length = (j + 1) * sz.half * sz.tile
+        start = begin[:, pl.ds(pl.multiple_of(first, sz.tile), sz.tile)]
+        key_at = lax.broadcasted_iota(jnp.int32, (length, sz.tile), 0)
+        query_at = first + lax.broadcasted_iota(jnp.int32, (1, sz.tile), 1)
+        allowed = (key_at >= start) & (key_at <= query_at)
+
+        def head(h, carry):
+            scores = nt_dot(k_s[h, 0:length, :], q_s[h, rows, :])
+            scores = jnp.where(allowed, scores * (LOG2E / math.sqrt(d)), masked_score)
+            top = jnp.max(scores, axis=0, keepdims=True)
+            weight = jnp.exp2(scores - top)
+            total = jnp.sum(weight, axis=0, keepdims=True)
+            mixed_t = tn_dot(v_s[h, 0:length, :], weight.astype(jnp.bfloat16))
+            result = jnp.transpose(mixed_t / total)
+            head_s[rows, pl.ds(pl.multiple_of(h * d, d), d)] = result.astype(jnp.bfloat16)
+            return carry
+
+        lax.fori_loop(0, sz.heads, head, 0)
+
+    def give(q, j):
+        rows = place.tile(q, j)
+        scatter.part[...] = nn_dot(head_s[rows, :], wout[...])
+        scatter.give(q, j)
+
+    far = range(1, sz.half)
+    for j in range(sz.seqs):
+        gather.wait_near(j)
+        project(0, j)
+    for copy in out_loads:
+        copy.wait()
+    for j in range(sz.seqs):
+        for q in far:
+            gather.forward(q, j)
+        for q in far:
+            gather.wait_far(sz.half - q, j)
+            project(q, j)
+        for q in far:
+            attend(q, j)
+            give(q, j)
+        attend(0, j)
+        gather.passed_on(j)
+        for q in far:
+            scatter.onward(q, j)
+        give(0, j)
+    gather.finish(forwards=False)
+    for j in range(sz.seqs):
+        span = slice(j * sz.block, (j + 1) * sz.block)
+        rows = mixed[span, :] + scatter.total(j)
+        mixed[span, :] = rows
+        normed = (rows * rms_factor(rows)) * gains[1:2, :]
+        rows_s[again.own(j), :] = normed.astype(jnp.bfloat16)
+        again.start(j)
+    scatter.finish()
+    gate_load.wait()
+    up_load.wait()
+    for copy in down_loads:
+        copy.wait()
+
+    def work(q, j):
+        x = rows_s[place.tile(q, j), :]
+        gate = nn_dot(x, wg[...])
+        up = nn_dot(x, wu[...])
+        hidden = (gate / (1.0 + jnp.exp(-gate)) * up).astype(jnp.bfloat16)
+        scatter.part[...] = nn_dot(hidden, wd[...])
+        scatter.give(q, j)
+
+    for j in range(sz.seqs):
+        again.wait_near(j)
+        work(0, j)
+    for j in range(sz.seqs):
+        for q in far:
+            again.forward(q, j)
+        for q in far:
+            again.wait_far(sz.half - q, j)
+            work(q, j)
+        for q in far:
+            scatter.onward(q, j)
+    again.finish()
+    for j in range(sz.seqs):
+        span = slice(j * sz.block, (j + 1) * sz.block)
+        total = mixed[span, :] + scatter.total(j)
+        result[span, :] = jnp.where(active[...] > 0, total, latent[span, :])
+    scatter.finish()
+
+
+def run_round(sz, latent, active, gains, cos_t, sin_t, begin, embed, adapter, qkv, out, gate, up, down):
+    f32, bf16, dma = jnp.float32, jnp.bfloat16, pltpu.SemaphoreType.DMA
+    heads_shape = (sz.heads, sz.seq_len, sz.head_dim)
+    return pl.pallas_call(
+        partial(round_kernel, sz),
+        out_shape=jax.ShapeDtypeStruct((sz.rows, sz.width), f32),
+        in_specs=[full_spec()] * 6 + [any_spec()] * 7,
+        out_specs=full_spec(),
+        scratch_shapes=[
+            pltpu.VMEM((sz.width, sz.width), bf16),
+            pltpu.VMEM(qkv.shape, bf16),
+            pltpu.VMEM((sz.heads * sz.head_dim, sz.width), bf16),
+            pltpu.VMEM(gate.shape, bf16),
+            pltpu.VMEM(up.shape, bf16),
+            pltpu.VMEM((sz.rows, sz.width), f32),
+            pltpu.VMEM((sz.seq_len, sz.width), bf16),
+            pltpu.VMEM(heads_shape, bf16),
+            pltpu.VMEM(heads_shape, bf16),
+            pltpu.VMEM(heads_shape, bf16),
+            pltpu.VMEM((sz.seq_len, sz.heads * sz.head_dim), bf16),
+            dma,
+            dma((4, adapter.shape[0] // 2)),
+            dma,
+            dma((out.shape[0],)),
+            dma((2,)),
+            dma((down.shape[0],)),
+        ]
+        + Gather.scratch(sz)
+        + Gather.scratch(sz)
+        + Scatter.scratch(sz),
+        compiler_params=pltpu.CompilerParams(
+            collective_id=1, has_side_effects=True, vmem_limit_bytes=VMEM_BYTES
+        ),
+        cost_estimate=pl.CostEstimate(
+            flops=8 * sz.seq_len * sz.width * sz.ff, bytes_accessed=40 << 20, transcendentals=0
+        ),
+        name="round",
+    )(latent, active, gains, cos_t, sin_t, begin, embed, adapter, qkv, out, gate, up, down)
+
+
 def other_group(place):
     return (place.dp, (1 - place.group) * place.sz.half + place.part, place.ctx)
 
@@ -762,7 +964,6 @@
         )
 
     for i in range(3):
-        swap(i).start()
         keep(i).start()
     gather = Gather(place, cot_all, *gather_refs)
 
@@ -879,11 +1080,15 @@
     around(0).start()
     own = pltpu.make_async_copy(own_rows, adapter_rows(0, ctx, part), own_sem.at[count])
     own.start()
-    for w in range(count):
+
+    def start_move(w):
         for g in range(sz.seqs):
             here = at_home & (place.group == g)
             pl.when(jnp.logical_not(here))(lambda w=w, g=g: move(w, g).start())
         pl.when(at_home)(lambda w=w: stay(w).start())
+
+    start_move(0)
+    start_move(1)
     for kind in range(half):
         across(kind, 0).start()
 
@@ -923,9 +1128,14 @@
             else:
                 hopped(w, way, s - 1).wait_recv()
             hop(w, way, s).start()
+        if s == 0 and w + 2 < count:
+            start_move(w + 2)
+        if s == 0 and w == count - 2:
+            for i in range(3):
+                swap(i).start()
         if done < steps:
             adapter_step(done)
-        if done == 5:
+        if s == min(1, steps - 1) and w == count - 1:
             for i in range(3):
                 keep(i).wait()
                 swapped(i).wait_recv()
@@ -1992,8 +2202,8 @@
     )
     (
         adapter_all,
+        out_blocks,
         qkv_use,
-        out_blocks,
         gate_use,
         up_use,
         down_blocks,
@@ -2008,8 +2218,8 @@
         adapter_rows,
         adapter_block,
         [
+            output_head_weight.reshape(heads_here * head_dim, -1),
             qkv_weight.reshape(qkv_weight.shape[0], -1),
-            output_head_weight.reshape(heads_here * head_dim, -1),
             gate_up_weight[:, 0],
             gate_up_weight[:, 1],
             down_weight,
@@ -2035,13 +2245,10 @@
     begin = jnp.sum((docs[None, :] < docs[:, None]).astype(jnp.int32), axis=1)[None, :]
     steps_own = lax.dynamic_index_in_dim(recurrences, own_seq, 0, keepdims=False) - BACK
     for step_index in range(MAXR - BACK):
-        (mixed,) = run_attn(
-            sz, n_dp, False, current, embed_part, gains_f, cos_full, sin_full, begin,
-            adapter_all, qkv_use, out_blocks,
-        )
         active = jnp.broadcast_to((step_index < steps_own).astype(jnp.float32), (1, model_width))
-        (current,) = run_ffn(
-            sz, False, mixed, current, active, gains_f, gate_use, up_use, down_blocks
+        current = run_round(
+            sz, current, active, gains_f, cos_full, sin_full, begin, embed_part,
+            adapter_all, qkv_use, out_blocks, gate_use, up_use, down_blocks,
         )
     detached = current
     (mixed_rows, adapted, feature_rows, query_hm, key_hm, value_hm, head_flat, lse, joined) = run_attn(

time: 1280 us -> 1200 us (0.938)
  Pallas kernels: 1230 us -> 1160 us
    pallas_call x0 -> x3, Pallas kernels: none -> 327 us  [run_round(): pl.pallas_call(partial(round_kernel, sz), out_shape=jax.ShapeDtypeStruct(...]
    pallas_call x4 -> x1, Pallas kernels: 279 us -> 60.7 us  [run_attn(): pl.pallas_call(partial(attn_kernel, sz, n_dp, keep), out_shape=outs, in_s...]
    pallas_call x4 -> x1, Pallas kernels: 221 us -> 53 us  [run_ffn(): pl.pallas_call(partial(ffn_kernel, sz, keep), out_shape=outs, in_specs=[f...]
    pallas_call x1, Pallas kernels: 314 us -> 290 us  [run_weights(): pl.pallas_call(partial(weights_kernel, sz, n_dp), out_shape=outs, in_spec...]
where the time goes in v6:
time: 1200 us; the launch traced here: 1190 us
  Pallas kernels  1160 us (97%)
  local copies, waits for them, and re-layouts  27 us (2%)
    pallas_call x3, Pallas kernels, run_round(): pl.pallas_call(partial(round_kernel, sz), out_shape=jax.ShapeDtypeStruct(...  327 us
    pallas_call x1, Pallas kernels, run_weights(): pl.pallas_call(partial(weights_kernel, sz, n_dp), out_shape=outs, in_spec...  290 us
    pallas_call x1, Pallas kernels, run_grads(): pl.pallas_call(partial(grads_kernel, sz, n_dp, count), out_shape=[shape((...  243 us
    pallas_call x1, Pallas kernels, run_attn_back(): pl.pallas_call(partial(attn_back_kernel, sz, n_dp), out_shape=[shape((sz....  103 us
    pallas_call x1, Pallas kernels, run_ffn_back(): pl.pallas_call(partial(ffn_back_kernel, sz, n_dp), out_shape=[shape((sz.r...  79.1 us
    pallas_call x1, Pallas kernels, run_attn(): pl.pallas_call(partial(attn_kernel, sz, n_dp, keep), out_shape=outs, in_s...  60.7 us
    pallas_call x1, Pallas kernels, run_ffn(): pl.pallas_call(partial(ffn_kernel, sz, keep), out_shape=outs, in_specs=[f...  53 us

profile of v6, /device:TPU:1, one launch (start us, length us, event | category | flops | bytes accessed | tf_op | source)
XLA Modules:
  0.0 1193.1 jit_solution(8845973267419088129)
XLA Ops:
  0.7 1.2 dynamic_slice.11
  5.6 2.1 copy.34
  7.8 3.4 fusion.1.refs_0_
  11.2 2.0 fusion.3
  13.2 1.3 copy_bitcast_fusion
  14.5 290.4 %weights.1 = (bf16[8,544,2048]{2,1,0:T(8,128)(2,1)}, bf16[8,512,256]{2,1,0:T(8,128)(2,1)}, bf16[8,256,1536]{2,1,0:T(8,128)(2,1)}, bf16[8,256,1408]{2,1,0:T(8,128...) custom-call(bf16[544,2048]{1,0:T(8,128)(2,1)} %fusion.1.refs_0_, ...), custom_call_target="tpu_custom_call" | custom-call | tf_op jit(solution)/shard_map/weights/pallas_call | solution.py:1217
  304.9 1.4 fusion.2
  306.9 113.7 %round.3.refs_0_ = f32[256,2048]{1,0:T(8,128)} custom-call(f32[256,2048]{1,0:T(8,128)} %get-tuple-element.52.refs_0_, f32[1,2048]{1,0:T(1,128)} %broadcast_in_dim.27.refs_1_, f32[2,2048]{1,0:T(2,128)} %bitcast.42, f32[1024,128]{1,0:T(8,128)} %constant.56.clone.refs_3_, f32[1024,128]{1,0:T(8,128)} %constant.57.clone.refs_4_, s32[1,1024]{1,0:T(1,128)} %bitcast.50, ...), custom_call_target="tpu_custom_call" | custom-call | flops 23622320128 | bytes 41943040 | tf_op jit(solution)/shard_map/round/pallas_call | solution.py:835
  420.6 106.8 %round.4.refs_0_ = f32[256,2048]{1,0:T(8,128)} custom-call(f32[256,2048]{1,0:T(8,128)} %round.3.refs_0_, f32[1,2048]{1,0:T(1,128)} %broadcast_in_dim.29.refs_1_, f32[2,2048]{1,0:T(2,128)} %bitcast.43, f32[1024,128]{1,0:T(8,128)} %constant.56.clone.refs_3_, f32[1024,128]{1,0:T(8,128)} %constant.57.clone.refs_4_, s32[1,1024]{1,0:T(1,128)} %bitcast.51, ...), custom_call_target="tpu_custom_call" | custom-call | flops 23622320128 | bytes 41943040 | tf_op jit(solution)/shard_map/round/pallas_call | solution.py:835
  527.4 106.9 %round.5.refs_0_.refs_1_ = f32[256,2048]{1,0:T(8,128)} custom-call(f32[256,2048]{1,0:T(8,128)} %round.4.refs_0_, f32[1,2048]{1,0:T(1,128)} %broadcast_in_dim.30.refs_1_, f32[2,2048]{1,0:T(2,128)} %bitcast.44, f32[1024,128]{1,0:T(8,128)} %constant.56.clone.refs_3_, f32[1024,128]{1,0:T(8,128)} %constant.57.clone.refs_4_, s32[1,1024]{1,0:T(1,128)} %bitcast.52, ...), custom_call_target="tpu_custom_call" | custom-call | flops 23622320128 | bytes 41943040 | tf_op jit(solution)/shard_map/round/pallas_call | solution.py:835
  634.3 60.7 %attn_keep.1 = (f32[256,2048]{1,0:T(8,128)}, f32[256,2048]{1,0:T(8,128)}, bf16[1024,2048]{1,0:T(8,128)(2,1)}, bf16[4,1024,128]{2,1,0:T(8,128)(2,1)}, bf16[4,1024...) custom-call(f32[256,2048]{1,0:T(8,128)} %round.5.refs_0_.refs_1_, ...), custom_call_target="tpu_custom_call" | custom-call | flops 8589934592 | bytes 20971520 | tf_op jit(solution)/shard_map/attn_keep/pallas_call | solution.py:531
  695.0 53.0 %ffn_keep.1 = (f32[256,2048]{1,0:T(8,128)}, bf16[1024,2048]{1,0:T(8,128)(2,1)}, bf16[1024,1408]{1,0:T(8,128)(2,1)}, bf16[1024,1408]{1,0:T(8,128)(2,1)}, bf16[1024,1408]{1,0:T(8,128)(2,1)}) custom-call(f32[256,2048]{1,0:T(8,128)} %get-tuple-element.61.refs_0_.refs_1_, f32[256,2048]{1,0:T(8,128)} %round.5.refs_0_.refs_1_, f32[1,2048]{1,0:T(1,128)} %bitcast.55, ...), custom_call_target="tpu_custom_call" | custom-call | flops 17716740096 | bytes 20971520 | tf_op jit(solution)/shard_map/ffn_keep/pallas_call | solution.py:658
  748.0 79.1 %ffn_back.1 = (f32[256,2048]{1,0:T(8,128)}, f32[1,2048]{1,0:T(1,128)}, f32[2,128,2048]{2,1,0:T(8,128)}, bf16[1024,1408]{1,0:T(8,128)(2,1)}, bf16[1024,1408]{1,0:T(8,128)(2,1)}, /*index=5*/bf16[2,256,1408]{2,1,0:T(8,128)(2,1)}) custom-call(bf16[256,2048]{1,0:T(8,128)(2,1)} %get-tuple-element.51.refs_0_, f32[256,2048]{1,0:T(8,128)} %get-tuple-element.61.refs_0_.refs_1_, ...), custom_call_target="tpu_custom_call" | custom-call | flops 23622320128 | bytes 41943040 | tf_op jit(solution)/shard_map/ffn_back/pallas_call | solution.py:1545
  827.2 103.3 %attn_back.1 = (bf16[272,2048]{1,0:T(8,128)(2,1)}, f32[256,1408]{1,0:T(8,128)}, bf16[1024,2048]{1,0:T(8,128)(2,1)}, bf16[1024,1536]{1,0:T(8,128)(2,1)}, bf16[2,256,1408]{2,1,0:T(8,128)(2,1)}) custom-call(f32[256,2048]{1,0:T(8,128)} %get-tuple-element.68.refs_0_, f32[256,2048]{1,0:T(8,128)} %get-tuple-element.69.refs_1_, f32[2,2048]{1,0:T(2,128)} %bitcast.48, ...), custom_call_target="tpu_custom_call" | custom-call | flops 12884901888 | bytes 31457280 | tf_op jit(solution)/shard_map/attn_back/pallas_call | solution.py:1731
  930.5 242.7 %grads.1 = (f32[256,1408]{1,0:T(8,128)}, f32[256,1408]{1,0:T(8,128)}, f32[256,1536]{1,0:T(8,128)}, f32[256,512]{1,0:T(8,128)}, f32[2,128,2048]{2,1,0:T(8,128)}, ...) custom-call(bf16[2,256,1408]{2,1,0:T(8,128)(2,1)} %get-tuple-element.78.refs_0_, ...), custom_call_target="tpu_custom_call" | custom-call | flops 14495514624 | bytes 62914560 | tf_op jit(solution)/shard_map/grads/pallas_call | solution.py:2087
  1174.8 2.0 copy.31
  1176.8 1.5 copy.30
  1178.3 1.6 reshape.61
  1180.0 1.5 pad_maximum_fusion
  1181.5 3.8 copy.29
  1185.4 1.3 copy.40
  1187.7 1.3 copy.41
  1189.0 1.6 copy-done.3
  1190.6 2.0 copy.42
  (25 shorter events, 6.3 us)
Async XLA Ops:
  0.6 1.9 copy-start
  7.8 3.4 copy-start.2
  930.4 246.3 %copy-start.7 = (f32[256,1408]{1,0:T(8,128)S(1)}, f32[256,1408]{1,0:T(8,128)}, u32[]{:S(2)}) copy-start(f32[256,1408]{1,0:T(8,128)} %get-tuple-element.93) | copy-start | bytes 4325380
  1173.2 5.1 copy-start.6
  1178.3 1.7 copy-start.8
  1181.5 3.8 copy-start.4
  1185.4 2.3 copy-start.5
  1187.7 2.9 copy-start.3
  1187.7 5.0 copy-start.1

commit v7 on v6

--- a/solution.py
+++ b/solution.py
@@ -1254,40 +1254,65 @@
 
 class GradRing:
     @staticmethod
-    def scratch(sz, n_dp, wide):
-        slots, ways, steps, dma = n_dp * sz.n_context, sz.n_context, n_dp - 1, pltpu.SemaphoreType.DMA
-        depth, bf16, count = sz.width // slots, jnp.bfloat16, len(wide)
+    def scratch(sz, n_dp, tasks, wide, own_rows=None):
+        slots, ways, dma = n_dp * sz.n_context, sz.n_context, pltpu.SemaphoreType.DMA
+        depth, bf16, count, last = sz.width // slots, jnp.bfloat16, len(wide), n_dp - 1
+        own_rows = [True] * count if own_rows is None else own_rows
+        hops = [[s for w, s in tasks if w == i] for i in range(count)]
         return (
-            [pltpu.VMEM((sz.seq_len, n), bf16) for n in wide]
-            + [pltpu.VMEM((ways, depth, n), bf16) for n in wide]
-            + [pltpu.VMEM((ways, steps, depth, n), bf16) for n in wide]
+            [pltpu.VMEM((sz.seq_len, n), bf16) for n, own in zip(wide, own_rows) if own]
+            + [pltpu.VMEM((ways, depth, n) if 0 in h else (ways, 16, 128), bf16) for n, h in zip(wide, hops)]
+            + [pltpu.VMEM((ways, min(max(h) + 1, last), depth, n), bf16) for n, h in zip(wide, hops)]
             + [
                 pltpu.VMEM((2, ways, sz.seq_len, depth), bf16),
                 dma((count,)),
                 dma((2, ways)),
-                dma((count, ways, steps)),
-                dma((count, ways, steps)),
+                dma((count, ways, last)),
+                dma((count, ways, last)),
+                dma((ways,)),
             ]
         )
 
-    def __init__(self, sz, place, ring, xs, ys, refs):
-        count = len(xs)
-        self.sz, self.place, self.ring, self.xs, self.count = sz, place, ring, xs, count
-        self.ys, self.first, self.held = (refs[i * count : (i + 1) * count] for i in range(3))
-        self.x_s, self.load_y, self.load_x, self.send, self.recv = refs[3 * count :]
-        self.y_loads = [
-            pltpu.make_async_copy(ys[w], self.ys[w], self.load_y.at[w]) for w in range(count)
-        ]
-        self.tasks = [
+    @staticmethod
+    def size(wide, own_rows=None):
+        return 2 * len(wide) + (len(wide) if own_rows is None else sum(own_rows)) + 6
+
+    @staticmethod
+    def all_tasks(n_dp, count):
+        return [
             (k - s, s)
-            for k in range(count + ring.count)
-            for s in range(min(k, ring.count - 1), -1, -1)
+            for k in range(count + n_dp)
+            for s in range(min(k, n_dp - 1), -1, -1)
             if k - s < count
         ]
-        self.done, self.seen = 0, set()
+
+    def __init__(self, sz, place, ring, tasks, xs, ys, refs, rows=None, given=None):
+        count, refs = len(xs), list(refs)
+        self.sz, self.place, self.ring, self.xs, self.count = sz, place, ring, xs, count
+        self.tasks = tasks
+        self.ys = [refs.pop(0) if ys[w] is not None else rows[w] for w in range(count)]
+        self.first, self.held = refs[:count], refs[count : 2 * count]
+        self.x_s, self.load_y, self.load_x, self.send, self.recv, load_given = refs[2 * count :]
+        self.y_loads = [
+            pltpu.make_async_copy(ys[w], self.ys[w], self.load_y.at[w])
+            for w in range(count)
+            if ys[w] is not None
+        ]
+        self.unread = {w: self.y_loads[i] for i, w in enumerate(
+            w for w in range(count) if ys[w] is not None
+        )}
+        self.given = []
+        if given is not None:
+            self.given = [
+                pltpu.make_async_copy(
+                    given.at[way], self.held[0].at[way, tasks[0][1] - 1], load_given.at[way]
+                )
+                for way in range(sz.n_context)
+            ]
+        self.done = 0
 
     def start(self):
-        for copy in self.y_loads:
+        for copy in self.y_loads + self.given:
             copy.start()
         for way in range(self.sz.n_context):
             self.x_load(0, way).start()
@@ -1329,14 +1354,16 @@
         if k + 1 < len(self.tasks):
             for way in ways:
                 self.x_load(k + 1, way).start()
-        if w not in self.seen:
-            self.y_loads[w].wait()
-            self.seen.add(w)
+        if w in self.unread:
+            self.unread.pop(w).wait()
         for way in ways:
             self.x_load(k, way).wait()
             value = tn_dot(self.x_s[k % 2, way], self.ys[w][...])
+            if k == 0 and self.given:
+                self.given[way].wait()
+            elif s:
+                self.hop(w, way, s - 1).wait_recv()
             if s:
-                self.hop(w, way, s - 1).wait_recv()
                 value = value + self.held[w][way, s - 1].astype(jnp.float32)
             ref = self.source(w, way, s)
             ref[...] = value.astype(jnp.bfloat16)
@@ -1348,9 +1375,9 @@
         return len(self.tasks) - self.done
 
     def finish(self):
-        for w in range(self.count):
-            for way in range(self.sz.n_context):
-                for s in range(self.ring.count - 1):
+        for w, s in self.tasks:
+            if s < self.ring.count - 1:
+                for way in range(self.sz.n_context):
                     self.hop(w, way, s).wait_send()
 
 
@@ -1444,15 +1471,18 @@
 
 
 def ffn_back_kernel(sz, n_dp, *refs):
-    (cot, mixed, gains, state) = refs[:4]
-    (rows_hbm, gate_hbm, up_hbm, wg_hbm, wu_hbm, down_hbm, x_hbm, hidden_hbm) = refs[4:12]
-    (grad_mixed, gain_grad, state_out, dgate_out, dup_out, down_sum) = refs[12:18]
+    (cot, mixed, gains) = refs[:3]
+    (rows_hbm, gate_hbm, up_hbm, wg_hbm, wu_hbm, down_hbm) = refs[3:9]
+    (x_hbm, normed_hbm, hidden_hbm) = refs[9:12]
+    (grad_mixed, gain_grad, dgate_out, dup_out, down_sum, gate_part) = refs[12:18]
     (rows_s, gate_s, up_s, wg, wu, wd, load, load_down, keep_sem) = refs[18:27]
-    (swap_out, swap_in, swap_sem) = refs[27:30]
-    scatter_refs, ring_refs = refs[30:38], refs[38:]
+    scatter_refs, ring_refs = refs[27:35], refs[35:]
     place = Place(sz)
     ring = Ring(place, n_dp)
-    grads = GradRing(sz, place, ring, [x_hbm], [hidden_hbm], ring_refs)
+    grads = GradRing(
+        sz, place, ring, ffn_back_tasks(n_dp), [x_hbm, normed_hbm], [hidden_hbm, None], ring_refs,
+        rows=[None, gate_s],
+    )
     grads.start()
     pairs = ((rows_hbm, rows_s), (gate_hbm, gate_s), (up_hbm, up_s), (wg_hbm, wg), (wu_hbm, wu))
     loads = [
@@ -1462,24 +1492,11 @@
     loads[0].start()
     for copy in down_loads + loads[1:]:
         copy.start()
-    other = (place.dp, (1 - place.group) * sz.half + place.part, place.ctx)
-    place.enter([ring.device(1), ring.device(n_dp - 1), other])
+    place.enter([ring.device(1), ring.device(n_dp - 1)])
     scatter = Scatter(place, *scatter_refs)
     grads.step()
     for copy in [loads[0]] + down_loads + loads[1:]:
         copy.wait()
-    give_rows = pl.ds(pl.multiple_of((1 - place.group) * sz.block, sz.block), sz.block)
-    keep_rows = pl.ds(pl.multiple_of(place.group * sz.block, sz.block), sz.block)
-    swap = pltpu.make_async_remote_copy(
-        src_ref=swap_out,
-        dst_ref=swap_in,
-        send_sem=swap_sem.at[0],
-        recv_sem=swap_sem.at[1],
-        device_id=other,
-        device_id_type=MESH,
-    )
-    swap_out[...] = state[give_rows, :].astype(jnp.bfloat16)
-    state_out[place.group] = state[keep_rows, :]
 
     def work(q, j):
         rows = place.tile(q, j)
@@ -1504,10 +1521,10 @@
     work(0, 0)
     for q in far:
         scatter.onward(q, sz.seqs - 1)
-    swap.start()
     grads.step()
     for j in range(1, sz.seqs):
         work(0, j)
+    grads.step()
     copies = [
         pltpu.make_async_copy(gate_s, dgate_out, keep_sem.at[0]),
         pltpu.make_async_copy(up_s, dup_out, keep_sem.at[1]),
@@ -1522,23 +1539,28 @@
         grad_mixed[span, :] = cot[span, :].astype(jnp.float32) + grad
         gain_total = gain_here if gain_total is None else gain_total + gain_here
     gain_grad[...] = gain_total
-    while grads.left() > 1:
+    while grads.left():
         grads.step()
-    swap.wait()
-    state_out[1 - place.group] = swap_in[...].astype(jnp.float32)
-    grads.step()
     for way in range(sz.n_context):
-        copies.append(
-            pltpu.make_async_copy(grads.result(0, way), down_sum.at[way], keep_sem.at[2 + way])
-        )
-        copies[-1].start()
+        grads.hop(1, way, 0).wait_recv()
+        for i, (src, dst) in enumerate(
+            ((grads.result(0, way), down_sum), (grads.held[1].at[way, 0], gate_part))
+        ):
+            copies.append(
+                pltpu.make_async_copy(src, dst.at[way], keep_sem.at[2 + 2 * way + i])
+            )
+            copies[-1].start()
     scatter.finish()
     grads.finish()
     for copy in copies:
         copy.wait()
 
 
-def run_ffn_back(sz, n_dp, cot, mixed, gains, state, rows, gate, up, wg, wu, down, hidden):
+def ffn_back_tasks(n_dp):
+    return [(0, 0), (0, 1), (1, 0)] + [(0, s) for s in range(2, n_dp)]
+
+
+def run_ffn_back(sz, n_dp, cot, mixed, gains, rows, gate, up, wg, wu, down, normed, hidden):
     f32, bf16, shape = jnp.float32, jnp.bfloat16, jax.ShapeDtypeStruct
     dma = pltpu.SemaphoreType.DMA
     depth = sz.width // (n_dp * sz.n_context)
@@ -1547,13 +1569,13 @@
         out_shape=[
             shape((sz.rows, sz.width), f32),
             shape((1, sz.width), f32),
-            shape((sz.seqs, sz.block, sz.width), f32),
             shape((sz.seq_len, sz.ff), bf16),
             shape((sz.seq_len, sz.ff), bf16),
             shape((sz.n_context, depth, sz.ff), bf16),
+            shape((sz.n_context, depth, sz.ff), bf16),
         ],
-        in_specs=[full_spec()] * 4 + [any_spec()] * 8,
-        out_specs=[full_spec()] * 3 + [any_spec()] * 3,
+        in_specs=[full_spec()] * 3 + [any_spec()] * 9,
+        out_specs=[full_spec()] * 2 + [any_spec()] * 4,
         scratch_shapes=[
             pltpu.VMEM((sz.seq_len, sz.width), bf16),
             pltpu.VMEM((sz.seq_len, sz.ff), bf16),
@@ -1563,13 +1585,10 @@
             pltpu.VMEM((sz.ff, sz.width), bf16),
             dma((5,)),
             dma((down.shape[0],)),
-            dma((2 + sz.n_context,)),
-            pltpu.VMEM((sz.block, sz.width), bf16),
-            pltpu.VMEM((sz.block, sz.width), bf16),
-            dma((2,)),
+            dma((2 + 2 * sz.n_context,)),
         ]
         + Scatter.scratch(sz)
-        + GradRing.scratch(sz, n_dp, [sz.ff]),
+        + GradRing.scratch(sz, n_dp, ffn_back_tasks(n_dp), [sz.ff, sz.ff], [True, False]),
         compiler_params=pltpu.CompilerParams(
             collective_id=6, has_side_effects=True, vmem_limit_bytes=VMEM_BYTES
         ),
@@ -1577,20 +1596,27 @@
             flops=8 * sz.seq_len * sz.width * sz.ff, bytes_accessed=40 << 20, transcendentals=0
         ),
         name="ffn_back",
-    )(cot, mixed, gains, state, rows, gate, up, wg, wu, down, slot_columns(sz, n_dp, rows), hidden)
+    )(
+        cot, mixed, gains, rows, gate, up, wg, wu, down,
+        slot_columns(sz, n_dp, rows), slot_columns(sz, n_dp, normed), hidden,
+    )
 
 
 def attn_back_kernel(sz, n_dp, *refs):
-    (grad_mixed, adapted, gains, cos_t, sin_t, begin, gain_b) = refs[:7]
-    (q_hbm, k_hbm, v_hbm, lse_hbm, out_hbm, qkv_hbm, x_hbm, dgate_hbm, down_sum) = refs[7:16]
-    (grad_low, down_grad, rows_out, proj_out, gate_sum) = refs[16:21]
-    (rows_s, q_s, k_s, v_s, lse_s, do_s, dk_s, dv_s, proj_s, wout, wqkv) = refs[21:32]
-    (load, load_out, keep_sem) = refs[32:35]
-    gather_refs, scatter_refs = refs[35:37], refs[37:45]
-    ring_refs, deliver_refs = refs[45:53], refs[53:]
+    (grad_mixed, adapted, gains, cos_t, sin_t, begin, gain_b, state) = refs[:8]
+    (q_hbm, k_hbm, v_hbm, lse_hbm, out_hbm, qkv_hbm) = refs[8:14]
+    (x_hbm, dgate_hbm, down_sum, gate_part) = refs[14:18]
+    (grad_low, down_grad, gate_grad, state_out, rows_out, proj_out) = refs[18:24]
+    (rows_s, q_s, k_s, v_s, lse_s, do_s, dk_s, dv_s, proj_s, wout, wqkv) = refs[24:35]
+    (load, load_out, keep_sem, swap_out, swap_in, swap_sem) = refs[35:41]
+    gather_refs, scatter_refs = refs[41:43], refs[43:51]
+    ring_refs, deliver_refs = refs[51:60], refs[60:]
     place = Place(sz)
     ring = Ring(place, n_dp)
-    grads = GradRing(sz, place, ring, [x_hbm], [dgate_hbm], ring_refs)
+    tasks = [(0, s) for s in range(1, n_dp)]
+    grads = GradRing(
+        sz, place, ring, tasks, [x_hbm], [dgate_hbm], ring_refs, given=gate_part
+    )
     deliver = Deliver(sz, place, deliver_refs)
     grads.start()
     pairs = ((q_hbm, q_s), (k_hbm, k_s), (v_hbm, v_s), (lse_hbm, lse_s), (qkv_hbm, wqkv))
@@ -1601,7 +1627,8 @@
     for copy in out_loads + loads:
         copy.start()
     targets = deliver.greet()
-    place.enter([ring.device(1), ring.device(n_dp - 1)], targets)
+    other = other_group(place)
+    place.enter([ring.device(1), ring.device(n_dp - 1), other], targets)
     gather = Gather(place, rows_s, *gather_refs)
     scatter = Scatter(place, *scatter_refs)
     for j in range(sz.seqs):
@@ -1610,6 +1637,19 @@
         gather.start(j)
     grads.step()
     deliver.start(0, [down_sum.at[way] for way in range(sz.n_context)])
+    give_rows = pl.ds(pl.multiple_of((1 - place.group) * sz.block, sz.block), sz.block)
+    keep_rows = pl.ds(pl.multiple_of(place.group * sz.block, sz.block), sz.block)
+    swap = pltpu.make_async_remote_copy(
+        src_ref=swap_out,
+        dst_ref=swap_in,
+        send_sem=swap_sem.at[0],
+        recv_sem=swap_sem.at[1],
+        device_id=other,
+        device_id_type=MESH,
+    )
+    swap_out[...] = state[give_rows, :].astype(jnp.bfloat16)
+    state_out[place.group] = state[keep_rows, :]
+    swap.start()
     for copy in out_loads:
         copy.wait()
     d = sz.head_dim
@@ -1627,6 +1667,8 @@
     for copy in loads:
         copy.wait()
     for j in range(sz.seqs):
+        if j == sz.seqs - 1:
+            grads.step()
         for q in far:
             gather.forward(q, j)
         for q in far:
@@ -1634,7 +1676,6 @@
             heads_grad(q, j)
     copies = [pltpu.make_async_copy(rows_s, rows_out, keep_sem.at[0])]
     copies[0].start()
-    grads.step()
 
     tiles = sz.n_tensor
     scale = 1.0 / math.sqrt(d)
@@ -1673,9 +1714,7 @@
         proj_s[:, pl.ds(pl.multiple_of(h * 3 * d + 2 * d, d), d)] = dv_s[...].astype(jnp.bfloat16)
         return carry
 
-    lax.fori_loop(0, sz.heads // 2, head, 0)
-    grads.step()
-    lax.fori_loop(sz.heads // 2, sz.heads, head, 0)
+    lax.fori_loop(0, sz.heads, head, 0)
     copies.append(pltpu.make_async_copy(proj_s, proj_out, keep_sem.at[1]))
     copies[1].start()
 
@@ -1692,17 +1731,15 @@
     give(0, 0)
     for q in far:
         scatter.onward(q, sz.seqs - 1)
+    while grads.left():
+        grads.step()
+    deliver.start(1, [grads.result(0, way) for way in range(sz.n_context)])
     for j in range(1, sz.seqs):
         give(0, j)
     gather.finish()
+    swap.wait()
+    state_out[1 - place.group] = swap_in[...].astype(jnp.float32)
     down_grad[...] = deliver.total(0)
-    while grads.left():
-        grads.step()
-    for way in range(sz.n_context):
-        copies.append(
-            pltpu.make_async_copy(grads.result(0, way), gate_sum.at[way], keep_sem.at[2 + way])
-        )
-        copies[-1].start()
     gain_total = None
     for j in range(sz.seqs):
         span = slice(j * sz.block, (j + 1) * sz.block)
@@ -1714,6 +1751,7 @@
     at_row = lax.broadcasted_iota(jnp.int32, (extra, sz.width), 0)
     shares = jnp.where(at_row == 0, gain_total, jnp.where(at_row == 1, gain_b[...], 0.0))
     grad_low[sz.rows :, :] = shares.astype(jnp.bfloat16)
+    gate_grad[...] = deliver.total(1)
     scatter.finish()
     grads.finish()
     deliver.finish()
@@ -1722,8 +1760,8 @@
 
 
 def run_attn_back(
-    sz, n_dp, grad_mixed, adapted, gains, cos_t, sin_t, begin, gain_b, q, k, v, lse, out, qkv,
-    x, dgate, down_sum,
+    sz, n_dp, grad_mixed, adapted, gains, cos_t, sin_t, begin, gain_b, state, q, k, v, lse, out,
+    qkv, x, dgate, down_sum, gate_part,
 ):
     f32, bf16, shape = jnp.float32, jnp.bfloat16, jax.ShapeDtypeStruct
     dma = pltpu.SemaphoreType.DMA
@@ -1733,12 +1771,13 @@
         out_shape=[
             shape((sz.rows + 16, sz.width), bf16),
             shape(down_sum.shape[1:], f32),
+            shape(gate_part.shape[1:], f32),
+            shape((sz.seqs, sz.block, sz.width), f32),
             shape((sz.seq_len, sz.width), bf16),
             shape((sz.seq_len, qkv.shape[1]), bf16),
-            shape(down_sum.shape, bf16),
         ],
-        in_specs=[full_spec()] * 7 + [any_spec()] * 9,
-        out_specs=[full_spec()] * 2 + [any_spec()] * 3,
+        in_specs=[full_spec()] * 8 + [any_spec()] * 10,
+        out_specs=[full_spec()] * 4 + [any_spec()] * 2,
         scratch_shapes=[
             pltpu.VMEM((sz.seq_len, sz.width), bf16),
             pltpu.VMEM(heads_shape, bf16),
@@ -1753,12 +1792,15 @@
             pltpu.VMEM(qkv.shape, bf16),
             dma((5,)),
             dma((out.shape[0],)),
-            dma((2 + sz.n_context,)),
+            dma((2,)),
+            pltpu.VMEM((sz.block, sz.width), bf16),
+            pltpu.VMEM((sz.block, sz.width), bf16),
+            dma((2,)),
         ]
         + Gather.scratch(sz)
         + Scatter.scratch(sz)
-        + GradRing.scratch(sz, n_dp, [sz.ff])
-        + Deliver.scratch(sz, n_dp, [sz.ff]),
+        + GradRing.scratch(sz, n_dp, [(0, s) for s in range(1, n_dp)], [sz.ff])
+        + Deliver.scratch(sz, n_dp, [sz.ff, sz.ff]),
         compiler_params=pltpu.CompilerParams(
             collective_id=7, has_side_effects=True, vmem_limit_bytes=VMEM_BYTES
         ),
@@ -1767,8 +1809,8 @@
         ),
         name="attn_back",
     )(
-        grad_mixed, adapted, gains, cos_t, sin_t, begin, gain_b, q, k, v, lse, out, qkv,
-        slot_columns(sz, n_dp, x), dgate, down_sum,
+        grad_mixed, adapted, gains, cos_t, sin_t, begin, gain_b, state, q, k, v, lse, out, qkv,
+        slot_columns(sz, n_dp, x), dgate, down_sum, gate_part,
     )
 
 
@@ -1928,25 +1970,26 @@
 
 
 def grads_kernel(sz, n_dp, count, *refs):
-    n_in = 4 + 2 * count
-    gate_sum, low, joined, adapter = refs[:4]
-    xs, ys = refs[4 : 4 + count], refs[4 + count : n_in]
-    outs = refs[n_in : n_in + 1 + count]
-    embed_grad, adapter_out, gains_out, landed = refs[n_in + 1 + count : n_in + 5 + count]
-    refs = refs[n_in + 5 + count :]
+    n_in = 3 + 2 * count
+    low, joined, adapter = refs[:3]
+    xs, ys = refs[3 : 3 + count], refs[3 + count : n_in]
+    outs = refs[n_in : n_in + count]
+    embed_grad, adapter_out, gains_out, landed = refs[n_in + count : n_in + 4 + count]
+    refs = refs[n_in + 4 + count :]
 
     def take(n):
         nonlocal refs
         head, refs = refs[:n], refs[n:]
         return head
 
-    ring_refs, deliver_refs = take(3 * count + 5), take(count + 4)
+    ring_refs, deliver_refs = take(3 * count + 6), take(count + 3)
     plane_refs, sum_refs = take(4), take(8)
     adapter_grad, d_s, j_s, weight_s, rows_s, swap_in = refs[:6]
     d_sem, j_sem, weight_sem, swap_sem, out_sem = refs[6:]
     place = Place(sz)
     ring = Ring(place, n_dp)
-    grads = GradRing(sz, place, ring, xs, ys, ring_refs)
+    tasks = GradRing.all_tasks(n_dp, count)
+    grads = GradRing(sz, place, ring, tasks, xs, ys, ring_refs)
     deliver = Deliver(sz, place, deliver_refs)
     plane = PlaneRows(place, ring, low, landed, plane_refs)
     line = LineSum(place, adapter_grad, SUM_PARTS, sum_refs)
@@ -1972,13 +2015,12 @@
         device_id_type=MESH,
     )
     swap.start()
-    deliver.start(0, [gate_sum.at[way] for way in range(sz.n_context)])
 
     def ring_step():
         if grads.left():
             w, complete = grads.step()
             if complete:
-                deliver.start(1 + w, [grads.result(w, way) for way in range(sz.n_context)])
+                deliver.start(w, [grads.result(w, way) for way in range(sz.n_context)])
 
     depth = joined.shape[2]
 
@@ -2027,7 +2069,8 @@
     if rest:
         adapter_grad[depth + 16 :, :] = jnp.zeros((rest, sz.width), jnp.float32)
     for s in range(n_dp - 1):
-        ring_step()
+        if s == n_dp - 2:
+            ring_step()
         plane.step(s)
     own.wait()
     product(place.ctx, True)
@@ -2036,6 +2079,7 @@
     product(1 - place.ctx, False)
     for k in range(SUM_PARTS):
         line.start(k)
+    ring_step()
     ring_step()
     swap.wait()
     rows_s[place.group] = low[keep_rows, :]
@@ -2065,7 +2109,7 @@
     ]
     for copy in saves:
         copy.start()
-    for w in range(1 + count):
+    for w in range(count):
         outs[w][...] = deliver.total(w)
     for copy in saves:
         copy.wait()
@@ -2075,28 +2119,27 @@
     line.finish()
 
 
-def run_grads(sz, n_dp, gate_sum, low, joined, adapter, xs, ys):
+def run_grads(sz, n_dp, low, joined, adapter, xs, ys):
     count, bf16, f32, dma = len(xs), jnp.bfloat16, jnp.float32, pltpu.SemaphoreType.DMA
     shape = jax.ShapeDtypeStruct
     depth = sz.width // (n_dp * sz.n_context)
     wide = [y.shape[1] for y in ys]
-    all_wide = [gate_sum.shape[2]] + wide
     slots, columns = joined.shape[0], joined.shape[2]
     unit = 16 * sz.half * SUM_PARTS
     total_rows = -(-(columns + 16) // unit) * unit
     return pl.pallas_call(
         partial(grads_kernel, sz, n_dp, count),
-        out_shape=[shape((depth, n), f32) for n in all_wide]
+        out_shape=[shape((depth, n), f32) for n in wide]
         + [
             shape((sz.seqs, sz.block, sz.width), f32),
             shape((columns, sz.width), f32),
             shape((16, sz.width), f32),
             shape((slots,) + low.shape, bf16),
         ],
-        in_specs=[any_spec(), full_spec()] + [any_spec()] * (2 + 2 * count),
-        out_specs=[full_spec()] * (2 + count) + [any_spec()] * 3,
-        scratch_shapes=GradRing.scratch(sz, n_dp, wide)
-        + Deliver.scratch(sz, n_dp, all_wide)
+        in_specs=[full_spec()] + [any_spec()] * (2 + 2 * count),
+        out_specs=[full_spec()] * (1 + count) + [any_spec()] * 3,
+        scratch_shapes=GradRing.scratch(sz, n_dp, GradRing.all_tasks(n_dp, count), wide)
+        + Deliver.scratch(sz, n_dp, wide)
         + PlaneRows.scratch(n_dp)
         + LineSum.scratch(sz, SUM_PARTS, total_rows // (sz.half * SUM_PARTS))
         + [
@@ -2119,7 +2162,7 @@
             flops=2 * sz.seq_len * sz.width * sum(wide), bytes_accessed=60 << 20, transcendentals=0
         ),
         name="grads",
-    )(gate_sum, low, joined, adapter, *[slot_columns(sz, n_dp, x) for x in xs], *ys)
+    )(low, joined, adapter, *[slot_columns(sz, n_dp, x) for x in xs], *ys)
 
 
 def shards(
@@ -2258,23 +2301,23 @@
     (current, ffn_input, gate_pre, up_pre, hidden) = run_ffn(
         sz, True, mixed_rows, detached, gains_f[:1], gains_f, gate_use, up_use, down_blocks
     )
-    grad_mixed, gain_b, state_out, grad_gate, grad_up, down_sum = run_ffn_back(
-        sz, n_dp, cot_rows, mixed_rows, gains_f, current, grad_ffn, gate_pre, up_pre,
-        gate_use, up_use, down_blocks, hidden,
+    grad_mixed, gain_b, grad_gate, grad_up, down_sum, gate_part = run_ffn_back(
+        sz, n_dp, cot_rows, mixed_rows, gains_f, grad_ffn, gate_pre, up_pre,
+        gate_use, up_use, down_blocks, ffn_input, hidden,
     )
-    grad_low, down_t, grad_rows, grad_proj, gate_sum = run_attn_back(
-        sz, n_dp, grad_mixed, adapted, gains_f, cos_full, sin_full, begin, gain_b,
+    grad_low, down_t, gate_s, state_out, grad_rows, grad_proj = run_attn_back(
+        sz, n_dp, grad_mixed, adapted, gains_f, cos_full, sin_full, begin, gain_b, current,
         query_hm, key_hm, value_hm, lse, out_blocks, qkv_use, ffn_input, grad_gate, down_sum,
+        gate_part,
     )
-    gate_s, up_s, qkv_s, out_t, embed_out, adapter_s, gains_rows, _ = run_grads(
+    qkv_s, up_s, out_t, embed_out, adapter_s, gains_rows, _ = run_grads(
         sz,
         n_dp,
-        gate_sum,
         grad_low,
         joined,
         adapter_all,
-        [ffn_input, feature_rows, grad_rows],
-        [grad_up, grad_proj, head_flat],
+        [feature_rows, ffn_input, grad_rows],
+        [grad_proj, grad_up, head_flat],
     )
     place_at = (dp_index * n_context + ctx_index) * gain_columns
     gains_s = lax.dynamic_slice_in_dim(gains_rows[:2], place_at, gain_columns, 1)

time: 1200 us -> 1190 us (level)
  Pallas kernels: 1160 us -> 1140 us
    pallas_call x1, Pallas kernels: 243 us -> 219 us  [run_grads(): pl.pallas_call(partial(grads_kernel, sz, n_dp, count), out_shape=[shape((...]
where the time goes in v7:
time: 1190 us; the launch traced here: 1180 us
  Pallas kernels  1140 us (96%)
  local copies, waits for them, and re-layouts  28.1 us (2%)
    pallas_call x3, Pallas kernels, run_round(): pl.pallas_call(partial(round_kernel, sz), out_shape=jax.ShapeDtypeStruct(...  332 us
    pallas_call x1, Pallas kernels, run_weights(): pl.pallas_call(partial(weights_kernel, sz, n_dp), out_shape=outs, in_spec...  290 us
    pallas_call x1, Pallas kernels, run_grads(): pl.pallas_call(partial(grads_kernel, sz, n_dp, count), out_shape=[shape((...  219 us
    pallas_call x1, Pallas kernels, run_attn_back(): pl.pallas_call(partial(attn_back_kernel, sz, n_dp), out_shape=[shape((sz....  107 us
    pallas_call x1, Pallas kernels, run_ffn_back(): pl.pallas_call(partial(ffn_back_kernel, sz, n_dp), out_shape=[shape((sz.r...  82.2 us
    pallas_call x1, Pallas kernels, run_attn(): pl.pallas_call(partial(attn_kernel, sz, n_dp, keep), out_shape=outs, in_s...  60.6 us
    pallas_call x1, Pallas kernels, run_ffn(): pl.pallas_call(partial(ffn_kernel, sz, keep), out_shape=outs, in_specs=[f...  53.3 us

profile of v7, /device:TPU:1, one launch (start us, length us, event | category | flops | bytes accessed | tf_op | source)
XLA Modules:
  0.0 1181.3 jit_solution(2804979852824319359)
XLA Ops:
  0.7 1.2 dynamic_slice.11
  5.6 2.1 copy.34
  7.8 3.4 fusion.1.refs_0_
  11.2 2.0 fusion.3
  13.2 1.3 copy_bitcast_fusion
  14.5 290.4 %weights.1 = (bf16[8,544,2048]{2,1,0:T(8,128)(2,1)}, bf16[8,512,256]{2,1,0:T(8,128)(2,1)}, bf16[8,256,1536]{2,1,0:T(8,128)(2,1)}, bf16[8,256,1408]{2,1,0:T(8,128...) custom-call(bf16[544,2048]{1,0:T(8,128)(2,1)} %fusion.1.refs_0_, ...), custom_call_target="tpu_custom_call" | custom-call | tf_op jit(solution)/shard_map/weights/pallas_call | solution.py:1217
  304.9 1.4 fusion.2
  306.8 117.9 %round.3.refs_0_ = f32[256,2048]{1,0:T(8,128)} custom-call(f32[256,2048]{1,0:T(8,128)} %get-tuple-element.52.refs_0_, f32[1,2048]{1,0:T(1,128)} %broadcast_in_dim.28.refs_1_, f32[2,2048]{1,0:T(2,128)} %bitcast.42, f32[1024,128]{1,0:T(8,128)} %constant.56.clone.refs_3_, f32[1024,128]{1,0:T(8,128)} %constant.57.clone.refs_4_, s32[1,1024]{1,0:T(1,128)} %bitcast.50, ...), custom_call_target="tpu_custom_call" | custom-call | flops 23622320128 | bytes 41943040 | tf_op jit(solution)/shard_map/round/pallas_call | solution.py:835
  424.7 106.7 %round.4.refs_0_ = f32[256,2048]{1,0:T(8,128)} custom-call(f32[256,2048]{1,0:T(8,128)} %round.3.refs_0_, f32[1,2048]{1,0:T(1,128)} %broadcast_in_dim.30.refs_1_, f32[2,2048]{1,0:T(2,128)} %bitcast.43, f32[1024,128]{1,0:T(8,128)} %constant.56.clone.refs_3_, f32[1024,128]{1,0:T(8,128)} %constant.57.clone.refs_4_, s32[1,1024]{1,0:T(1,128)} %bitcast.51, ...), custom_call_target="tpu_custom_call" | custom-call | flops 23622320128 | bytes 41943040 | tf_op jit(solution)/shard_map/round/pallas_call | solution.py:835
  531.4 107.0 %round.5.refs_0_.refs_1_ = f32[256,2048]{1,0:T(8,128)} custom-call(f32[256,2048]{1,0:T(8,128)} %round.4.refs_0_, f32[1,2048]{1,0:T(1,128)} %broadcast_in_dim.31.refs_1_, f32[2,2048]{1,0:T(2,128)} %bitcast.44, f32[1024,128]{1,0:T(8,128)} %constant.56.clone.refs_3_, f32[1024,128]{1,0:T(8,128)} %constant.57.clone.refs_4_, s32[1,1024]{1,0:T(1,128)} %bitcast.52, ...), custom_call_target="tpu_custom_call" | custom-call | flops 23622320128 | bytes 41943040 | tf_op jit(solution)/shard_map/round/pallas_call | solution.py:835
  638.4 60.6 %attn_keep.1 = (f32[256,2048]{1,0:T(8,128)}, f32[256,2048]{1,0:T(8,128)}, bf16[1024,2048]{1,0:T(8,128)(2,1)}, bf16[4,1024,128]{2,1,0:T(8,128)(2,1)}, bf16[4,1024...) custom-call(f32[256,2048]{1,0:T(8,128)} %round.5.refs_0_.refs_1_, ...), custom_call_target="tpu_custom_call" | custom-call | flops 8589934592 | bytes 20971520 | tf_op jit(solution)/shard_map/attn_keep/pallas_call | solution.py:531
  699.0 53.3 %ffn_keep.1 = (f32[256,2048]{1,0:T(8,128)}, bf16[1024,2048]{1,0:T(8,128)(2,1)}, bf16[1024,1408]{1,0:T(8,128)(2,1)}, bf16[1024,1408]{1,0:T(8,128)(2,1)}, bf16[1024,1408]{1,0:T(8,128)(2,1)}) custom-call(f32[256,2048]{1,0:T(8,128)} %get-tuple-element.61.refs_0_.refs_1_, f32[256,2048]{1,0:T(8,128)} %round.5.refs_0_.refs_1_, f32[1,2048]{1,0:T(1,128)} %bitcast.55, ...), custom_call_target="tpu_custom_call" | custom-call | flops 17716740096 | bytes 20971520 | tf_op jit(solution)/shard_map/ffn_keep/pallas_call | solution.py:658
  752.4 82.2 %ffn_back.1 = (f32[256,2048]{1,0:T(8,128)}, f32[1,2048]{1,0:T(1,128)}, bf16[1024,1408]{1,0:T(8,128)(2,1)}, bf16[1024,1408]{1,0:T(8,128)(2,1)}, bf16[2,256,1408]{...) custom-call(bf16[256,2048]{1,0:T(8,128)(2,1)} %get-tuple-element.51.refs_0_, f32[256,2048]{1,0:T(8,128)} %get-tuple-element.61.refs_0_.refs_1_, ...), custom_call_target="tpu_custom_call" | custom-call | flops 23622320128 | bytes 41943040 | tf_op jit(solution)/shard_map/ffn_back/pallas_call | solution.py:1567
  834.6 107.3 %attn_back.1 = (bf16[272,2048]{1,0:T(8,128)(2,1)}, f32[256,1408]{1,0:T(8,128)}, f32[256,1408]{1,0:T(8,128)}, f32[2,128,2048]{2,1,0:T(8,128)}, bf16[1024,2048]{1,0:T(8,128)(2,1)}, /*index=5*/bf16[1024,1536]{1,0:T(8,128)(2,1)}) custom-call(f32[256,2048]{1,0:T(8,128)} %get-tuple-element.67.refs_0_, f32[256,2048]{1,0:T(8,128)} %get-tuple-element.68.refs_1_, ...), custom_call_target="tpu_custom_call" | custom-call | flops 12884901888 | bytes 31457280 | tf_op jit(solution)/shard_map/attn_back/pallas_call | solution.py:1769
  941.9 218.7 %grads.1 = (f32[256,1536]{1,0:T(8,128)}, f32[256,1408]{1,0:T(8,128)}, f32[256,512]{1,0:T(8,128)}, f32[2,128,2048]{2,1,0:T(8,128)}, f32[512,2048]{1,0:T(8,128)}, ...) custom-call(bf16[272,2048]{1,0:T(8,128)(2,1)} %get-tuple-element.79.refs_0_, ...), custom_call_target="tpu_custom_call" | custom-call | flops 14495514624 | bytes 62914560 | tf_op jit(solution)/shard_map/grads/pallas_call | solution.py:2130
  1162.0 2.0 copy.31
  1164.0 1.5 pad_maximum_fusion
  1165.6 3.8 copy.29
  1169.4 1.5 copy.30
  1170.9 2.9 reshape.61
  1173.8 1.3 copy.40
  1176.2 1.3 copy.41
  1177.5 1.6 copy-done.3
  1179.1 2.0 copy.42
  (23 shorter events, 6.1 us)
Async XLA Ops:
  0.6 1.9 copy-start
  7.8 3.4 copy-start.2
  941.9 222.1 %copy-start.7 = (f32[256,1408]{1,0:T(8,128)S(1)}, f32[256,1408]{1,0:T(8,128)}, u32[]{:S(2)}) copy-start(f32[256,1408]{1,0:T(8,128)} %get-tuple-element.91) | copy-start | bytes 4325380
  1165.6 3.8 copy-start.6
  1170.9 2.9 copy-start.4
  1173.8 2.3 copy-start.5
  1176.2 2.9 copy-start.3
  1176.2 5.0 copy-start.1

commit v8 on v7

--- a/solution.py
+++ b/solution.py
@@ -1489,11 +1489,10 @@
         pltpu.make_async_copy(src, dst, load.at[i]) for i, (src, dst) in enumerate(pairs)
     ]
     down_loads = column_loads(down_hbm, wd, load_down)
-    loads[0].start()
-    for copy in down_loads + loads[1:]:
-        copy.start()
     place.enter([ring.device(1), ring.device(n_dp - 1)])
     scatter = Scatter(place, *scatter_refs)
+    for copy in [loads[0]] + down_loads + loads[1:]:
+        copy.start()
     grads.step()
     for copy in [loads[0]] + down_loads + loads[1:]:
         copy.wait()
@@ -1518,10 +1517,10 @@
         if j:
             for q in far:
                 scatter.onward(q, j - 1)
+    grads.step()
     work(0, 0)
     for q in far:
         scatter.onward(q, sz.seqs - 1)
-    grads.step()
     for j in range(1, sz.seqs):
         work(0, j)
     grads.step()
@@ -1603,23 +1602,27 @@
 
 
 def attn_back_kernel(sz, n_dp, *refs):
-    (grad_mixed, adapted, gains, cos_t, sin_t, begin, gain_b, state) = refs[:8]
+    (grad_mixed, gains, cos_t, sin_t, begin, gain_b, adapted_hbm, state_hbm) = refs[:8]
     (q_hbm, k_hbm, v_hbm, lse_hbm, out_hbm, qkv_hbm) = refs[8:14]
-    (x_hbm, dgate_hbm, down_sum, gate_part) = refs[14:18]
-    (grad_low, down_grad, gate_grad, state_out, rows_out, proj_out) = refs[18:24]
-    (rows_s, q_s, k_s, v_s, lse_s, do_s, dk_s, dv_s, proj_s, wout, wqkv) = refs[24:35]
-    (load, load_out, keep_sem, swap_out, swap_in, swap_sem) = refs[35:41]
-    gather_refs, scatter_refs = refs[41:43], refs[43:51]
-    ring_refs, deliver_refs = refs[51:60], refs[60:]
+    (x_hbm, dgate_hbm, dup_hbm, down_sum, gate_part) = refs[14:19]
+    (grad_low, down_grad, gate_grad, state_out, rows_out, proj_out, up_part) = refs[19:26]
+    (rows_s, q_s, k_s, v_s, lse_s, do_s, dk_s, dv_s, proj_s, wout, wqkv) = refs[26:37]
+    (load, load_out, keep_sem, swap_out, swap_in, swap_sem, late) = refs[37:44]
+    gather_refs, scatter_refs = refs[44:46], refs[46:54]
+    ring_refs, deliver_refs = refs[54:66], refs[66:]
     place = Place(sz)
     ring = Ring(place, n_dp)
-    tasks = [(0, s) for s in range(1, n_dp)]
     grads = GradRing(
-        sz, place, ring, tasks, [x_hbm], [dgate_hbm], ring_refs, given=gate_part
+        sz, place, ring, attn_back_tasks(n_dp), [x_hbm, x_hbm], [dgate_hbm, dup_hbm], ring_refs,
+        given=gate_part,
     )
     deliver = Deliver(sz, place, deliver_refs)
     grads.start()
-    pairs = ((q_hbm, q_s), (k_hbm, k_s), (v_hbm, v_s), (lse_hbm, lse_s), (qkv_hbm, wqkv))
+    split = wqkv.shape[0]
+    pairs = (
+        (q_hbm, q_s), (k_hbm, k_s), (v_hbm, v_s), (lse_hbm, lse_s),
+        (qkv_hbm.at[pl.ds(split, split)], wqkv),
+    )
     loads = [
         pltpu.make_async_copy(src, dst, load.at[i]) for i, (src, dst) in enumerate(pairs)
     ]
@@ -1647,8 +1650,16 @@
         device_id=other,
         device_id_type=MESH,
     )
-    swap_out[...] = state[give_rows, :].astype(jnp.bfloat16)
-    state_out[place.group] = state[keep_rows, :]
+    state_load = pltpu.make_async_copy(
+        state_hbm.at[give_rows], scatter.part.at[pl.ds(0, sz.block)], late.at[0]
+    )
+    state_keep = pltpu.make_async_copy(
+        state_hbm.at[keep_rows], state_out.at[place.group], late.at[1]
+    )
+    state_load.start()
+    state_keep.start()
+    state_load.wait()
+    swap_out[...] = scatter.part[: sz.block, :].astype(jnp.bfloat16)
     swap.start()
     for copy in out_loads:
         copy.wait()
@@ -1669,13 +1680,19 @@
     for j in range(sz.seqs):
         if j == sz.seqs - 1:
             grads.step()
+            grads.step()
         for q in far:
             gather.forward(q, j)
         for q in far:
             gather.wait_far(sz.half - q, j)
             heads_grad(q, j)
-    copies = [pltpu.make_async_copy(rows_s, rows_out, keep_sem.at[0])]
-    copies[0].start()
+    rows_copy = pltpu.make_async_copy(rows_s, rows_out, keep_sem.at[0])
+    rows_copy.start()
+    gather.finish()
+    rows_copy.wait()
+    upper = rows_s.at[pl.ds(0, split), pl.ds(0, wqkv.shape[1])]
+    upper_load = pltpu.make_async_copy(qkv_hbm.at[pl.ds(0, split)], upper, late.at[2])
+    upper_load.start()
 
     tiles = sz.n_tensor
     scale = 1.0 / math.sqrt(d)
@@ -1715,11 +1732,17 @@
         return carry
 
     lax.fori_loop(0, sz.heads, head, 0)
-    copies.append(pltpu.make_async_copy(proj_s, proj_out, keep_sem.at[1]))
-    copies[1].start()
+    copies = [pltpu.make_async_copy(proj_s, proj_out, keep_sem.at[1])]
+    copies[0].start()
+    upper_load.wait()
+    while grads.left() > 1:
+        grads.step()
+    deliver.start(1, [grads.result(0, way) for way in range(sz.n_context)])
 
     def give(q, j):
-        scatter.part[...] = nt_dot(proj_s[place.tile(q, j), :], wqkv[...])
+        proj = proj_s[place.tile(q, j), :]
+        scatter.part[:, :split] = nt_dot(proj, upper[...])
+        scatter.part[:, split:] = nt_dot(proj, wqkv[...])
         scatter.give(q, j)
 
     for j in range(sz.seqs):
@@ -1731,13 +1754,15 @@
     give(0, 0)
     for q in far:
         scatter.onward(q, sz.seqs - 1)
-    while grads.left():
-        grads.step()
-    deliver.start(1, [grads.result(0, way) for way in range(sz.n_context)])
     for j in range(1, sz.seqs):
         give(0, j)
-    gather.finish()
+    adapted = scatter.part
+    adapted_load = pltpu.make_async_copy(adapted_hbm, adapted, late.at[3])
+    adapted_load.start()
+    grads.step()
     swap.wait()
+    state_keep.wait()
+    adapted_load.wait()
     state_out[1 - place.group] = swap_in[...].astype(jnp.float32)
     down_grad[...] = deliver.total(0)
     gain_total = None
@@ -1751,6 +1776,14 @@
     at_row = lax.broadcasted_iota(jnp.int32, (extra, sz.width), 0)
     shares = jnp.where(at_row == 0, gain_total, jnp.where(at_row == 1, gain_b[...], 0.0))
     grad_low[sz.rows :, :] = shares.astype(jnp.bfloat16)
+    for way in range(sz.n_context):
+        grads.hop(1, way, 1).wait_recv()
+        copies.append(
+            pltpu.make_async_copy(
+                grads.held[1].at[way, 1], up_part.at[way], keep_sem.at[2 + way]
+            )
+        )
+        copies[-1].start()
     gate_grad[...] = deliver.total(1)
     scatter.finish()
     grads.finish()
@@ -1759,9 +1792,13 @@
         copy.wait()
 
 
+def attn_back_tasks(n_dp):
+    return [(0, 1), (0, 2), (1, 0)] + [(0, s) for s in range(3, n_dp)] + [(1, 1)]
+
+
 def run_attn_back(
     sz, n_dp, grad_mixed, adapted, gains, cos_t, sin_t, begin, gain_b, state, q, k, v, lse, out,
-    qkv, x, dgate, down_sum, gate_part,
+    qkv, x, dgate, dup, down_sum, gate_part,
 ):
     f32, bf16, shape = jnp.float32, jnp.bfloat16, jax.ShapeDtypeStruct
     dma = pltpu.SemaphoreType.DMA
@@ -1775,9 +1812,10 @@
             shape((sz.seqs, sz.block, sz.width), f32),
             shape((sz.seq_len, sz.width), bf16),
             shape((sz.seq_len, qkv.shape[1]), bf16),
+            shape(gate_part.shape, bf16),
         ],
-        in_specs=[full_spec()] * 8 + [any_spec()] * 10,
-        out_specs=[full_spec()] * 4 + [any_spec()] * 2,
+        in_specs=[full_spec()] * 6 + [any_spec()] * 13,
+        out_specs=[full_spec()] * 4 + [any_spec()] * 3,
         scratch_shapes=[
             pltpu.VMEM((sz.seq_len, sz.width), bf16),
             pltpu.VMEM(heads_shape, bf16),
@@ -1789,17 +1827,18 @@
             pltpu.VMEM((sz.seq_len, sz.head_dim), f32),
             pltpu.VMEM((sz.seq_len, qkv.shape[1]), bf16),
             pltpu.VMEM((sz.heads * sz.head_dim, sz.width), bf16),
-            pltpu.VMEM(qkv.shape, bf16),
+            pltpu.VMEM((sz.width // 2, qkv.shape[1]), bf16),
             dma((5,)),
             dma((out.shape[0],)),
-            dma((2,)),
+            dma((2 + sz.n_context,)),
             pltpu.VMEM((sz.block, sz.width), bf16),
             pltpu.VMEM((sz.block, sz.width), bf16),
             dma((2,)),
+            dma((4,)),
         ]
         + Gather.scratch(sz)
         + Scatter.scratch(sz)
-        + GradRing.scratch(sz, n_dp, [(0, s) for s in range(1, n_dp)], [sz.ff])
+        + GradRing.scratch(sz, n_dp, attn_back_tasks(n_dp), [sz.ff, sz.ff])
         + Deliver.scratch(sz, n_dp, [sz.ff, sz.ff]),
         compiler_params=pltpu.CompilerParams(
             collective_id=7, has_side_effects=True, vmem_limit_bytes=VMEM_BYTES
@@ -1809,8 +1848,8 @@
         ),
         name="attn_back",
     )(
-        grad_mixed, adapted, gains, cos_t, sin_t, begin, gain_b, state, q, k, v, lse, out, qkv,
-        slot_columns(sz, n_dp, x), dgate, down_sum, gate_part,
+        grad_mixed, gains, cos_t, sin_t, begin, gain_b, adapted, state, q, k, v, lse, out, qkv,
+        slot_columns(sz, n_dp, x), dgate, dup, down_sum, gate_part,
     )
 
 
@@ -1970,9 +2009,9 @@
 
 
 def grads_kernel(sz, n_dp, count, *refs):
-    n_in = 3 + 2 * count
-    low, joined, adapter = refs[:3]
-    xs, ys = refs[3 : 3 + count], refs[3 + count : n_in]
+    n_in = 4 + 2 * count
+    low, joined, adapter, up_part = refs[:4]
+    xs, ys = refs[4 : 4 + count], refs[4 + count : n_in]
     outs = refs[n_in : n_in + count]
     embed_grad, adapter_out, gains_out, landed = refs[n_in + count : n_in + 4 + count]
     refs = refs[n_in + 4 + count :]
@@ -1988,8 +2027,9 @@
     d_sem, j_sem, weight_sem, swap_sem, out_sem = refs[6:]
     place = Place(sz)
     ring = Ring(place, n_dp)
-    tasks = GradRing.all_tasks(n_dp, count)
-    grads = GradRing(sz, place, ring, tasks, xs, ys, ring_refs)
+    grads = GradRing(
+        sz, place, ring, grads_tasks(n_dp, count), xs, ys, ring_refs, given=up_part
+    )
     deliver = Deliver(sz, place, deliver_refs)
     plane = PlaneRows(place, ring, low, landed, plane_refs)
     line = LineSum(place, adapter_grad, SUM_PARTS, sum_refs)
@@ -2069,8 +2109,7 @@
     if rest:
         adapter_grad[depth + 16 :, :] = jnp.zeros((rest, sz.width), jnp.float32)
     for s in range(n_dp - 1):
-        if s == n_dp - 2:
-            ring_step()
+        ring_step()
         plane.step(s)
     own.wait()
     product(place.ctx, True)
@@ -2119,7 +2158,12 @@
     line.finish()
 
 
-def run_grads(sz, n_dp, low, joined, adapter, xs, ys):
+def grads_tasks(n_dp, count):
+    others = [(w + 1, s) for w, s in GradRing.all_tasks(n_dp, count - 1)]
+    return [(0, s) for s in range(2, n_dp)] + others
+
+
+def run_grads(sz, n_dp, low, joined, adapter, up_part, xs, ys):
     count, bf16, f32, dma = len(xs), jnp.bfloat16, jnp.float32, pltpu.SemaphoreType.DMA
     shape = jax.ShapeDtypeStruct
     depth = sz.width // (n_dp * sz.n_context)
@@ -2136,9 +2180,9 @@
             shape((16, sz.width), f32),
             shape((slots,) + low.shape, bf16),
         ],
-        in_specs=[full_spec()] + [any_spec()] * (2 + 2 * count),
+        in_specs=[full_spec()] + [any_spec()] * (3 + 2 * count),
         out_specs=[full_spec()] * (1 + count) + [any_spec()] * 3,
-        scratch_shapes=GradRing.scratch(sz, n_dp, GradRing.all_tasks(n_dp, count), wide)
+        scratch_shapes=GradRing.scratch(sz, n_dp, grads_tasks(n_dp, count), wide)
         + Deliver.scratch(sz, n_dp, wide)
         + PlaneRows.scratch(n_dp)
         + LineSum.scratch(sz, SUM_PARTS, total_rows // (sz.half * SUM_PARTS))
@@ -2162,7 +2206,7 @@
             flops=2 * sz.seq_len * sz.width * sum(wide), bytes_accessed=60 << 20, transcendentals=0
         ),
         name="grads",
-    )(low, joined, adapter, *[slot_columns(sz, n_dp, x) for x in xs], *ys)
+    )(low, joined, adapter, up_part, *[slot_columns(sz, n_dp, x) for x in xs], *ys)
 
 
 def shards(
@@ -2305,19 +2349,20 @@
         sz, n_dp, cot_rows, mixed_rows, gains_f, grad_ffn, gate_pre, up_pre,
         gate_use, up_use, down_blocks, ffn_input, hidden,
     )
-    grad_low, down_t, gate_s, state_out, grad_rows, grad_proj = run_attn_back(
+    grad_low, down_t, gate_s, state_out, grad_rows, grad_proj, up_part = run_attn_back(
         sz, n_dp, grad_mixed, adapted, gains_f, cos_full, sin_full, begin, gain_b, current,
-        query_hm, key_hm, value_hm, lse, out_blocks, qkv_use, ffn_input, grad_gate, down_sum,
+        query_hm, key_hm, value_hm, lse, out_blocks, qkv_use, ffn_input, grad_gate, grad_up, down_sum,
         gate_part,
     )
-    qkv_s, up_s, out_t, embed_out, adapter_s, gains_rows, _ = run_grads(
+    up_s, qkv_s, out_t, embed_out, adapter_s, gains_rows, _ = run_grads(
         sz,
         n_dp,
         grad_low,
         joined,
         adapter_all,
-        [feature_rows, ffn_input, grad_rows],
-        [grad_proj, grad_up, head_flat],
+        up_part,
+        [ffn_input, feature_rows, grad_rows],
+        [grad_up, grad_proj, head_flat],
     )
     place_at = (dp_index * n_context + ctx_index) * gain_columns
     gains_s = lax.dynamic_slice_in_dim(gains_rows[:2], place_at, gain_columns, 1)

time: 1190 us -> 1170 us (0.983)
  Pallas kernels: 1140 us -> 1120 us
    pallas_call x1, Pallas kernels: 219 us -> 199 us  [run_grads(): pl.pallas_call(partial(grads_kernel, sz, n_dp, count), out_shape=[shape((...]
where the time goes in v8:
time: 1170 us; the launch traced here: 1160 us
  Pallas kernels  1120 us (96%)
  local copies, waits for them, and re-layouts  28.1 us (2%)
    pallas_call x3, Pallas kernels, run_round(): pl.pallas_call(partial(round_kernel, sz), out_shape=jax.ShapeDtypeStruct(...  327 us
    pallas_call x1, Pallas kernels, run_weights(): pl.pallas_call(partial(weights_kernel, sz, n_dp), out_shape=outs, in_spec...  290 us
    pallas_call x1, Pallas kernels, run_grads(): pl.pallas_call(partial(grads_kernel, sz, n_dp, count), out_shape=[shape((...  199 us
    pallas_call x1, Pallas kernels, run_attn_back(): pl.pallas_call(partial(attn_back_kernel, sz, n_dp), out_shape=[shape((sz....  113 us
    pallas_call x1, Pallas kernels, run_ffn_back(): pl.pallas_call(partial(ffn_back_kernel, sz, n_dp), out_shape=[shape((sz.r...  78.1 us
    pallas_call x1, Pallas kernels, run_attn(): pl.pallas_call(partial(attn_kernel, sz, n_dp, keep), out_shape=outs, in_s...  60.8 us
    pallas_call x1, Pallas kernels, run_ffn(): pl.pallas_call(partial(ffn_kernel, sz, keep), out_shape=outs, in_specs=[f...  53 us

profile of v8, /device:TPU:1, one launch (start us, length us, event | category | flops | bytes accessed | tf_op | source)
XLA Modules:
  0.0 1159.7 jit_solution(15227693213956519888)
XLA Ops:
  0.7 1.2 dynamic_slice.11
  5.6 2.1 copy.34
  7.8 3.4 fusion.1.refs_0_
  11.2 2.0 fusion.3
  13.2 1.3 copy_bitcast_fusion
  14.5 290.4 %weights.1 = (bf16[8,544,2048]{2,1,0:T(8,128)(2,1)}, bf16[8,512,256]{2,1,0:T(8,128)(2,1)}, bf16[8,256,1536]{2,1,0:T(8,128)(2,1)}, bf16[8,256,1408]{2,1,0:T(8,128...) custom-call(bf16[544,2048]{1,0:T(8,128)(2,1)} %fusion.1.refs_0_, ...), custom_call_target="tpu_custom_call" | custom-call | tf_op jit(solution)/shard_map/weights/pallas_call | solution.py:1217
  304.9 1.4 fusion.2
  306.8 113.7 %round.3.refs_0_ = f32[256,2048]{1,0:T(8,128)} custom-call(f32[256,2048]{1,0:T(8,128)} %get-tuple-element.53.refs_0_, f32[1,2048]{1,0:T(1,128)} %broadcast_in_dim.28.refs_1_, f32[2,2048]{1,0:T(2,128)} %bitcast.42, f32[1024,128]{1,0:T(8,128)} %constant.56.clone.refs_3_.refs_2_, f32[1024,128]{1,0:T(8,128)} %constant.57.clone.refs_4_.refs_3_, ...), custom_call_target="tpu_custom_call" | custom-call | flops 23622320128 | bytes 41943040 | tf_op jit(solution)/shard_map/round/pallas_call | solution.py:835
  420.6 106.8 %round.4.refs_0_ = f32[256,2048]{1,0:T(8,128)} custom-call(f32[256,2048]{1,0:T(8,128)} %round.3.refs_0_, f32[1,2048]{1,0:T(1,128)} %broadcast_in_dim.30.refs_1_, f32[2,2048]{1,0:T(2,128)} %bitcast.43, f32[1024,128]{1,0:T(8,128)} %constant.56.clone.refs_3_.refs_2_, f32[1024,128]{1,0:T(8,128)} %constant.57.clone.refs_4_.refs_3_, s32[1,1024]{1,0:T(1,128)} %bitcast.51, ...), custom_call_target="tpu_custom_call" | custom-call | flops 23622320128 | bytes 41943040 | tf_op jit(solution)/shard_map/round/pallas_call | solution.py:835
  527.4 106.9 %round.5.refs_0_.refs_1_ = f32[256,2048]{1,0:T(8,128)} custom-call(f32[256,2048]{1,0:T(8,128)} %round.4.refs_0_, f32[1,2048]{1,0:T(1,128)} %broadcast_in_dim.31.refs_1_, f32[2,2048]{1,0:T(2,128)} %bitcast.44, f32[1024,128]{1,0:T(8,128)} %constant.56.clone.refs_3_.refs_2_, f32[1024,128]{1,0:T(8,128)} %constant.57.clone.refs_4_.refs_3_, s32[1,1024]{1,0:T(1,128)} %bitcast.52, ...), custom_call_target="tpu_custom_call" | custom-call | flops 23622320128 | bytes 41943040 | tf_op jit(solution)/shard_map/round/pallas_call | solution.py:835
  634.3 60.8 %attn_keep.1 = (f32[256,2048]{1,0:T(8,128)}, f32[256,2048]{1,0:T(8,128)}, bf16[1024,2048]{1,0:T(8,128)(2,1)}, bf16[4,1024,128]{2,1,0:T(8,128)(2,1)}, bf16[4,1024...) custom-call(f32[256,2048]{1,0:T(8,128)} %round.5.refs_0_.refs_1_, ...), custom_call_target="tpu_custom_call" | custom-call | flops 8589934592 | bytes 20971520 | tf_op jit(solution)/shard_map/attn_keep/pallas_call | solution.py:531
  695.1 53.0 %ffn_keep.1 = (f32[256,2048]{1,0:T(8,128)}, bf16[1024,2048]{1,0:T(8,128)(2,1)}, bf16[1024,1408]{1,0:T(8,128)(2,1)}, bf16[1024,1408]{1,0:T(8,128)(2,1)}, bf16[1024,1408]{1,0:T(8,128)(2,1)}) custom-call(f32[256,2048]{1,0:T(8,128)} %get-tuple-element.62.refs_0_.refs_1_, f32[256,2048]{1,0:T(8,128)} %round.5.refs_0_.refs_1_, f32[1,2048]{1,0:T(1,128)} %bitcast.55, ...), custom_call_target="tpu_custom_call" | custom-call | flops 17716740096 | bytes 20971520 | tf_op jit(solution)/shard_map/ffn_keep/pallas_call | solution.py:658
  748.1 78.1 %ffn_back.1 = (f32[256,2048]{1,0:T(8,128)}, f32[1,2048]{1,0:T(1,128)}, bf16[1024,1408]{1,0:T(8,128)(2,1)}, bf16[1024,1408]{1,0:T(8,128)(2,1)}, bf16[2,256,1408]{...) custom-call(bf16[256,2048]{1,0:T(8,128)(2,1)} %get-tuple-element.52.refs_0_, f32[256,2048]{1,0:T(8,128)} %get-tuple-element.62.refs_0_.refs_1_, ...), custom_call_target="tpu_custom_call" | custom-call | flops 23622320128 | bytes 41943040 | tf_op jit(solution)/shard_map/ffn_back/pallas_call | solution.py:1566
  826.2 113.2 %attn_back.1 = (bf16[272,2048]{1,0:T(8,128)(2,1)}, f32[256,1408]{1,0:T(8,128)}, f32[256,1408]{1,0:T(8,128)}, f32[2,128,2048]{2,1,0:T(8,128)}, bf16[1024,2048]{1,...) custom-call(f32[256,2048]{1,0:T(8,128)} %get-tuple-element.68.refs_0_, f32[2,2048]{1,0:T(2,128)} %bitcast.48, ...), custom_call_target="tpu_custom_call" | custom-call | flops 12884901888 | bytes 31457280 | tf_op jit(solution)/shard_map/attn_back/pallas_call | solution.py:1806
  939.5 199.3 %grads.1 = (f32[256,1408]{1,0:T(8,128)}, f32[256,1536]{1,0:T(8,128)}, f32[256,512]{1,0:T(8,128)}, f32[2,128,2048]{2,1,0:T(8,128)}, f32[512,2048]{1,0:T(8,128)}, ...) custom-call(bf16[272,2048]{1,0:T(8,128)(2,1)} %get-tuple-element.81.refs_0_, ...), custom_call_target="tpu_custom_call" | custom-call | flops 14495514624 | bytes 62914560 | tf_op jit(solution)/shard_map/grads/pallas_call | solution.py:2174
  1140.2 2.0 copy.31
  1142.2 1.5 pad_maximum_fusion
  1143.8 3.8 copy.29
  1147.6 1.5 copy.30
  1149.1 2.9 reshape.61
  1152.0 1.3 copy.40
  1154.4 1.3 copy.41
  1155.7 1.6 copy-done.3
  1157.3 2.0 copy.42
  (23 shorter events, 6.1 us)
Async XLA Ops:
  0.6 1.9 copy-start
  7.8 3.4 copy-start.2
  939.5 202.8 %copy-start.7 = (f32[256,1408]{1,0:T(8,128)S(1)}, f32[256,1408]{1,0:T(8,128)}, u32[]{:S(2)}) copy-start(f32[256,1408]{1,0:T(8,128)} %get-tuple-element.93) | copy-start | bytes 4325380
  1143.8 3.8 copy-start.6
  1149.1 2.9 copy-start.4
  1152.0 2.3 copy-start.5
  1154.4 2.9 copy-start.3
  1154.4 5.0 copy-start.1

commit v9 on v8

--- a/solution.py
+++ b/solution.py
@@ -671,57 +671,102 @@
     )(mixed, latent, active, gains, gate, up, down)
 
 
-def round_kernel(sz, *refs):
-    (latent, active, gains, cos_t, sin_t, begin) = refs[:6]
-    (embed_hbm, adapter_hbm, qkv_hbm, out_hbm, gate_hbm, up_hbm, down_hbm, result) = refs[6:14]
-    (wa, wqkv, wout, wg, wu, mixed, rows_s, q_s, k_s, v_s, head_s) = refs[14:25]
-    load_embed, load_a, load_qkv, load_out, load_gu, load_down = refs[25:31]
-    gather_refs, again_refs, scatter_refs = refs[31:33], refs[33:35], refs[35:43]
+def rounds_kernel(sz, count, *refs):
+    (active, gains, cos_t, sin_t, begin) = refs[:5]
+    (latent_hbm, embed_hbm, adapter_hbm, qkv_hbm, out_hbm, gate_hbm, up_hbm, down_hbm) = refs[5:13]
+    result = refs[13]
+    (wide, narrow, wg, wu, wd, embed, mixed, rows_s, q_s, k_s, v_s, head_s) = refs[14:26]
+    load_rows, load_a, load_qkv, load_out, load_gu, load_down = refs[26:32]
+    gather_refs, again_refs, scatter_refs = refs[32:34], refs[34:36], refs[36:44]
+    columns = sz.width // 4
+    depth_out = sz.heads * sz.head_dim
 
     place = Place(sz)
-    embed_load = pltpu.make_async_copy(embed_hbm, mixed, load_embed)
-    a_loads = adapter_loads(adapter_hbm, wa, load_a)
+    row_loads = [
+        pltpu.make_async_copy(latent_hbm, result, load_rows.at[0]),
+        pltpu.make_async_copy(embed_hbm, embed, load_rows.at[1]),
+    ]
+
+    def adapter_columns(n):
+        return wide.at[:, pl.ds(n * columns, columns)] if n < 3 else narrow
+
+    tops = load_a.shape[1]
+    depth = sz.width // tops
+    a_loads = [
+        [
+            pltpu.make_async_copy(
+                adapter_hbm.at[b, pl.ds(0, depth), pl.ds(n * columns, columns)],
+                adapter_columns(n).at[pl.ds(b * depth, depth)],
+                load_a.at[n, b],
+            )
+            for b in range(tops)
+        ]
+        for n in range(4)
+    ]
+    wqkv = wide.at[:, pl.ds(0, qkv_hbm.shape[1])]
     qkv_load = pltpu.make_async_copy(qkv_hbm, wqkv, load_qkv)
-    out_loads = column_loads(out_hbm, wout, load_out)
-    gate_load = pltpu.make_async_copy(gate_hbm, wg, load_gu.at[0])
-    up_load = pltpu.make_async_copy(up_hbm, wu, load_gu.at[1])
-    wd = wa.at[pl.ds(0, sz.ff)]
-    down_loads = column_loads(down_hbm, wd, load_down)
-    embed_load.start()
-    for group in a_loads:
-        for copy in group:
+    out_loads = []
+    for b in range(out_hbm.shape[0]):
+        size = min(out_hbm.shape[2], columns)
+        for at in range(0, out_hbm.shape[2], size):
+            n, to = divmod(b * out_hbm.shape[2] + at, columns)
+            out_loads.append(
+                pltpu.make_async_copy(
+                    out_hbm.at[b, :, pl.ds(at, size)],
+                    narrow.at[pl.ds(n * depth_out, depth_out), pl.ds(to, size)],
+                    load_out.at[len(out_loads)],
+                )
+            )
+    ffn_loads = [
+        pltpu.make_async_copy(gate_hbm, wg, load_gu.at[0]),
+        pltpu.make_async_copy(up_hbm, wu, load_gu.at[1]),
+    ] + column_loads(down_hbm, wd, load_down)
+
+    def start_adapter():
+        for group in a_loads:
+            for copy in group:
+                copy.start()
+
+    def start_heads():
+        qkv_load.start()
+        for copy in out_loads:
             copy.start()
-    qkv_load.start()
-    for copy in out_loads:
+
+    for copy in row_loads:
         copy.start()
+    start_adapter()
     place.enter()
     gather = Gather(place, rows_s, *gather_refs)
     again = Gather(place, rows_s, *again_refs)
     scatter = Scatter(place, *scatter_refs)
-
-    low = latent[...].astype(jnp.bfloat16)
-    columns = sz.width // len(a_loads)
-    square = None
-    embed_load.wait()
-    for n, group in enumerate(a_loads):
-        for copy in group:
-            copy.wait()
-        cols = pl.ds(n * columns, columns)
-        chunk = nn_dot(low, wa[:, cols]) + mixed[:, cols]
-        mixed[:, cols] = chunk
-        here = jnp.sum(chunk * chunk, axis=-1, keepdims=True)
-        square = here if square is None else square + here
-    factor = lax.rsqrt(square / sz.width + norm_eps)
-    for j in range(sz.seqs):
-        span = slice(j * sz.block, (j + 1) * sz.block)
-        normed = (mixed[span, :] * factor[span]) * gains[0:1, :]
+    for copy in row_loads:
+        copy.wait()
+
+    def spans(j):
+        return slice(j * sz.block, (j + 1) * sz.block)
+
+    def open_block(j):
+        low = result[spans(j), :].astype(jnp.bfloat16)
+        square = None
+        for n, group in enumerate(a_loads):
+            if j == 0:
+                for copy in group:
+                    copy.wait()
+            cols = slice(n * columns, (n + 1) * columns)
+            chunk = nn_dot(low, adapter_columns(n)[...]) + embed[spans(j), cols]
+            mixed[spans(j), cols] = chunk
+            here = jnp.sum(chunk * chunk, axis=-1, keepdims=True)
+            square = here if square is None else square + here
+        factor = lax.rsqrt(square / sz.width + norm_eps)
+        normed = (mixed[spans(j), :] * factor) * gains[0:1, :]
         rows_s[gather.own(j), :] = normed.astype(jnp.bfloat16)
         gather.start(j)
-    gate_load.start()
-    up_load.start()
-    for copy in down_loads:
+
+    for j in range(sz.seqs):
+        open_block(j)
+    start_heads()
+    for copy in ffn_loads:
         copy.start()
-    qkv_load.wait()
     pair = min(2, sz.heads)
     d = sz.head_dim
 
@@ -765,42 +810,11 @@
 
     def give(q, j):
         rows = place.tile(q, j)
-        scatter.part[...] = nn_dot(head_s[rows, :], wout[...])
+        for n in range(4):
+            scatter.part[:, n * columns : (n + 1) * columns] = nn_dot(
+                head_s[rows, :], narrow[n * depth_out : (n + 1) * depth_out, :]
+            )
         scatter.give(q, j)
-
-    far = range(1, sz.half)
-    for j in range(sz.seqs):
-        gather.wait_near(j)
-        project(0, j)
-    for copy in out_loads:
-        copy.wait()
-    for j in range(sz.seqs):
-        for q in far:
-            gather.forward(q, j)
-        for q in far:
-            gather.wait_far(sz.half - q, j)
-            project(q, j)
-        for q in far:
-            attend(q, j)
-            give(q, j)
-        attend(0, j)
-        gather.passed_on(j)
-        for q in far:
-            scatter.onward(q, j)
-        give(0, j)
-    gather.finish(forwards=False)
-    for j in range(sz.seqs):
-        span = slice(j * sz.block, (j + 1) * sz.block)
-        rows = mixed[span, :] + scatter.total(j)
-        mixed[span, :] = rows
-        normed = (rows * rms_factor(rows)) * gains[1:2, :]
-        rows_s[again.own(j), :] = normed.astype(jnp.bfloat16)
-        again.start(j)
-    scatter.finish()
-    gate_load.wait()
-    up_load.wait()
-    for copy in down_loads:
-        copy.wait()
 
     def work(q, j):
         x = rows_s[place.tile(q, j), :]
@@ -810,49 +824,95 @@
         scatter.part[...] = nn_dot(hidden, wd[...])
         scatter.give(q, j)
 
-    for j in range(sz.seqs):
-        again.wait_near(j)
-        work(0, j)
-    for j in range(sz.seqs):
-        for q in far:
-            again.forward(q, j)
-        for q in far:
-            again.wait_far(sz.half - q, j)
-            work(q, j)
-        for q in far:
-            scatter.onward(q, j)
-    again.finish()
-    for j in range(sz.seqs):
-        span = slice(j * sz.block, (j + 1) * sz.block)
-        total = mixed[span, :] + scatter.total(j)
-        result[span, :] = jnp.where(active[...] > 0, total, latent[span, :])
-    scatter.finish()
-
-
-def run_round(sz, latent, active, gains, cos_t, sin_t, begin, embed, adapter, qkv, out, gate, up, down):
+    far = range(1, sz.half)
+
+    def one_round(r, carry):
+        more = r + 1 < count
+        qkv_load.wait()
+        for j in range(sz.seqs):
+            gather.wait_near(j)
+            project(0, j)
+        for copy in out_loads:
+            copy.wait()
+        for j in range(sz.seqs):
+            for q in far:
+                gather.forward(q, j)
+            for q in far:
+                gather.wait_far(sz.half - q, j)
+                project(q, j)
+            for q in far:
+                attend(q, j)
+                give(q, j)
+            attend(0, j)
+            gather.passed_on(j)
+            for q in far:
+                scatter.onward(q, j)
+            give(0, j)
+        gather.finish(forwards=False)
+        pl.when(more)(start_adapter)
+        for j in range(sz.seqs):
+            rows = mixed[spans(j), :] + scatter.total(j)
+            mixed[spans(j), :] = rows
+            normed = (rows * rms_factor(rows)) * gains[1:2, :]
+            rows_s[again.own(j), :] = normed.astype(jnp.bfloat16)
+            again.start(j)
+        scatter.finish()
+
+        def first_loads():
+            for copy in ffn_loads:
+                copy.wait()
+
+        pl.when(r == 0)(first_loads)
+        for j in range(sz.seqs):
+            again.wait_near(j)
+            work(0, j)
+        for j in range(sz.seqs):
+            for q in far:
+                again.forward(q, j)
+            for q in far:
+                again.wait_far(sz.half - q, j)
+                work(q, j)
+            again.passed_on(j)
+            for q in far:
+                scatter.onward(q, j)
+        again.finish(forwards=False)
+        on = active[pl.ds(r, 1), :] > 0
+        for j in range(sz.seqs):
+            total = mixed[spans(j), :] + scatter.total(j)
+            result[spans(j), :] = jnp.where(on, total, result[spans(j), :])
+            pl.when(more)(lambda j=j: open_block(j))
+        pl.when(more)(start_heads)
+        scatter.finish()
+        return carry
+
+    lax.fori_loop(0, count, one_round, 0)
+
+
+def run_rounds(sz, latent, active, gains, cos_t, sin_t, begin, embed, adapter, qkv, out, gate, up, down):
     f32, bf16, dma = jnp.float32, jnp.bfloat16, pltpu.SemaphoreType.DMA
     heads_shape = (sz.heads, sz.seq_len, sz.head_dim)
     return pl.pallas_call(
-        partial(round_kernel, sz),
+        partial(rounds_kernel, sz, active.shape[0]),
         out_shape=jax.ShapeDtypeStruct((sz.rows, sz.width), f32),
-        in_specs=[full_spec()] * 6 + [any_spec()] * 7,
+        in_specs=[full_spec()] * 5 + [any_spec()] * 8,
         out_specs=full_spec(),
         scratch_shapes=[
-            pltpu.VMEM((sz.width, sz.width), bf16),
-            pltpu.VMEM(qkv.shape, bf16),
-            pltpu.VMEM((sz.heads * sz.head_dim, sz.width), bf16),
+            pltpu.VMEM((sz.width, max(3 * sz.width // 4, qkv.shape[1])), bf16),
+            pltpu.VMEM((sz.width, sz.width // 4), bf16),
             pltpu.VMEM(gate.shape, bf16),
             pltpu.VMEM(up.shape, bf16),
+            pltpu.VMEM((sz.ff, sz.width), bf16),
+            pltpu.VMEM((sz.rows, sz.width), f32),
             pltpu.VMEM((sz.rows, sz.width), f32),
             pltpu.VMEM((sz.seq_len, sz.width), bf16),
             pltpu.VMEM(heads_shape, bf16),
             pltpu.VMEM(heads_shape, bf16),
             pltpu.VMEM(heads_shape, bf16),
             pltpu.VMEM((sz.seq_len, sz.heads * sz.head_dim), bf16),
-            dma,
+            dma((2,)),
             dma((4, adapter.shape[0] // 2)),
             dma,
-            dma((out.shape[0],)),
+            dma((max(4, out.shape[0]),)),
             dma((2,)),
             dma((down.shape[0],)),
         ]
@@ -863,10 +923,10 @@
             collective_id=1, has_side_effects=True, vmem_limit_bytes=VMEM_BYTES
         ),
         cost_estimate=pl.CostEstimate(
-            flops=8 * sz.seq_len * sz.width * sz.ff, bytes_accessed=40 << 20, transcendentals=0
+            flops=24 * sz.seq_len * sz.width * sz.ff, bytes_accessed=80 << 20, transcendentals=0
         ),
-        name="round",
-    )(latent, active, gains, cos_t, sin_t, begin, embed, adapter, qkv, out, gate, up, down)
+        name="rounds",
+    )(active, gains, cos_t, sin_t, begin, latent, embed, adapter, qkv, out, gate, up, down)
 
 
 def other_group(place):
@@ -1089,8 +1149,16 @@
 
     start_move(0)
     start_move(1)
-    for kind in range(half):
-        across(kind, 0).start()
+    across(0, 0).start()
+    swaps = []
+
+    def across_z():
+        if swaps:
+            s = swaps.pop(0)
+            for q in range(1, half):
+                across(q, s).start()
+
+    swaps.append(0)
 
     def adapter_step(s):
         if s < steps:
@@ -1105,8 +1173,8 @@
             arrival.wait_recv()
             if s + 1 < steps:
                 around(s + 1).start()
-            for kind in range(half):
-                across(kind, s + 1).start()
+            across(0, s + 1).start()
+            swaps.append(s + 1)
 
     def adapter_pass(s):
         for q in range(1, half):
@@ -1130,6 +1198,8 @@
             hop(w, way, s).start()
         if s == 0 and w + 2 < count:
             start_move(w + 2)
+        if s == 0 and w >= 1:
+            across_z()
         if s == 0 and w == count - 2:
             for i in range(3):
                 swap(i).start()
@@ -1149,6 +1219,8 @@
         done += 1
     for s in range(done, steps):
         adapter_step(s)
+    while swaps:
+        across_z()
     for s in range(n_dp):
         adapter_pass(s)
     for j in range(sz.seqs):
@@ -1731,13 +1803,14 @@
         proj_s[:, pl.ds(pl.multiple_of(h * 3 * d + 2 * d, d), d)] = dv_s[...].astype(jnp.bfloat16)
         return carry
 
-    lax.fori_loop(0, sz.heads, head, 0)
+    lax.fori_loop(0, sz.heads // 2, head, 0)
+    while grads.left() > 1:
+        grads.step()
+    deliver.start(1, [grads.result(0, way) for way in range(sz.n_context)])
+    lax.fori_loop(sz.heads // 2, sz.heads, head, 0)
     copies = [pltpu.make_async_copy(proj_s, proj_out, keep_sem.at[1])]
     copies[0].start()
     upper_load.wait()
-    while grads.left() > 1:
-        grads.step()
-    deliver.start(1, [grads.result(0, way) for way in range(sz.n_context)])
 
     def give(q, j):
         proj = proj_s[place.tile(q, j), :]
@@ -2331,13 +2404,14 @@
     docs = lax.dynamic_index_in_dim(doc_ids, own_seq, 0, keepdims=False)
     begin = jnp.sum((docs[None, :] < docs[:, None]).astype(jnp.int32), axis=1)[None, :]
     steps_own = lax.dynamic_index_in_dim(recurrences, own_seq, 0, keepdims=False) - BACK
-    for step_index in range(MAXR - BACK):
-        active = jnp.broadcast_to((step_index < steps_own).astype(jnp.float32), (1, model_width))
-        current = run_round(
-            sz, current, active, gains_f, cos_full, sin_full, begin, embed_part,
-            adapter_all, qkv_use, out_blocks, gate_use, up_use, down_blocks,
-        )
-    detached = current
+    active = jnp.arange(MAXR - BACK, dtype=jnp.int32)[:, None] < steps_own
+    detached = run_rounds(
+        sz,
+        current,
+        jnp.broadcast_to(active.astype(jnp.float32), (MAXR - BACK, model_width)),
+        gains_f, cos_full, sin_full, begin, embed_part,
+        adapter_all, qkv_use, out_blocks, gate_use, up_use, down_blocks,
+    )
     (mixed_rows, adapted, feature_rows, query_hm, key_hm, value_hm, head_flat, lse, joined) = run_attn(
         sz, n_dp, True, detached, embed_part, gains_f, cos_full, sin_full, begin,
         adapter_all, qkv_use, out_blocks, embed_rows,

time: 1170 us -> 1160 us (level)
    pallas_call x3 -> x1, Pallas kernels: 327 us -> 312 us  [run_rounds(): pl.pallas_call(partial(rounds_kernel, sz, active.shape[0]), out_shape=jax...]
where the time goes in v9:
time: 1160 us; the launch traced here: 1150 us
  Pallas kernels  1110 us (96%)
  local copies, waits for them, and re-layouts  27 us (2%)
    pallas_call x1, Pallas kernels, run_rounds(): pl.pallas_call(partial(rounds_kernel, sz, active.shape[0]), out_shape=jax...  312 us
    pallas_call x1, Pallas kernels, run_weights(): pl.pallas_call(partial(weights_kernel, sz, n_dp), out_shape=outs, in_spec...  290 us
    pallas_call x1, Pallas kernels, run_grads(): pl.pallas_call(partial(grads_kernel, sz, n_dp, count), out_shape=[shape((...  199 us
    pallas_call x1, Pallas kernels, run_attn_back(): pl.pallas_call(partial(attn_back_kernel, sz, n_dp), out_shape=[shape((sz....  121 us
    pallas_call x1, Pallas kernels, run_ffn_back(): pl.pallas_call(partial(ffn_back_kernel, sz, n_dp), out_shape=[shape((sz.r...  78.7 us
    pallas_call x1, Pallas kernels, run_attn(): pl.pallas_call(partial(attn_kernel, sz, n_dp, keep), out_shape=outs, in_s...  60.5 us
    pallas_call x1, Pallas kernels, run_ffn(): pl.pallas_call(partial(ffn_kernel, sz, keep), out_shape=outs, in_specs=[f...  52.9 us

profile of v9, /device:TPU:1, one launch (start us, length us, event | category | flops | bytes accessed | tf_op | source)
XLA Modules:
  0.0 1151.0 jit_solution(1655330914680432391)
XLA Ops:
  0.7 1.2 dynamic_slice.11
  2.6 1.2 convert_reduce_fusion
  4.5 2.1 copy.34
  6.7 3.4 fusion.1.refs_0_
  10.1 2.0 fusion.3
  12.1 1.3 copy_bitcast_fusion
  13.4 289.8 %weights.1 = (bf16[8,544,2048]{2,1,0:T(8,128)(2,1)}, bf16[8,512,256]{2,1,0:T(8,128)(2,1)}, bf16[8,256,1536]{2,1,0:T(8,128)(2,1)}, bf16[8,256,1408]{2,1,0:T(8,128...) custom-call(bf16[544,2048]{1,0:T(8,128)(2,1)} %fusion.1.refs_0_, ...), custom_call_target="tpu_custom_call" | custom-call | tf_op jit(solution)/shard_map/weights/pallas_call | solution.py:1289
  303.2 1.4 fusion.2
  305.2 312.0 %rounds.1.refs_0_.refs_1_ = f32[256,2048]{1,0:T(8,128)} custom-call(f32[3,2048]{1,0:T(4,128)} %broadcast_in_dim.12.refs_0_, f32[2,2048]{1,0:T(2,128)} %bitcast.38, f32[1024,128]{1,0:T(8,128)} %constant.50.clone.refs_2_.refs_3_, f32[1024,128]{1,0:T(8,128)} %constant.51.clone.refs_3_.refs_4_, s32[1,1024]{1,0:T(1,128)} %bitcast.44, ...), custom_call_target="tpu_custom_call" | custom-call | flops 70866960384 | bytes 83886080 | tf_op jit(solution)/shard_map/rounds/pallas_call | solution.py:894
  617.2 60.5 %attn_keep.1 = (f32[256,2048]{1,0:T(8,128)}, f32[256,2048]{1,0:T(8,128)}, bf16[1024,2048]{1,0:T(8,128)(2,1)}, bf16[4,1024,128]{2,1,0:T(8,128)(2,1)}, bf16[4,1024...) custom-call(f32[256,2048]{1,0:T(8,128)} %rounds.1.refs_0_.refs_1_, ...), custom_call_target="tpu_custom_call" | custom-call | flops 8589934592 | bytes 20971520 | tf_op jit(solution)/shard_map/attn_keep/pallas_call | solution.py:531
  677.7 52.9 %ffn_keep.1 = (f32[256,2048]{1,0:T(8,128)}, bf16[1024,2048]{1,0:T(8,128)(2,1)}, bf16[1024,1408]{1,0:T(8,128)(2,1)}, bf16[1024,1408]{1,0:T(8,128)(2,1)}, bf16[1024,1408]{1,0:T(8,128)(2,1)}) custom-call(f32[256,2048]{1,0:T(8,128)} %get-tuple-element.62.refs_0_.refs_1_, f32[256,2048]{1,0:T(8,128)} %rounds.1.refs_0_.refs_1_, f32[1,2048]{1,0:T(1,128)} %bitcast.47, ...), custom_call_target="tpu_custom_call" | custom-call | flops 17716740096 | bytes 20971520 | tf_op jit(solution)/shard_map/ffn_keep/pallas_call | solution.py:658
  730.7 78.7 %ffn_back.1 = (f32[256,2048]{1,0:T(8,128)}, f32[1,2048]{1,0:T(1,128)}, bf16[1024,1408]{1,0:T(8,128)(2,1)}, bf16[1024,1408]{1,0:T(8,128)(2,1)}, bf16[2,256,1408]{...) custom-call(bf16[256,2048]{1,0:T(8,128)(2,1)} %get-tuple-element.52.refs_0_, f32[256,2048]{1,0:T(8,128)} %get-tuple-element.62.refs_0_.refs_1_, ...), custom_call_target="tpu_custom_call" | custom-call | flops 23622320128 | bytes 41943040 | tf_op jit(solution)/shard_map/ffn_back/pallas_call | solution.py:1638
  809.4 121.4 %attn_back.1 = (bf16[272,2048]{1,0:T(8,128)(2,1)}, f32[256,1408]{1,0:T(8,128)}, f32[256,1408]{1,0:T(8,128)}, f32[2,128,2048]{2,1,0:T(8,128)}, bf16[1024,2048]{1,...) custom-call(f32[256,2048]{1,0:T(8,128)} %get-tuple-element.68.refs_0_, f32[2,2048]{1,0:T(2,128)} %bitcast.42, ...), custom_call_target="tpu_custom_call" | custom-call | flops 12884901888 | bytes 31457280 | tf_op jit(solution)/shard_map/attn_back/pallas_call | solution.py:1879
  930.8 199.4 %grads.1 = (f32[256,1408]{1,0:T(8,128)}, f32[256,1536]{1,0:T(8,128)}, f32[256,512]{1,0:T(8,128)}, f32[2,128,2048]{2,1,0:T(8,128)}, f32[512,2048]{1,0:T(8,128)}, ...) custom-call(bf16[272,2048]{1,0:T(8,128)(2,1)} %get-tuple-element.81.refs_0_, ...), custom_call_target="tpu_custom_call" | custom-call | flops 14495514624 | bytes 62914560 | tf_op jit(solution)/shard_map/grads/pallas_call | solution.py:2247
  1131.6 2.0 copy.31
  1133.7 1.5 pad_maximum_fusion
  1135.2 3.8 copy.29
  1139.0 1.5 copy.30
  1140.6 2.9 reshape.56
  1143.5 1.3 copy.40
  1144.8 1.0 copy-done.5
  1145.8 1.3 copy.41
  1147.1 1.6 copy-done.3
  1148.8 2.0 copy.42
  (20 shorter events, 2.8 us)
Async XLA Ops:
  0.6 1.9 copy-start
  6.7 3.4 copy-start.2
  930.8 202.9 %copy-start.7 = (f32[256,1408]{1,0:T(8,128)S(1)}, f32[256,1408]{1,0:T(8,128)}, u32[]{:S(2)}) copy-start(f32[256,1408]{1,0:T(8,128)} %get-tuple-element.93) | copy-start | bytes 4325380
  1135.2 3.8 copy-start.6
  1140.6 2.9 copy-start.4
  1143.5 2.3 copy-start.5
  1145.8 2.9 copy-start.3
  1145.8 5.0 copy-start.1

commit v10 on v9

--- a/solution.py
+++ b/solution.py
@@ -295,19 +295,22 @@
 def attn_kernel(sz, n_dp, keep, *refs):
     (latent, embed, gains, cos_t, sin_t, begin, adapter_hbm, qkv_hbm, out_hbm) = refs[:9]
     refs = refs[9:]
-    if keep:
-        embed_hbm, refs = refs[0], refs[1:]
+    extra_in, refs = refs[0], refs[1:]
     mixed = refs[0]
     refs = refs[1:]
     if keep:
         adapted_out, rows_out, q_out, k_out, v_out, head_out, lse_out, joined_out = refs[:8]
         refs = refs[8:]
+    else:
+        blocks_out, refs = refs[0], refs[1:]
     (wa, wqkv, wout, adapted, rows_s, q_s, k_s, v_s, head_s, lse_s) = refs[:10]
     load_a, load_qkv, load_out, keep_sem = refs[10:14]
     gather_refs = refs[14:16]
     scatter_refs = refs[16:24]
     if keep:
         joined_s, load_embed, x_send, x_recv = refs[24:]
+    else:
+        hop_send, hop_recv, own_sem = refs[24:]
 
     place = Place(sz)
     a_loads = adapter_loads(adapter_hbm, wa, load_a)
@@ -319,12 +322,55 @@
     qkv_load.start()
     for copy in out_loads:
         copy.start()
-    others = []
+    ring = Ring(place, n_dp)
+    if not keep:
+        others = [ring.device(1), ring.device(n_dp - 1)]
+        ways = range(sz.n_context)
+
+        def hop(way, s):
+            offset = -s if way == 0 else s
+            slot = blocks_out.at[ring.index(offset) * sz.n_context + way]
+            return pltpu.make_async_remote_copy(
+                src_ref=extra_in.at[way] if s == 0 else slot,
+                dst_ref=slot,
+                send_sem=hop_send.at[way, s],
+                recv_sem=hop_recv.at[way, s],
+                device_id=ring.device(1 if way == 0 else n_dp - 1),
+                device_id_type=MESH,
+            )
+
+        def hopped(way, s):
+            offset = -(s + 1) if way == 0 else s + 1
+            slot = blocks_out.at[ring.index(offset) * sz.n_context + way]
+            return pltpu.make_async_remote_copy(
+                src_ref=slot,
+                dst_ref=slot,
+                send_sem=hop_send.at[way, s],
+                recv_sem=hop_recv.at[way, s],
+                device_id=ring.device(1),
+                device_id_type=MESH,
+            )
+
+        own_blocks = [
+            pltpu.make_async_copy(
+                extra_in.at[way], blocks_out.at[place.dp * sz.n_context + way], own_sem.at[way]
+            )
+            for way in ways
+        ]
+        hops = list(range(n_dp - 1))
+
+        def next_hop():
+            if hops:
+                s = hops.pop(0)
+                for way in ways:
+                    if s:
+                        hopped(way, s - 1).wait_recv()
+                    hop(way, s).start()
+
     if keep:
-        ring = Ring(place, n_dp)
         t = lax.axis_index("tensor")
         embed_load = pltpu.make_async_copy(
-            embed_hbm, joined_s.at[:, pl.ds(sz.width, sz.width)], load_embed
+            extra_in, joined_s.at[:, pl.ds(sz.width, sz.width)], load_embed
         )
         embed_load.start()
         plane = [(o, c) for o in range(n_dp) for c in range(2) if (o, c) != (0, 0)]
@@ -360,6 +406,10 @@
 
         others = [member(o, c) for o, c in plane if o]
     place.enter(others)
+    if not keep:
+        next_hop()
+        for copy in own_blocks:
+            copy.start()
     gather = Gather(place, rows_s, *gather_refs)
     scatter = Scatter(place, *scatter_refs)
 
@@ -463,6 +513,8 @@
         for q in far:
             attend(q, j)
             give(q, j)
+        if not keep:
+            next_hop()
         attend(0, j)
         for q in far:
             scatter.onward(q, j)
@@ -481,12 +533,20 @@
         for o, c in plane:
             columns_from(o, c).wait_recv()
             columns_to(o, c).wait_send()
+    else:
+        while hops:
+            next_hop()
+        for way in ways:
+            hopped(way, n_dp - 2).wait_recv()
+            own_blocks[way].wait()
+            for s in range(n_dp - 1):
+                hop(way, s).wait_send()
     for copy in copies:
         copy.wait()
 
 
 def run_attn(
-    sz, n_dp, keep, latent, embed_part, gains, cos_t, sin_t, begin, adapter, qkv, out, *embed
+    sz, n_dp, keep, latent, embed_part, gains, cos_t, sin_t, begin, adapter, qkv, out, extra
 ):
     f32, bf16 = jnp.float32, jnp.bfloat16
     heads_shape = (sz.heads, sz.seq_len, sz.head_dim)
@@ -503,6 +563,8 @@
             shape((sz.heads, 1, sz.seq_len), f32),
             shape((adapter.shape[0], sz.rows, 2 * sz.width // adapter.shape[0]), bf16),
         ]
+    else:
+        outs.append(shape((n_dp * sz.n_context,) + extra.shape[1:], bf16))
     scratch = [
         pltpu.VMEM((sz.width, sz.width), bf16),
         pltpu.VMEM(qkv.shape, bf16),
@@ -527,21 +589,27 @@
             pltpu.SemaphoreType.DMA((n_dp, 2)),
             pltpu.SemaphoreType.DMA((n_dp, 2)),
         ]
+    else:
+        scratch += [
+            pltpu.SemaphoreType.DMA((sz.n_context, n_dp - 1)),
+            pltpu.SemaphoreType.DMA((sz.n_context, n_dp - 1)),
+            pltpu.SemaphoreType.DMA((sz.n_context,)),
+        ]
     flops = 2 * sz.rows * sz.width * sz.width + 2 * sz.seq_len * sz.width * qkv.shape[1]
     return pl.pallas_call(
         partial(attn_kernel, sz, n_dp, keep),
         out_shape=outs,
-        in_specs=[full_spec()] * 6 + [any_spec()] * (3 + len(embed)),
+        in_specs=[full_spec()] * 6 + [any_spec()] * 4,
         out_specs=[full_spec()] + [any_spec()] * (len(outs) - 1),
         scratch_shapes=scratch,
         compiler_params=pltpu.CompilerParams(
-            collective_id=2 if keep else 1, has_side_effects=True, vmem_limit_bytes=VMEM_BYTES
+            collective_id=2 if keep else 9, has_side_effects=True, vmem_limit_bytes=VMEM_BYTES
         ),
         cost_estimate=pl.CostEstimate(
             flops=flops, bytes_accessed=20 << 20, transcendentals=0
         ),
         name="attn_keep" if keep else "attn_round",
-    )(latent, embed_part, gains, cos_t, sin_t, begin, adapter, qkv, out, *embed)
+    )(latent, embed_part, gains, cos_t, sin_t, begin, adapter, qkv, out, extra)
 
 
 def ffn_kernel(sz, keep, *refs):
@@ -1032,8 +1100,13 @@
             cot_out.at[pl.ds(j * sz.block, sz.block)], cot_all.at[gather.own(j)], keep_sem.at[3 + j]
         )
 
+    rings = count - 1
+
+    def landing(w, c):
+        return c if w == rings else place.dp * n_c + c
+
     def move(w, g):
-        slot = place.dp * n_c + ctx
+        slot = landing(w, ctx)
         return pltpu.make_async_remote_copy(
             src_ref=blocks_in[w],
             dst_ref=blocks_out[w].at[slot],
@@ -1045,11 +1118,11 @@
 
     def stay(w):
         return pltpu.make_async_copy(
-            blocks_in[w], blocks_out[w].at[place.dp * n_c + ctx], own_sem.at[w]
+            blocks_in[w], blocks_out[w].at[landing(w, ctx)], own_sem.at[w]
         )
 
     def moved(w, c):
-        slot = place.dp * n_c + c
+        slot = landing(w, c)
         arrival = pltpu.make_async_remote_copy(
             src_ref=blocks_in[w],
             dst_ref=blocks_out[w].at[slot],
@@ -1183,10 +1256,10 @@
 
     embed_save = pltpu.make_async_copy(embed_s, embed_out, keep_sem.at[3 + sz.seqs])
     todo = []
-    for k in range(count + steps):
+    for k in range(rings + steps):
         for s in range(min(k, steps - 1), -1, -1):
             w = k - s
-            if w < count:
+            if w < rings:
                 todo.append((w, s))
     done = 0
     for w, s in todo:
@@ -1200,12 +1273,12 @@
             start_move(w + 2)
         if s == 0 and w >= 1:
             across_z()
-        if s == 0 and w == count - 2:
+        if s == 0 and w == rings - 1:
             for i in range(3):
                 swap(i).start()
         if done < steps:
             adapter_step(done)
-        if s == min(1, steps - 1) and w == count - 1:
+        if s == min(2, steps - 1) and w == rings - 1:
             for i in range(3):
                 keep(i).wait()
                 swapped(i).wait_recv()
@@ -1249,9 +1322,10 @@
             embed_part[...] += part_here
         else:
             embed_part[...] = part_here
-    for w in range(count):
-        for way in range(n_c):
+    for way in range(n_c):
+        for w in range(rings):
             hopped(w, way, steps - 1).wait_recv()
+        moved(rings, way)
     for j in range(sz.seqs):
         for q in range(1, half):
             gather.wait_far(q, j)
@@ -1263,7 +1337,7 @@
         for g in range(sz.seqs):
             here = at_home & (place.group == g)
             pl.when(jnp.logical_not(here))(lambda w=w, g=g: move(w, g).wait_send())
-        for way in range(n_c):
+        for way in range(n_c if w < rings else 0):
             for s in range(steps):
                 hop(w, way, s).wait_send()
     for s in range(steps):
@@ -1276,7 +1350,8 @@
 def run_weights(sz, n_dp, adapter, adapter_block, blocks, rows):
     bf16, f32 = jnp.bfloat16, jnp.float32
     slots = n_dp * sz.n_context
-    outs = [jax.ShapeDtypeStruct((slots,) + a.shape, bf16) for a in [adapter] + blocks]
+    outs = [jax.ShapeDtypeStruct((slots,) + a.shape, bf16) for a in [adapter] + blocks[:-1]]
+    outs.append(jax.ShapeDtypeStruct((sz.n_context,) + blocks[-1].shape, bf16))
     outs += [
         jax.ShapeDtypeStruct((sz.rows, sz.width), bf16),
         jax.ShapeDtypeStruct((sz.rows, sz.width), bf16),
@@ -2366,7 +2441,7 @@
         qkv_use,
         gate_use,
         up_use,
-        down_blocks,
+        down_pair,
         embed_rows,
         cot_rows,
         grad_ffn,
@@ -2396,7 +2471,6 @@
     )
     if out_blocks.shape[2] % 128:
         out_blocks = side_by_side(out_blocks)[None]
-        down_blocks = side_by_side(down_blocks)[None]
     gains_f = gains_full.astype(jnp.float32)
 
     cos_full, sin_full = rope_tables(seq_len, head_dim)
@@ -2405,11 +2479,18 @@
     begin = jnp.sum((docs[None, :] < docs[:, None]).astype(jnp.int32), axis=1)[None, :]
     steps_own = lax.dynamic_index_in_dim(recurrences, own_seq, 0, keepdims=False) - BACK
     active = jnp.arange(MAXR - BACK, dtype=jnp.int32)[:, None] < steps_own
+    active = jnp.broadcast_to(active.astype(jnp.float32), (MAXR - BACK, model_width))
+    mixed, down_blocks = run_attn(
+        sz, n_dp, False, current, embed_part, gains_f, cos_full, sin_full, begin,
+        adapter_all, qkv_use, out_blocks, down_pair,
+    )
+    if down_blocks.shape[2] % 128:
+        down_blocks = side_by_side(down_blocks)[None]
+    (current,) = run_ffn(
+        sz, False, mixed, current, active[:1], gains_f, gate_use, up_use, down_blocks
+    )
     detached = run_rounds(
-        sz,
-        current,
-        jnp.broadcast_to(active.astype(jnp.float32), (MAXR - BACK, model_width)),
-        gains_f, cos_full, sin_full, begin, embed_part,
+        sz, current, active[1:], gains_f, cos_full, sin_full, begin, embed_part,
         adapter_all, qkv_use, out_blocks, gate_use, up_use, down_blocks,
     )
     (mixed_rows, adapted, feature_rows, query_hm, key_hm, value_hm, head_flat, lse, joined) = run_attn(

time: 1160 us -> 1180 us (1.017)
  Pallas kernels: 1110 us -> 1130 us
    pallas_call x1, Pallas kernels: 312 us -> 220 us  [run_rounds(): pl.pallas_call(partial(rounds_kernel, sz, active.shape[0]), out_shape=jax...]
    pallas_call x1 -> x2, Pallas kernels: 60.5 us -> 126 us  [run_attn(): pl.pallas_call(partial(attn_kernel, sz, n_dp, keep), out_shape=outs, in_s...]
    pallas_call x1 -> x2, Pallas kernels: 52.9 us -> 106 us  [run_ffn(): pl.pallas_call(partial(ffn_kernel, sz, keep), out_shape=outs, in_specs=[f...]
where the time goes in v10:
time: 1180 us; the launch traced here: 1170 us
  Pallas kernels  1130 us (96%)
  local copies, waits for them, and re-layouts  27.7 us (2%)
    pallas_call x1, Pallas kernels, run_weights(): pl.pallas_call(partial(weights_kernel, sz, n_dp), out_shape=outs, in_spec...  289 us
    pallas_call x1, Pallas kernels, run_rounds(): pl.pallas_call(partial(rounds_kernel, sz, active.shape[0]), out_shape=jax...  220 us
    pallas_call x1, Pallas kernels, run_grads(): pl.pallas_call(partial(grads_kernel, sz, n_dp, count), out_shape=[shape((...  199 us
    pallas_call x2, Pallas kernels, run_attn(): pl.pallas_call(partial(attn_kernel, sz, n_dp, keep), out_shape=outs, in_s...  126 us
    pallas_call x1, Pallas kernels, run_attn_back(): pl.pallas_call(partial(attn_back_kernel, sz, n_dp), out_shape=[shape((sz....  111 us
    pallas_call x2, Pallas kernels, run_ffn(): pl.pallas_call(partial(ffn_kernel, sz, keep), out_shape=outs, in_specs=[f...  106 us
    pallas_call x1, Pallas kernels, run_ffn_back(): pl.pallas_call(partial(ffn_back_kernel, sz, n_dp), out_shape=[shape((sz.r...  79 us

profile of v10, /device:TPU:1, one launch (start us, length us, event | category | flops | bytes accessed | tf_op | source)
XLA Modules:
  0.0 1167.1 jit_solution(13640011450318272326)
XLA Ops:
  0.7 1.2 dynamic_slice.11
  5.2 2.1 copy.34
  7.3 3.4 fusion.1.refs_0_
  10.7 2.0 fusion.3
  12.8 1.3 copy_bitcast_fusion
  14.1 289.0 %weights.1 = (bf16[8,544,2048]{2,1,0:T(8,128)(2,1)}, bf16[8,512,256]{2,1,0:T(8,128)(2,1)}, bf16[8,256,1536]{2,1,0:T(8,128)(2,1)}, bf16[8,256,1408]{2,1,0:T(8,128...) custom-call(bf16[544,2048]{1,0:T(8,128)(2,1)} %fusion.1.refs_0_, ...), custom_call_target="tpu_custom_call" | custom-call | tf_op jit(solution)/shard_map/weights/pallas_call | solution.py:1364
  303.1 1.4 fusion.2
  305.0 64.9 %attn_round.1 = (f32[256,2048]{1,0:T(8,128)}, bf16[8,1408,256]{2,1,0:T(8,128)(2,1)}) custom-call(f32[256,2048]{1,0:T(8,128)} %get-tuple-element.56.refs_0_.refs_1_, f32[256,2048]{1,0:T(8,128)} %get-tuple-element.57.refs_1_.refs_6_, f32[2,2048]{1,0:T(2,128)} %bitcast.43, f32[1024,128]{1,0:T(8,128)} %constant.50.clone.refs_3_.refs_2_, ...), custom_call_target="tpu_custom_call" | custom-call | flops 8589934592 | bytes 20971520 | tf_op jit(solution)/shard_map/attn_round/pallas_call | solution.py:599
  369.9 53.3 %ffn_round.1.refs_5_ = f32[256,2048]{1,0:T(8,128)} custom-call(f32[256,2048]{1,0:T(8,128)} %get-tuple-element.61.refs_0_, f32[256,2048]{1,0:T(8,128)} %get-tuple-element.56.refs_0_.refs_1_, f32[1,2048]{1,0:T(1,128)} %broadcast_in_dim.29.refs_2_, f32[2,2048]{1,0:T(2,128)} %bitcast.44, bf16[2048,1408]{1,0:T(8,128)(2,1)} %bitcast.57, ...), custom_call_target="tpu_custom_call" | custom-call | flops 17716740096 | bytes 20971520 | tf_op jit(solution)/shard_map/ffn_round/pallas_call | solution.py:726
  423.2 220.1 %rounds.1.refs_0_.refs_1_ = f32[256,2048]{1,0:T(8,128)} custom-call(f32[2,2048]{1,0:T(2,128)} %broadcast_in_dim.27.refs_0_, f32[2,2048]{1,0:T(2,128)} %bitcast.45, f32[1024,128]{1,0:T(8,128)} %constant.50.clone.refs_3_.refs_2_, f32[1024,128]{1,0:T(8,128)} %constant.51.clone.refs_4_.refs_3_, s32[1,1024]{1,0:T(1,128)} %bitcast.52, ...), custom_call_target="tpu_custom_call" | custom-call | flops 70866960384 | bytes 83886080 | tf_op jit(solution)/shard_map/rounds/pallas_call | solution.py:962
  643.3 60.7 %attn_keep.1 = (f32[256,2048]{1,0:T(8,128)}, f32[256,2048]{1,0:T(8,128)}, bf16[1024,2048]{1,0:T(8,128)(2,1)}, bf16[4,1024,128]{2,1,0:T(8,128)(2,1)}, bf16[4,1024...) custom-call(f32[256,2048]{1,0:T(8,128)} %rounds.1.refs_0_.refs_1_, ...), custom_call_target="tpu_custom_call" | custom-call | flops 8589934592 | bytes 20971520 | tf_op jit(solution)/shard_map/attn_keep/pallas_call | solution.py:599
  704.0 53.0 %ffn_keep.1 = (f32[256,2048]{1,0:T(8,128)}, bf16[1024,2048]{1,0:T(8,128)(2,1)}, bf16[1024,1408]{1,0:T(8,128)(2,1)}, bf16[1024,1408]{1,0:T(8,128)(2,1)}, bf16[1024,1408]{1,0:T(8,128)(2,1)}) custom-call(f32[256,2048]{1,0:T(8,128)} %get-tuple-element.66.refs_0_.refs_1_, f32[256,2048]{1,0:T(8,128)} %rounds.1.refs_0_.refs_1_, f32[1,2048]{1,0:T(1,128)} %bitcast.55, ...), custom_call_target="tpu_custom_call" | custom-call | flops 17716740096 | bytes 20971520 | tf_op jit(solution)/shard_map/ffn_keep/pallas_call | solution.py:726
  757.0 79.0 %ffn_back.1 = (f32[256,2048]{1,0:T(8,128)}, f32[1,2048]{1,0:T(1,128)}, bf16[1024,1408]{1,0:T(8,128)(2,1)}, bf16[1024,1408]{1,0:T(8,128)(2,1)}, bf16[2,256,1408]{...) custom-call(bf16[256,2048]{1,0:T(8,128)(2,1)} %get-tuple-element.54.refs_0_, f32[256,2048]{1,0:T(8,128)} %get-tuple-element.66.refs_0_.refs_1_, ...), custom_call_target="tpu_custom_call" | custom-call | flops 23622320128 | bytes 41943040 | tf_op jit(solution)/shard_map/ffn_back/pallas_call | solution.py:1713
  836.0 111.3 %attn_back.1 = (bf16[272,2048]{1,0:T(8,128)(2,1)}, f32[256,1408]{1,0:T(8,128)}, f32[256,1408]{1,0:T(8,128)}, f32[2,128,2048]{2,1,0:T(8,128)}, bf16[1024,2048]{1,...) custom-call(f32[256,2048]{1,0:T(8,128)} %get-tuple-element.72.refs_0_, f32[2,2048]{1,0:T(2,128)} %bitcast.49, ...), custom_call_target="tpu_custom_call" | custom-call | flops 12884901888 | bytes 31457280 | tf_op jit(solution)/shard_map/attn_back/pallas_call | solution.py:1954
  947.4 198.9 %grads.1 = (f32[256,1408]{1,0:T(8,128)}, f32[256,1536]{1,0:T(8,128)}, f32[256,512]{1,0:T(8,128)}, f32[2,128,2048]{2,1,0:T(8,128)}, f32[512,2048]{1,0:T(8,128)}, ...) custom-call(bf16[272,2048]{1,0:T(8,128)(2,1)} %get-tuple-element.85.refs_0_, ...), custom_call_target="tpu_custom_call" | custom-call | flops 14495514624 | bytes 62914560 | tf_op jit(solution)/shard_map/grads/pallas_call | solution.py:2322
  1147.7 2.0 copy.31
  1149.7 1.5 pad_maximum_fusion
  1151.3 3.8 copy.29
  1155.1 1.5 copy.30
  1156.6 2.9 reshape.65
  1159.5 1.3 copy.40
  1161.9 1.3 copy.41
  1163.2 1.6 copy-done.3
  1164.8 2.0 copy.42
  (24 shorter events, 5.7 us)
Async XLA Ops:
  0.6 2.0 copy-start
  7.3 3.4 copy-start.2
  947.4 202.4 %copy-start.7 = (f32[256,1408]{1,0:T(8,128)S(1)}, f32[256,1408]{1,0:T(8,128)}, u32[]{:S(2)}) copy-start(f32[256,1408]{1,0:T(8,128)} %get-tuple-element.97) | copy-start | bytes 4325380
  1151.3 3.8 copy-start.6
  1156.6 2.9 copy-start.4
  1159.5 2.3 copy-start.5
  1161.9 2.9 copy-start.3
  1164.8 2.0 copy-start.1

commit v11 on v10

--- a/solution.py
+++ b/solution.py
@@ -1036,7 +1036,6 @@
     role = part * n_c + ctx
     at_home = role == t
     steps = n_dp - 1
-    sub = adapter_in.shape[0] // half
     ahead = 1 - 2 * ctx
 
     def holder(g):
@@ -1135,17 +1134,13 @@
         pl.when(here)(lambda: stay(w).wait())
         pl.when(jnp.logical_not(here))(lambda: arrival.wait_recv())
 
-    def adapter_rows(offset, c, p):
-        return adapter_out.at[
-            ring.index(offset) * n_c + c, pl.ds(pl.multiple_of(p * sub, sub), sub)
-        ]
-
-    own_rows = adapter_in.at[pl.ds(pl.multiple_of(part * sub, sub), sub)]
+    def adapter_rows(offset, c):
+        return adapter_out.at[ring.index(offset) * n_c + c]
 
     def around(s):
-        rows = adapter_rows(-ahead * s, ctx, part)
+        rows = adapter_rows(-ahead * s, ctx)
         return pltpu.make_async_remote_copy(
-            src_ref=own_rows if s == 0 else rows,
+            src_ref=adapter_in if s == 0 else rows,
             dst_ref=rows,
             send_sem=a_send.at[s],
             recv_sem=a_recv.at[s],
@@ -1153,35 +1148,24 @@
             device_id_type=MESH,
         )
 
-    def across(kind, s):
-        offset = -ahead * s
-        if kind < half:
-            dst = adapter_rows(offset, ctx, part)
-            src = own_rows if s == 0 else dst
-        else:
-            src = dst = adapter_rows(offset, ctx, place.behind(kind - half + 1))
-        target = place.device(place.ahead(kind), ctx) if 0 < kind < half else place.sibling()
+    def across(s):
+        rows = adapter_rows(-ahead * s, ctx)
         return pltpu.make_async_remote_copy(
-            src_ref=src,
-            dst_ref=dst,
-            send_sem=x_send.at[kind, s],
-            recv_sem=x_recv.at[kind, s],
-            device_id=target,
+            src_ref=adapter_in if s == 0 else rows,
+            dst_ref=rows,
+            send_sem=x_send.at[s],
+            recv_sem=x_recv.at[s],
+            device_id=place.sibling(),
             device_id_type=MESH,
         )
 
-    def crossed(kind, s):
-        if kind == 0:
-            rows = adapter_rows(ahead * s, 1 - ctx, part)
-        elif kind < half:
-            rows = adapter_rows(-ahead * s, ctx, place.behind(kind))
-        else:
-            rows = adapter_rows(ahead * s, 1 - ctx, place.behind(kind - half + 1))
+    def crossed(s):
+        rows = adapter_rows(ahead * s, 1 - ctx)
         return pltpu.make_async_remote_copy(
             src_ref=rows,
             dst_ref=rows,
-            send_sem=x_send.at[kind, s],
-            recv_sem=x_recv.at[kind, s],
+            send_sem=x_send.at[s],
+            recv_sem=x_recv.at[s],
             device_id=place.sibling(),
             device_id_type=MESH,
         )
@@ -1211,7 +1195,7 @@
         )
 
     around(0).start()
-    own = pltpu.make_async_copy(own_rows, adapter_rows(0, ctx, part), own_sem.at[count])
+    own = pltpu.make_async_copy(adapter_in, adapter_rows(0, ctx), own_sem.at[count])
     own.start()
 
     def start_move(w):
@@ -1222,37 +1206,22 @@
 
     start_move(0)
     start_move(1)
-    across(0, 0).start()
-    swaps = []
-
-    def across_z():
-        if swaps:
-            s = swaps.pop(0)
-            for q in range(1, half):
-                across(q, s).start()
-
-    swaps.append(0)
+    across(0).start()
 
     def adapter_step(s):
-        if s < steps:
-            arrival = pltpu.make_async_remote_copy(
-                src_ref=own_rows,
-                dst_ref=adapter_rows(-ahead * (s + 1), ctx, part),
-                send_sem=a_send.at[s],
-                recv_sem=a_recv.at[s],
-                device_id=ring.device(1),
-                device_id_type=MESH,
-            )
-            arrival.wait_recv()
-            if s + 1 < steps:
-                around(s + 1).start()
-            across(0, s + 1).start()
-            swaps.append(s + 1)
-
-    def adapter_pass(s):
-        for q in range(1, half):
-            crossed(q, s).wait_recv()
-            across(half - 1 + q, s).start()
+        rows = adapter_rows(-ahead * (s + 1), ctx)
+        arrival = pltpu.make_async_remote_copy(
+            src_ref=rows,
+            dst_ref=rows,
+            send_sem=a_send.at[s],
+            recv_sem=a_recv.at[s],
+            device_id=ring.device(1),
+            device_id_type=MESH,
+        )
+        arrival.wait_recv()
+        if s + 1 < steps:
+            around(s + 1).start()
+        across(s + 1).start()
 
     embed_save = pltpu.make_async_copy(embed_s, embed_out, keep_sem.at[3 + sz.seqs])
     todo = []
@@ -1269,16 +1238,16 @@
             else:
                 hopped(w, way, s - 1).wait_recv()
             hop(w, way, s).start()
-        if s == 0 and w + 2 < count:
+        if s == 0 and w + 2 < rings:
             start_move(w + 2)
-        if s == 0 and w >= 1:
-            across_z()
-        if s == 0 and w == rings - 1:
+        if s == 0 and w == rings - 2:
             for i in range(3):
                 swap(i).start()
+        if s == 0 and w == rings - 1:
+            start_move(rings)
         if done < steps:
             adapter_step(done)
-        if s == min(2, steps - 1) and w == rings - 1:
+        if s == min(1, steps - 1) and w == rings - 1:
             for i in range(3):
                 keep(i).wait()
                 swapped(i).wait_recv()
@@ -1292,18 +1261,12 @@
         done += 1
     for s in range(done, steps):
         adapter_step(s)
-    while swaps:
-        across_z()
-    for s in range(n_dp):
-        adapter_pass(s)
     for j in range(sz.seqs):
         gather.wait_near(j)
         for q in range(1, half):
             gather.forward(q, j)
     for s in range(n_dp):
-        crossed(0, s).wait_recv()
-        for q in range(1, half):
-            crossed(half - 1 + q, s).wait_recv()
+        crossed(s).wait_recv()
     own.wait()
     slots, depth = adapter_out.shape[0], weight_s.shape[1]
     loads = [
@@ -1343,8 +1306,7 @@
     for s in range(steps):
         around(s).wait_send()
     for s in range(n_dp):
-        for kind in range(2 * half - 1):
-            across(kind, s).wait_send()
+        across(s).wait_send()
 
 
 def run_weights(sz, n_dp, adapter, adapter_block, blocks, rows):
@@ -1360,7 +1322,6 @@
         jax.ShapeDtypeStruct((sz.rows, sz.width), f32),
     ]
     count, steps, dma = len(blocks), n_dp - 1, pltpu.SemaphoreType.DMA
-    kinds = 2 * sz.half - 1
     return pl.pallas_call(
         partial(weights_kernel, sz, n_dp),
         out_shape=outs,
@@ -1373,8 +1334,8 @@
             dma((count, sz.n_context, steps)),
             dma((steps,)),
             dma((steps,)),
-            dma((kinds, n_dp)),
-            dma((kinds, n_dp)),
+            dma((n_dp,)),
+            dma((n_dp,)),
             dma((count + 1,)),
             pltpu.VMEM((sz.rows, sz.width), bf16),
             pltpu.VMEM((sz.rows, sz.width), bf16),

time: 1180 us -> 1190 us (level)
  Pallas kernels: 1130 us -> 1150 us
where the time goes in v11:
time: 1190 us; the launch traced here: 1180 us
  Pallas kernels  1150 us (97%)
  local copies, waits for them, and re-layouts  27.7 us (2%)
    pallas_call x1, Pallas kernels, run_weights(): pl.pallas_call(partial(weights_kernel, sz, n_dp), out_shape=outs, in_spec...  300 us
    pallas_call x1, Pallas kernels, run_rounds(): pl.pallas_call(partial(rounds_kernel, sz, active.shape[0]), out_shape=jax...  219 us
    pallas_call x1, Pallas kernels, run_grads(): pl.pallas_call(partial(grads_kernel, sz, n_dp, count), out_shape=[shape((...  199 us
    pallas_call x2, Pallas kernels, run_attn(): pl.pallas_call(partial(attn_kernel, sz, n_dp, keep), out_shape=outs, in_s...  131 us
    pallas_call x1, Pallas kernels, run_attn_back(): pl.pallas_call(partial(attn_back_kernel, sz, n_dp), out_shape=[shape((sz....  114 us
    pallas_call x2, Pallas kernels, run_ffn(): pl.pallas_call(partial(ffn_kernel, sz, keep), out_shape=outs, in_specs=[f...  107 us
    pallas_call x1, Pallas kernels, run_ffn_back(): pl.pallas_call(partial(ffn_back_kernel, sz, n_dp), out_shape=[shape((sz.r...  78.6 us

profile of v11, /device:TPU:1, one launch (start us, length us, event | category | flops | bytes accessed | tf_op | source)
XLA Modules:
  0.0 1185.0 jit_solution(11353060138626232995)
XLA Ops:
  0.7 1.2 dynamic_slice.11
  5.2 2.1 copy.34
  7.3 3.4 fusion.1.refs_0_
  10.7 2.0 fusion.3
  12.8 1.3 copy_bitcast_fusion
  14.1 299.8 %weights.1 = (bf16[8,544,2048]{2,1,0:T(8,128)(2,1)}, bf16[8,512,256]{2,1,0:T(8,128)(2,1)}, bf16[8,256,1536]{2,1,0:T(8,128)(2,1)}, bf16[8,256,1408]{2,1,0:T(8,128...) custom-call(bf16[544,2048]{1,0:T(8,128)(2,1)} %fusion.1.refs_0_, ...), custom_call_target="tpu_custom_call" | custom-call | tf_op jit(solution)/shard_map/weights/pallas_call | solution.py:1325
  313.9 1.4 fusion.2
  315.9 70.6 %attn_round.1 = (f32[256,2048]{1,0:T(8,128)}, bf16[8,1408,256]{2,1,0:T(8,128)(2,1)}) custom-call(f32[256,2048]{1,0:T(8,128)} %get-tuple-element.56.refs_0_.refs_1_, f32[256,2048]{1,0:T(8,128)} %get-tuple-element.57.refs_1_.refs_6_, f32[2,2048]{1,0:T(2,128)} %bitcast.43, f32[1024,128]{1,0:T(8,128)} %constant.50.clone.refs_3_.refs_2_, ...), custom_call_target="tpu_custom_call" | custom-call | flops 8589934592 | bytes 20971520 | tf_op jit(solution)/shard_map/attn_round/pallas_call | solution.py:599
  386.4 53.9 %ffn_round.1.refs_5_ = f32[256,2048]{1,0:T(8,128)} custom-call(f32[256,2048]{1,0:T(8,128)} %get-tuple-element.61.refs_0_, f32[256,2048]{1,0:T(8,128)} %get-tuple-element.56.refs_0_.refs_1_, f32[1,2048]{1,0:T(1,128)} %broadcast_in_dim.29.refs_2_, f32[2,2048]{1,0:T(2,128)} %bitcast.44, bf16[2048,1408]{1,0:T(8,128)(2,1)} %bitcast.57, ...), custom_call_target="tpu_custom_call" | custom-call | flops 17716740096 | bytes 20971520 | tf_op jit(solution)/shard_map/ffn_round/pallas_call | solution.py:726
  440.4 219.3 %rounds.1.refs_0_.refs_1_ = f32[256,2048]{1,0:T(8,128)} custom-call(f32[2,2048]{1,0:T(2,128)} %broadcast_in_dim.27.refs_0_, f32[2,2048]{1,0:T(2,128)} %bitcast.45, f32[1024,128]{1,0:T(8,128)} %constant.50.clone.refs_3_.refs_2_, f32[1024,128]{1,0:T(8,128)} %constant.51.clone.refs_4_.refs_3_, s32[1,1024]{1,0:T(1,128)} %bitcast.52, ...), custom_call_target="tpu_custom_call" | custom-call | flops 70866960384 | bytes 83886080 | tf_op jit(solution)/shard_map/rounds/pallas_call | solution.py:962
  659.7 60.4 %attn_keep.1 = (f32[256,2048]{1,0:T(8,128)}, f32[256,2048]{1,0:T(8,128)}, bf16[1024,2048]{1,0:T(8,128)(2,1)}, bf16[4,1024,128]{2,1,0:T(8,128)(2,1)}, bf16[4,1024...) custom-call(f32[256,2048]{1,0:T(8,128)} %rounds.1.refs_0_.refs_1_, ...), custom_call_target="tpu_custom_call" | custom-call | flops 8589934592 | bytes 20971520 | tf_op jit(solution)/shard_map/attn_keep/pallas_call | solution.py:599
  720.1 53.1 %ffn_keep.1 = (f32[256,2048]{1,0:T(8,128)}, bf16[1024,2048]{1,0:T(8,128)(2,1)}, bf16[1024,1408]{1,0:T(8,128)(2,1)}, bf16[1024,1408]{1,0:T(8,128)(2,1)}, bf16[1024,1408]{1,0:T(8,128)(2,1)}) custom-call(f32[256,2048]{1,0:T(8,128)} %get-tuple-element.66.refs_0_.refs_1_, f32[256,2048]{1,0:T(8,128)} %rounds.1.refs_0_.refs_1_, f32[1,2048]{1,0:T(1,128)} %bitcast.55, ...), custom_call_target="tpu_custom_call" | custom-call | flops 17716740096 | bytes 20971520 | tf_op jit(solution)/shard_map/ffn_keep/pallas_call | solution.py:726
  773.2 78.6 %ffn_back.1 = (f32[256,2048]{1,0:T(8,128)}, f32[1,2048]{1,0:T(1,128)}, bf16[1024,1408]{1,0:T(8,128)(2,1)}, bf16[1024,1408]{1,0:T(8,128)(2,1)}, bf16[2,256,1408]{...) custom-call(bf16[256,2048]{1,0:T(8,128)(2,1)} %get-tuple-element.54.refs_0_, f32[256,2048]{1,0:T(8,128)} %get-tuple-element.66.refs_0_.refs_1_, ...), custom_call_target="tpu_custom_call" | custom-call | flops 23622320128 | bytes 41943040 | tf_op jit(solution)/shard_map/ffn_back/pallas_call | solution.py:1674
  851.9 113.6 %attn_back.1 = (bf16[272,2048]{1,0:T(8,128)(2,1)}, f32[256,1408]{1,0:T(8,128)}, f32[256,1408]{1,0:T(8,128)}, f32[2,128,2048]{2,1,0:T(8,128)}, bf16[1024,2048]{1,...) custom-call(f32[256,2048]{1,0:T(8,128)} %get-tuple-element.72.refs_0_, f32[2,2048]{1,0:T(2,128)} %bitcast.49, ...), custom_call_target="tpu_custom_call" | custom-call | flops 12884901888 | bytes 31457280 | tf_op jit(solution)/shard_map/attn_back/pallas_call | solution.py:1915
  965.4 198.7 %grads.1 = (f32[256,1408]{1,0:T(8,128)}, f32[256,1536]{1,0:T(8,128)}, f32[256,512]{1,0:T(8,128)}, f32[2,128,2048]{2,1,0:T(8,128)}, f32[512,2048]{1,0:T(8,128)}, ...) custom-call(bf16[272,2048]{1,0:T(8,128)(2,1)} %get-tuple-element.85.refs_0_, ...), custom_call_target="tpu_custom_call" | custom-call | flops 14495514624 | bytes 62914560 | tf_op jit(solution)/shard_map/grads/pallas_call | solution.py:2283
  1165.6 2.0 copy.31
  1167.6 1.5 pad_maximum_fusion
  1169.2 3.8 copy.29
  1173.0 1.5 copy.30
  1174.5 2.9 reshape.65
  1177.4 1.3 copy.40
  1179.8 1.3 copy.41
  1181.1 1.6 copy-done.3
  1182.7 2.0 copy.42
  (24 shorter events, 5.7 us)
Async XLA Ops:
  0.6 2.0 copy-start
  7.3 3.4 copy-start.2
  965.4 202.2 %copy-start.7 = (f32[256,1408]{1,0:T(8,128)S(1)}, f32[256,1408]{1,0:T(8,128)}, u32[]{:S(2)}) copy-start(f32[256,1408]{1,0:T(8,128)} %get-tuple-element.97) | copy-start | bytes 4325380
  1169.2 3.8 copy-start.6
  1174.5 2.9 copy-start.4
  1177.4 2.3 copy-start.5
  1179.8 2.9 copy-start.3
  1182.7 2.0 copy-start.1

commit v12 on v9

--- a/solution.py
+++ b/solution.py
@@ -1147,8 +1147,8 @@
             pl.when(jnp.logical_not(here))(lambda w=w, g=g: move(w, g).start())
         pl.when(at_home)(lambda w=w: stay(w).start())
 
-    start_move(0)
-    start_move(1)
+    for w in range(count):
+        start_move(w)
     across(0, 0).start()
     swaps = []
 
@@ -1196,8 +1196,6 @@
             else:
                 hopped(w, way, s - 1).wait_recv()
             hop(w, way, s).start()
-        if s == 0 and w + 2 < count:
-            start_move(w + 2)
         if s == 0 and w >= 1:
             across_z()
         if s == 0 and w == count - 2:
@@ -1837,7 +1835,7 @@
     state_keep.wait()
     adapted_load.wait()
     state_out[1 - place.group] = swap_in[...].astype(jnp.float32)
-    down_grad[...] = deliver.total(0)
+    down_grad[...] = jnp.transpose(deliver.total(0))
     gain_total = None
     for j in range(sz.seqs):
         span = slice(j * sz.block, (j + 1) * sz.block)
@@ -1880,7 +1878,7 @@
         partial(attn_back_kernel, sz, n_dp),
         out_shape=[
             shape((sz.rows + 16, sz.width), bf16),
-            shape(down_sum.shape[1:], f32),
+            shape(down_sum.shape[:0:-1], f32),
             shape(gate_part.shape[1:], f32),
             shape((sz.seqs, sz.block, sz.width), f32),
             shape((sz.seq_len, sz.width), bf16),
@@ -2084,6 +2082,7 @@
 def grads_kernel(sz, n_dp, count, *refs):
     n_in = 4 + 2 * count
     low, joined, adapter, up_part = refs[:4]
+    gate_grad, refs = refs[4], refs[:4] + refs[5:]
     xs, ys = refs[4 : 4 + count], refs[4 + count : n_in]
     outs = refs[n_in : n_in + count]
     embed_grad, adapter_out, gains_out, landed = refs[n_in + count : n_in + 4 + count]
@@ -2216,13 +2215,15 @@
     for k in range(SUM_PARTS):
         line.complete(k)
     saves = [
+        pltpu.make_async_copy(gate_grad, outs[0].at[0], out_sem.at[2]),
         pltpu.make_async_copy(adapter_grad.at[pl.ds(0, depth)], adapter_out, out_sem.at[0]),
         pltpu.make_async_copy(adapter_grad.at[pl.ds(depth, 16)], gains_out, out_sem.at[1]),
     ]
     for copy in saves:
         copy.start()
-    for w in range(count):
-        outs[w][...] = deliver.total(w)
+    outs[0][1] = deliver.total(0)
+    outs[1][...] = deliver.total(1)
+    outs[2][...] = jnp.transpose(deliver.total(2))
     for copy in saves:
         copy.wait()
     grads.finish()
@@ -2236,7 +2237,7 @@
     return [(0, s) for s in range(2, n_dp)] + others
 
 
-def run_grads(sz, n_dp, low, joined, adapter, up_part, xs, ys):
+def run_grads(sz, n_dp, low, joined, adapter, up_part, gate_grad, xs, ys):
     count, bf16, f32, dma = len(xs), jnp.bfloat16, jnp.float32, pltpu.SemaphoreType.DMA
     shape = jax.ShapeDtypeStruct
     depth = sz.width // (n_dp * sz.n_context)
@@ -2246,14 +2247,18 @@
     total_rows = -(-(columns + 16) // unit) * unit
     return pl.pallas_call(
         partial(grads_kernel, sz, n_dp, count),
-        out_shape=[shape((depth, n), f32) for n in wide]
+        out_shape=[
+            shape((2, depth, wide[0]), f32),
+            shape((depth, wide[1]), f32),
+            shape((wide[2], depth), f32),
+        ]
         + [
             shape((sz.seqs, sz.block, sz.width), f32),
             shape((columns, sz.width), f32),
             shape((16, sz.width), f32),
             shape((slots,) + low.shape, bf16),
         ],
-        in_specs=[full_spec()] + [any_spec()] * (3 + 2 * count),
+        in_specs=[full_spec()] + [any_spec()] * (4 + 2 * count),
         out_specs=[full_spec()] * (1 + count) + [any_spec()] * 3,
         scratch_shapes=GradRing.scratch(sz, n_dp, grads_tasks(n_dp, count), wide)
         + Deliver.scratch(sz, n_dp, wide)
@@ -2270,7 +2275,7 @@
             dma((n_dp,)),
             dma,
             dma((2,)),
-            dma((2,)),
+            dma((3,)),
         ],
         compiler_params=pltpu.CompilerParams(
             collective_id=8, has_side_effects=True, vmem_limit_bytes=VMEM_BYTES
@@ -2279,7 +2284,7 @@
             flops=2 * sz.seq_len * sz.width * sum(wide), bytes_accessed=60 << 20, transcendentals=0
         ),
         name="grads",
-    )(low, joined, adapter, up_part, *[slot_columns(sz, n_dp, x) for x in xs], *ys)
+    )(low, joined, adapter, up_part, gate_grad, *[slot_columns(sz, n_dp, x) for x in xs], *ys)
 
 
 def shards(
@@ -2423,27 +2428,27 @@
         sz, n_dp, cot_rows, mixed_rows, gains_f, grad_ffn, gate_pre, up_pre,
         gate_use, up_use, down_blocks, ffn_input, hidden,
     )
-    grad_low, down_t, gate_s, state_out, grad_rows, grad_proj, up_part = run_attn_back(
+    grad_low, down_s, gate_s, state_out, grad_rows, grad_proj, up_part = run_attn_back(
         sz, n_dp, grad_mixed, adapted, gains_f, cos_full, sin_full, begin, gain_b, current,
         query_hm, key_hm, value_hm, lse, out_blocks, qkv_use, ffn_input, grad_gate, grad_up, down_sum,
         gate_part,
     )
-    up_s, qkv_s, out_t, embed_out, adapter_s, gains_rows, _ = run_grads(
+    pair_s, qkv_s, out_s, embed_out, adapter_s, gains_rows, _ = run_grads(
         sz,
         n_dp,
         grad_low,
         joined,
         adapter_all,
         up_part,
+        gate_s,
         [ffn_input, feature_rows, grad_rows],
         [grad_up, grad_proj, head_flat],
     )
     place_at = (dp_index * n_context + ctx_index) * gain_columns
     gains_s = lax.dynamic_slice_in_dim(gains_rows[:2], place_at, gain_columns, 1)
-    down_s = down_t.T
-    out_s = out_t.T.reshape(heads_here, head_dim, -1)
+    out_s = out_s.reshape(heads_here, head_dim, -1)
     qkv_s = qkv_s.reshape(-1, heads_here, 3 * head_dim)
-    gate_up_s = jnp.stack([gate_s, up_s], axis=1)
+    gate_up_s = pair_s.transpose(1, 0, 2)
     return (state_out, embed_out, adapter_s, gains_s, qkv_s, out_s, gate_up_s, down_s)
 
 

time: 1160 us -> 1150 us (level)
  no operation moved by 1% of the time
where the time goes in v12:
time: 1150 us; the launch traced here: 1140 us
  Pallas kernels  1110 us (97%)
  local copies, waits for them, and re-layouts  25.5 us (2%)
    pallas_call x1, Pallas kernels, run_rounds(): pl.pallas_call(partial(rounds_kernel, sz, active.shape[0]), out_shape=jax...  312 us
    pallas_call x1, Pallas kernels, run_weights(): pl.pallas_call(partial(weights_kernel, sz, n_dp), out_shape=outs, in_spec...  285 us
    pallas_call x1, Pallas kernels, run_grads(): pl.pallas_call(partial(grads_kernel, sz, n_dp, count), out_shape=[shape((...  199 us
    pallas_call x1, Pallas kernels, run_attn_back(): pl.pallas_call(partial(attn_back_kernel, sz, n_dp), out_shape=[shape((sz....  118 us
    pallas_call x1, Pallas kernels, run_ffn_back(): pl.pallas_call(partial(ffn_back_kernel, sz, n_dp), out_shape=[shape((sz.r...  78 us
    pallas_call x1, Pallas kernels, run_attn(): pl.pallas_call(partial(attn_kernel, sz, n_dp, keep), out_shape=outs, in_s...  61.6 us
    pallas_call x1, Pallas kernels, run_ffn(): pl.pallas_call(partial(ffn_kernel, sz, keep), out_shape=outs, in_specs=[f...  53 us

profile of v12, /device:TPU:1, one launch (start us, length us, event | category | flops | bytes accessed | tf_op | source)
XLA Modules:
  0.0 1140.1 jit_solution(11997842347863503673)
XLA Ops:
  0.7 1.2 dynamic_slice.11
  2.6 1.2 convert_reduce_fusion
  4.5 2.1 copy.29
  6.7 3.4 fusion.1.refs_0_
  10.1 2.0 fusion.3
  12.1 1.3 copy_bitcast_fusion
  13.4 284.7 %weights.1 = (bf16[8,544,2048]{2,1,0:T(8,128)(2,1)}, bf16[8,512,256]{2,1,0:T(8,128)(2,1)}, bf16[8,256,1536]{2,1,0:T(8,128)(2,1)}, bf16[8,256,1408]{2,1,0:T(8,128...) custom-call(bf16[544,2048]{1,0:T(8,128)(2,1)} %fusion.1.refs_0_, ...), custom_call_target="tpu_custom_call" | custom-call | tf_op jit(solution)/shard_map/weights/pallas_call | solution.py:1287
  298.1 1.4 fusion.2
  300.1 312.2 %rounds.1.refs_0_.refs_1_ = f32[256,2048]{1,0:T(8,128)} custom-call(f32[3,2048]{1,0:T(4,128)} %broadcast_in_dim.12.refs_0_, f32[2,2048]{1,0:T(2,128)} %bitcast.32, f32[1024,128]{1,0:T(8,128)} %constant.50.clone.refs_2_.refs_3_, f32[1024,128]{1,0:T(8,128)} %constant.51.clone.refs_3_.refs_4_, s32[1,1024]{1,0:T(1,128)} %bitcast.38, ...), custom_call_target="tpu_custom_call" | custom-call | flops 70866960384 | bytes 83886080 | tf_op jit(solution)/shard_map/rounds/pallas_call | solution.py:894
  612.3 61.6 %attn_keep.1 = (f32[256,2048]{1,0:T(8,128)}, f32[256,2048]{1,0:T(8,128)}, bf16[1024,2048]{1,0:T(8,128)(2,1)}, bf16[4,1024,128]{2,1,0:T(8,128)(2,1)}, bf16[4,1024...) custom-call(f32[256,2048]{1,0:T(8,128)} %rounds.1.refs_0_.refs_1_, ...), custom_call_target="tpu_custom_call" | custom-call | flops 8589934592 | bytes 20971520 | tf_op jit(solution)/shard_map/attn_keep/pallas_call | solution.py:531
  674.0 53.0 %ffn_keep.1 = (f32[256,2048]{1,0:T(8,128)}, bf16[1024,2048]{1,0:T(8,128)(2,1)}, bf16[1024,1408]{1,0:T(8,128)(2,1)}, bf16[1024,1408]{1,0:T(8,128)(2,1)}, bf16[1024,1408]{1,0:T(8,128)(2,1)}) custom-call(f32[256,2048]{1,0:T(8,128)} %get-tuple-element.62.refs_0_.refs_1_, f32[256,2048]{1,0:T(8,128)} %rounds.1.refs_0_.refs_1_, f32[1,2048]{1,0:T(1,128)} %bitcast.41, ...), custom_call_target="tpu_custom_call" | custom-call | flops 17716740096 | bytes 20971520 | tf_op jit(solution)/shard_map/ffn_keep/pallas_call | solution.py:658
  726.9 78.0 %ffn_back.1 = (f32[256,2048]{1,0:T(8,128)}, f32[1,2048]{1,0:T(1,128)}, bf16[1024,1408]{1,0:T(8,128)(2,1)}, bf16[1024,1408]{1,0:T(8,128)(2,1)}, bf16[2,256,1408]{...) custom-call(bf16[256,2048]{1,0:T(8,128)(2,1)} %get-tuple-element.52.refs_0_, f32[256,2048]{1,0:T(8,128)} %get-tuple-element.62.refs_0_.refs_1_, ...), custom_call_target="tpu_custom_call" | custom-call | flops 23622320128 | bytes 41943040 | tf_op jit(solution)/shard_map/ffn_back/pallas_call | solution.py:1636
  804.9 118.2 %attn_back.1 = (bf16[272,2048]{1,0:T(8,128)(2,1)}, f32[1408,256]{1,0:T(8,128)}, f32[256,1408]{1,0:T(8,128)}, f32[2,128,2048]{2,1,0:T(8,128)}, bf16[1024,2048]{1,...) custom-call(f32[256,2048]{1,0:T(8,128)} %get-tuple-element.68.refs_0_, f32[2,2048]{1,0:T(2,128)} %bitcast.36, ...), custom_call_target="tpu_custom_call" | custom-call | flops 12884901888 | bytes 31457280 | tf_op jit(solution)/shard_map/attn_back/pallas_call | solution.py:1877
  923.1 199.3 %grads.1 = (f32[2,256,1408]{2,1,0:T(8,128)}, f32[256,1536]{1,0:T(8,128)}, f32[512,256]{1,0:T(8,128)}, f32[2,128,2048]{2,1,0:T(8,128)}, f32[512,2048]{1,0:T(8,128...) custom-call(bf16[272,2048]{1,0:T(8,128)(2,1)} %get-tuple-element.81.refs_0_, ...), custom_call_target="tpu_custom_call" | custom-call | flops 14495514624 | bytes 62914560 | tf_op jit(solution)/shard_map/grads/pallas_call | solution.py:2248
  1122.4 1.0 slice.23
  1124.0 2.7 reshape.56
  1126.7 3.8 copy.26
  1130.5 1.3 copy.37
  1131.9 1.0 copy-done.6
  1132.9 1.3 copy.38
  1134.2 1.6 copy-done.3
  1135.8 2.1 copy.39
  1138.0 0.8 copy.40
  1138.8 1.1 copy.41
  (21 shorter events, 2.0 us)
Async XLA Ops:
  0.6 1.9 copy-start
  6.7 3.4 copy-start.2
  1122.4 4.3 copy-start.4
  1126.7 3.8 copy-start.5
  1130.5 2.3 copy-start.6
  1132.9 2.9 copy-start.3
  1135.8 2.1 copy-start.8
  1135.8 3.0 copy-start.7
  1135.8 4.0 copy-start.1

commit v13 on v12

--- a/solution.py
+++ b/solution.py
@@ -2076,7 +2076,7 @@
                 self.collect(q, k).wait_send()
 
 
-SUM_PARTS = 2
+SUM_PARTS = 3
 
 
 def grads_kernel(sz, n_dp, count, *refs):

time: 1150 us -> 1150 us (level)
  no operation moved by 1% of the time
where the time goes in v13:
time: 1150 us; the launch traced here: 1140 us
  Pallas kernels  1110 us (97%)
  local copies, waits for them, and re-layouts  25.5 us (2%)
    pallas_call x1, Pallas kernels, run_rounds(): pl.pallas_call(partial(rounds_kernel, sz, active.shape[0]), out_shape=jax...  312 us
    pallas_call x1, Pallas kernels, run_weights(): pl.pallas_call(partial(weights_kernel, sz, n_dp), out_shape=outs, in_spec...  285 us
    pallas_call x1, Pallas kernels, run_grads(): pl.pallas_call(partial(grads_kernel, sz, n_dp, count), out_shape=[shape((...  199 us
    pallas_call x1, Pallas kernels, run_attn_back(): pl.pallas_call(partial(attn_back_kernel, sz, n_dp), out_shape=[shape((sz....  118 us
    pallas_call x1, Pallas kernels, run_ffn_back(): pl.pallas_call(partial(ffn_back_kernel, sz, n_dp), out_shape=[shape((sz.r...  78 us
    pallas_call x1, Pallas kernels, run_attn(): pl.pallas_call(partial(attn_kernel, sz, n_dp, keep), out_shape=outs, in_s...  61.6 us
    pallas_call x1, Pallas kernels, run_ffn(): pl.pallas_call(partial(ffn_kernel, sz, keep), out_shape=outs, in_specs=[f...  53 us

profile of v13, /device:TPU:1, one launch (start us, length us, event | category | flops | bytes accessed | tf_op | source)
XLA Modules:
  0.0 1140.0 jit_solution(14944693151150964280)
XLA Ops:
  0.7 1.2 dynamic_slice.11
  2.6 1.2 convert_reduce_fusion
  4.5 2.1 copy.29
  6.7 3.4 fusion.1.refs_0_
  10.1 2.0 fusion.3
  12.1 1.3 copy_bitcast_fusion
  13.4 284.7 %weights.1 = (bf16[8,544,2048]{2,1,0:T(8,128)(2,1)}, bf16[8,512,256]{2,1,0:T(8,128)(2,1)}, bf16[8,256,1536]{2,1,0:T(8,128)(2,1)}, bf16[8,256,1408]{2,1,0:T(8,128...) custom-call(bf16[544,2048]{1,0:T(8,128)(2,1)} %fusion.1.refs_0_, ...), custom_call_target="tpu_custom_call" | custom-call | tf_op jit(solution)/shard_map/weights/pallas_call | solution.py:1287
  298.1 1.4 fusion.2
  300.1 312.2 %rounds.1.refs_0_.refs_1_ = f32[256,2048]{1,0:T(8,128)} custom-call(f32[3,2048]{1,0:T(4,128)} %broadcast_in_dim.12.refs_0_, f32[2,2048]{1,0:T(2,128)} %bitcast.32, f32[1024,128]{1,0:T(8,128)} %constant.50.clone.refs_2_.refs_3_, f32[1024,128]{1,0:T(8,128)} %constant.51.clone.refs_3_.refs_4_, s32[1,1024]{1,0:T(1,128)} %bitcast.38, ...), custom_call_target="tpu_custom_call" | custom-call | flops 70866960384 | bytes 83886080 | tf_op jit(solution)/shard_map/rounds/pallas_call | solution.py:894
  612.3 61.6 %attn_keep.1 = (f32[256,2048]{1,0:T(8,128)}, f32[256,2048]{1,0:T(8,128)}, bf16[1024,2048]{1,0:T(8,128)(2,1)}, bf16[4,1024,128]{2,1,0:T(8,128)(2,1)}, bf16[4,1024...) custom-call(f32[256,2048]{1,0:T(8,128)} %rounds.1.refs_0_.refs_1_, ...), custom_call_target="tpu_custom_call" | custom-call | flops 8589934592 | bytes 20971520 | tf_op jit(solution)/shard_map/attn_keep/pallas_call | solution.py:531
  674.0 53.0 %ffn_keep.1 = (f32[256,2048]{1,0:T(8,128)}, bf16[1024,2048]{1,0:T(8,128)(2,1)}, bf16[1024,1408]{1,0:T(8,128)(2,1)}, bf16[1024,1408]{1,0:T(8,128)(2,1)}, bf16[1024,1408]{1,0:T(8,128)(2,1)}) custom-call(f32[256,2048]{1,0:T(8,128)} %get-tuple-element.62.refs_0_.refs_1_, f32[256,2048]{1,0:T(8,128)} %rounds.1.refs_0_.refs_1_, f32[1,2048]{1,0:T(1,128)} %bitcast.41, ...), custom_call_target="tpu_custom_call" | custom-call | flops 17716740096 | bytes 20971520 | tf_op jit(solution)/shard_map/ffn_keep/pallas_call | solution.py:658
  726.9 78.0 %ffn_back.1 = (f32[256,2048]{1,0:T(8,128)}, f32[1,2048]{1,0:T(1,128)}, bf16[1024,1408]{1,0:T(8,128)(2,1)}, bf16[1024,1408]{1,0:T(8,128)(2,1)}, bf16[2,256,1408]{...) custom-call(bf16[256,2048]{1,0:T(8,128)(2,1)} %get-tuple-element.52.refs_0_, f32[256,2048]{1,0:T(8,128)} %get-tuple-element.62.refs_0_.refs_1_, ...), custom_call_target="tpu_custom_call" | custom-call | flops 23622320128 | bytes 41943040 | tf_op jit(solution)/shard_map/ffn_back/pallas_call | solution.py:1636
  804.9 118.2 %attn_back.1 = (bf16[272,2048]{1,0:T(8,128)(2,1)}, f32[1408,256]{1,0:T(8,128)}, f32[256,1408]{1,0:T(8,128)}, f32[2,128,2048]{2,1,0:T(8,128)}, bf16[1024,2048]{1,...) custom-call(f32[256,2048]{1,0:T(8,128)} %get-tuple-element.68.refs_0_, f32[2,2048]{1,0:T(2,128)} %bitcast.36, ...), custom_call_target="tpu_custom_call" | custom-call | flops 12884901888 | bytes 31457280 | tf_op jit(solution)/shard_map/attn_back/pallas_call | solution.py:1877
  923.1 199.2 %grads.1 = (f32[2,256,1408]{2,1,0:T(8,128)}, f32[256,1536]{1,0:T(8,128)}, f32[512,256]{1,0:T(8,128)}, f32[2,128,2048]{2,1,0:T(8,128)}, f32[512,2048]{1,0:T(8,128...) custom-call(bf16[272,2048]{1,0:T(8,128)(2,1)} %get-tuple-element.81.refs_0_, ...), custom_call_target="tpu_custom_call" | custom-call | flops 14495514624 | bytes 62914560 | tf_op jit(solution)/shard_map/grads/pallas_call | solution.py:2248
  1122.4 1.0 slice.23
  1123.9 2.7 reshape.56
  1126.7 3.8 copy.26
  1130.5 1.3 copy.37
  1131.8 1.0 copy-done.6
  1132.8 1.3 copy.38
  1134.1 1.6 copy-done.3
  1135.8 2.1 copy.39
  1137.9 0.8 copy.40
  1138.7 1.1 copy.41
  (21 shorter events, 2.0 us)
Async XLA Ops:
  0.6 1.9 copy-start
  6.7 3.4 copy-start.2
  1122.3 4.3 copy-start.4
  1126.7 3.8 copy-start.5
  1130.5 2.3 copy-start.6
  1132.8 2.9 copy-start.3
  1135.8 2.1 copy-start.8
  1135.8 3.0 copy-start.7
  1135.8 4.0 copy-start.1
